TPU v7x, 32 devices: a whole 2x2x4 slice. The times are simulated.
32 devices in a mesh: tm: 4 (over z), space: 8 (over y, x, core).
Axes of the slice: x: 2, y: 2, z: 4, core: 2. Of those that a mesh axis runs over, the one named last changes fastest.
Arguments:
- forcing: float32 [4, 2, 64, 1024], P('tm', None, None, 'space'), may hold values from -6 to 6
- initial_state: float32 [2, 64, 1024], P(None, None, 'space'), may hold values from -6 to 6
- previous: float32 [4, 2, 64, 1024], P('tm', None, None, 'space'), may hold values from -60 to 60
- zone_diffusion: float32 [2, 8], replicated, may hold values from 0.2 to 5
- drift_rate: float32 [2], replicated, may hold values from 0.2 to 1
- column_zone: int32 [1024], P('space'), may hold values from 0 to 7
- bottom_flag: int32 [1024], P('space'), may hold values 0 or 1
- open_faces: int32 [64, 1024], P(None, 'space'), may hold values 0 or 1
Outputs:
- new_iterate: float32 [4, 2, 64, 1024], P('tm', None, None, 'space')
- increment_norm: float32 [], replicated
All inputs are finite; a program needn't handle non-finite values. No bound on the sum of `bottom_flag` or of `open_faces` on one device may be relied on, other than what follows from the above.
Results may differ from a plain program's by a relative error of at most 0.00015.
Values sent between devices are 32-bit elements; how exact they have to be, the bound alone decides.
No kernel may reach another device: no remote copies, remote signals or barrier semaphores. Data moves between devices by JAX's collectives and lax.ppermute only.
A program may use at most 64 MiB of HBM per device.

v0:
```python
import math

import jax
import jax.numpy as jnp
from jax import lax
from jax.sharding import PartitionSpec as P

alpha_corner = 0.3
highest = lax.Precision.HIGHEST


def broadcast(block, axis, owner):
    block = jnp.where(lax.axis_index(axis) == owner, block, jnp.zeros_like(block))
    return lax.psum(block, axis)


def coefficients(zone_diffusion, drift_rate, column_zone, bottom_flag, open_faces):
    zone_count = zone_diffusion.shape[1]
    zone_hot = (column_zone[None, :] == jnp.arange(zone_count, dtype=jnp.int32)[:, None]).astype(
        jnp.float32
    )
    spread = jnp.dot(zone_diffusion, zone_hot, precision=highest)
    face_open = open_faces.astype(jnp.float32)
    empty_row = jnp.zeros_like(face_open[:1])
    link_below = jnp.concatenate([empty_row, face_open[:-1]], 0)
    link_above = jnp.concatenate([face_open[:-1], empty_row], 0)
    ground = jnp.concatenate(
        [bottom_flag.astype(jnp.float32)[None], jnp.zeros_like(face_open[1:])], 0
    )
    diffusion = spread[:, None, :]
    drift = drift_rate[:, None, None]
    below = -(diffusion + drift) * link_below
    above = -diffusion * link_above
    centre = diffusion * (link_below + link_above) + drift + 2.0 * diffusion * ground
    return (below, centre, above)


def line_solve(below, centre, shift_imag, above, right_real, right_imag):
    moved = [jnp.moveaxis(item, -2, 0) for item in (below, centre, above, right_real, right_imag)]
    empty_field = jnp.zeros_like(moved[3][0])

    def forward(running, item):
        prime_real, prime_imag, partial_real, partial_imag = running
        lower_coef, centre_coef, upper_coef, rhs_real, rhs_imag = item
        denom_real = centre_coef - lower_coef * prime_real
        denom_imag = shift_imag - lower_coef * prime_imag
        inverse = 1.0 / (denom_real * denom_real + denom_imag * denom_imag)
        next_prime_real = upper_coef * denom_real * inverse
        next_prime_imag = -upper_coef * denom_imag * inverse
        numer_real = rhs_real - lower_coef * partial_real
        numer_imag = rhs_imag - lower_coef * partial_imag
        next_real = (numer_real * denom_real + numer_imag * denom_imag) * inverse
        next_imag = (numer_imag * denom_real - numer_real * denom_imag) * inverse
        result = (next_prime_real, next_prime_imag, next_real, next_imag)
        return (result, result)

    start_state = (empty_field, empty_field, empty_field, empty_field)
    unused, stacked = lax.scan(forward, start_state, tuple(moved))

    def backward(value, item):
        prime_real, prime_imag, partial_real, partial_imag = item
        new_real = partial_real - (prime_real * value[0] - prime_imag * value[1])
        new_imag = partial_imag - (prime_real * value[1] + prime_imag * value[0])
        return ((new_real, new_imag), (new_real, new_imag))

    unused_back, solved = lax.scan(backward, (empty_field, empty_field), stacked, reverse=True)
    return (jnp.moveaxis(solved[0], 0, -2), jnp.moveaxis(solved[1], 0, -2))


def shards(
    forcing,
    initial_state,
    previous,
    zone_diffusion,
    drift_rate,
    column_zone,
    bottom_flag,
    open_faces,
):
    length = lax.axis_size("tm")
    tm_index = lax.axis_index("tm")
    turn_unit = 2.0 * math.pi / length
    log_alpha = math.log(alpha_corner)
    root_factor = math.exp(log_alpha / length)
    last_step = broadcast(previous[0], "tm", length - 1)
    correction = initial_state - alpha_corner * last_step
    ramp_up = jnp.exp(log_alpha * tm_index.astype(jnp.float32) / length)
    scaled = forcing[0] * ramp_up
    below, centre, above = coefficients(
        zone_diffusion, drift_rate, column_zone, bottom_flag, open_faces
    )
    empty_field = jnp.zeros_like(scaled)
    shard_rows = lax.all_gather(scaled[None], "tm", axis=0, tiled=True)
    piece_rows = shard_rows.shape[0]
    time_ids = jnp.arange(piece_rows, dtype=jnp.int32)
    phases = (time_ids * tm_index % length).astype(jnp.float32) * turn_unit
    real_part = jnp.einsum("n,nscz->scz", jnp.cos(phases), shard_rows, precision=highest)
    imag_part = (empty_field, empty_field)[1] - jnp.einsum(
        "n,nscz->scz", jnp.sin(phases), shard_rows, precision=highest
    )
    spectrum_real = real_part
    spectrum_real = spectrum_real + correction
    freq_angle = tm_index.astype(jnp.float32) * turn_unit
    shift_real = 1.0 - root_factor * jnp.cos(freq_angle)
    shift_imag = root_factor * jnp.sin(freq_angle)
    back_real, back_imag = line_solve(
        below, centre + shift_real, shift_imag, above, spectrum_real, imag_part
    )
    shard_rows = (
        lax.all_gather(back_real[None], "tm", axis=0, tiled=True),
        lax.all_gather(back_imag[None], "tm", axis=0, tiled=True),
    )
    piece_rows = shard_rows[0].shape[0]
    freq_ids = jnp.arange(piece_rows, dtype=jnp.int32)
    phases = (freq_ids * tm_index % length).astype(jnp.float32) * turn_unit
    cosine_part = jnp.einsum("n,nscz->scz", jnp.cos(phases), shard_rows[0], precision=highest)
    sine_part = jnp.einsum("n,nscz->scz", jnp.sin(phases), shard_rows[1], precision=highest)
    restored = (cosine_part - sine_part) / length
    ramp_down = jnp.exp(-log_alpha * tm_index.astype(jnp.float32) / length)
    new_iterate = restored * ramp_down
    change = new_iterate - previous[0]
    total = lax.psum(jnp.sum(change * change), ("tm", "space"))
    entry_count = (
        length * change.shape[0] * change.shape[1] * change.shape[2] * lax.axis_size("space")
    )
    increment_norm = jnp.sqrt(total / entry_count)
    return (new_iterate[None], increment_norm)


def solution(mesh):
    placed = (
        P("tm", None, None, "space"),
        P(None, None, "space"),
        P("tm", None, None, "space"),
        P(),
        P(),
        P("space"),
        P("space"),
        P(None, "space"),
    )
    return jax.shard_map(
        shards,
        mesh=mesh,
        in_specs=placed,
        out_specs=(P("tm", None, None, "space"), P()),
        check_vma=False,
    )
```

profile of v0, /device:TPU:0, one launch (start us, length us, event | category | flops | bytes accessed | tf_op | source)
XLA Modules:
  0.0 140.4 jit_solution(5228346454077490457)
XLA Ops:
  7.2 0.0 copy-start
  7.2 0.0 all-reduce.4.cloned.1.call-start
  7.2 1.5 %bitcast_select_fusion = f32[2,64,128]{2,1,0:T(8,128)} fusion(f32[1,2,64,128]{3,2,1,0:T(8,128)} %param.14, pred[]{:T(512)S(6)} %eq.22), kind=kLoop, calls=%fused_computation.47 | loop fusion | flops 16384 | bytes 131073 | tf_op jit(solution)/shard_map/jit(_where)/select_n | solution.py:13
  8.7 0.0 all-reduce.4.cloned.1.call-update
  8.8 0.8 copy-done.3
  9.6 16.0 %all_gather.9 = f32[4,2,64,128]{3,2,1,0:T(8,128)S(1)} all-gather(f32[1,2,64,128]{3,2,1,0:T(8,128)S(1)} %broadcast_multiply_fusion), channel_id=1, replica_groups=mesh['tm'=4,'space'=8] {'tm'}, dimensions={0}, use_global_device_ids=true | all-gather | bytes 327680 | tf_op jit(solution)/shard_map/all_gather | solution.py:93
  25.5 0.7 fusion.16
  26.2 0.0 copy-start.2
  26.3 0.7 fusion.14
  27.0 0.0 copy-done.2
  27.0 0.0 copy-start.7
  27.1 0.6 copy-done.7
  27.7 0.0 copy-start.6
  27.7 0.6 copy-done.6
  28.4 0.1 pad_add_fusion
  28.5 0.0 copy-start.8
  28.5 0.6 copy-done.5
  29.1 0.0 copy-done.8
  29.1 0.1 add_negate_fusion
  29.2 0.2 add_add_fusion
  29.4 0.0 copy-start.4
  29.6 18.0 %all-reduce.4.cloned.1.call-done = f32[2,64,128]{2,1,0:T(8,128)} async-done(((f32[2,64,128]{2,1,0:T(8,128)}), f32[2,64,128]{2,1,0:T(8,128)}) %all-reduce.4.cloned.1.call-update) | async-done | bytes 65552 | tf_op jit(solution)/shard_map/psum | solution.py:14
  47.6 0.9 add_bitcast_fusion
  48.5 6.0 %while.46 = (s32[]{:T(128)}, f32[2,128]{1,0:T(2,128)S(1)}, f32[2,128]{1,0:T(2,128)S(1)}, f32[2,128]{1,0:T(2,128)S(1)}, f32[2,128]{1,0:T(2,128)S(1)}, /*index=5*/...) while((s32[]{:T(128)}, f32[2,128]{1,0:T(2,128)S(1)}, ...), condition=%wide.region_2.3_spmd.clone, body=%wide.region_1.2_spmd.clone.sunk | while | flops 8451 | bytes 29879 | solution.py:58
  54.5 7.5 %while.47 = (s32[]{:T(128)}, f32[2,128]{1,0:T(2,128)S(1)}, f32[2,128]{1,0:T(2,128)S(1)}, f32[64,2,128]{2,0,1:T(8,128)S(1)}, f32[64,2,128]{2,0,1:T(8,128)S(1)}, /...) while((s32[]{:T(128)}, f32[2,128]{1,0:T(2,128)S(1)}, ...), condition=%wide.region_4.5_spmd.clone, body=%wide.region_3.4_spmd.clone.sunk | while | flops 2564 | bytes 12439 | solution.py:66
  62.0 14.4 %all-gather.1 = f32[8,64,128]{2,1,0:T(8,128)S(1)} all-gather(f32[2,64,128]{2,1,0:T(8,128)S(1)} %bitcast.139), channel_id=3, replica_groups=mesh['tm'=4,'space'=8] {'tm'}, dimensions={0}, use_global_device_ids=true | all-gather | bytes 327680 | tf_op jit(solution)/shard_map/all_gather | solution.py:111
  76.4 0.7 fusion.10
  77.1 13.9 %all-gather = f32[8,64,128]{2,1,0:T(8,128)S(1)} all-gather(f32[2,64,128]{2,1,0:T(8,128)S(1)} %bitcast.138), channel_id=2, replica_groups=mesh['tm'=4,'space'=8] {'tm'}, dimensions={0}, use_global_device_ids=true | all-gather | bytes 327680 | tf_op jit(solution)/shard_map/all_gather | solution.py:110
  91.0 0.7 fusion.12
  91.7 0.1 copy-done.1
  91.8 1.2 fusion.19
  93.0 38.7 %psum.15 = f32[]{:T(128)} all-reduce(f32[]{:T(128)} %get-tuple-element.446), channel_id=1, replica_groups=mesh['tm'=4,'space'=8] {'tm','space'}, use_global_device_ids=true, to_apply=%region_6.7 | all-reduce | flops 1 | bytes 8 | tf_op jit(solution)/shard_map/psum | solution.py:122
  (407 shorter events, 9.9 us)
Async XLA Ops:
  7.2 21.3 %copy-start = (f32[2,8]{1,0:T(2,128)S(1)}, f32[2,8]{1,0:T(2,128)}, u32[]{:S(2)}) copy-start(f32[2,8]{1,0:T(2,128)} %param.15) | copy-start | bytes 196
  7.2 40.5 %all-reduce.4.cloned.1.call-start = ((), (), s32[]{:S(2)}) async-start(), calls=%async_computation | async-start | bytes 131072 | tf_op jit(solution)/shard_map/psum | solution.py:14
  8.7 0.8 copy-start.3
  26.2 0.8 copy-start.2
  27.0 0.7 copy-start.7
  27.7 0.7 copy-start.6
  28.5 0.7 copy-start.5
  28.5 0.7 copy-start.8
  29.4 18.3 %copy-start.4 = (f32[2,64,128]{2,1,0:T(8,128)S(1)}, f32[2,64,128]{2,1,0:T(8,128)}, u32[]{:S(2)}) copy-start(f32[2,64,128]{2,1,0:T(8,128)} %param.13) | copy-start | bytes 196612
  91.0 0.8 copy-start.1
Sparse Core Ops, SparseCore 0:
  10.9 36.6 all-reduce.3
where the time goes:
time: 141 us; the launch traced here: 140 us
  blocking collectives  82.9 us (59%)
  waiting for transfers between devices  18 us (13%)
  between operations  16.4 us (12%)
  other arithmetic  8.39 us (6%)
  local copies, waits for them, and re-layouts  8.19 us (6%)
  loops' own time  3.64 us (3%)
  matrix products  2.84 us (2%)
    psum x1, blocking collectives, shards(): total = lax.psum(jnp.sum(change * change), ('tm', 'space'))  38.7 us
    psum x1, waiting for transfers between devices, broadcast(): return lax.psum(block, axis)  18 us
    all_gather x1, blocking collectives, shards(): shard_rows = lax.all_gather(scaled[None], 'tm', axis=0, tiled=True)  16 us
    all_gather x1, blocking collectives, shards(): lax.all_gather(back_imag[None], 'tm', axis=0, tiled=True)  14.4 us
    all_gather x1, blocking collectives, shards(): lax.all_gather(back_real[None], 'tm', axis=0, tiled=True)  13.9 us
    dynamic_update_slice x128, local copies, waits for them, and re-layouts, line_solve(): unused, stacked = lax.scan(forward, start_state, tuple(moved))  4.58 us
    dynamic_update_slice x128, other arithmetic, line_solve(): unused, stacked = lax.scan(forward, start_state, tuple(moved))  3.17 us
    unnamed x18, local copies, waits for them, and re-layouts  2.85 us
  transfers between devices with their start and end apart: 1, of which 1 were waited for; matrix products, arithmetic and copies ran while one was open for 1% of the time, Pallas kernels for 0%

commit v1 on v0

v1 whole, which is shorter than its diff:
```python
import functools
import math

import jax
import jax.numpy as jnp
from jax import lax
from jax.experimental import pallas as pl
from jax.experimental.pallas import tpu as pltpu
from jax.sharding import PartitionSpec as P

alpha_corner = 0.3
tile = 8
near_steps = 3


def roll_down(block, distance):
    return pltpu.roll(block, distance, 0)


def roll_up(block, distance):
    return pltpu.roll(block, block.shape[0] - distance, 0)


def c_mul(x, y):
    if len(x) == 1 and len(y) == 1:
        return (x[0] * y[0],)
    if len(x) == 1:
        return (x[0] * y[0], x[0] * y[1])
    if len(y) == 1:
        return (x[0] * y[0], x[1] * y[0])
    return (x[0] * y[0] - x[1] * y[1], x[0] * y[1] + x[1] * y[0])


def c_add(x, y):
    return tuple(p + q for p, q in zip(x, y))


def c_sub(x, y):
    return tuple(p - q for p, q in zip(x, y))


def c_neg(x):
    return tuple(-p for p in x)


def c_inverse(x):
    if len(x) == 1:
        return (1.0 / x[0],)
    scale = 1.0 / (x[0] * x[0] + x[1] * x[1])
    return (x[0] * scale, -x[1] * scale)


def c_map(f, x):
    return tuple(f(p) for p in x)


def frequencies(length):
    root = math.exp(math.log(alpha_corner) / length)
    listed = []
    for j in range(length // 2 + 1):
        angle = 2.0 * math.pi * j / length
        if j == 0 or 2 * j == length:
            listed.append((j, (1.0 - root * math.cos(angle),)))
        else:
            listed.append((j, (1.0 - root * math.cos(angle), root * math.sin(angle))))
    return listed


def planes(length):
    return sum(len(shift) for unused, shift in frequencies(length))


def factor_kernel(length, zones_ref, drift_ref, zone_ref, flag_ref, faces_ref, near_ref, far_ref):
    cells, lanes = faces_ref.shape
    faces = faces_ref[...].astype(jnp.float32)
    row = lax.broadcasted_iota(jnp.int32, (cells, lanes), 0)
    link_above = jnp.where(row == cells - 1, 0.0, faces)
    link_below = jnp.where(row == 0, 0.0, roll_down(faces, 1))
    ground = jnp.where(row == 0, flag_ref[...].astype(jnp.float32), 0.0)
    zone = zone_ref[...]
    for species in range(2):
        diffusion = jnp.zeros(zone.shape, jnp.float32)
        for index in range(zones_ref.shape[1]):
            diffusion = jnp.where(zone == index, zones_ref[species, index], diffusion)
        drift = drift_ref[species]
        below = -(diffusion + drift) * link_below
        above = -diffusion * link_above
        centre = diffusion * (link_below + link_above) + drift + 2.0 * diffusion * ground
        plane = 0
        for unused, shift in frequencies(length):
            parts = len(shift)
            a = (below,)
            c = (above,)
            b = (centre + shift[0],)
            if parts == 2:
                b = b + (jnp.full_like(centre, shift[1]),)
            for step in range(near_steps):
                distance = 1 << step
                inverse = c_inverse(b)
                low = c_neg(c_mul(a, c_map(lambda p: roll_down(p, distance), inverse)))
                high = c_neg(c_mul(c, c_map(lambda p: roll_up(p, distance), inverse)))
                down_c = c_map(lambda p: roll_down(p, distance), c)
                up_a = c_map(lambda p: roll_up(p, distance), a)
                b = c_add(b, c_add(c_mul(low, down_c), c_mul(high, up_a)))
                a = c_mul(low, c_map(lambda p: roll_down(p, distance), a))
                c = c_mul(high, c_map(lambda p: roll_up(p, distance), c))
                for part in range(parts):
                    near_ref[species, plane + part, 2 * step] = low[part]
                    near_ref[species, plane + part, 2 * step + 1] = high[part]
            carry = None
            for block in range(cells // tile):
                rows = slice(block * tile, (block + 1) * tile)
                ak, bk, ck = (c_map(lambda p: p[rows], item) for item in (a, b, c))
                if carry is None:
                    eliminate = c_map(jnp.zeros_like, ak)
                else:
                    eliminate = c_mul(ak, carry[0])
                    bk = c_sub(bk, c_mul(eliminate, carry[1]))
                inverse = c_inverse(bk)
                substitute = c_mul(ck, inverse)
                for part in range(parts):
                    far_ref[species, plane + part, 0, rows] = eliminate[part]
                    far_ref[species, plane + part, 1, rows] = inverse[part]
                    far_ref[species, plane + part, 2, rows] = substitute[part]
                carry = (inverse, ck)
            plane += parts


def sweep_kernel(length, peers, corners, *refs):
    loads = refs[: peers + 1]
    corner_refs = refs[peers + 1 : peers + 1 + corners]
    initial_ref, previous_ref, near_ref, far_ref, new_ref, sum_ref = refs[peers + 1 + corners :]
    cells, lanes = initial_ref.shape[1:]
    me = lax.axis_index("tm")
    total = jnp.zeros((tile, lanes), jnp.float32)
    for species in range(2):
        mine = previous_ref[0, species]
        last = jnp.where(me == length - 1, mine, 0.0)
        for ref in corner_refs:
            last = last + ref[species]
        correction = initial_ref[species] - alpha_corner * last
        scaled = []
        for behind in range(length):
            factor = math.exp(-math.log(alpha_corner) * behind / length)
            load = loads[behind][0, species]
            load = jnp.where(me == behind, load + correction, load)
            scaled.append(load * jnp.where(me < behind, alpha_corner * factor, factor))
        answer = jnp.zeros((cells, lanes), jnp.float32)
        plane = 0
        for j, shift in frequencies(length):
            parts = len(shift)
            rhs = []
            for part in range(parts):
                value = jnp.zeros((cells, lanes), jnp.float32)
                for behind in range(length):
                    turn = j * behind % length * 4
                    exact = {0: (1.0, 0.0), 1: (0.0, 1.0), 2: (-1.0, 0.0), 3: (0.0, -1.0)}
                    if turn % length == 0:
                        weight = exact[turn // length][part]
                    else:
                        angle = 2.0 * math.pi * j * behind / length
                        weight = (math.cos(angle), math.sin(angle))[part]
                    if weight == 1.0:
                        value = value + scaled[behind]
                    elif weight == -1.0:
                        value = value - scaled[behind]
                    elif weight != 0.0:
                        value = value + weight * scaled[behind]
                rhs.append(value)
            rhs = tuple(rhs)
            for step in range(near_steps):
                distance = 1 << step
                low = tuple(near_ref[species, plane + p, 2 * step] for p in range(parts))
                high = tuple(near_ref[species, plane + p, 2 * step + 1] for p in range(parts))
                down = c_map(lambda p: roll_down(p, distance), rhs)
                up = c_map(lambda p: roll_up(p, distance), rhs)
                rhs = c_add(rhs, c_add(c_mul(low, down), c_mul(high, up)))
            blocks = []
            carry = None
            for block in range(cells // tile):
                rows = slice(block * tile, (block + 1) * tile)
                value = c_map(lambda p: p[rows], rhs)
                if carry is not None:
                    eliminate = tuple(far_ref[species, plane + p, 0, rows] for p in range(parts))
                    value = c_sub(value, c_mul(eliminate, carry))
                blocks.append(value)
                carry = value
            solved = [None] * len(blocks)
            carry = None
            for block in reversed(range(cells // tile)):
                rows = slice(block * tile, (block + 1) * tile)
                inverse = tuple(far_ref[species, plane + p, 1, rows] for p in range(parts))
                value = c_mul(inverse, blocks[block])
                if carry is not None:
                    substitute = tuple(far_ref[species, plane + p, 2, rows] for p in range(parts))
                    value = c_sub(value, c_mul(substitute, carry))
                solved[block] = value[0]
                carry = value
            weight = parts / length
            answer = answer + weight * jnp.concatenate(solved, 0)
            plane += parts
        new_ref[0, species] = answer
        change = answer - mine
        square = change * change
        for block in range(cells // tile):
            total = total + square[block * tile : (block + 1) * tile]
    sum_ref[...] = jnp.sum(total, axis=0, keepdims=True)


def spread_sum(value, axis):
    size = lax.axis_size(axis)
    pieces = [value]
    for step in range(1, size):
        pieces.append(lax.ppermute(value, axis, [(i, (i + step) % size) for i in range(size)]))
    result = pieces[0]
    for piece in pieces[1:]:
        result = result + piece
    return result


def shards(
    forcing,
    initial_state,
    previous,
    zone_diffusion,
    drift_rate,
    column_zone,
    bottom_flag,
    open_faces,
):
    length = lax.axis_size("tm")
    cells, lanes = open_faces.shape
    corners = [
        lax.ppermute(previous[0], "tm", [(length - 1, target)]) for target in range(length - 1)
    ]
    loads = [forcing]
    for step in range(1, length):
        loads.append(
            lax.ppermute(forcing, "tm", [(i, (i + step) % length) for i in range(length)])
        )
    whole = pl.BlockSpec(memory_space=pltpu.VMEM)
    scalars = pl.BlockSpec(memory_space=pltpu.SMEM)
    count = planes(length)
    near, far = pl.pallas_call(
        functools.partial(factor_kernel, length),
        out_shape=(
            jax.ShapeDtypeStruct((2, count, 2 * near_steps, cells, lanes), jnp.float32),
            jax.ShapeDtypeStruct((2, count, 3, cells, lanes), jnp.float32),
        ),
        in_specs=[scalars, scalars, whole, whole, whole],
        out_specs=(whole, whole),
        compiler_params=pltpu.CompilerParams(vmem_limit_bytes=40 * 1024 * 1024),
        cost_estimate=pl.CostEstimate(flops=4000000, bytes_accessed=3000000, transcendentals=0),
        name="factor_lines",
    )(zone_diffusion, drift_rate, column_zone[None], bottom_flag[None], open_faces)
    new_iterate, squares = pl.pallas_call(
        functools.partial(sweep_kernel, length, length - 1, len(corners)),
        out_shape=(
            jax.ShapeDtypeStruct(forcing.shape, jnp.float32),
            jax.ShapeDtypeStruct((1, lanes), jnp.float32),
        ),
        in_specs=[whole] * (length + len(corners) + 4),
        out_specs=(whole, whole),
        compiler_params=pltpu.CompilerParams(vmem_limit_bytes=40 * 1024 * 1024),
        cost_estimate=pl.CostEstimate(flops=4000000, bytes_accessed=3000000, transcendentals=0),
        name="solve_lines",
    )(*loads, *corners, initial_state, previous, near, far)
    total = jnp.sum(spread_sum(spread_sum(squares, "tm"), "space"))
    entry_count = length * forcing.shape[1] * cells * lanes * lax.axis_size("space")
    return (new_iterate, jnp.sqrt(total / entry_count))


def solution(mesh):
    placed = (
        P("tm", None, None, "space"),
        P(None, None, "space"),
        P("tm", None, None, "space"),
        P(),
        P(),
        P("space"),
        P("space"),
        P(None, "space"),
    )
    return jax.shard_map(
        shards,
        mesh=mesh,
        in_specs=placed,
        out_specs=(P("tm", None, None, "space"), P()),
        check_vma=False,
    )
```

time: 141 us -> 41.2 us (0.29)
  blocking collectives: 82.9 us -> 0 us
  starting transfers between devices: 0.04 us -> 20 us
  between operations: 16.4 us -> 2.53 us
  waiting for transfers between devices: 18 us -> 9.34 us
  other arithmetic: 8.39 us -> 0.61 us
  loops' own time: 3.64 us -> 0 us
  matrix products: 2.84 us -> 0 us
  Pallas kernels: 0 us -> 2.41 us
  local copies, waits for them, and re-layouts: 8.19 us -> 5.92 us
    all_gather x3 -> x0, blocking collectives: 44.2 us -> none  [the longest x1 16 us: shards(): shard_rows = lax.all_gather(scaled[None], 'tm', axis=0, tiled=True)]
    psum x1 -> x0, blocking collectives: 38.7 us -> none  [shards(): total = lax.psum(jnp.sum(change * change), ('tm', 'space'))]
    ppermute x0 -> x16, starting transfers between devices: none -> 20 us  [the longest x10 9.34 us: spread_sum(): lax.ppermute(value, axis, [(i, (i + step) % size) for i in range(size)])]
    psum x1 -> x0, waiting for transfers between devices: 18 us -> none  [broadcast(): return lax.psum(block, axis)]
    ppermute x0 -> x16, waiting for transfers between devices: none -> 9.34 us  [the longest x10 8.66 us: spread_sum(): lax.ppermute(value, axis, [(i, (i + step) % size) for i in range(size)])]
    dynamic_update_slice x128 -> x0, local copies, waits for them, and re-layouts: 4.58 us -> none  [line_solve(): unused, stacked = lax.scan(forward, start_state, tuple(moved))]
    another operation x2 -> x0, loops' own time: 3.64 us -> none  [the longest x1 2.05 us: line_solve(): unused, stacked = lax.scan(forward, start_state, tuple(moved))]
    dynamic_update_slice x128 -> x0, other arithmetic: 3.17 us -> none  [line_solve(): unused, stacked = lax.scan(forward, start_state, tuple(moved))]
  transfers between devices with their start and end apart: 1 -> 16, of which waited for: 1 -> 8; matrix products, arithmetic and copies ran while one was open for 1% -> 0% of each run, Pallas kernels for 0% -> 3%
where the time goes in v1:
time: 41.2 us; the launch traced here: 40.8 us
  starting transfers between devices  20 us (49%)
  waiting for transfers between devices  9.34 us (23%)
  local copies, waits for them, and re-layouts  5.92 us (14%)
  between operations  2.53 us (6%)
  Pallas kernels  2.41 us (6%)
  other arithmetic  0.61 us (1%)
    ppermute x10, starting transfers between devices, spread_sum(): lax.ppermute(value, axis, [(i, (i + step) % size) for i in range(size)])  9.34 us
    ppermute x10, waiting for transfers between devices, spread_sum(): lax.ppermute(value, axis, [(i, (i + step) % size) for i in range(size)])  8.66 us
    ppermute x3, starting transfers between devices, shards(): lax.ppermute(forcing, 'tm', [(i, (i + step) % length) for i in range(leng...  8.01 us
    unnamed x16, local copies, waits for them, and re-layouts  5.92 us
    ppermute x3, starting transfers between devices, shards(): lax.ppermute(previous[0], 'tm', [(length - 1, target)])  2.62 us
    pallas_call x1, Pallas kernels, shards(): pl.pallas_call(functools.partial(factor_kernel, length), out_shape=(jax.S...  1.35 us
    pallas_call x1, Pallas kernels, shards(): pl.pallas_call(functools.partial(sweep_kernel, length, length - 1, len(co...  1.06 us
  transfers between devices with their start and end apart: 16, of which 8 were waited for; matrix products, arithmetic and copies ran while one was open for 0% of the time, Pallas kernels for 3%

profile of v1, /device:TPU:0, one launch (start us, length us, event | category | flops | bytes accessed | tf_op | source)
XLA Modules:
  0.0 40.8 jit_solution(8656712586925324633)
XLA Ops:
  0.6 0.7 %collective-permute-start.5 = (f32[2,64,128]{2,1,0:T(8,128)}, f32[2,64,128]{2,1,0:T(8,128)S(1)}, u32[]{:S(2)}, u32[]{:S(2)}) collective-permute-start(f32[2,64,128]{2,1,0:T(8,128)} %bitcast.3), channel_id=1, source_target_pairs={{24,16},{25,17},{26,18},{27,19},{28,20},{29,21},{30,22},{31,23}} | collective-permute-start | bytes 196616 | tf_op jit(solution)/shard_map/ppermute | solution.py:234
  1.3 0.7 %collective-permute-start.4 = (f32[2,64,128]{2,1,0:T(8,128)}, f32[2,64,128]{2,1,0:T(8,128)S(1)}, u32[]{:S(2)}, u32[]{:S(2)}) collective-permute-start(f32[2,64,128]{2,1,0:T(8,128)} %bitcast.4), channel_id=1, source_target_pairs={{24,8},{25,9},{26,10},{27,11},{28,12},{29,13},{30,14},{31,15}} | collective-permute-start | bytes 196616 | tf_op jit(solution)/shard_map/ppermute | solution.py:234
  2.0 1.3 %collective-permute-start.3 = (f32[2,64,128]{2,1,0:T(8,128)}, f32[2,64,128]{2,1,0:T(8,128)S(1)}, u32[]{:S(2)}, u32[]{:S(2)}) collective-permute-start(f32[2,64,128]{2,1,0:T(8,128)} %bitcast.5), channel_id=1, source_target_pairs={{24,0},{25,1},{26,2},{27,3},{28,4},{29,5},{30,6},{31,7}} | collective-permute-start | bytes 196616 | tf_op jit(solution)/shard_map/ppermute | solution.py:234
  3.3 4.1 %collective-permute-start.1 = (f32[1,2,64,128]{3,2,1,0:T(8,128)}, f32[1,2,64,128]{3,2,1,0:T(8,128)S(1)}, u32[]{:S(2)}, u32[]{:S(2)}) collective-permute-start(f32[1,2,64,128]{3,2,1,0:T(8,128)} %refs_0_.1), channel_id=1, source_target_pairs={{0,16},{8,24},{16,0},{24,8},{1,17},{9,25},{17,1},{25,9},{2,18},{10... | collective-permute-start | bytes 196616 | tf_op jit(solution)/shard_map/ppermute | solution.py:239
  7.4 3.9 %collective-permute-start = (f32[1,2,64,128]{3,2,1,0:T(8,128)}, f32[1,2,64,128]{3,2,1,0:T(8,128)S(1)}, u32[]{:S(2)}, u32[]{:S(2)}) collective-permute-start(f32[1,2,64,128]{3,2,1,0:T(8,128)} %refs_0_.1), channel_id=1, source_target_pairs={{0,8},{8,16},{16,24},{24,0},{1,9},{9,17},{17,25},{25,1},{2,10},{10... | collective-permute-start | bytes 196616 | tf_op jit(solution)/shard_map/ppermute | solution.py:239
  11.3 0.8 %copy-done.3 = s32[64,128]{1,0:T(8,128)S(1)} copy-done((s32[64,128]{1,0:T(8,128)S(1)}, s32[64,128]{1,0:T(8,128)}, u32[]{:S(2)}) %copy-start.3) | copy-done | bytes 32792
  12.1 0.7 %copy-done.4 = f32[2,8]{1,0:T(2,128)S(1)} copy-done((f32[2,8]{1,0:T(2,128)S(1)}, f32[2,8]{1,0:T(2,128)}, u32[]{:S(2)}) %copy-start.4) | copy-done | bytes 88
  12.7 0.7 %copy-done.5 = f32[2]{0:T(128)S(1)} copy-done((f32[2]{0:T(128)S(1)}, f32[2]{0:T(128)}, u32[]{:S(2)}) %copy-start.5) | copy-done | bytes 32
  13.4 0.7 %copy-done.6 = s32[128]{0:T(128)S(1)} copy-done((s32[128]{0:T(128)S(1)}, s32[128]{0:T(128)}, u32[]{:S(2)}) %copy-start.6) | copy-done | bytes 536
  14.0 0.7 %copy-done.7 = s32[128]{0:T(128)S(1)} copy-done((s32[128]{0:T(128)S(1)}, s32[128]{0:T(128)}, u32[]{:S(2)}) %copy-start.7) | copy-done | bytes 536
  14.7 1.4 %factor_lines.1 = (f32[2,4,6,64,128]{4,3,2,1,0:T(8,128)S(1)}, f32[2,4,3,64,128]{4,3,2,1,0:T(8,128)S(1)}) custom-call(f32[2,8]{1,0:T(2,128)S(1)} %copy-done.4, f32[2]{0:T(128)S(1)} %copy-done.5, s32[1,128]{1,0:T(1,128)S(1)} %bitcast.6, s32[1,128]{1,0:T(1,128)S(1)} %bitcast.7, s32[64,128]{1,0:T(8,128)S(1)} %copy-done.3), custom_call_target="tpu_custom_call" | custom-call | flops 4000000 | bytes 3000000 | tf_op jit(solution)/shard_map/factor_lines/pallas_call | solution.py:244
  16.1 0.7 %collective-permute-done.refs_1_ = f32[1,2,64,128]{3,2,1,0:T(8,128)S(1)} collective-permute-done((f32[1,2,64,128]{3,2,1,0:T(8,128)}, f32[1,2,64,128]{3,2,1,0:T(8,128)S(1)}, u32[]{:S(2)}, u32[]{:S(2)}) %collective-permute-start) | collective-permute-done | bytes 65568 | tf_op jit(solution)/shard_map/ppermute | solution.py:239
  16.8 0.8 %copy-done = f32[1,2,64,128]{3,2,1,0:T(8,128)S(1)} copy-done((f32[1,2,64,128]{3,2,1,0:T(8,128)S(1)}, f32[1,2,64,128]{3,2,1,0:T(8,128)}, u32[]{:S(2)}) %copy-start) | copy-done | bytes 65560
  17.6 0.8 %copy-done.1 = f32[1,2,64,128]{3,2,1,0:T(8,128)S(1)} copy-done((f32[1,2,64,128]{3,2,1,0:T(8,128)S(1)}, f32[1,2,64,128]{3,2,1,0:T(8,128)}, u32[]{:S(2)}) %copy-start.1) | copy-done | bytes 65560
  18.4 0.8 %copy-done.2 = f32[2,64,128]{2,1,0:T(8,128)S(1)} copy-done((f32[2,64,128]{2,1,0:T(8,128)S(1)}, f32[2,64,128]{2,1,0:T(8,128)}, u32[]{:S(2)}) %copy-start.2) | copy-done | bytes 65560
  19.3 1.1 %solve_lines.1 = (f32[1,2,64,128]{3,2,1,0:T(8,128)}, f32[1,128]{1,0:T(1,128)S(1)}) custom-call(f32[1,2,64,128]{3,2,1,0:T(8,128)S(1)} %copy-done, f32[1,2,64,128]{3,2,1,0:T(8,128)S(1)} %collective-permute-done.refs_1_, f32[1,2,64,128]{3,2,1,0:T(8,128)S(1)} %collective-permute-done.1.refs_2_, f32[1,2,64,128]{3,2,1,0:T(8,128)S(1)} %collective-permute-done.2.refs_3_, ...), custom_call_target="tpu_custom_call" | custom-call | flops 4000000 | bytes 3000000 | tf_op jit(solution)/shard_map/solve_lines/pallas_call | solution.py:256
  20.3 1.5 %collective-permute-start.8 = (f32[1,128]{1,0:T(1,128)S(1)}, f32[1,128]{1,0:T(1,128)S(1)}, u32[]{:S(2)}, u32[]{:S(2)}) collective-permute-start(f32[1,128]{1,0:T(1,128)S(1)} %get-tuple-element.9), channel_id=1, source_target_pairs={{0,24},{8,0},{16,8},{24,16},{1,25},{9,1},{17,9},{25,17},{2,26},{10... | collective-permute-start | bytes 1544 | tf_op jit(solution)/shard_map/ppermute | solution.py:214
  21.8 1.3 %collective-permute-start.7 = (f32[1,128]{1,0:T(1,128)S(1)}, f32[1,128]{1,0:T(1,128)S(1)}, u32[]{:S(2)}, u32[]{:S(2)}) collective-permute-start(f32[1,128]{1,0:T(1,128)S(1)} %get-tuple-element.9), channel_id=1, source_target_pairs={{0,16},{8,24},{16,0},{24,8},{1,17},{9,25},{17,1},{25,9},{2,18},{10... | collective-permute-start | bytes 1544 | tf_op jit(solution)/shard_map/ppermute | solution.py:214
  23.2 0.5 %collective-permute-start.6 = (f32[1,128]{1,0:T(1,128)S(1)}, f32[1,128]{1,0:T(1,128)S(1)}, u32[]{:S(2)}, u32[]{:S(2)}) collective-permute-start(f32[1,128]{1,0:T(1,128)S(1)} %get-tuple-element.9), channel_id=1, source_target_pairs={{0,8},{8,16},{16,24},{24,0},{1,9},{9,17},{17,25},{25,1},{2,10},{10... | collective-permute-start | bytes 1544 | tf_op jit(solution)/shard_map/ppermute | solution.py:214
  23.9 2.4 %collective-permute-done.7 = f32[1,128]{1,0:T(1,128)S(1)} collective-permute-done((f32[1,128]{1,0:T(1,128)S(1)}, f32[1,128]{1,0:T(1,128)S(1)}, u32[]{:S(2)}, u32[]{:S(2)}) %collective-permute-start.7) | collective-permute-done | bytes 544 | tf_op jit(solution)/shard_map/ppermute | solution.py:214
  26.3 2.2 %collective-permute-done.6 = f32[1,128]{1,0:T(1,128)S(1)} collective-permute-done((f32[1,128]{1,0:T(1,128)S(1)}, f32[1,128]{1,0:T(1,128)S(1)}, u32[]{:S(2)}, u32[]{:S(2)}) %collective-permute-start.6) | collective-permute-done | bytes 544 | tf_op jit(solution)/shard_map/ppermute | solution.py:214
  28.5 0.3 collective-permute-start.15
  28.8 2.2 %collective-permute-start.14 = (f32[1,128]{1,0:T(1,128)S(1)}, f32[1,128]{1,0:T(1,128)S(1)}, u32[]{:S(2)}, u32[]{:S(2)}) collective-permute-start(f32[1,128]{1,0:T(1,128)S(1)} %add_add_fusion), channel_id=1, source_target_pairs={{0,6},{1,7},{2,0},{3,1},{4,2},{5,3},{6,4},{7,5},{8,14},{9,15},{10,... | collective-permute-start | bytes 1544 | tf_op jit(solution)/shard_map/ppermute | solution.py:214
  31.0 0.3 collective-permute-start.13
  31.3 1.5 %collective-permute-start.12 = (f32[1,128]{1,0:T(1,128)S(1)}, f32[1,128]{1,0:T(1,128)S(1)}, u32[]{:S(2)}, u32[]{:S(2)}) collective-permute-start(f32[1,128]{1,0:T(1,128)S(1)} %add_add_fusion), channel_id=1, source_target_pairs={{0,4},{1,5},{2,6},{3,7},{4,0},{5,1},{6,2},{7,3},{8,12},{9,13},{10,... | collective-permute-start | bytes 1544 | tf_op jit(solution)/shard_map/ppermute | solution.py:214
  32.8 0.2 collective-permute-start.11
  33.0 1.5 %collective-permute-start.10 = (f32[1,128]{1,0:T(1,128)S(1)}, f32[1,128]{1,0:T(1,128)S(1)}, u32[]{:S(2)}, u32[]{:S(2)}) collective-permute-start(f32[1,128]{1,0:T(1,128)S(1)} %add_add_fusion), channel_id=1, source_target_pairs={{0,2},{1,3},{2,4},{3,5},{4,6},{5,7},{6,0},{7,1},{8,10},{9,11},{10,... | collective-permute-start | bytes 1544 | tf_op jit(solution)/shard_map/ppermute | solution.py:214
  34.5 0.4 collective-permute-done.12
  34.9 0.9 %collective-permute-done.11 = f32[1,128]{1,0:T(1,128)S(1)} collective-permute-done((f32[1,128]{1,0:T(1,128)S(1)}, f32[1,128]{1,0:T(1,128)S(1)}, u32[]{:S(2)}, u32[]{:S(2)}) %collective-permute-start.11) | collective-permute-done | bytes 544 | tf_op jit(solution)/shard_map/ppermute | solution.py:214
  35.8 1.6 %collective-permute-done.10 = f32[1,128]{1,0:T(1,128)S(1)} collective-permute-done((f32[1,128]{1,0:T(1,128)S(1)}, f32[1,128]{1,0:T(1,128)S(1)}, u32[]{:S(2)}, u32[]{:S(2)}) %collective-permute-start.10) | collective-permute-done | bytes 544 | tf_op jit(solution)/shard_map/ppermute | solution.py:214
  37.4 0.9 %collective-permute-done.9 = f32[1,128]{1,0:T(1,128)S(1)} collective-permute-done((f32[1,128]{1,0:T(1,128)S(1)}, f32[1,128]{1,0:T(1,128)S(1)}, u32[]{:S(2)}, u32[]{:S(2)}) %collective-permute-start.9) | collective-permute-done | bytes 544 | tf_op jit(solution)/shard_map/ppermute | solution.py:214
  38.4 0.6 %add_reduce_fusion = f32[]{:T(128)} fusion(f32[1,128]{1,0:T(1,128)S(1)} %collective-permute-done.15, f32[1,128]{1,0:T(1,128)S(1)} %collective-permute-done.14, f32[1,128]{1,0:T(1,128)S(1)} %collective-permute-done.13, f32[1,128]{1,0:T(1,128)S(1)} %collective-permute-done.12, f32[1,128]{1,0:T(1,128)S(1)} %collective-permute-done.11, ...), kind=kLoop, calls=%fused_computation | loop fusion | flops 1023 | bytes 4100 | tf_op jit(solution)/shard_map/reduce_sum | solution.py:268
  (20 shorter events, 0.2 us)
Async XLA Ops:
  0.6 10.7 %collective-permute-start.5 = (f32[2,64,128]{2,1,0:T(8,128)}, f32[2,64,128]{2,1,0:T(8,128)S(1)}, u32[]{:S(2)}, u32[]{:S(2)}) collective-permute-start(f32[2,64,128]{2,1,0:T(8,128)} %bitcast.3), channel_id=1, source_target_pairs={{24,16},{25,17},{26,18},{27,19},{28,20},{29,21},{30,22},{31,23}} | collective-permute-start | bytes 196616 | tf_op jit(solution)/shard_map/ppermute | solution.py:234
  1.3 14.8 %collective-permute-start.4 = (f32[2,64,128]{2,1,0:T(8,128)}, f32[2,64,128]{2,1,0:T(8,128)S(1)}, u32[]{:S(2)}, u32[]{:S(2)}) collective-permute-start(f32[2,64,128]{2,1,0:T(8,128)} %bitcast.4), channel_id=1, source_target_pairs={{24,8},{25,9},{26,10},{27,11},{28,12},{29,13},{30,14},{31,15}} | collective-permute-start | bytes 196616 | tf_op jit(solution)/shard_map/ppermute | solution.py:234
  2.0 14.1 %collective-permute-start.3 = (f32[2,64,128]{2,1,0:T(8,128)}, f32[2,64,128]{2,1,0:T(8,128)S(1)}, u32[]{:S(2)}, u32[]{:S(2)}) collective-permute-start(f32[2,64,128]{2,1,0:T(8,128)} %bitcast.5), channel_id=1, source_target_pairs={{24,0},{25,1},{26,2},{27,3},{28,4},{29,5},{30,6},{31,7}} | collective-permute-start | bytes 196616 | tf_op jit(solution)/shard_map/ppermute | solution.py:234
  3.3 12.8 %collective-permute-start.1 = (f32[1,2,64,128]{3,2,1,0:T(8,128)}, f32[1,2,64,128]{3,2,1,0:T(8,128)S(1)}, u32[]{:S(2)}, u32[]{:S(2)}) collective-permute-start(f32[1,2,64,128]{3,2,1,0:T(8,128)} %refs_0_.1), channel_id=1, source_target_pairs={{0,16},{8,24},{16,0},{24,8},{1,17},{9,25},{17,1},{25,9},{2,18},{10... | collective-permute-start | bytes 196616 | tf_op jit(solution)/shard_map/ppermute | solution.py:239
  7.4 9.4 %collective-permute-start = (f32[1,2,64,128]{3,2,1,0:T(8,128)}, f32[1,2,64,128]{3,2,1,0:T(8,128)S(1)}, u32[]{:S(2)}, u32[]{:S(2)}) collective-permute-start(f32[1,2,64,128]{3,2,1,0:T(8,128)} %refs_0_.1), channel_id=1, source_target_pairs={{0,8},{8,16},{16,24},{24,0},{1,9},{9,17},{17,25},{25,1},{2,10},{10... | collective-permute-start | bytes 196616 | tf_op jit(solution)/shard_map/ppermute | solution.py:239
  11.3 5.5 %collective-permute-start.2 = (f32[1,2,64,128]{3,2,1,0:T(8,128)}, f32[1,2,64,128]{3,2,1,0:T(8,128)S(1)}, u32[]{:S(2)}, u32[]{:S(2)}) collective-permute-start(f32[1,2,64,128]{3,2,1,0:T(8,128)} %refs_0_.1), channel_id=1, source_target_pairs={{0,24},{8,0},{16,8},{24,16},{1,25},{9,1},{17,9},{25,17},{2,26},{10... | collective-permute-start | bytes 196616 | tf_op jit(solution)/shard_map/ppermute | solution.py:239
  11.3 0.8 %copy-start.3 = (s32[64,128]{1,0:T(8,128)S(1)}, s32[64,128]{1,0:T(8,128)}, u32[]{:S(2)}) copy-start(s32[64,128]{1,0:T(8,128)} %faces_ref.1) | copy-start | bytes 98308
  12.0 0.7 %copy-start.4 = (f32[2,8]{1,0:T(2,128)S(1)}, f32[2,8]{1,0:T(2,128)}, u32[]{:S(2)}) copy-start(f32[2,8]{1,0:T(2,128)} %zones_ref.1) | copy-start | bytes 196
  12.7 0.7 %copy-start.5 = (f32[2]{0:T(128)S(1)}, f32[2]{0:T(128)}, u32[]{:S(2)}) copy-start(f32[2]{0:T(128)} %drift_ref.1) | copy-start | bytes 28
  13.4 0.7 %copy-start.6 = (s32[128]{0:T(128)S(1)}, s32[128]{0:T(128)}, u32[]{:S(2)}) copy-start(s32[128]{0:T(128)} %param.13) | copy-start | bytes 1540
  14.0 0.7 %copy-start.7 = (s32[128]{0:T(128)S(1)}, s32[128]{0:T(128)}, u32[]{:S(2)}) copy-start(s32[128]{0:T(128)} %param.14) | copy-start | bytes 1540
  16.8 0.8 %copy-start = (f32[1,2,64,128]{3,2,1,0:T(8,128)S(1)}, f32[1,2,64,128]{3,2,1,0:T(8,128)}, u32[]{:S(2)}) copy-start(f32[1,2,64,128]{3,2,1,0:T(8,128)} %refs_0_.1) | copy-start | bytes 196612
  17.6 0.8 %copy-start.1 = (f32[1,2,64,128]{3,2,1,0:T(8,128)S(1)}, f32[1,2,64,128]{3,2,1,0:T(8,128)}, u32[]{:S(2)}) copy-start(f32[1,2,64,128]{3,2,1,0:T(8,128)} %refs_8_.1) | copy-start | bytes 196612
  18.4 0.8 %copy-start.2 = (f32[2,64,128]{2,1,0:T(8,128)S(1)}, f32[2,64,128]{2,1,0:T(8,128)}, u32[]{:S(2)}) copy-start(f32[2,64,128]{2,1,0:T(8,128)} %refs_7_.1) | copy-start | bytes 196612
  20.3 3.5 %collective-permute-start.8 = (f32[1,128]{1,0:T(1,128)S(1)}, f32[1,128]{1,0:T(1,128)S(1)}, u32[]{:S(2)}, u32[]{:S(2)}) collective-permute-start(f32[1,128]{1,0:T(1,128)S(1)} %get-tuple-element.9), channel_id=1, source_target_pairs={{0,24},{8,0},{16,8},{24,16},{1,25},{9,1},{17,9},{25,17},{2,26},{10... | collective-permute-start | bytes 1544 | tf_op jit(solution)/shard_map/ppermute | solution.py:214
  21.8 4.4 %collective-permute-start.7 = (f32[1,128]{1,0:T(1,128)S(1)}, f32[1,128]{1,0:T(1,128)S(1)}, u32[]{:S(2)}, u32[]{:S(2)}) collective-permute-start(f32[1,128]{1,0:T(1,128)S(1)} %get-tuple-element.9), channel_id=1, source_target_pairs={{0,16},{8,24},{16,0},{24,8},{1,17},{9,25},{17,1},{25,9},{2,18},{10... | collective-permute-start | bytes 1544 | tf_op jit(solution)/shard_map/ppermute | solution.py:214
  23.2 5.3 %collective-permute-start.6 = (f32[1,128]{1,0:T(1,128)S(1)}, f32[1,128]{1,0:T(1,128)S(1)}, u32[]{:S(2)}, u32[]{:S(2)}) collective-permute-start(f32[1,128]{1,0:T(1,128)S(1)} %get-tuple-element.9), channel_id=1, source_target_pairs={{0,8},{8,16},{16,24},{24,0},{1,9},{9,17},{17,25},{25,1},{2,10},{10... | collective-permute-start | bytes 1544 | tf_op jit(solution)/shard_map/ppermute | solution.py:214
  28.5 4.5 %collective-permute-start.15 = (f32[1,128]{1,0:T(1,128)S(1)}, f32[1,128]{1,0:T(1,128)S(1)}, u32[]{:S(2)}, u32[]{:S(2)}) collective-permute-start(f32[1,128]{1,0:T(1,128)S(1)} %add_add_fusion), channel_id=1, source_target_pairs={{0,7},{1,0},{2,1},{3,2},{4,3},{5,4},{6,5},{7,6},{8,15},{9,8},{10,9... | collective-permute-start | bytes 1544 | tf_op jit(solution)/shard_map/ppermute | solution.py:214
  28.8 5.7 %collective-permute-start.14 = (f32[1,128]{1,0:T(1,128)S(1)}, f32[1,128]{1,0:T(1,128)S(1)}, u32[]{:S(2)}, u32[]{:S(2)}) collective-permute-start(f32[1,128]{1,0:T(1,128)S(1)} %add_add_fusion), channel_id=1, source_target_pairs={{0,6},{1,7},{2,0},{3,1},{4,2},{5,3},{6,4},{7,5},{8,14},{9,15},{10,... | collective-permute-start | bytes 1544 | tf_op jit(solution)/shard_map/ppermute | solution.py:214
  31.0 3.5 %collective-permute-start.13 = (f32[1,128]{1,0:T(1,128)S(1)}, f32[1,128]{1,0:T(1,128)S(1)}, u32[]{:S(2)}, u32[]{:S(2)}) collective-permute-start(f32[1,128]{1,0:T(1,128)S(1)} %add_add_fusion), channel_id=1, source_target_pairs={{0,5},{1,6},{2,7},{3,0},{4,1},{5,2},{6,3},{7,4},{8,13},{9,14},{10,... | collective-permute-start | bytes 1544 | tf_op jit(solution)/shard_map/ppermute | solution.py:214
  31.3 3.6 %collective-permute-start.12 = (f32[1,128]{1,0:T(1,128)S(1)}, f32[1,128]{1,0:T(1,128)S(1)}, u32[]{:S(2)}, u32[]{:S(2)}) collective-permute-start(f32[1,128]{1,0:T(1,128)S(1)} %add_add_fusion), channel_id=1, source_target_pairs={{0,4},{1,5},{2,6},{3,7},{4,0},{5,1},{6,2},{7,3},{8,12},{9,13},{10,... | collective-permute-start | bytes 1544 | tf_op jit(solution)/shard_map/ppermute | solution.py:214
  32.8 3.0 %collective-permute-start.11 = (f32[1,128]{1,0:T(1,128)S(1)}, f32[1,128]{1,0:T(1,128)S(1)}, u32[]{:S(2)}, u32[]{:S(2)}) collective-permute-start(f32[1,128]{1,0:T(1,128)S(1)} %add_add_fusion), channel_id=1, source_target_pairs={{0,3},{1,4},{2,5},{3,6},{4,7},{5,0},{6,1},{7,2},{8,11},{9,12},{10,... | collective-permute-start | bytes 1544 | tf_op jit(solution)/shard_map/ppermute | solution.py:214
  33.0 4.4 %collective-permute-start.10 = (f32[1,128]{1,0:T(1,128)S(1)}, f32[1,128]{1,0:T(1,128)S(1)}, u32[]{:S(2)}, u32[]{:S(2)}) collective-permute-start(f32[1,128]{1,0:T(1,128)S(1)} %add_add_fusion), channel_id=1, source_target_pairs={{0,2},{1,3},{2,4},{3,5},{4,6},{5,7},{6,0},{7,1},{8,10},{9,11},{10,... | collective-permute-start | bytes 1544 | tf_op jit(solution)/shard_map/ppermute | solution.py:214
  34.5 3.9 %collective-permute-start.9 = (f32[1,128]{1,0:T(1,128)S(1)}, f32[1,128]{1,0:T(1,128)S(1)}, u32[]{:S(2)}, u32[]{:S(2)}) collective-permute-start(f32[1,128]{1,0:T(1,128)S(1)} %add_add_fusion), channel_id=1, source_target_pairs={{0,1},{1,2},{2,3},{3,4},{4,5},{5,6},{6,7},{7,0},{8,9},{9,10},{10,1... | collective-permute-start | bytes 1544 | tf_op jit(solution)/shard_map/ppermute | solution.py:214

commit v2 on v1

--- a/solution.py
+++ b/solution.py
@@ -70,7 +70,46 @@
     return sum(len(shift) for unused, shift in frequencies(length))
 
 
-def factor_kernel(length, zones_ref, drift_ref, zone_ref, flag_ref, faces_ref, near_ref, far_ref):
+def factor_kernel(
+    length,
+    zones_hbm,
+    drift_hbm,
+    zone_hbm,
+    flag_hbm,
+    faces_hbm,
+    forcing_hbm,
+    previous_hbm,
+    initial_hbm,
+    near_ref,
+    far_ref,
+    forcing_ref,
+    previous_ref,
+    initial_ref,
+    zones_ref,
+    drift_ref,
+    zone_ref,
+    flag_ref,
+    faces_ref,
+    sems,
+):
+    pairs = (
+        (faces_hbm, faces_ref),
+        (zones_hbm, zones_ref),
+        (drift_hbm, drift_ref),
+        (zone_hbm, zone_ref),
+        (flag_hbm, flag_ref),
+        (forcing_hbm, forcing_ref),
+        (previous_hbm, previous_ref),
+        (initial_hbm, initial_ref),
+    )
+    copies = [
+        pltpu.make_async_copy(source, target, sems.at[index])
+        for index, (source, target) in enumerate(pairs)
+    ]
+    for copy in copies:
+        copy.start()
+    for copy in copies[:5]:
+        copy.wait()
     cells, lanes = faces_ref.shape
     faces = faces_ref[...].astype(jnp.float32)
     row = lax.broadcasted_iota(jnp.int32, (cells, lanes), 0)
@@ -124,20 +163,22 @@
                     far_ref[species, plane + part, 2, rows] = substitute[part]
                 carry = (inverse, ck)
             plane += parts
-
-
-def sweep_kernel(length, peers, corners, *refs):
-    loads = refs[: peers + 1]
-    corner_refs = refs[peers + 1 : peers + 1 + corners]
-    initial_ref, previous_ref, near_ref, far_ref, new_ref, sum_ref = refs[peers + 1 + corners :]
+    for copy in copies[5:]:
+        copy.wait()
+
+
+def sweep_kernel(length, *refs):
+    loads = refs[:length]
+    befores = refs[length : 2 * length]
+    initial_ref, near_ref, far_ref, new_ref, sum_ref = refs[2 * length :]
     cells, lanes = initial_ref.shape[1:]
     me = lax.axis_index("tm")
     total = jnp.zeros((tile, lanes), jnp.float32)
     for species in range(2):
-        mine = previous_ref[0, species]
-        last = jnp.where(me == length - 1, mine, 0.0)
-        for ref in corner_refs:
-            last = last + ref[species]
+        mine = befores[0][0, species]
+        last = mine
+        for behind in range(1, length):
+            last = jnp.where(me == (behind + length - 1) % length, befores[behind][0, species], last)
         correction = initial_ref[species] - alpha_corner * last
         scaled = []
         for behind in range(length):
@@ -204,18 +245,7 @@
         square = change * change
         for block in range(cells // tile):
             total = total + square[block * tile : (block + 1) * tile]
-    sum_ref[...] = jnp.sum(total, axis=0, keepdims=True)
-
-
-def spread_sum(value, axis):
-    size = lax.axis_size(axis)
-    pieces = [value]
-    for step in range(1, size):
-        pieces.append(lax.ppermute(value, axis, [(i, (i + step) % size) for i in range(size)]))
-    result = pieces[0]
-    for piece in pieces[1:]:
-        result = result + piece
-    return result
+    sum_ref[...] = jnp.broadcast_to(jnp.sum(total, axis=0, keepdims=True), sum_ref.shape)
 
 
 def shards(
@@ -230,44 +260,60 @@
 ):
     length = lax.axis_size("tm")
     cells, lanes = open_faces.shape
-    corners = [
-        lax.ppermute(previous[0], "tm", [(length - 1, target)]) for target in range(length - 1)
-    ]
-    loads = [forcing]
-    for step in range(1, length):
-        loads.append(
-            lax.ppermute(forcing, "tm", [(i, (i + step) % length) for i in range(length)])
-        )
+    ring = [[(i, (i + step) % length) for i in range(length)] for step in range(length)]
+    loads = [lax.ppermute(forcing, "tm", ring[step]) for step in range(1, length)]
+    befores = [lax.ppermute(previous, "tm", ring[step]) for step in range(1, length)]
     whole = pl.BlockSpec(memory_space=pltpu.VMEM)
-    scalars = pl.BlockSpec(memory_space=pltpu.SMEM)
+    outside = pl.BlockSpec(memory_space=pltpu.HBM)
     count = planes(length)
-    near, far = pl.pallas_call(
+    near, far, own_load, own_before, initial = pl.pallas_call(
         functools.partial(factor_kernel, length),
         out_shape=(
             jax.ShapeDtypeStruct((2, count, 2 * near_steps, cells, lanes), jnp.float32),
             jax.ShapeDtypeStruct((2, count, 3, cells, lanes), jnp.float32),
+            jax.ShapeDtypeStruct(forcing.shape, jnp.float32),
+            jax.ShapeDtypeStruct(previous.shape, jnp.float32),
+            jax.ShapeDtypeStruct(initial_state.shape, jnp.float32),
         ),
-        in_specs=[scalars, scalars, whole, whole, whole],
-        out_specs=(whole, whole),
+        in_specs=[outside] * 8,
+        out_specs=[whole] * 5,
+        scratch_shapes=[
+            pltpu.SMEM(zone_diffusion.shape, jnp.float32),
+            pltpu.SMEM(drift_rate.shape, jnp.float32),
+            pltpu.VMEM((1, lanes), jnp.int32),
+            pltpu.VMEM((1, lanes), jnp.int32),
+            pltpu.VMEM((cells, lanes), jnp.int32),
+            pltpu.SemaphoreType.DMA((8,)),
+        ],
         compiler_params=pltpu.CompilerParams(vmem_limit_bytes=40 * 1024 * 1024),
         cost_estimate=pl.CostEstimate(flops=4000000, bytes_accessed=3000000, transcendentals=0),
         name="factor_lines",
-    )(zone_diffusion, drift_rate, column_zone[None], bottom_flag[None], open_faces)
+    )(
+        zone_diffusion,
+        drift_rate,
+        column_zone[None],
+        bottom_flag[None],
+        open_faces,
+        forcing,
+        previous,
+        initial_state,
+    )
+    everyone = length * lax.axis_size("space")
     new_iterate, squares = pl.pallas_call(
-        functools.partial(sweep_kernel, length, length - 1, len(corners)),
+        functools.partial(sweep_kernel, length),
         out_shape=(
             jax.ShapeDtypeStruct(forcing.shape, jnp.float32),
-            jax.ShapeDtypeStruct((1, lanes), jnp.float32),
+            jax.ShapeDtypeStruct((everyone, 1, lanes), jnp.float32),
         ),
-        in_specs=[whole] * (length + len(corners) + 4),
+        in_specs=[whole] * (2 * length + 3),
         out_specs=(whole, whole),
         compiler_params=pltpu.CompilerParams(vmem_limit_bytes=40 * 1024 * 1024),
         cost_estimate=pl.CostEstimate(flops=4000000, bytes_accessed=3000000, transcendentals=0),
         name="solve_lines",
-    )(*loads, *corners, initial_state, previous, near, far)
-    total = jnp.sum(spread_sum(spread_sum(squares, "tm"), "space"))
-    entry_count = length * forcing.shape[1] * cells * lanes * lax.axis_size("space")
-    return (new_iterate, jnp.sqrt(total / entry_count))
+    )(own_load, *loads, own_before, *befores, initial, near, far)
+    squares = lax.all_to_all(squares, ("tm", "space"), 0, 0, tiled=True)
+    entry_count = everyone * forcing.shape[1] * cells * lanes
+    return (new_iterate, jnp.sqrt(jnp.sum(squares) / entry_count))
 
 
 def solution(mesh):

time: 41.2 us -> 34.1 us (0.83)
  blocking collectives: 0 us -> 11.9 us
  starting transfers between devices: 20 us -> 10.1 us
  waiting for transfers between devices: 9.34 us -> 0.02 us
    all_to_all x0 -> x1, blocking collectives: none -> 11.9 us  [shards(): squares = lax.all_to_all(squares, ('tm', 'space'), 0, 0, tiled=True)]
    ppermute x16 -> x6, starting transfers between devices: 20 us -> 10.1 us  [the longest x3 6.11 us: shards(): lax.ppermute(forcing, 'tm', ring[step])]
    ppermute x16 -> x6, waiting for transfers between devices: 9.34 us -> 0.02 us  [the longest x3 0.01 us: shards(): lax.ppermute(forcing, 'tm', ring[step])]
  transfers between devices with their start and end apart: 16 -> 6, of which waited for: 8 -> 0; matrix products, arithmetic and copies ran while one was open for 0% -> 0% of each run, Pallas kernels for 3% -> 4%
where the time goes in v2:
time: 34.1 us; the launch traced here: 33.7 us
  blocking collectives  11.9 us (35%)
  starting transfers between devices  10.1 us (30%)
  local copies, waits for them, and re-layouts  5.92 us (17%)
  Pallas kernels  2.52 us (7%)
  between operations  2.51 us (7%)
  other arithmetic  0.63 us (2%)
    all_to_all x1, blocking collectives, shards(): squares = lax.all_to_all(squares, ('tm', 'space'), 0, 0, tiled=True)  11.9 us
    ppermute x3, starting transfers between devices, shards(): lax.ppermute(forcing, 'tm', ring[step])  6.11 us
    unnamed x16, local copies, waits for them, and re-layouts  5.92 us
    ppermute x3, starting transfers between devices, shards(): lax.ppermute(previous, 'tm', ring[step])  4 us
    pallas_call x1, Pallas kernels, shards(): pl.pallas_call(functools.partial(factor_kernel, length), out_shape=(jax.S...  1.47 us
    pallas_call x1, Pallas kernels, shards(): pl.pallas_call(functools.partial(sweep_kernel, length), out_shape=(jax.Sh...  1.05 us
  transfers between devices with their start and end apart: 6, of which 0 were waited for; matrix products, arithmetic and copies ran while one was open for 0% of the time, Pallas kernels for 4%

profile of v2, /device:TPU:0, one launch (start us, length us, event | category | flops | bytes accessed | tf_op | source)
XLA Modules:
  0.0 33.7 jit_solution(2758180227781101220)
XLA Ops:
  0.6 3.1 %collective-permute-start = (f32[1,2,64,128]{3,2,1,0:T(8,128)}, f32[1,2,64,128]{3,2,1,0:T(8,128)S(1)}, u32[]{:S(2)}, u32[]{:S(2)}) collective-permute-start(f32[1,2,64,128]{3,2,1,0:T(8,128)} %forcing_hbm.1), channel_id=1, source_target_pairs={{0,8},{8,16},{16,24},{24,0},{1,9},{9,17},{17,25},{25,1},{2,10},{10... | collective-permute-start | bytes 196616 | tf_op jit(solution)/shard_map/ppermute | solution.py:264
  3.7 2.1 %collective-permute-start.2 = (f32[1,2,64,128]{3,2,1,0:T(8,128)}, f32[1,2,64,128]{3,2,1,0:T(8,128)S(1)}, u32[]{:S(2)}, u32[]{:S(2)}) collective-permute-start(f32[1,2,64,128]{3,2,1,0:T(8,128)} %forcing_hbm.1), channel_id=1, source_target_pairs={{0,24},{8,0},{16,8},{24,16},{1,25},{9,1},{17,9},{25,17},{2,26},{10... | collective-permute-start | bytes 196616 | tf_op jit(solution)/shard_map/ppermute | solution.py:264
  5.8 0.9 %collective-permute-start.1 = (f32[1,2,64,128]{3,2,1,0:T(8,128)}, f32[1,2,64,128]{3,2,1,0:T(8,128)S(1)}, u32[]{:S(2)}, u32[]{:S(2)}) collective-permute-start(f32[1,2,64,128]{3,2,1,0:T(8,128)} %forcing_hbm.1), channel_id=1, source_target_pairs={{0,16},{8,24},{16,0},{24,8},{1,17},{9,25},{17,1},{25,9},{2,18},{10... | collective-permute-start | bytes 196616 | tf_op jit(solution)/shard_map/ppermute | solution.py:264
  6.7 1.6 %collective-permute-start.3 = (f32[1,2,64,128]{3,2,1,0:T(8,128)}, f32[1,2,64,128]{3,2,1,0:T(8,128)S(1)}, u32[]{:S(2)}, u32[]{:S(2)}) collective-permute-start(f32[1,2,64,128]{3,2,1,0:T(8,128)} %previous_hbm.1), channel_id=1, source_target_pairs={{0,8},{8,16},{16,24},{24,0},{1,9},{9,17},{17,25},{25,1},{2,10},{10... | collective-permute-start | bytes 196616 | tf_op jit(solution)/shard_map/ppermute | solution.py:265
  8.3 2.2 %collective-permute-start.5 = (f32[1,2,64,128]{3,2,1,0:T(8,128)}, f32[1,2,64,128]{3,2,1,0:T(8,128)S(1)}, u32[]{:S(2)}, u32[]{:S(2)}) collective-permute-start(f32[1,2,64,128]{3,2,1,0:T(8,128)} %previous_hbm.1), channel_id=1, source_target_pairs={{0,24},{8,0},{16,8},{24,16},{1,25},{9,1},{17,9},{25,17},{2,26},{10... | collective-permute-start | bytes 196616 | tf_op jit(solution)/shard_map/ppermute | solution.py:265
  10.6 0.0 collective-permute-done.refs_1_
  10.6 0.2 collective-permute-start.4
  10.8 0.0 copy-start
  10.8 0.8 %copy-done = f32[2,64,128]{2,1,0:T(8,128)S(1)} copy-done((f32[2,64,128]{2,1,0:T(8,128)S(1)}, f32[2,64,128]{2,1,0:T(8,128)}, u32[]{:S(2)}) %copy-start) | copy-done | bytes 65560
  11.6 0.0 copy-start.1
  11.6 0.8 %copy-done.1 = f32[1,2,64,128]{3,2,1,0:T(8,128)S(1)} copy-done((f32[1,2,64,128]{3,2,1,0:T(8,128)S(1)}, f32[1,2,64,128]{3,2,1,0:T(8,128)}, u32[]{:S(2)}) %copy-start.1) | copy-done | bytes 65560
  12.4 0.0 copy-start.2
  12.4 0.8 %copy-done.2 = f32[1,2,64,128]{3,2,1,0:T(8,128)S(1)} copy-done((f32[1,2,64,128]{3,2,1,0:T(8,128)S(1)}, f32[1,2,64,128]{3,2,1,0:T(8,128)}, u32[]{:S(2)}) %copy-start.2) | copy-done | bytes 65560
  13.3 0.0 copy-start.3
  13.3 0.8 %copy-done.3 = s32[64,128]{1,0:T(8,128)S(1)} copy-done((s32[64,128]{1,0:T(8,128)S(1)}, s32[64,128]{1,0:T(8,128)}, u32[]{:S(2)}) %copy-start.3) | copy-done | bytes 32792
  14.0 0.0 copy-start.4
  14.0 0.7 %copy-done.4 = f32[2,8]{1,0:T(2,128)S(1)} copy-done((f32[2,8]{1,0:T(2,128)S(1)}, f32[2,8]{1,0:T(2,128)}, u32[]{:S(2)}) %copy-start.4) | copy-done | bytes 88
  14.7 0.0 copy-start.5
  14.7 0.7 %copy-done.5 = f32[2]{0:T(128)S(1)} copy-done((f32[2]{0:T(128)S(1)}, f32[2]{0:T(128)}, u32[]{:S(2)}) %copy-start.5) | copy-done | bytes 32
  15.4 0.0 copy-start.6
  15.4 0.7 %copy-done.6 = s32[128]{0:T(128)S(1)} copy-done((s32[128]{0:T(128)S(1)}, s32[128]{0:T(128)}, u32[]{:S(2)}) %copy-start.6) | copy-done | bytes 536
  16.0 0.0 copy-start.7
  16.0 0.7 %copy-done.7 = s32[128]{0:T(128)S(1)} copy-done((s32[128]{0:T(128)S(1)}, s32[128]{0:T(128)}, u32[]{:S(2)}) %copy-start.7) | copy-done | bytes 536
  16.7 1.5 %factor_lines.1 = (f32[2,4,6,64,128]{4,3,2,1,0:T(8,128)S(1)}, f32[2,4,3,64,128]{4,3,2,1,0:T(8,128)S(1)}, f32[1,2,64,128]{3,2,1,0:T(8,128)S(1)}, f32[1,2,64,128]{3,2,1,0:T(8,128)S(1)}, f32[2,64,128]{2,1,0:T(8,128)S(1)}) custom-call(f32[2,8]{1,0:T(2,128)S(1)} %copy-done.4, f32[2]{0:T(128)S(1)} %copy-done.5, s32[1,128]{1,0:T(1,128)S(1)} %bitcast.2, ...), custom_call_target="tpu_custom_call" | custom-call | flops 4000000 | bytes 3000000 | tf_op jit(solution)/shard_map/factor_lines/pallas_call | solution.py:269
  18.2 0.0 collective-permute-done.2.refs_3_
  18.2 0.0 collective-permute-done.1.refs_2_
  18.2 0.0 collective-permute-done.3.refs_5_
  18.2 0.0 collective-permute-done.5.refs_7_
  18.2 0.0 collective-permute-done.4.refs_6_
  18.2 1.1 %solve_lines.1 = (f32[1,2,64,128]{3,2,1,0:T(8,128)}, f32[32,1,128]{2,1,0:T(1,128)S(1)}) custom-call(f32[1,2,64,128]{3,2,1,0:T(8,128)S(1)} %get-tuple-element.9.refs_0_, f32[1,2,64,128]{3,2,1,0:T(8,128)S(1)} %collective-permute-done.refs_1_, f32[1,2,64,128]{3,2,1,0:T(8,128)S(1)} %collective-permute-done.1.refs_2_, ...), custom_call_target="tpu_custom_call" | custom-call | flops 4000000 | bytes 3000000 | tf_op jit(solution)/shard_map/solve_lines/pallas_call | solution.py:302
  19.3 11.9 %all_to_all.5 = f32[32,1,128]{2,1,0:T(1,128)S(1)} all-to-all(f32[32,1,128]{2,1,0:T(1,128)S(1)} %get-tuple-element.15), channel_id=1, replica_groups=mesh['tm'=4,'space'=8] {'tm','space'}, dimensions={0} | all-to-all | bytes 32768 | tf_op jit(solution)/shard_map/all_to_all | solution.py:314
  31.2 0.6 %reduce_sum.9 = f32[]{:T(128)} reduce(f32[32,1,128]{2,1,0:T(1,128)S(1)} %all_to_all.5, f32[]{:T(128)} %constant.1.clone.1), dimensions={0,1,2}, to_apply=%region_0.0 | reduce | flops 4095 | bytes 16392 | tf_op jit(solution)/shard_map/reduce_sum | solution.py:316
Async XLA Ops:
  0.6 9.9 %collective-permute-start = (f32[1,2,64,128]{3,2,1,0:T(8,128)}, f32[1,2,64,128]{3,2,1,0:T(8,128)S(1)}, u32[]{:S(2)}, u32[]{:S(2)}) collective-permute-start(f32[1,2,64,128]{3,2,1,0:T(8,128)} %forcing_hbm.1), channel_id=1, source_target_pairs={{0,8},{8,16},{16,24},{24,0},{1,9},{9,17},{17,25},{25,1},{2,10},{10... | collective-permute-start | bytes 196616 | tf_op jit(solution)/shard_map/ppermute | solution.py:264
  3.7 14.5 %collective-permute-start.2 = (f32[1,2,64,128]{3,2,1,0:T(8,128)}, f32[1,2,64,128]{3,2,1,0:T(8,128)S(1)}, u32[]{:S(2)}, u32[]{:S(2)}) collective-permute-start(f32[1,2,64,128]{3,2,1,0:T(8,128)} %forcing_hbm.1), channel_id=1, source_target_pairs={{0,24},{8,0},{16,8},{24,16},{1,25},{9,1},{17,9},{25,17},{2,26},{10... | collective-permute-start | bytes 196616 | tf_op jit(solution)/shard_map/ppermute | solution.py:264
  5.8 12.4 %collective-permute-start.1 = (f32[1,2,64,128]{3,2,1,0:T(8,128)}, f32[1,2,64,128]{3,2,1,0:T(8,128)S(1)}, u32[]{:S(2)}, u32[]{:S(2)}) collective-permute-start(f32[1,2,64,128]{3,2,1,0:T(8,128)} %forcing_hbm.1), channel_id=1, source_target_pairs={{0,16},{8,24},{16,0},{24,8},{1,17},{9,25},{17,1},{25,9},{2,18},{10... | collective-permute-start | bytes 196616 | tf_op jit(solution)/shard_map/ppermute | solution.py:264
  6.7 11.4 %collective-permute-start.3 = (f32[1,2,64,128]{3,2,1,0:T(8,128)}, f32[1,2,64,128]{3,2,1,0:T(8,128)S(1)}, u32[]{:S(2)}, u32[]{:S(2)}) collective-permute-start(f32[1,2,64,128]{3,2,1,0:T(8,128)} %previous_hbm.1), channel_id=1, source_target_pairs={{0,8},{8,16},{16,24},{24,0},{1,9},{9,17},{17,25},{25,1},{2,10},{10... | collective-permute-start | bytes 196616 | tf_op jit(solution)/shard_map/ppermute | solution.py:265
  8.3 9.9 %collective-permute-start.5 = (f32[1,2,64,128]{3,2,1,0:T(8,128)}, f32[1,2,64,128]{3,2,1,0:T(8,128)S(1)}, u32[]{:S(2)}, u32[]{:S(2)}) collective-permute-start(f32[1,2,64,128]{3,2,1,0:T(8,128)} %previous_hbm.1), channel_id=1, source_target_pairs={{0,24},{8,0},{16,8},{24,16},{1,25},{9,1},{17,9},{25,17},{2,26},{10... | collective-permute-start | bytes 196616 | tf_op jit(solution)/shard_map/ppermute | solution.py:265
  10.6 7.6 %collective-permute-start.4 = (f32[1,2,64,128]{3,2,1,0:T(8,128)}, f32[1,2,64,128]{3,2,1,0:T(8,128)S(1)}, u32[]{:S(2)}, u32[]{:S(2)}) collective-permute-start(f32[1,2,64,128]{3,2,1,0:T(8,128)} %previous_hbm.1), channel_id=1, source_target_pairs={{0,16},{8,24},{16,0},{24,8},{1,17},{9,25},{17,1},{25,9},{2,18},{10... | collective-permute-start | bytes 196616 | tf_op jit(solution)/shard_map/ppermute | solution.py:265
  10.8 0.8 %copy-start = (f32[2,64,128]{2,1,0:T(8,128)S(1)}, f32[2,64,128]{2,1,0:T(8,128)}, u32[]{:S(2)}) copy-start(f32[2,64,128]{2,1,0:T(8,128)} %initial_hbm.1) | copy-start | bytes 196612
  11.6 0.8 %copy-start.1 = (f32[1,2,64,128]{3,2,1,0:T(8,128)S(1)}, f32[1,2,64,128]{3,2,1,0:T(8,128)}, u32[]{:S(2)}) copy-start(f32[1,2,64,128]{3,2,1,0:T(8,128)} %forcing_hbm.1) | copy-start | bytes 196612
  12.4 0.8 %copy-start.2 = (f32[1,2,64,128]{3,2,1,0:T(8,128)S(1)}, f32[1,2,64,128]{3,2,1,0:T(8,128)}, u32[]{:S(2)}) copy-start(f32[1,2,64,128]{3,2,1,0:T(8,128)} %previous_hbm.1) | copy-start | bytes 196612
  13.3 0.8 %copy-start.3 = (s32[64,128]{1,0:T(8,128)S(1)}, s32[64,128]{1,0:T(8,128)}, u32[]{:S(2)}) copy-start(s32[64,128]{1,0:T(8,128)} %faces_hbm.1) | copy-start | bytes 98308
  14.0 0.7 %copy-start.4 = (f32[2,8]{1,0:T(2,128)S(1)}, f32[2,8]{1,0:T(2,128)}, u32[]{:S(2)}) copy-start(f32[2,8]{1,0:T(2,128)} %zones_hbm.1) | copy-start | bytes 196
  14.7 0.7 %copy-start.5 = (f32[2]{0:T(128)S(1)}, f32[2]{0:T(128)}, u32[]{:S(2)}) copy-start(f32[2]{0:T(128)} %drift_hbm.1) | copy-start | bytes 28
  15.4 0.7 %copy-start.6 = (s32[128]{0:T(128)S(1)}, s32[128]{0:T(128)}, u32[]{:S(2)}) copy-start(s32[128]{0:T(128)} %param.13) | copy-start | bytes 1540
  16.0 0.7 %copy-start.7 = (s32[128]{0:T(128)S(1)}, s32[128]{0:T(128)}, u32[]{:S(2)}) copy-start(s32[128]{0:T(128)} %param.14) | copy-start | bytes 1540

commit v3 on v2

--- a/solution.py
+++ b/solution.py
@@ -70,36 +70,53 @@
     return sum(len(shift) for unused, shift in frequencies(length))
 
 
-def factor_kernel(
-    length,
+def turn(j, n, length):
+    count = j * n % length
+    if 4 * count % length == 0:
+        return ((1.0, 0.0), (0.0, 1.0), (-1.0, 0.0), (0.0, -1.0))[4 * count // length]
+    angle = 2.0 * math.pi * count / length
+    return (math.cos(angle), math.sin(angle))
+
+
+def weighted(total, weight, value):
+    if weight == 0.0:
+        return total
+    if weight == 1.0:
+        term = value
+    elif weight == -1.0:
+        return -value if total is None else total - value
+    else:
+        term = weight * value
+    return term if total is None else total + term
+
+
+def stack_kernel(
+    forcing_hbm,
+    previous_hbm,
+    initial_hbm,
     zones_hbm,
     drift_hbm,
     zone_hbm,
     flag_hbm,
     faces_hbm,
-    forcing_hbm,
-    previous_hbm,
-    initial_hbm,
-    near_ref,
-    far_ref,
-    forcing_ref,
-    previous_ref,
+    stack_ref,
     initial_ref,
+    faces_ref,
+    rows_ref,
     zones_ref,
     drift_ref,
     zone_ref,
     flag_ref,
-    faces_ref,
     sems,
 ):
     pairs = (
-        (faces_hbm, faces_ref),
         (zones_hbm, zones_ref),
         (drift_hbm, drift_ref),
         (zone_hbm, zone_ref),
         (flag_hbm, flag_ref),
-        (forcing_hbm, forcing_ref),
-        (previous_hbm, previous_ref),
+        (forcing_hbm, stack_ref.at[0:1]),
+        (previous_hbm, stack_ref.at[1:2]),
+        (faces_hbm, faces_ref),
         (initial_hbm, initial_ref),
     )
     copies = [
@@ -108,20 +125,30 @@
     ]
     for copy in copies:
         copy.start()
-    for copy in copies[:5]:
+    for copy in copies[:4]:
         copy.wait()
+    zone = zone_ref[...]
+    for species in range(2):
+        diffusion = jnp.zeros(zone.shape, jnp.float32)
+        for index in range(zones_ref.shape[1]):
+            diffusion = jnp.where(zone == index, zones_ref[species, index], diffusion)
+        rows_ref[species : species + 1] = diffusion
+        rows_ref[2 + species : 3 + species] = jnp.full(zone.shape, drift_ref[species], jnp.float32)
+    rows_ref[4:5] = flag_ref[...].astype(jnp.float32)
+    for copy in copies[4:]:
+        copy.wait()
+
+
+def factor_kernel(length, rows_ref, faces_ref, near_ref, far_ref):
     cells, lanes = faces_ref.shape
     faces = faces_ref[...].astype(jnp.float32)
     row = lax.broadcasted_iota(jnp.int32, (cells, lanes), 0)
     link_above = jnp.where(row == cells - 1, 0.0, faces)
     link_below = jnp.where(row == 0, 0.0, roll_down(faces, 1))
-    ground = jnp.where(row == 0, flag_ref[...].astype(jnp.float32), 0.0)
-    zone = zone_ref[...]
+    ground = jnp.where(row == 0, rows_ref[4:5], 0.0)
     for species in range(2):
-        diffusion = jnp.zeros(zone.shape, jnp.float32)
-        for index in range(zones_ref.shape[1]):
-            diffusion = jnp.where(zone == index, zones_ref[species, index], diffusion)
-        drift = drift_ref[species]
+        diffusion = rows_ref[species : species + 1]
+        drift = rows_ref[2 + species : 3 + species]
         below = -(diffusion + drift) * link_below
         above = -diffusion * link_above
         centre = diffusion * (link_below + link_above) + drift + 2.0 * diffusion * ground
@@ -163,51 +190,40 @@
                     far_ref[species, plane + part, 2, rows] = substitute[part]
                 carry = (inverse, ck)
             plane += parts
-    for copy in copies[5:]:
-        copy.wait()
+
+
+def in_order(me, held):
+    bit = 1
+    while bit < len(held):
+        swap = (me & bit) != 0
+        held = [
+            jnp.where(swap, held[index ^ bit], held[index]) for index in range(len(held))
+        ]
+        bit *= 2
+    return held
 
 
 def sweep_kernel(length, *refs):
-    loads = refs[:length]
-    befores = refs[length : 2 * length]
-    initial_ref, near_ref, far_ref, new_ref, sum_ref = refs[2 * length :]
+    stacks = refs[:length]
+    initial_ref, near_ref, far_ref, new_ref, sum_ref = refs[length:]
     cells, lanes = initial_ref.shape[1:]
+    log_alpha = math.log(alpha_corner)
     me = lax.axis_index("tm")
     total = jnp.zeros((tile, lanes), jnp.float32)
     for species in range(2):
-        mine = befores[0][0, species]
-        last = mine
-        for behind in range(1, length):
-            last = jnp.where(me == (behind + length - 1) % length, befores[behind][0, species], last)
-        correction = initial_ref[species] - alpha_corner * last
-        scaled = []
-        for behind in range(length):
-            factor = math.exp(-math.log(alpha_corner) * behind / length)
-            load = loads[behind][0, species]
-            load = jnp.where(me == behind, load + correction, load)
-            scaled.append(load * jnp.where(me < behind, alpha_corner * factor, factor))
-        answer = jnp.zeros((cells, lanes), jnp.float32)
+        loads = in_order(me, [ref[0, species] for ref in stacks])
+        befores = in_order(me, [ref[1, species] for ref in stacks])
+        loads[0] = loads[0] + (initial_ref[species] - alpha_corner * befores[length - 1])
+        scaled = [math.exp(log_alpha * n / length) * load for n, load in enumerate(loads)]
+        spectrum = []
         plane = 0
         for j, shift in frequencies(length):
             parts = len(shift)
-            rhs = []
-            for part in range(parts):
-                value = jnp.zeros((cells, lanes), jnp.float32)
-                for behind in range(length):
-                    turn = j * behind % length * 4
-                    exact = {0: (1.0, 0.0), 1: (0.0, 1.0), 2: (-1.0, 0.0), 3: (0.0, -1.0)}
-                    if turn % length == 0:
-                        weight = exact[turn // length][part]
-                    else:
-                        angle = 2.0 * math.pi * j * behind / length
-                        weight = (math.cos(angle), math.sin(angle))[part]
-                    if weight == 1.0:
-                        value = value + scaled[behind]
-                    elif weight == -1.0:
-                        value = value - scaled[behind]
-                    elif weight != 0.0:
-                        value = value + weight * scaled[behind]
-                rhs.append(value)
+            rhs = [None] * parts
+            for n in range(length):
+                weights = turn(j, -n, length)
+                for part in range(parts):
+                    rhs[part] = weighted(rhs[part], weights[part], scaled[n])
             rhs = tuple(rhs)
             for step in range(near_steps):
                 distance = 1 << step
@@ -235,16 +251,25 @@
                 if carry is not None:
                     substitute = tuple(far_ref[species, plane + p, 2, rows] for p in range(parts))
                     value = c_sub(value, c_mul(substitute, carry))
-                solved[block] = value[0]
+                solved[block] = value
                 carry = value
-            weight = parts / length
-            answer = answer + weight * jnp.concatenate(solved, 0)
+            spectrum.append((j, parts, solved))
             plane += parts
-        new_ref[0, species] = answer
-        change = answer - mine
-        square = change * change
         for block in range(cells // tile):
-            total = total + square[block * tile : (block + 1) * tile]
+            rows = slice(block * tile, (block + 1) * tile)
+            mine = None
+            for n in range(length):
+                fresh = None
+                for j, parts, solved in spectrum:
+                    weights = turn(j, n, length)
+                    fresh = weighted(fresh, parts * weights[0], solved[block][0])
+                    if parts == 2:
+                        fresh = weighted(fresh, -parts * weights[1], solved[block][1])
+                fresh = fresh * (math.exp(-log_alpha * n / length) / length)
+                mine = fresh if mine is None else jnp.where(me == n, fresh, mine)
+                change = fresh - befores[n][rows]
+                total = total + change * change
+            new_ref[0, species, rows] = mine
     sum_ref[...] = jnp.broadcast_to(jnp.sum(total, axis=0, keepdims=True), sum_ref.shape)
 
 
@@ -259,60 +284,71 @@
     open_faces,
 ):
     length = lax.axis_size("tm")
+    space = lax.axis_size("space")
     cells, lanes = open_faces.shape
-    ring = [[(i, (i + step) % length) for i in range(length)] for step in range(length)]
-    loads = [lax.ppermute(forcing, "tm", ring[step]) for step in range(1, length)]
-    befores = [lax.ppermute(previous, "tm", ring[step]) for step in range(1, length)]
     whole = pl.BlockSpec(memory_space=pltpu.VMEM)
     outside = pl.BlockSpec(memory_space=pltpu.HBM)
     count = planes(length)
-    near, far, own_load, own_before, initial = pl.pallas_call(
-        functools.partial(factor_kernel, length),
+    params = pltpu.CompilerParams(vmem_limit_bytes=40 * 1024 * 1024)
+    stack, initial, faces, rows = pl.pallas_call(
+        stack_kernel,
         out_shape=(
-            jax.ShapeDtypeStruct((2, count, 2 * near_steps, cells, lanes), jnp.float32),
-            jax.ShapeDtypeStruct((2, count, 3, cells, lanes), jnp.float32),
-            jax.ShapeDtypeStruct(forcing.shape, jnp.float32),
-            jax.ShapeDtypeStruct(previous.shape, jnp.float32),
-            jax.ShapeDtypeStruct(initial_state.shape, jnp.float32),
+            pltpu.VMEM((2,) + forcing.shape[1:], jnp.float32),
+            pltpu.VMEM(initial_state.shape, jnp.float32),
+            pltpu.VMEM(open_faces.shape, jnp.int32),
+            pltpu.VMEM((tile, lanes), jnp.float32),
         ),
         in_specs=[outside] * 8,
-        out_specs=[whole] * 5,
+        out_specs=[whole] * 4,
         scratch_shapes=[
             pltpu.SMEM(zone_diffusion.shape, jnp.float32),
             pltpu.SMEM(drift_rate.shape, jnp.float32),
             pltpu.VMEM((1, lanes), jnp.int32),
             pltpu.VMEM((1, lanes), jnp.int32),
-            pltpu.VMEM((cells, lanes), jnp.int32),
             pltpu.SemaphoreType.DMA((8,)),
         ],
-        compiler_params=pltpu.CompilerParams(vmem_limit_bytes=40 * 1024 * 1024),
-        cost_estimate=pl.CostEstimate(flops=4000000, bytes_accessed=3000000, transcendentals=0),
-        name="factor_lines",
+        compiler_params=pltpu.CompilerParams(vmem_limit_bytes=62 * 1024 * 1024),
+        cost_estimate=pl.CostEstimate(flops=4000, bytes_accessed=500000, transcendentals=0),
+        name="stack_arrays",
     )(
+        forcing,
+        previous,
+        initial_state,
         zone_diffusion,
         drift_rate,
         column_zone[None],
         bottom_flag[None],
         open_faces,
-        forcing,
-        previous,
-        initial_state,
     )
-    everyone = length * lax.axis_size("space")
+    stacks = [stack]
+    for bits in range(1, length):
+        stacks.append(lax.ppermute(stack, "tm", [(i, i ^ bits) for i in range(length)]))
+    near, far = pl.pallas_call(
+        functools.partial(factor_kernel, length),
+        out_shape=(
+            jax.ShapeDtypeStruct((2, count, 2 * near_steps, cells, lanes), jnp.float32),
+            jax.ShapeDtypeStruct((2, count, 3, cells, lanes), jnp.float32),
+        ),
+        in_specs=[whole] * 2,
+        out_specs=[whole] * 2,
+        compiler_params=params,
+        cost_estimate=pl.CostEstimate(flops=4000000, bytes_accessed=3000000, transcendentals=0),
+        name="factor_lines",
+    )(rows, faces)
     new_iterate, squares = pl.pallas_call(
         functools.partial(sweep_kernel, length),
         out_shape=(
             jax.ShapeDtypeStruct(forcing.shape, jnp.float32),
-            jax.ShapeDtypeStruct((everyone, 1, lanes), jnp.float32),
+            jax.ShapeDtypeStruct((space, 1, lanes), jnp.float32),
         ),
-        in_specs=[whole] * (2 * length + 3),
+        in_specs=[whole] * (length + 3),
         out_specs=(whole, whole),
-        compiler_params=pltpu.CompilerParams(vmem_limit_bytes=40 * 1024 * 1024),
+        compiler_params=params,
         cost_estimate=pl.CostEstimate(flops=4000000, bytes_accessed=3000000, transcendentals=0),
         name="solve_lines",
-    )(own_load, *loads, own_before, *befores, initial, near, far)
-    squares = lax.all_to_all(squares, ("tm", "space"), 0, 0, tiled=True)
-    entry_count = everyone * forcing.shape[1] * cells * lanes
+    )(*stacks, initial, near, far)
+    squares = lax.all_to_all(squares, "space", 0, 0, tiled=True)
+    entry_count = length * space * forcing.shape[1] * cells * lanes
     return (new_iterate, jnp.sqrt(jnp.sum(squares) / entry_count))
 
 

time: 34.1 us -> 29.8 us (0.87)
  waiting for transfers between devices: 0.02 us -> 9.63 us
  local copies, waits for them, and re-layouts: 5.92 us -> 0 us
  starting transfers between devices: 10.1 us -> 5.76 us
  blocking collectives: 11.9 us -> 8.17 us
  Pallas kernels: 2.52 us -> 2.93 us
    ppermute x6 -> x3, waiting for transfers between devices: 0.02 us -> 9.63 us  [shards(): lax.ppermute(stack, 'tm', [(i, i ^ bits) for i in range(length)])]
    unnamed x16 -> x0, local copies, waits for them, and re-layouts: 5.92 us -> none
    ppermute x6 -> x3, starting transfers between devices: 10.1 us -> 5.76 us  [shards(): lax.ppermute(stack, 'tm', [(i, i ^ bits) for i in range(length)])]
    all_to_all x1, blocking collectives: 11.9 us -> 8.17 us  [shards(): squares = lax.all_to_all(squares, 'space', 0, 0, tiled=True)]
    pallas_call x0 -> x1, Pallas kernels: none -> 1.02 us  [shards(): pl.pallas_call(stack_kernel, out_shape=(pltpu.VMEM((2,) + forcing.shape[1...]
    pallas_call x1, Pallas kernels: 1.47 us -> 0.79 us  [shards(): pl.pallas_call(functools.partial(factor_kernel, length), out_shape=(jax.S...]
  transfers between devices with their start and end apart: 6 -> 3, of which waited for: 0 -> 2; matrix products, arithmetic and copies ran while one was open for 0% -> 0% of each run, Pallas kernels for 4% -> 3%
where the time goes in v3:
time: 29.8 us; the launch traced here: 29.6 us
  waiting for transfers between devices  9.63 us (32%)
  blocking collectives  8.17 us (27%)
  starting transfers between devices  5.76 us (19%)
  Pallas kernels  2.93 us (10%)
  between operations  2.47 us (8%)
  other arithmetic  0.61 us (2%)
    ppermute x3, waiting for transfers between devices, shards(): lax.ppermute(stack, 'tm', [(i, i ^ bits) for i in range(length)])  9.63 us
    all_to_all x1, blocking collectives, shards(): squares = lax.all_to_all(squares, 'space', 0, 0, tiled=True)  8.17 us
    ppermute x3, starting transfers between devices, shards(): lax.ppermute(stack, 'tm', [(i, i ^ bits) for i in range(length)])  5.76 us
    pallas_call x1, Pallas kernels, shards(): pl.pallas_call(functools.partial(sweep_kernel, length), out_shape=(jax.Sh...  1.12 us
    pallas_call x1, Pallas kernels, shards(): pl.pallas_call(stack_kernel, out_shape=(pltpu.VMEM((2,) + forcing.shape[1...  1.02 us
    pallas_call x1, Pallas kernels, shards(): pl.pallas_call(functools.partial(factor_kernel, length), out_shape=(jax.S...  0.79 us
    reduce_sum x1, other arithmetic, shards(): return (new_iterate, jnp.sqrt(jnp.sum(squares) / entry_count))  0.61 us
  transfers between devices with their start and end apart: 3, of which 2 were waited for; matrix products, arithmetic and copies ran while one was open for 0% of the time, Pallas kernels for 3%

profile of v3, /device:TPU:0, one launch (start us, length us, event | category | flops | bytes accessed | tf_op | source)
XLA Modules:
  0.0 29.6 jit_solution(708435288090789890)
XLA Ops:
  0.6 1.0 %stack_arrays.1 = (f32[2,2,64,128]{3,2,1,0:T(8,128)S(1)}, f32[2,64,128]{2,1,0:T(8,128)S(1)}, s32[64,128]{1,0:T(8,128)S(1)}, f32[8,128]{1,0:T(8,128)S(1)}) custom-call(f32[1,2,64,128]{3,2,1,0:T(8,128)} %forcing_hbm.1, f32[1,2,64,128]{3,2,1,0:T(8,128)} %previous_hbm.1, f32[2,64,128]{2,1,0:T(8,128)} %initial_hbm.1, f32[2,8]{1,0:T(2,128)} %zones_hbm.1, ...), custom_call_target="tpu_custom_call" | custom-call | flops 4000 | bytes 500000 | tf_op jit(solution)/shard_map/stack_arrays/pallas_call | solution.py:293
  1.7 5.1 %collective-permute-start.2 = (f32[2,2,64,128]{3,2,1,0:T(8,128)S(1)}, f32[2,2,64,128]{3,2,1,0:T(8,128)S(1)}, u32[]{:S(2)}, u32[]{:S(2)}) collective-permute-start(f32[2,2,64,128]{3,2,1,0:T(8,128)S(1)} %get-tuple-element.10.refs_0_), channel_id=1, source_target_pairs={{0,24},{8,16},{16,8},{24,0},{1,25},{9,17},{17,9},{25,1},{2,26},{10... | collective-permute-start | bytes 393224 | tf_op jit(solution)/shard_map/ppermute | solution.py:325
  6.8 0.0 collective-permute-start.1
  6.8 0.6 %collective-permute-start = (f32[2,2,64,128]{3,2,1,0:T(8,128)S(1)}, f32[2,2,64,128]{3,2,1,0:T(8,128)S(1)}, u32[]{:S(2)}, u32[]{:S(2)}) collective-permute-start(f32[2,2,64,128]{3,2,1,0:T(8,128)S(1)} %get-tuple-element.10.refs_0_), channel_id=1, source_target_pairs={{0,8},{8,0},{16,24},{24,16},{1,9},{9,1},{17,25},{25,17},{2,10},{10... | collective-permute-start | bytes 393224 | tf_op jit(solution)/shard_map/ppermute | solution.py:325
  7.4 0.8 %factor_lines.1 = (f32[2,4,6,64,128]{4,3,2,1,0:T(8,128)S(1)}, f32[2,4,3,64,128]{4,3,2,1,0:T(8,128)S(1)}) custom-call(f32[8,128]{1,0:T(8,128)S(1)} %get-tuple-element.12.rows_ref, s32[64,128]{1,0:T(8,128)S(1)} %get-tuple-element.13.faces_ref), custom_call_target="tpu_custom_call" | custom-call | flops 4000000 | bytes 3000000 | tf_op jit(solution)/shard_map/factor_lines/pallas_call | solution.py:326
  8.2 3.0 %collective-permute-done.2.refs_3_ = f32[2,2,64,128]{3,2,1,0:T(8,128)S(1)} collective-permute-done((f32[2,2,64,128]{3,2,1,0:T(8,128)S(1)}, f32[2,2,64,128]{3,2,1,0:T(8,128)S(1)}, u32[]{:S(2)}, u32[]{:S(2)}) %collective-permute-start.2) | collective-permute-done | bytes 131104 | tf_op jit(solution)/shard_map/ppermute | solution.py:325
  11.2 6.6 %collective-permute-done.1.refs_2_ = f32[2,2,64,128]{3,2,1,0:T(8,128)S(1)} collective-permute-done((f32[2,2,64,128]{3,2,1,0:T(8,128)S(1)}, f32[2,2,64,128]{3,2,1,0:T(8,128)S(1)}, u32[]{:S(2)}, u32[]{:S(2)}) %collective-permute-start.1) | collective-permute-done | bytes 131104 | tf_op jit(solution)/shard_map/ppermute | solution.py:325
  17.9 0.0 collective-permute-done.refs_1_
  17.9 1.1 %solve_lines.1 = (f32[1,2,64,128]{3,2,1,0:T(8,128)}, f32[8,1,128]{2,1,0:T(1,128)S(1)}) custom-call(f32[2,2,64,128]{3,2,1,0:T(8,128)S(1)} %get-tuple-element.10.refs_0_, f32[2,2,64,128]{3,2,1,0:T(8,128)S(1)} %collective-permute-done.refs_1_, f32[2,2,64,128]{3,2,1,0:T(8,128)S(1)} %collective-permute-done.1.refs_2_, ...), custom_call_target="tpu_custom_call" | custom-call | flops 4000000 | bytes 3000000 | tf_op jit(solution)/shard_map/solve_lines/pallas_call | solution.py:338
  19.0 8.2 %all_to_all.5 = f32[8,1,128]{2,1,0:T(1,128)S(1)} all-to-all(f32[8,1,128]{2,1,0:T(1,128)S(1)} %get-tuple-element.17), channel_id=1, replica_groups=mesh['tm'=4,'space'=8] {'space'}, dimensions={0} | all-to-all | bytes 8192 | tf_op jit(solution)/shard_map/all_to_all | solution.py:350
  27.1 0.6 %reduce_sum.9 = f32[]{:T(128)} reduce(f32[8,1,128]{2,1,0:T(1,128)S(1)} %all_to_all.5, f32[]{:T(128)} %constant.1.clone.1), dimensions={0,1,2}, to_apply=%region_0.0 | reduce | flops 1023 | bytes 4104 | tf_op jit(solution)/shard_map/reduce_sum | solution.py:352
Async XLA Ops:
  1.7 9.5 %collective-permute-start.2 = (f32[2,2,64,128]{3,2,1,0:T(8,128)S(1)}, f32[2,2,64,128]{3,2,1,0:T(8,128)S(1)}, u32[]{:S(2)}, u32[]{:S(2)}) collective-permute-start(f32[2,2,64,128]{3,2,1,0:T(8,128)S(1)} %get-tuple-element.10.refs_0_), channel_id=1, source_target_pairs={{0,24},{8,16},{16,8},{24,0},{1,25},{9,17},{17,9},{25,1},{2,26},{10... | collective-permute-start | bytes 393224 | tf_op jit(solution)/shard_map/ppermute | solution.py:325
  6.8 11.1 %collective-permute-start.1 = (f32[2,2,64,128]{3,2,1,0:T(8,128)S(1)}, f32[2,2,64,128]{3,2,1,0:T(8,128)S(1)}, u32[]{:S(2)}, u32[]{:S(2)}) collective-permute-start(f32[2,2,64,128]{3,2,1,0:T(8,128)S(1)} %get-tuple-element.10.refs_0_), channel_id=1, source_target_pairs={{0,16},{8,24},{16,0},{24,8},{1,17},{9,25},{17,1},{25,9},{2,18},{10... | collective-permute-start | bytes 393224 | tf_op jit(solution)/shard_map/ppermute | solution.py:325
  6.8 11.1 %collective-permute-start = (f32[2,2,64,128]{3,2,1,0:T(8,128)S(1)}, f32[2,2,64,128]{3,2,1,0:T(8,128)S(1)}, u32[]{:S(2)}, u32[]{:S(2)}) collective-permute-start(f32[2,2,64,128]{3,2,1,0:T(8,128)S(1)} %get-tuple-element.10.refs_0_), channel_id=1, source_target_pairs={{0,8},{8,0},{16,24},{24,16},{1,9},{9,1},{17,25},{25,17},{2,10},{10... | collective-permute-start | bytes 393224 | tf_op jit(solution)/shard_map/ppermute | solution.py:325

commit v4 on v3

v4 whole, which is shorter than its diff:
```python
import functools
import math

import jax
import jax.numpy as jnp
from jax import lax
from jax.experimental import pallas as pl
from jax.experimental.pallas import tpu as pltpu
from jax.sharding import PartitionSpec as P

alpha_corner = 0.3
tile = 8
near_steps = 3


def roll_down(block, distance):
    return pltpu.roll(block, distance, 0)


def roll_up(block, distance):
    return pltpu.roll(block, block.shape[0] - distance, 0)


def c_mul(x, y):
    if len(x) == 1 and len(y) == 1:
        return (x[0] * y[0],)
    if len(x) == 1:
        return (x[0] * y[0], x[0] * y[1])
    if len(y) == 1:
        return (x[0] * y[0], x[1] * y[0])
    return (x[0] * y[0] - x[1] * y[1], x[0] * y[1] + x[1] * y[0])


def c_add(x, y):
    return tuple(p + q for p, q in zip(x, y))


def c_sub(x, y):
    return tuple(p - q for p, q in zip(x, y))


def c_neg(x):
    return tuple(-p for p in x)


def c_inverse(x):
    if len(x) == 1:
        return (1.0 / x[0],)
    scale = 1.0 / (x[0] * x[0] + x[1] * x[1])
    return (x[0] * scale, -x[1] * scale)


def c_map(f, x):
    return tuple(f(p) for p in x)


def frequencies(length):
    root = math.exp(math.log(alpha_corner) / length)
    listed = []
    for j in range(length // 2 + 1):
        angle = 2.0 * math.pi * j / length
        if j == 0 or 2 * j == length:
            listed.append((j, (1.0 - root * math.cos(angle),)))
        else:
            listed.append((j, (1.0 - root * math.cos(angle), root * math.sin(angle))))
    return listed


def planes(length):
    return sum(len(shift) for unused, shift in frequencies(length))


def turn(j, n, length):
    count = j * n % length
    if 4 * count % length == 0:
        return ((1.0, 0.0), (0.0, 1.0), (-1.0, 0.0), (0.0, -1.0))[4 * count // length]
    angle = 2.0 * math.pi * count / length
    return (math.cos(angle), math.sin(angle))


def weighted(total, weight, value):
    if weight == 0.0:
        return total
    if weight == 1.0:
        term = value
    elif weight == -1.0:
        return -value if total is None else total - value
    else:
        term = weight * value
    return term if total is None else total + term


def stack_kernel(
    forcing_hbm,
    previous_hbm,
    initial_hbm,
    zones_hbm,
    drift_hbm,
    zone_hbm,
    flag_hbm,
    faces_hbm,
    mine_ref,
    other_ref,
    initial_ref,
    faces_ref,
    rows_ref,
    zones_ref,
    drift_ref,
    zone_ref,
    flag_ref,
    sems,
):
    species = lax.axis_index("tm") % 2
    pairs = (
        (zones_hbm, zones_ref),
        (drift_hbm, drift_ref),
        (zone_hbm, zone_ref),
        (flag_hbm, flag_ref),
        (forcing_hbm.at[0, species], mine_ref.at[0]),
        (previous_hbm.at[0, species], mine_ref.at[1]),
        (forcing_hbm.at[0, 1 - species], other_ref.at[0]),
        (previous_hbm.at[0, 1 - species], other_ref.at[1]),
        (faces_hbm, faces_ref),
        (initial_hbm.at[species], initial_ref),
    )
    copies = [
        pltpu.make_async_copy(source, target, sems.at[index])
        for index, (source, target) in enumerate(pairs)
    ]
    for copy in copies:
        copy.start()
    for copy in copies[:4]:
        copy.wait()
    zone = zone_ref[...]
    diffusion = jnp.zeros(zone.shape, jnp.float32)
    for index in range(zones_ref.shape[1]):
        diffusion = jnp.where(zone == index, zones_ref[species, index], diffusion)
    rows_ref[0:1] = diffusion
    rows_ref[1:2] = jnp.full(zone.shape, drift_ref[species], jnp.float32)
    rows_ref[2:3] = flag_ref[...].astype(jnp.float32)
    for copy in copies[4:]:
        copy.wait()


def factor_kernel(length, rows_ref, faces_ref, near_ref, far_ref):
    cells, lanes = faces_ref.shape
    faces = faces_ref[...].astype(jnp.float32)
    row = lax.broadcasted_iota(jnp.int32, (cells, lanes), 0)
    link_above = jnp.where(row == cells - 1, 0.0, faces)
    link_below = jnp.where(row == 0, 0.0, roll_down(faces, 1))
    ground = jnp.where(row == 0, rows_ref[2:3], 0.0)
    diffusion = rows_ref[0:1]
    drift = rows_ref[1:2]
    below = -(diffusion + drift) * link_below
    above = -diffusion * link_above
    centre = diffusion * (link_below + link_above) + drift + 2.0 * diffusion * ground
    plane = 0
    for unused, shift in frequencies(length):
        parts = len(shift)
        a = (below,)
        c = (above,)
        b = (centre + shift[0],)
        if parts == 2:
            b = b + (jnp.full_like(centre, shift[1]),)
        for step in range(near_steps):
            distance = 1 << step
            inverse = c_inverse(b)
            low = c_neg(c_mul(a, c_map(lambda p: roll_down(p, distance), inverse)))
            high = c_neg(c_mul(c, c_map(lambda p: roll_up(p, distance), inverse)))
            down_c = c_map(lambda p: roll_down(p, distance), c)
            up_a = c_map(lambda p: roll_up(p, distance), a)
            b = c_add(b, c_add(c_mul(low, down_c), c_mul(high, up_a)))
            a = c_mul(low, c_map(lambda p: roll_down(p, distance), a))
            c = c_mul(high, c_map(lambda p: roll_up(p, distance), c))
            for part in range(parts):
                near_ref[plane + part, 2 * step] = low[part]
                near_ref[plane + part, 2 * step + 1] = high[part]
        carry = None
        for block in range(cells // tile):
            rows = slice(block * tile, (block + 1) * tile)
            ak, bk, ck = (c_map(lambda p: p[rows], item) for item in (a, b, c))
            if carry is None:
                eliminate = c_map(jnp.zeros_like, ak)
            else:
                eliminate = c_mul(ak, carry[0])
                bk = c_sub(bk, c_mul(eliminate, carry[1]))
            inverse = c_inverse(bk)
            substitute = c_mul(ck, inverse)
            for part in range(parts):
                far_ref[plane + part, 0, rows] = eliminate[part]
                far_ref[plane + part, 1, rows] = inverse[part]
                far_ref[plane + part, 2, rows] = substitute[part]
            carry = (inverse, ck)
        plane += parts


def in_order(me, held):
    bit = 1
    while bit < len(held):
        swap = (me & bit) != 0
        held = [
            jnp.where(swap, held[index ^ bit], held[index]) for index in range(len(held))
        ]
        bit *= 2
    return held


def sweep_kernel(length, *refs):
    stacks = refs[:length]
    initial_ref, near_ref, far_ref, own_ref, give_ref, sum_ref = refs[length:]
    cells, lanes = initial_ref.shape
    log_alpha = math.log(alpha_corner)
    me = lax.axis_index("tm")
    loads = in_order(me, [ref[0] for ref in stacks])
    befores = in_order(me, [ref[1] for ref in stacks])
    loads[0] = loads[0] + (initial_ref[...] - alpha_corner * befores[length - 1])
    scaled = [math.exp(log_alpha * n / length) * load for n, load in enumerate(loads)]
    spectrum = []
    plane = 0
    for j, shift in frequencies(length):
        parts = len(shift)
        rhs = [None] * parts
        for n in range(length):
            weights = turn(j, -n, length)
            for part in range(parts):
                rhs[part] = weighted(rhs[part], weights[part], scaled[n])
        rhs = tuple(rhs)
        for step in range(near_steps):
            distance = 1 << step
            low = tuple(near_ref[plane + p, 2 * step] for p in range(parts))
            high = tuple(near_ref[plane + p, 2 * step + 1] for p in range(parts))
            down = c_map(lambda p: roll_down(p, distance), rhs)
            up = c_map(lambda p: roll_up(p, distance), rhs)
            rhs = c_add(rhs, c_add(c_mul(low, down), c_mul(high, up)))
        blocks = []
        carry = None
        for block in range(cells // tile):
            rows = slice(block * tile, (block + 1) * tile)
            value = c_map(lambda p: p[rows], rhs)
            if carry is not None:
                eliminate = tuple(far_ref[plane + p, 0, rows] for p in range(parts))
                value = c_sub(value, c_mul(eliminate, carry))
            blocks.append(value)
            carry = value
        solved = [None] * len(blocks)
        carry = None
        for block in reversed(range(cells // tile)):
            rows = slice(block * tile, (block + 1) * tile)
            inverse = tuple(far_ref[plane + p, 1, rows] for p in range(parts))
            value = c_mul(inverse, blocks[block])
            if carry is not None:
                substitute = tuple(far_ref[plane + p, 2, rows] for p in range(parts))
                value = c_sub(value, c_mul(substitute, carry))
            solved[block] = value
            carry = value
        spectrum.append((j, parts, solved))
        plane += parts
    total = jnp.zeros((tile, lanes), jnp.float32)
    for block in range(cells // tile):
        rows = slice(block * tile, (block + 1) * tile)
        steps = []
        for n in range(length):
            fresh = None
            for j, parts, solved in spectrum:
                weights = turn(j, n, length)
                fresh = weighted(fresh, parts * weights[0], solved[block][0])
                if parts == 2:
                    fresh = weighted(fresh, -parts * weights[1], solved[block][1])
            fresh = fresh * (math.exp(-log_alpha * n / length) / length)
            steps.append(fresh)
            change = fresh - befores[n][rows]
            total = total + change * change
        own = steps[0]
        give = steps[1]
        for n in range(1, length):
            own = jnp.where(me == n, steps[n], own)
            give = jnp.where(me == n, steps[n ^ 1], give)
        own_ref[rows] = own
        give_ref[rows] = give
    give_ref[cells:] = total
    sum_ref[...] = total


def join_kernel(own_ref, got_ref, new_hbm, sems):
    species = lax.axis_index("tm") % 2
    cells = own_ref.shape[0]
    copies = (
        pltpu.make_async_copy(own_ref, new_hbm.at[0, species], sems.at[0]),
        pltpu.make_async_copy(got_ref.at[:cells], new_hbm.at[0, 1 - species], sems.at[1]),
    )
    for copy in copies:
        copy.start()
    for copy in copies:
        copy.wait()


def exchange(value, axis, bits):
    pairs = [(index, index ^ bits) for index in range(lax.axis_size(axis))]
    return lax.ppermute(value, axis, pairs)


def shards(
    forcing,
    initial_state,
    previous,
    zone_diffusion,
    drift_rate,
    column_zone,
    bottom_flag,
    open_faces,
):
    length = lax.axis_size("tm")
    space = lax.axis_size("space")
    cells, lanes = open_faces.shape
    whole = pl.BlockSpec(memory_space=pltpu.VMEM)
    outside = pl.BlockSpec(memory_space=pltpu.HBM)
    count = planes(length)
    params = pltpu.CompilerParams(vmem_limit_bytes=40 * 1024 * 1024)
    mine, other, initial, faces, rows = pl.pallas_call(
        stack_kernel,
        out_shape=(
            pltpu.VMEM((2, cells, lanes), jnp.float32),
            pltpu.VMEM((2, cells, lanes), jnp.float32),
            pltpu.VMEM((cells, lanes), jnp.float32),
            pltpu.VMEM((cells, lanes), jnp.int32),
            pltpu.VMEM((tile, lanes), jnp.float32),
        ),
        in_specs=[outside] * 8,
        out_specs=[whole] * 5,
        scratch_shapes=[
            pltpu.SMEM(zone_diffusion.shape, jnp.float32),
            pltpu.SMEM(drift_rate.shape, jnp.float32),
            pltpu.VMEM((1, lanes), jnp.int32),
            pltpu.VMEM((1, lanes), jnp.int32),
            pltpu.SemaphoreType.DMA((10,)),
        ],
        compiler_params=pltpu.CompilerParams(vmem_limit_bytes=62 * 1024 * 1024),
        cost_estimate=pl.CostEstimate(flops=4000, bytes_accessed=500000, transcendentals=0),
        name="stack_arrays",
    )(
        forcing,
        previous,
        initial_state,
        zone_diffusion,
        drift_rate,
        column_zone[None],
        bottom_flag[None],
        open_faces,
    )
    stacks = [mine]
    for bits in range(1, length):
        stacks.append(exchange(other if bits % 2 else mine, "tm", bits))
    near, far = pl.pallas_call(
        functools.partial(factor_kernel, length),
        out_shape=(
            jax.ShapeDtypeStruct((count, 2 * near_steps, cells, lanes), jnp.float32),
            jax.ShapeDtypeStruct((count, 3, cells, lanes), jnp.float32),
        ),
        in_specs=[whole] * 2,
        out_specs=[whole] * 2,
        compiler_params=params,
        cost_estimate=pl.CostEstimate(flops=4000000, bytes_accessed=3000000, transcendentals=0),
        name="factor_lines",
    )(rows, faces)
    own, give, squares = pl.pallas_call(
        functools.partial(sweep_kernel, length),
        out_shape=(
            pltpu.VMEM((cells, lanes), jnp.float32),
            pltpu.VMEM((cells + tile, lanes), jnp.float32),
            pltpu.VMEM((tile, lanes), jnp.float32),
        ),
        in_specs=[whole] * (length + 3),
        out_specs=[whole] * 3,
        compiler_params=params,
        cost_estimate=pl.CostEstimate(flops=4000000, bytes_accessed=3000000, transcendentals=0),
        name="solve_lines",
    )(*stacks, initial, near, far)
    got = exchange(give, "tm", 1)
    new_iterate = pl.pallas_call(
        join_kernel,
        out_shape=jax.ShapeDtypeStruct(forcing.shape, jnp.float32),
        in_specs=[whole] * 2,
        out_specs=outside,
        scratch_shapes=[pltpu.SemaphoreType.DMA((2,))],
        compiler_params=params,
        cost_estimate=pl.CostEstimate(flops=4000, bytes_accessed=100000, transcendentals=0),
        name="join_species",
    )(own, got)
    squares = squares + got[cells:]
    bits = 1
    while bits < space:
        squares = squares + exchange(squares, "space", bits)
        bits *= 2
    entry_count = length * space * forcing.shape[1] * cells * lanes
    return (new_iterate, jnp.sqrt(jnp.sum(squares) / entry_count))


def solution(mesh):
    placed = (
        P("tm", None, None, "space"),
        P(None, None, "space"),
        P("tm", None, None, "space"),
        P(),
        P(),
        P("space"),
        P("space"),
        P(None, "space"),
    )
    return jax.shard_map(
        shards,
        mesh=mesh,
        in_specs=placed,
        out_specs=(P("tm", None, None, "space"), P()),
        check_vma=False,
    )
```

time: 29.8 us -> 27.3 us (0.916)
  blocking collectives: 8.17 us -> 0 us
  starting transfers between devices: 5.76 us -> 9.52 us
  waiting for transfers between devices: 9.63 us -> 12.2 us
  Pallas kernels: 2.93 us -> 2.28 us
    all_to_all x1 -> x0, blocking collectives: 8.17 us -> none  [shards(): squares = lax.all_to_all(squares, 'space', 0, 0, tiled=True)]
    ppermute x3 -> x7, starting transfers between devices: 5.76 us -> 9.52 us  [exchange(): return lax.ppermute(value, axis, pairs)]
    ppermute x3 -> x7, waiting for transfers between devices: 9.63 us -> 12.2 us  [exchange(): return lax.ppermute(value, axis, pairs)]
    pallas_call x1, Pallas kernels: 0.79 us -> 0.41 us  [shards(): pl.pallas_call(functools.partial(factor_kernel, length), out_shape=(jax.S...]
    pallas_call x2 -> x3, Pallas kernels: 2.14 us -> 1.87 us  [the longest x1 0.96 us: shards(): pl.pallas_call(stack_kernel, out_shape=(pltpu.VMEM((2, cells, lanes), jnp...]
  transfers between devices with their start and end apart: 3 -> 7, of which waited for: 2 -> 7; matrix products, arithmetic and copies ran while one was open for 0% -> 0% of each run, Pallas kernels for 3% -> 4%
where the time goes in v4:
time: 27.3 us; the launch traced here: 27.1 us
  waiting for transfers between devices  12.2 us (45%)
  starting transfers between devices  9.52 us (35%)
  between operations  2.48 us (9%)
  Pallas kernels  2.28 us (8%)
  other arithmetic  0.61 us (2%)
    ppermute x7, waiting for transfers between devices, exchange(): return lax.ppermute(value, axis, pairs)  12.2 us
    ppermute x7, starting transfers between devices, exchange(): return lax.ppermute(value, axis, pairs)  9.52 us
    pallas_call x1, Pallas kernels, shards(): pl.pallas_call(stack_kernel, out_shape=(pltpu.VMEM((2, cells, lanes), jnp...  0.96 us
    pallas_call x1, Pallas kernels, shards(): pl.pallas_call(join_kernel, out_shape=jax.ShapeDtypeStruct(forcing.shape,...  0.64 us
    reduce_sum x1, other arithmetic, shards(): return (new_iterate, jnp.sqrt(jnp.sum(squares) / entry_count))  0.6 us
  transfers between devices with their start and end apart: 7, of which 7 were waited for; matrix products, arithmetic and copies ran while one was open for 0% of the time, Pallas kernels for 4%

profile of v4, /device:TPU:0, one launch (start us, length us, event | category | flops | bytes accessed | tf_op | source)
XLA Modules:
  0.0 27.1 jit_solution(5826544529884349000)
XLA Ops:
  0.6 1.0 %stack_arrays.1 = (f32[2,64,128]{2,1,0:T(8,128)S(1)}, f32[2,64,128]{2,1,0:T(8,128)S(1)}, f32[64,128]{1,0:T(8,128)S(1)}, s32[64,128]{1,0:T(8,128)S(1)}, f32[8,128]{1,0:T(8,128)S(1)}) custom-call(f32[1,2,64,128]{3,2,1,0:T(8,128)} %forcing_hbm.1, f32[1,2,64,128]{3,2,1,0:T(8,128)} %previous_hbm.1, f32[2,64,128]{2,1,0:T(8,128)} %initial_hbm.1, f32[2,8]{1,0:T(2,128)} %zones_hbm.1, ...), custom_call_target="tpu_custom_call" | custom-call | flops 4000 | bytes 500000 | tf_op jit(solution)/shard_map/stack_arrays/pallas_call | solution.py:319
  1.6 4.1 %collective-permute-start.1 = (f32[2,64,128]{2,1,0:T(8,128)S(1)}, f32[2,64,128]{2,1,0:T(8,128)S(1)}, u32[]{:S(2)}, u32[]{:S(2)}) collective-permute-start(f32[2,64,128]{2,1,0:T(8,128)S(1)} %get-tuple-element.12.refs_0_), channel_id=1, source_target_pairs={{0,16},{8,24},{16,0},{24,8},{1,17},{9,25},{17,1},{25,9},{2,18},{10... | collective-permute-start | bytes 196616 | tf_op jit(solution)/shard_map/ppermute | solution.py:299
  5.7 1.3 %collective-permute-start.2 = (f32[2,64,128]{2,1,0:T(8,128)S(1)}, f32[2,64,128]{2,1,0:T(8,128)S(1)}, u32[]{:S(2)}, u32[]{:S(2)}) collective-permute-start(f32[2,64,128]{2,1,0:T(8,128)S(1)} %get-tuple-element.13), channel_id=1, source_target_pairs={{0,24},{8,16},{16,8},{24,0},{1,25},{9,17},{17,9},{25,1},{2,26},{10... | collective-permute-start | bytes 196616 | tf_op jit(solution)/shard_map/ppermute | solution.py:299
  7.1 0.2 collective-permute-start
  7.3 0.4 %factor_lines.1 = (f32[4,6,64,128]{3,2,1,0:T(8,128)S(1)}, f32[4,3,64,128]{3,2,1,0:T(8,128)S(1)}) custom-call(f32[8,128]{1,0:T(8,128)S(1)} %get-tuple-element.15.rows_ref, s32[64,128]{1,0:T(8,128)S(1)} %get-tuple-element.16.faces_ref), custom_call_target="tpu_custom_call" | custom-call | flops 4000000 | bytes 3000000 | tf_op jit(solution)/shard_map/factor_lines/pallas_call | solution.py:353
  7.7 1.8 %collective-permute-done.1.refs_2_ = f32[2,64,128]{2,1,0:T(8,128)S(1)} collective-permute-done((f32[2,64,128]{2,1,0:T(8,128)S(1)}, f32[2,64,128]{2,1,0:T(8,128)S(1)}, u32[]{:S(2)}, u32[]{:S(2)}) %collective-permute-start.1) | collective-permute-done | bytes 65568 | tf_op jit(solution)/shard_map/ppermute | solution.py:299
  9.5 2.5 %collective-permute-done.2.refs_3_ = f32[2,64,128]{2,1,0:T(8,128)S(1)} collective-permute-done((f32[2,64,128]{2,1,0:T(8,128)S(1)}, f32[2,64,128]{2,1,0:T(8,128)S(1)}, u32[]{:S(2)}, u32[]{:S(2)}) %collective-permute-start.2) | collective-permute-done | bytes 65568 | tf_op jit(solution)/shard_map/ppermute | solution.py:299
  11.9 0.1 collective-permute-done.refs_1_
  12.0 0.3 solve_lines.1
  12.3 0.8 %collective-permute-start.3 = (f32[72,128]{1,0:T(8,128)S(1)}, f32[72,128]{1,0:T(8,128)S(1)}, u32[]{:S(2)}, u32[]{:S(2)}) collective-permute-start(f32[72,128]{1,0:T(8,128)S(1)} %get-tuple-element.20), channel_id=1, source_target_pairs={{0,8},{8,0},{16,24},{24,16},{1,9},{9,1},{17,25},{25,17},{2,10},{10... | collective-permute-start | bytes 110600 | tf_op jit(solution)/shard_map/ppermute | solution.py:299
  13.1 3.2 %collective-permute-done.3.got_ref = f32[72,128]{1,0:T(8,128)S(1)} collective-permute-done((f32[72,128]{1,0:T(8,128)S(1)}, f32[72,128]{1,0:T(8,128)S(1)}, u32[]{:S(2)}, u32[]{:S(2)}) %collective-permute-start.3) | collective-permute-done | bytes 36896 | tf_op jit(solution)/shard_map/ppermute | solution.py:299
  16.3 0.0 collective-permute-start.4
  16.3 1.2 %collective-permute-done.4 = f32[8,128]{1,0:T(8,128)S(1)} collective-permute-done((f32[8,128]{1,0:T(8,128)S(1)}, f32[8,128]{1,0:T(8,128)S(1)}, u32[]{:S(2)}, u32[]{:S(2)}) %collective-permute-start.4) | collective-permute-done | bytes 4128 | tf_op jit(solution)/shard_map/ppermute | solution.py:299
  17.5 1.5 %collective-permute-start.5 = (f32[8,128]{1,0:T(8,128)S(1)}, f32[8,128]{1,0:T(8,128)S(1)}, u32[]{:S(2)}, u32[]{:S(2)}) collective-permute-start(f32[8,128]{1,0:T(8,128)S(1)} %add.13), channel_id=1, source_target_pairs={{0,2},{1,3},{2,0},{3,1},{4,6},{5,7},{6,4},{7,5},{8,10},{9,11},{10,... | collective-permute-start | bytes 12296 | tf_op jit(solution)/shard_map/ppermute | solution.py:299
  19.0 2.1 %collective-permute-done.5 = f32[8,128]{1,0:T(8,128)S(1)} collective-permute-done((f32[8,128]{1,0:T(8,128)S(1)}, f32[8,128]{1,0:T(8,128)S(1)}, u32[]{:S(2)}, u32[]{:S(2)}) %collective-permute-start.5) | collective-permute-done | bytes 4128 | tf_op jit(solution)/shard_map/ppermute | solution.py:299
  21.1 1.5 %collective-permute-start.6 = (f32[8,128]{1,0:T(8,128)S(1)}, f32[8,128]{1,0:T(8,128)S(1)}, u32[]{:S(2)}, u32[]{:S(2)}) collective-permute-start(f32[8,128]{1,0:T(8,128)S(1)} %add.14), channel_id=1, source_target_pairs={{0,4},{1,5},{2,6},{3,7},{4,0},{5,1},{6,2},{7,3},{8,12},{9,13},{10,... | collective-permute-start | bytes 12296 | tf_op jit(solution)/shard_map/ppermute | solution.py:299
  22.6 0.6 %join_species.1 = f32[1,2,64,128]{3,2,1,0:T(8,128)} custom-call(f32[64,128]{1,0:T(8,128)S(1)} %get-tuple-element.19.own_ref, f32[72,128]{1,0:T(8,128)S(1)} %collective-permute-done.3.got_ref), custom_call_target="tpu_custom_call" | custom-call | flops 4000 | bytes 100000 | tf_op jit(solution)/shard_map/join_species/pallas_call | solution.py:379
  23.3 1.4 %collective-permute-done.6 = f32[8,128]{1,0:T(8,128)S(1)} collective-permute-done((f32[8,128]{1,0:T(8,128)S(1)}, f32[8,128]{1,0:T(8,128)S(1)}, u32[]{:S(2)}, u32[]{:S(2)}) %collective-permute-start.6) | collective-permute-done | bytes 4128 | tf_op jit(solution)/shard_map/ppermute | solution.py:299
  24.7 0.6 %add_reduce_fusion = f32[]{:T(128)} fusion(f32[8,128]{1,0:T(8,128)S(1)} %add.14, f32[8,128]{1,0:T(8,128)S(1)} %collective-permute-done.6), kind=kLoop, calls=%fused_computation.1 | loop fusion | flops 2047 | bytes 8196 | tf_op jit(solution)/shard_map/reduce_sum | solution.py:395
  (3 shorter events, 0.0 us)
Async XLA Ops:
  1.6 7.9 %collective-permute-start.1 = (f32[2,64,128]{2,1,0:T(8,128)S(1)}, f32[2,64,128]{2,1,0:T(8,128)S(1)}, u32[]{:S(2)}, u32[]{:S(2)}) collective-permute-start(f32[2,64,128]{2,1,0:T(8,128)S(1)} %get-tuple-element.12.refs_0_), channel_id=1, source_target_pairs={{0,16},{8,24},{16,0},{24,8},{1,17},{9,25},{17,1},{25,9},{2,18},{10... | collective-permute-start | bytes 196616 | tf_op jit(solution)/shard_map/ppermute | solution.py:299
  5.7 6.2 %collective-permute-start.2 = (f32[2,64,128]{2,1,0:T(8,128)S(1)}, f32[2,64,128]{2,1,0:T(8,128)S(1)}, u32[]{:S(2)}, u32[]{:S(2)}) collective-permute-start(f32[2,64,128]{2,1,0:T(8,128)S(1)} %get-tuple-element.13), channel_id=1, source_target_pairs={{0,24},{8,16},{16,8},{24,0},{1,25},{9,17},{17,9},{25,1},{2,26},{10... | collective-permute-start | bytes 196616 | tf_op jit(solution)/shard_map/ppermute | solution.py:299
  7.1 5.0 %collective-permute-start = (f32[2,64,128]{2,1,0:T(8,128)S(1)}, f32[2,64,128]{2,1,0:T(8,128)S(1)}, u32[]{:S(2)}, u32[]{:S(2)}) collective-permute-start(f32[2,64,128]{2,1,0:T(8,128)S(1)} %get-tuple-element.13), channel_id=1, source_target_pairs={{0,8},{8,0},{16,24},{24,16},{1,9},{9,1},{17,25},{25,17},{2,10},{10... | collective-permute-start | bytes 196616 | tf_op jit(solution)/shard_map/ppermute | solution.py:299
  12.3 4.0 %collective-permute-start.3 = (f32[72,128]{1,0:T(8,128)S(1)}, f32[72,128]{1,0:T(8,128)S(1)}, u32[]{:S(2)}, u32[]{:S(2)}) collective-permute-start(f32[72,128]{1,0:T(8,128)S(1)} %get-tuple-element.20), channel_id=1, source_target_pairs={{0,8},{8,0},{16,24},{24,16},{1,9},{9,1},{17,25},{25,17},{2,10},{10... | collective-permute-start | bytes 110600 | tf_op jit(solution)/shard_map/ppermute | solution.py:299
  16.3 1.2 %collective-permute-start.4 = (f32[8,128]{1,0:T(8,128)S(1)}, f32[8,128]{1,0:T(8,128)S(1)}, u32[]{:S(2)}, u32[]{:S(2)}) collective-permute-start(f32[8,128]{1,0:T(8,128)S(1)} %slice_add_fusion), channel_id=1, source_target_pairs={{0,1},{1,0},{2,3},{3,2},{4,5},{5,4},{6,7},{7,6},{8,9},{9,8},{10,11... | collective-permute-start | bytes 12296 | tf_op jit(solution)/shard_map/ppermute | solution.py:299
  17.5 3.6 %collective-permute-start.5 = (f32[8,128]{1,0:T(8,128)S(1)}, f32[8,128]{1,0:T(8,128)S(1)}, u32[]{:S(2)}, u32[]{:S(2)}) collective-permute-start(f32[8,128]{1,0:T(8,128)S(1)} %add.13), channel_id=1, source_target_pairs={{0,2},{1,3},{2,0},{3,1},{4,6},{5,7},{6,4},{7,5},{8,10},{9,11},{10,... | collective-permute-start | bytes 12296 | tf_op jit(solution)/shard_map/ppermute | solution.py:299
  21.1 3.6 %collective-permute-start.6 = (f32[8,128]{1,0:T(8,128)S(1)}, f32[8,128]{1,0:T(8,128)S(1)}, u32[]{:S(2)}, u32[]{:S(2)}) collective-permute-start(f32[8,128]{1,0:T(8,128)S(1)} %add.14), channel_id=1, source_target_pairs={{0,4},{1,5},{2,6},{3,7},{4,0},{5,1},{6,2},{7,3},{8,12},{9,13},{10,... | collective-permute-start | bytes 12296 | tf_op jit(solution)/shard_map/ppermute | solution.py:299

commit v5 on v4

--- a/solution.py
+++ b/solution.py
@@ -297,6 +297,11 @@
 def exchange(value, axis, bits):
     pairs = [(index, index ^ bits) for index in range(lax.axis_size(axis))]
     return lax.ppermute(value, axis, pairs)
+
+
+def exchange_odd(value, bits):
+    pairs = [(index, index ^ bits) for index in range(1, lax.axis_size("space"), 2)]
+    return lax.ppermute(value, "space", pairs)
 
 
 def shards(
@@ -375,7 +380,15 @@
         cost_estimate=pl.CostEstimate(flops=4000000, bytes_accessed=3000000, transcendentals=0),
         name="solve_lines",
     )(*stacks, initial, near, far)
-    got = exchange(give, "tm", 1)
+    squares = squares + exchange(squares, "space", 1)
+    got = exchange(give.at[cells:].set(squares), "tm", 1)
+    squares = squares + got[cells:]
+    bits = 2
+    while bits < space:
+        squares = squares + exchange_odd(squares, bits)
+        bits *= 2
+    odd = lax.axis_index("space") % 2 == 1
+    squares = jnp.where(odd, squares, exchange(squares, "space", 1))
     new_iterate = pl.pallas_call(
         join_kernel,
         out_shape=jax.ShapeDtypeStruct(forcing.shape, jnp.float32),
@@ -386,11 +399,6 @@
         cost_estimate=pl.CostEstimate(flops=4000, bytes_accessed=100000, transcendentals=0),
         name="join_species",
     )(own, got)
-    squares = squares + got[cells:]
-    bits = 1
-    while bits < space:
-        squares = squares + exchange(squares, "space", bits)
-        bits *= 2
     entry_count = length * space * forcing.shape[1] * cells * lanes
     return (new_iterate, jnp.sqrt(jnp.sum(squares) / entry_count))
 

time: 27.3 us -> 30 us (1.099)
  starting transfers between devices: 9.52 us -> 13.4 us
  waiting for transfers between devices: 12.2 us -> 10.9 us
    ppermute x7 -> x6, starting transfers between devices: 9.52 us -> 12.1 us  [exchange(): return lax.ppermute(value, axis, pairs)]
    ppermute x0 -> x2, starting transfers between devices: none -> 1.31 us  [exchange_odd(): return lax.ppermute(value, 'space', pairs)]
    ppermute x7 -> x6, waiting for transfers between devices: 12.2 us -> 10.9 us  [exchange(): return lax.ppermute(value, axis, pairs)]
  transfers between devices with their start and end apart: 7 -> 8, of which waited for: 7 -> 5; matrix products, arithmetic and copies ran while one was open for 0% -> 0% of each run, Pallas kernels for 4% -> 4%
where the time goes in v5:
time: 30 us; the launch traced here: 29.8 us
  starting transfers between devices  13.4 us (45%)
  waiting for transfers between devices  10.9 us (36%)
  between operations  2.54 us (8%)
  Pallas kernels  2.28 us (8%)
  other arithmetic  0.61 us (2%)
    ppermute x6, starting transfers between devices, exchange(): return lax.ppermute(value, axis, pairs)  12.1 us
    ppermute x6, waiting for transfers between devices, exchange(): return lax.ppermute(value, axis, pairs)  10.9 us
    ppermute x2, starting transfers between devices, exchange_odd(): return lax.ppermute(value, 'space', pairs)  1.31 us
    pallas_call x1, Pallas kernels, shards(): pl.pallas_call(stack_kernel, out_shape=(pltpu.VMEM((2, cells, lanes), jnp...  0.96 us
    pallas_call x1, Pallas kernels, shards(): pl.pallas_call(join_kernel, out_shape=jax.ShapeDtypeStruct(forcing.shape,...  0.64 us
  transfers between devices with their start and end apart: 8, of which 5 were waited for; matrix products, arithmetic and copies ran while one was open for 0% of the time, Pallas kernels for 4%

profile of v5, /device:TPU:0, one launch (start us, length us, event | category | flops | bytes accessed | tf_op | source)
XLA Modules:
  0.0 29.8 jit_solution(2438433193936811412)
XLA Ops:
  0.6 1.0 %stack_arrays.1 = (f32[2,64,128]{2,1,0:T(8,128)S(1)}, f32[2,64,128]{2,1,0:T(8,128)S(1)}, f32[64,128]{1,0:T(8,128)S(1)}, s32[64,128]{1,0:T(8,128)S(1)}, f32[8,128]{1,0:T(8,128)S(1)}) custom-call(f32[1,2,64,128]{3,2,1,0:T(8,128)} %forcing_hbm.1, f32[1,2,64,128]{3,2,1,0:T(8,128)} %previous_hbm.1, f32[2,64,128]{2,1,0:T(8,128)} %initial_hbm.1, f32[2,8]{1,0:T(2,128)} %zones_hbm.1, ...), custom_call_target="tpu_custom_call" | custom-call | flops 4000 | bytes 500000 | tf_op jit(solution)/shard_map/stack_arrays/pallas_call | solution.py:324
  1.6 3.1 %collective-permute-start = (f32[2,64,128]{2,1,0:T(8,128)S(1)}, f32[2,64,128]{2,1,0:T(8,128)S(1)}, u32[]{:S(2)}, u32[]{:S(2)}) collective-permute-start(f32[2,64,128]{2,1,0:T(8,128)S(1)} %get-tuple-element.25), channel_id=1, source_target_pairs={{0,8},{8,0},{16,24},{24,16},{1,9},{9,1},{17,25},{25,17},{2,10},{10... | collective-permute-start | bytes 196616 | tf_op jit(solution)/shard_map/ppermute | solution.py:299
  4.7 2.6 %collective-permute-start.1 = (f32[2,64,128]{2,1,0:T(8,128)S(1)}, f32[2,64,128]{2,1,0:T(8,128)S(1)}, u32[]{:S(2)}, u32[]{:S(2)}) collective-permute-start(f32[2,64,128]{2,1,0:T(8,128)S(1)} %get-tuple-element.24.refs_0_), channel_id=1, source_target_pairs={{0,16},{8,24},{16,0},{24,8},{1,17},{9,25},{17,1},{25,9},{2,18},{10... | collective-permute-start | bytes 196616 | tf_op jit(solution)/shard_map/ppermute | solution.py:299
  7.3 0.0 collective-permute-start.2
  7.3 0.4 %factor_lines.1 = (f32[4,6,64,128]{3,2,1,0:T(8,128)S(1)}, f32[4,3,64,128]{3,2,1,0:T(8,128)S(1)}) custom-call(f32[8,128]{1,0:T(8,128)S(1)} %get-tuple-element.27.rows_ref, s32[64,128]{1,0:T(8,128)S(1)} %get-tuple-element.28.faces_ref), custom_call_target="tpu_custom_call" | custom-call | flops 4000000 | bytes 3000000 | tf_op jit(solution)/shard_map/factor_lines/pallas_call | solution.py:358
  7.7 0.0 collective-permute-done.refs_1_
  7.7 4.2 %collective-permute-done.1.refs_2_ = f32[2,64,128]{2,1,0:T(8,128)S(1)} collective-permute-done((f32[2,64,128]{2,1,0:T(8,128)S(1)}, f32[2,64,128]{2,1,0:T(8,128)S(1)}, u32[]{:S(2)}, u32[]{:S(2)}) %collective-permute-start.1) | collective-permute-done | bytes 65568 | tf_op jit(solution)/shard_map/ppermute | solution.py:299
  12.0 1.4 %collective-permute-done.2.refs_3_ = f32[2,64,128]{2,1,0:T(8,128)S(1)} collective-permute-done((f32[2,64,128]{2,1,0:T(8,128)S(1)}, f32[2,64,128]{2,1,0:T(8,128)S(1)}, u32[]{:S(2)}, u32[]{:S(2)}) %collective-permute-start.2) | collective-permute-done | bytes 65568 | tf_op jit(solution)/shard_map/ppermute | solution.py:299
  13.4 0.3 solve_lines.1
  13.6 0.1 collective-permute-start.3
  13.7 1.2 %collective-permute-done.3 = f32[8,128]{1,0:T(8,128)S(1)} collective-permute-done((f32[8,128]{1,0:T(8,128)S(1)}, f32[8,128]{1,0:T(8,128)S(1)}, u32[]{:S(2)}, u32[]{:S(2)}) %collective-permute-start.3) | collective-permute-done | bytes 4128 | tf_op jit(solution)/shard_map/ppermute | solution.py:299
  14.9 0.0 collective-permute-start.4
  14.9 4.0 %collective-permute-done.4.got_ref = f32[72,128]{1,0:T(8,128)S(1)} collective-permute-done((f32[72,128]{1,0:T(8,128)S(1)}, f32[72,128]{1,0:T(8,128)S(1)}, u32[]{:S(2)}, u32[]{:S(2)}) %collective-permute-start.4) | collective-permute-done | bytes 36896 | tf_op jit(solution)/shard_map/ppermute | solution.py:299
  18.8 0.7 %collective-permute-start.5 = (f32[8,128]{1,0:T(8,128)S(1)}, f32[8,128]{1,0:T(8,128)S(1)}, u32[]{:S(2)}, u32[]{:S(2)}) collective-permute-start(f32[8,128]{1,0:T(8,128)S(1)} %slice_add_fusion), channel_id=1, source_target_pairs={{1,3},{3,1},{5,7},{7,5},{9,11},{11,9},{13,15},{15,13},{17,19},{19,... | collective-permute-start | bytes 12296 | tf_op jit(solution)/shard_map/ppermute | solution.py:304
  19.5 0.0 collective-permute-done.5
  19.5 0.7 %collective-permute-start.6 = (f32[8,128]{1,0:T(8,128)S(1)}, f32[8,128]{1,0:T(8,128)S(1)}, u32[]{:S(2)}, u32[]{:S(2)}) collective-permute-start(f32[8,128]{1,0:T(8,128)S(1)} %add.21), channel_id=1, source_target_pairs={{1,5},{3,7},{5,1},{7,3},{9,13},{11,15},{13,9},{15,11},{17,21},{19,... | collective-permute-start | bytes 12296 | tf_op jit(solution)/shard_map/ppermute | solution.py:304
  20.2 0.0 collective-permute-done.6
  20.2 6.3 %collective-permute-start.7 = (f32[8,128]{1,0:T(8,128)S(1)}, f32[8,128]{1,0:T(8,128)S(1)}, u32[]{:S(2)}, u32[]{:S(2)}) collective-permute-start(f32[8,128]{1,0:T(8,128)S(1)} %add.22), channel_id=1, source_target_pairs={{0,1},{1,0},{2,3},{3,2},{4,5},{5,4},{6,7},{7,6},{8,9},{9,8},{10,11... | collective-permute-start | bytes 12296 | tf_op jit(solution)/shard_map/ppermute | solution.py:299
  26.5 0.6 %join_species.1 = f32[1,2,64,128]{3,2,1,0:T(8,128)} custom-call(f32[64,128]{1,0:T(8,128)S(1)} %get-tuple-element.31.own_ref, f32[72,128]{1,0:T(8,128)S(1)} %collective-permute-done.4.got_ref), custom_call_target="tpu_custom_call" | custom-call | flops 4000 | bytes 100000 | tf_op jit(solution)/shard_map/join_species/pallas_call | solution.py:392
  27.2 0.2 collective-permute-done.7
  27.4 0.6 %select_reduce_fusion = f32[]{:T(128)} fusion(f32[8,128]{1,0:T(8,128)S(1)} %add.22, f32[8,128]{1,0:T(8,128)S(1)} %collective-permute-done.7, pred[]{:T(512)S(6)} %eq.5), kind=kLoop, calls=%fused_computation.1 | loop fusion | flops 2047 | bytes 8197 | tf_op jit(solution)/shard_map/reduce_sum | solution.py:403
  (4 shorter events, 0.0 us)
Async XLA Ops:
  1.6 6.1 %collective-permute-start = (f32[2,64,128]{2,1,0:T(8,128)S(1)}, f32[2,64,128]{2,1,0:T(8,128)S(1)}, u32[]{:S(2)}, u32[]{:S(2)}) collective-permute-start(f32[2,64,128]{2,1,0:T(8,128)S(1)} %get-tuple-element.25), channel_id=1, source_target_pairs={{0,8},{8,0},{16,24},{24,16},{1,9},{9,1},{17,25},{25,17},{2,10},{10... | collective-permute-start | bytes 196616 | tf_op jit(solution)/shard_map/ppermute | solution.py:299
  4.7 7.3 %collective-permute-start.1 = (f32[2,64,128]{2,1,0:T(8,128)S(1)}, f32[2,64,128]{2,1,0:T(8,128)S(1)}, u32[]{:S(2)}, u32[]{:S(2)}) collective-permute-start(f32[2,64,128]{2,1,0:T(8,128)S(1)} %get-tuple-element.24.refs_0_), channel_id=1, source_target_pairs={{0,16},{8,24},{16,0},{24,8},{1,17},{9,25},{17,1},{25,9},{2,18},{10... | collective-permute-start | bytes 196616 | tf_op jit(solution)/shard_map/ppermute | solution.py:299
  7.3 6.1 %collective-permute-start.2 = (f32[2,64,128]{2,1,0:T(8,128)S(1)}, f32[2,64,128]{2,1,0:T(8,128)S(1)}, u32[]{:S(2)}, u32[]{:S(2)}) collective-permute-start(f32[2,64,128]{2,1,0:T(8,128)S(1)} %get-tuple-element.25), channel_id=1, source_target_pairs={{0,24},{8,16},{16,8},{24,0},{1,25},{9,17},{17,9},{25,1},{2,26},{10... | collective-permute-start | bytes 196616 | tf_op jit(solution)/shard_map/ppermute | solution.py:299
  13.6 1.2 %collective-permute-start.3 = (f32[8,128]{1,0:T(8,128)S(1)}, f32[8,128]{1,0:T(8,128)S(1)}, u32[]{:S(2)}, u32[]{:S(2)}) collective-permute-start(f32[8,128]{1,0:T(8,128)S(1)} %get-tuple-element.33), channel_id=1, source_target_pairs={{0,1},{1,0},{2,3},{3,2},{4,5},{5,4},{6,7},{7,6},{8,9},{9,8},{10,11... | collective-permute-start | bytes 12296 | tf_op jit(solution)/shard_map/ppermute | solution.py:299
  14.9 4.0 %collective-permute-start.4 = (f32[72,128]{1,0:T(8,128)S(1)}, f32[72,128]{1,0:T(8,128)S(1)}, u32[]{:S(2)}, u32[]{:S(2)}) collective-permute-start(f32[72,128]{1,0:T(8,128)S(1)} %get-tuple-element.34), channel_id=1, source_target_pairs={{0,8},{8,0},{16,24},{24,16},{1,9},{9,1},{17,25},{25,17},{2,10},{10... | collective-permute-start | bytes 110600 | tf_op jit(solution)/shard_map/ppermute | solution.py:299
  18.8 0.7 %collective-permute-start.5 = (f32[8,128]{1,0:T(8,128)S(1)}, f32[8,128]{1,0:T(8,128)S(1)}, u32[]{:S(2)}, u32[]{:S(2)}) collective-permute-start(f32[8,128]{1,0:T(8,128)S(1)} %slice_add_fusion), channel_id=1, source_target_pairs={{1,3},{3,1},{5,7},{7,5},{9,11},{11,9},{13,15},{15,13},{17,19},{19,... | collective-permute-start | bytes 12296 | tf_op jit(solution)/shard_map/ppermute | solution.py:304
  19.5 0.7 %collective-permute-start.6 = (f32[8,128]{1,0:T(8,128)S(1)}, f32[8,128]{1,0:T(8,128)S(1)}, u32[]{:S(2)}, u32[]{:S(2)}) collective-permute-start(f32[8,128]{1,0:T(8,128)S(1)} %add.21), channel_id=1, source_target_pairs={{1,5},{3,7},{5,1},{7,3},{9,13},{11,15},{13,9},{15,11},{17,21},{19,... | collective-permute-start | bytes 12296 | tf_op jit(solution)/shard_map/ppermute | solution.py:304
  20.2 7.2 %collective-permute-start.7 = (f32[8,128]{1,0:T(8,128)S(1)}, f32[8,128]{1,0:T(8,128)S(1)}, u32[]{:S(2)}, u32[]{:S(2)}) collective-permute-start(f32[8,128]{1,0:T(8,128)S(1)} %add.22), channel_id=1, source_target_pairs={{0,1},{1,0},{2,3},{3,2},{4,5},{5,4},{6,7},{7,6},{8,9},{9,8},{10,11... | collective-permute-start | bytes 12296 | tf_op jit(solution)/shard_map/ppermute | solution.py:299

commit v6 on v5

--- a/solution.py
+++ b/solution.py
@@ -300,7 +300,9 @@
 
 
 def exchange_odd(value, bits):
-    pairs = [(index, index ^ bits) for index in range(1, lax.axis_size("space"), 2)]
+    pairs = [
+        (index, index ^ bits if index % 2 else index) for index in range(lax.axis_size("space"))
+    ]
     return lax.ppermute(value, "space", pairs)
 
 

time: 30 us -> 30 us (level)
  no operation moved by 1% of the time
where the time goes in v6:
time: 30 us; the launch traced here: 29.8 us
  starting transfers between devices  13.4 us (45%)
  waiting for transfers between devices  10.9 us (36%)
  between operations  2.54 us (8%)
  Pallas kernels  2.28 us (8%)
  other arithmetic  0.61 us (2%)
    ppermute x6, starting transfers between devices, exchange(): return lax.ppermute(value, axis, pairs)  12.1 us
    ppermute x6, waiting for transfers between devices, exchange(): return lax.ppermute(value, axis, pairs)  10.9 us
    ppermute x2, starting transfers between devices, exchange_odd(): return lax.ppermute(value, 'space', pairs)  1.31 us
    pallas_call x1, Pallas kernels, shards(): pl.pallas_call(stack_kernel, out_shape=(pltpu.VMEM((2, cells, lanes), jnp...  0.96 us
    pallas_call x1, Pallas kernels, shards(): pl.pallas_call(join_kernel, out_shape=jax.ShapeDtypeStruct(forcing.shape,...  0.64 us
  transfers between devices with their start and end apart: 8, of which 5 were waited for; matrix products, arithmetic and copies ran while one was open for 0% of the time, Pallas kernels for 4%

profile of v6, /device:TPU:0, one launch (start us, length us, event | category | flops | bytes accessed | tf_op | source)
XLA Modules:
  0.0 29.8 jit_solution(6291015289909219455)
XLA Ops:
  0.6 1.0 %stack_arrays.1 = (f32[2,64,128]{2,1,0:T(8,128)S(1)}, f32[2,64,128]{2,1,0:T(8,128)S(1)}, f32[64,128]{1,0:T(8,128)S(1)}, s32[64,128]{1,0:T(8,128)S(1)}, f32[8,128]{1,0:T(8,128)S(1)}) custom-call(f32[1,2,64,128]{3,2,1,0:T(8,128)} %forcing_hbm.1, f32[1,2,64,128]{3,2,1,0:T(8,128)} %previous_hbm.1, f32[2,64,128]{2,1,0:T(8,128)} %initial_hbm.1, f32[2,8]{1,0:T(2,128)} %zones_hbm.1, ...), custom_call_target="tpu_custom_call" | custom-call | flops 4000 | bytes 500000 | tf_op jit(solution)/shard_map/stack_arrays/pallas_call | solution.py:326
  1.6 3.1 %collective-permute-start = (f32[2,64,128]{2,1,0:T(8,128)S(1)}, f32[2,64,128]{2,1,0:T(8,128)S(1)}, u32[]{:S(2)}, u32[]{:S(2)}) collective-permute-start(f32[2,64,128]{2,1,0:T(8,128)S(1)} %get-tuple-element.25), channel_id=1, source_target_pairs={{0,8},{8,0},{16,24},{24,16},{1,9},{9,1},{17,25},{25,17},{2,10},{10... | collective-permute-start | bytes 196616 | tf_op jit(solution)/shard_map/ppermute | solution.py:299
  4.7 2.6 %collective-permute-start.1 = (f32[2,64,128]{2,1,0:T(8,128)S(1)}, f32[2,64,128]{2,1,0:T(8,128)S(1)}, u32[]{:S(2)}, u32[]{:S(2)}) collective-permute-start(f32[2,64,128]{2,1,0:T(8,128)S(1)} %get-tuple-element.24.refs_0_), channel_id=1, source_target_pairs={{0,16},{8,24},{16,0},{24,8},{1,17},{9,25},{17,1},{25,9},{2,18},{10... | collective-permute-start | bytes 196616 | tf_op jit(solution)/shard_map/ppermute | solution.py:299
  7.3 0.0 collective-permute-start.2
  7.3 0.4 %factor_lines.1 = (f32[4,6,64,128]{3,2,1,0:T(8,128)S(1)}, f32[4,3,64,128]{3,2,1,0:T(8,128)S(1)}) custom-call(f32[8,128]{1,0:T(8,128)S(1)} %get-tuple-element.27.rows_ref, s32[64,128]{1,0:T(8,128)S(1)} %get-tuple-element.28.faces_ref), custom_call_target="tpu_custom_call" | custom-call | flops 4000000 | bytes 3000000 | tf_op jit(solution)/shard_map/factor_lines/pallas_call | solution.py:360
  7.7 0.0 collective-permute-done.refs_1_
  7.7 4.2 %collective-permute-done.1.refs_2_ = f32[2,64,128]{2,1,0:T(8,128)S(1)} collective-permute-done((f32[2,64,128]{2,1,0:T(8,128)S(1)}, f32[2,64,128]{2,1,0:T(8,128)S(1)}, u32[]{:S(2)}, u32[]{:S(2)}) %collective-permute-start.1) | collective-permute-done | bytes 65568 | tf_op jit(solution)/shard_map/ppermute | solution.py:299
  12.0 1.4 %collective-permute-done.2.refs_3_ = f32[2,64,128]{2,1,0:T(8,128)S(1)} collective-permute-done((f32[2,64,128]{2,1,0:T(8,128)S(1)}, f32[2,64,128]{2,1,0:T(8,128)S(1)}, u32[]{:S(2)}, u32[]{:S(2)}) %collective-permute-start.2) | collective-permute-done | bytes 65568 | tf_op jit(solution)/shard_map/ppermute | solution.py:299
  13.4 0.3 solve_lines.1
  13.6 0.1 collective-permute-start.3
  13.7 1.2 %collective-permute-done.3 = f32[8,128]{1,0:T(8,128)S(1)} collective-permute-done((f32[8,128]{1,0:T(8,128)S(1)}, f32[8,128]{1,0:T(8,128)S(1)}, u32[]{:S(2)}, u32[]{:S(2)}) %collective-permute-start.3) | collective-permute-done | bytes 4128 | tf_op jit(solution)/shard_map/ppermute | solution.py:299
  14.9 0.0 collective-permute-start.4
  14.9 4.0 %collective-permute-done.4.got_ref = f32[72,128]{1,0:T(8,128)S(1)} collective-permute-done((f32[72,128]{1,0:T(8,128)S(1)}, f32[72,128]{1,0:T(8,128)S(1)}, u32[]{:S(2)}, u32[]{:S(2)}) %collective-permute-start.4) | collective-permute-done | bytes 36896 | tf_op jit(solution)/shard_map/ppermute | solution.py:299
  18.8 0.7 %collective-permute-start.5 = (f32[8,128]{1,0:T(8,128)S(1)}, f32[8,128]{1,0:T(8,128)S(1)}, u32[]{:S(2)}, u32[]{:S(2)}) collective-permute-start(f32[8,128]{1,0:T(8,128)S(1)} %slice_add_fusion), channel_id=1, source_target_pairs={{0,0},{1,3},{2,2},{3,1},{4,4},{5,7},{6,6},{7,5},{8,8},{9,11},{10,1... | collective-permute-start | bytes 12296 | tf_op jit(solution)/shard_map/ppermute | solution.py:306
  19.5 0.0 collective-permute-done.5
  19.5 0.7 %collective-permute-start.6 = (f32[8,128]{1,0:T(8,128)S(1)}, f32[8,128]{1,0:T(8,128)S(1)}, u32[]{:S(2)}, u32[]{:S(2)}) collective-permute-start(f32[8,128]{1,0:T(8,128)S(1)} %add.21), channel_id=1, source_target_pairs={{0,0},{1,5},{2,2},{3,7},{4,4},{5,1},{6,6},{7,3},{8,8},{9,13},{10,1... | collective-permute-start | bytes 12296 | tf_op jit(solution)/shard_map/ppermute | solution.py:306
  20.2 0.0 collective-permute-done.6
  20.2 6.3 %collective-permute-start.7 = (f32[8,128]{1,0:T(8,128)S(1)}, f32[8,128]{1,0:T(8,128)S(1)}, u32[]{:S(2)}, u32[]{:S(2)}) collective-permute-start(f32[8,128]{1,0:T(8,128)S(1)} %add.22), channel_id=1, source_target_pairs={{0,1},{1,0},{2,3},{3,2},{4,5},{5,4},{6,7},{7,6},{8,9},{9,8},{10,11... | collective-permute-start | bytes 12296 | tf_op jit(solution)/shard_map/ppermute | solution.py:299
  26.5 0.6 %join_species.1 = f32[1,2,64,128]{3,2,1,0:T(8,128)} custom-call(f32[64,128]{1,0:T(8,128)S(1)} %get-tuple-element.31.own_ref, f32[72,128]{1,0:T(8,128)S(1)} %collective-permute-done.4.got_ref), custom_call_target="tpu_custom_call" | custom-call | flops 4000 | bytes 100000 | tf_op jit(solution)/shard_map/join_species/pallas_call | solution.py:394
  27.2 0.2 collective-permute-done.7
  27.4 0.6 %select_reduce_fusion = f32[]{:T(128)} fusion(f32[8,128]{1,0:T(8,128)S(1)} %add.22, f32[8,128]{1,0:T(8,128)S(1)} %collective-permute-done.7, pred[]{:T(512)S(6)} %eq.5), kind=kLoop, calls=%fused_computation.1 | loop fusion | flops 2047 | bytes 8197 | tf_op jit(solution)/shard_map/reduce_sum | solution.py:405
  (4 shorter events, 0.0 us)
Async XLA Ops:
  1.6 6.1 %collective-permute-start = (f32[2,64,128]{2,1,0:T(8,128)S(1)}, f32[2,64,128]{2,1,0:T(8,128)S(1)}, u32[]{:S(2)}, u32[]{:S(2)}) collective-permute-start(f32[2,64,128]{2,1,0:T(8,128)S(1)} %get-tuple-element.25), channel_id=1, source_target_pairs={{0,8},{8,0},{16,24},{24,16},{1,9},{9,1},{17,25},{25,17},{2,10},{10... | collective-permute-start | bytes 196616 | tf_op jit(solution)/shard_map/ppermute | solution.py:299
  4.7 7.3 %collective-permute-start.1 = (f32[2,64,128]{2,1,0:T(8,128)S(1)}, f32[2,64,128]{2,1,0:T(8,128)S(1)}, u32[]{:S(2)}, u32[]{:S(2)}) collective-permute-start(f32[2,64,128]{2,1,0:T(8,128)S(1)} %get-tuple-element.24.refs_0_), channel_id=1, source_target_pairs={{0,16},{8,24},{16,0},{24,8},{1,17},{9,25},{17,1},{25,9},{2,18},{10... | collective-permute-start | bytes 196616 | tf_op jit(solution)/shard_map/ppermute | solution.py:299
  7.3 6.1 %collective-permute-start.2 = (f32[2,64,128]{2,1,0:T(8,128)S(1)}, f32[2,64,128]{2,1,0:T(8,128)S(1)}, u32[]{:S(2)}, u32[]{:S(2)}) collective-permute-start(f32[2,64,128]{2,1,0:T(8,128)S(1)} %get-tuple-element.25), channel_id=1, source_target_pairs={{0,24},{8,16},{16,8},{24,0},{1,25},{9,17},{17,9},{25,1},{2,26},{10... | collective-permute-start | bytes 196616 | tf_op jit(solution)/shard_map/ppermute | solution.py:299
  13.6 1.2 %collective-permute-start.3 = (f32[8,128]{1,0:T(8,128)S(1)}, f32[8,128]{1,0:T(8,128)S(1)}, u32[]{:S(2)}, u32[]{:S(2)}) collective-permute-start(f32[8,128]{1,0:T(8,128)S(1)} %get-tuple-element.33), channel_id=1, source_target_pairs={{0,1},{1,0},{2,3},{3,2},{4,5},{5,4},{6,7},{7,6},{8,9},{9,8},{10,11... | collective-permute-start | bytes 12296 | tf_op jit(solution)/shard_map/ppermute | solution.py:299
  14.9 4.0 %collective-permute-start.4 = (f32[72,128]{1,0:T(8,128)S(1)}, f32[72,128]{1,0:T(8,128)S(1)}, u32[]{:S(2)}, u32[]{:S(2)}) collective-permute-start(f32[72,128]{1,0:T(8,128)S(1)} %get-tuple-element.34), channel_id=1, source_target_pairs={{0,8},{8,0},{16,24},{24,16},{1,9},{9,1},{17,25},{25,17},{2,10},{10... | collective-permute-start | bytes 110600 | tf_op jit(solution)/shard_map/ppermute | solution.py:299
  18.8 0.7 %collective-permute-start.5 = (f32[8,128]{1,0:T(8,128)S(1)}, f32[8,128]{1,0:T(8,128)S(1)}, u32[]{:S(2)}, u32[]{:S(2)}) collective-permute-start(f32[8,128]{1,0:T(8,128)S(1)} %slice_add_fusion), channel_id=1, source_target_pairs={{0,0},{1,3},{2,2},{3,1},{4,4},{5,7},{6,6},{7,5},{8,8},{9,11},{10,1... | collective-permute-start | bytes 12296 | tf_op jit(solution)/shard_map/ppermute | solution.py:306
  19.5 0.7 %collective-permute-start.6 = (f32[8,128]{1,0:T(8,128)S(1)}, f32[8,128]{1,0:T(8,128)S(1)}, u32[]{:S(2)}, u32[]{:S(2)}) collective-permute-start(f32[8,128]{1,0:T(8,128)S(1)} %add.21), channel_id=1, source_target_pairs={{0,0},{1,5},{2,2},{3,7},{4,4},{5,1},{6,6},{7,3},{8,8},{9,13},{10,1... | collective-permute-start | bytes 12296 | tf_op jit(solution)/shard_map/ppermute | solution.py:306
  20.2 7.2 %collective-permute-start.7 = (f32[8,128]{1,0:T(8,128)S(1)}, f32[8,128]{1,0:T(8,128)S(1)}, u32[]{:S(2)}, u32[]{:S(2)}) collective-permute-start(f32[8,128]{1,0:T(8,128)S(1)} %add.22), channel_id=1, source_target_pairs={{0,1},{1,0},{2,3},{3,2},{4,5},{5,4},{6,7},{7,6},{8,9},{9,8},{10,11... | collective-permute-start | bytes 12296 | tf_op jit(solution)/shard_map/ppermute | solution.py:299

commit v7 on v4

--- a/solution.py
+++ b/solution.py
@@ -277,19 +277,18 @@
             give = jnp.where(me == n, steps[n ^ 1], give)
         own_ref[rows] = own
         give_ref[rows] = give
-    give_ref[cells:] = total
-    sum_ref[...] = total
-
-
-def join_kernel(own_ref, got_ref, new_hbm, sems):
+    sum_ref[...] = jnp.broadcast_to(jnp.sum(total, axis=0, keepdims=True), sum_ref.shape)
+
+
+def join_kernel(entry_count, own_ref, got_ref, squares_ref, new_hbm, norm_ref, sems):
     species = lax.axis_index("tm") % 2
-    cells = own_ref.shape[0]
     copies = (
         pltpu.make_async_copy(own_ref, new_hbm.at[0, species], sems.at[0]),
-        pltpu.make_async_copy(got_ref.at[:cells], new_hbm.at[0, 1 - species], sems.at[1]),
+        pltpu.make_async_copy(got_ref, new_hbm.at[0, 1 - species], sems.at[1]),
     )
     for copy in copies:
         copy.start()
+    norm_ref[0, 0] = jnp.sqrt(jnp.sum(squares_ref[...]) / entry_count)
     for copy in copies:
         copy.wait()
 
@@ -366,8 +365,8 @@
         functools.partial(sweep_kernel, length),
         out_shape=(
             pltpu.VMEM((cells, lanes), jnp.float32),
-            pltpu.VMEM((cells + tile, lanes), jnp.float32),
-            pltpu.VMEM((tile, lanes), jnp.float32),
+            pltpu.VMEM((cells, lanes), jnp.float32),
+            pltpu.VMEM((2 * space, 1, lanes), jnp.float32),
         ),
         in_specs=[whole] * (length + 3),
         out_specs=[whole] * 3,
@@ -376,23 +375,28 @@
         name="solve_lines",
     )(*stacks, initial, near, far)
     got = exchange(give, "tm", 1)
-    new_iterate = pl.pallas_call(
-        join_kernel,
-        out_shape=jax.ShapeDtypeStruct(forcing.shape, jnp.float32),
-        in_specs=[whole] * 2,
-        out_specs=outside,
+    groups = [
+        [(step + half) * space + index for half in range(2) for index in range(space)]
+        for step in range(0, length, 2)
+    ]
+    squares = lax.all_to_all(
+        squares, ("tm", "space"), 0, 0, axis_index_groups=groups, tiled=True
+    )
+    entry_count = length * space * forcing.shape[1] * cells * lanes
+    new_iterate, norm = pl.pallas_call(
+        functools.partial(join_kernel, entry_count),
+        out_shape=(
+            jax.ShapeDtypeStruct(forcing.shape, jnp.float32),
+            jax.ShapeDtypeStruct((1, 1), jnp.float32),
+        ),
+        in_specs=[whole] * 3,
+        out_specs=(outside, pl.BlockSpec(memory_space=pltpu.SMEM)),
         scratch_shapes=[pltpu.SemaphoreType.DMA((2,))],
         compiler_params=params,
         cost_estimate=pl.CostEstimate(flops=4000, bytes_accessed=100000, transcendentals=0),
         name="join_species",
-    )(own, got)
-    squares = squares + got[cells:]
-    bits = 1
-    while bits < space:
-        squares = squares + exchange(squares, "space", bits)
-        bits *= 2
-    entry_count = length * space * forcing.shape[1] * cells * lanes
-    return (new_iterate, jnp.sqrt(jnp.sum(squares) / entry_count))
+    )(own, got, squares)
+    return (new_iterate, norm[0, 0])
 
 
 def solution(mesh):

time: 27.3 us -> 24.3 us (0.89)
  blocking collectives: 0 us -> 9.81 us
  waiting for transfers between devices: 12.2 us -> 4.32 us
  starting transfers between devices: 9.52 us -> 6.5 us
  between operations: 2.48 us -> 0.65 us
  other arithmetic: 0.61 us -> 0 us
  Pallas kernels: 2.28 us -> 2.83 us
    all_to_all x0 -> x1, blocking collectives: none -> 9.81 us  [shards(): lax.all_to_all(squares, ('tm', 'space'), 0, 0, axis_index_groups=groups,...]
    ppermute x7 -> x4, waiting for transfers between devices: 12.2 us -> 4.32 us  [exchange(): return lax.ppermute(value, axis, pairs)]
    ppermute x7 -> x4, starting transfers between devices: 9.52 us -> 6.5 us  [exchange(): return lax.ppermute(value, axis, pairs)]
    reduce_sum x1 -> x0, other arithmetic: 0.6 us -> none  [shards(): return (new_iterate, jnp.sqrt(jnp.sum(squares) / entry_count))]
    pallas_call x1, Pallas kernels: 0.64 us -> 1.18 us  [shards(): pl.pallas_call(functools.partial(join_kernel, entry_count), out_shape=(ja...]
  transfers between devices with their start and end apart: 7 -> 4, of which waited for: 7 -> 3; matrix products, arithmetic and copies ran while one was open for 0% -> 0% of each run, Pallas kernels for 4% -> 2%
where the time goes in v7:
time: 24.3 us; the launch traced here: 24.1 us
  blocking collectives  9.81 us (40%)
  starting transfers between devices  6.5 us (27%)
  waiting for transfers between devices  4.32 us (18%)
  Pallas kernels  2.83 us (12%)
  between operations  0.65 us (3%)
    all_to_all x1, blocking collectives, shards(): lax.all_to_all(squares, ('tm', 'space'), 0, 0, axis_index_groups=groups,...  9.81 us
    ppermute x4, starting transfers between devices, exchange(): return lax.ppermute(value, axis, pairs)  6.5 us
    ppermute x4, waiting for transfers between devices, exchange(): return lax.ppermute(value, axis, pairs)  4.32 us
    pallas_call x1, Pallas kernels, shards(): pl.pallas_call(functools.partial(join_kernel, entry_count), out_shape=(ja...  1.18 us
    pallas_call x1, Pallas kernels, shards(): pl.pallas_call(stack_kernel, out_shape=(pltpu.VMEM((2, cells, lanes), jnp...  0.96 us
  transfers between devices with their start and end apart: 4, of which 3 were waited for; matrix products, arithmetic and copies ran while one was open for 0% of the time, Pallas kernels for 2%

profile of v7, /device:TPU:0, one launch (start us, length us, event | category | flops | bytes accessed | tf_op | source)
XLA Modules:
  0.0 24.1 jit_solution(18204467454987039152)
XLA Ops:
  0.6 1.0 %stack_arrays.1 = (f32[2,64,128]{2,1,0:T(8,128)S(1)}, f32[2,64,128]{2,1,0:T(8,128)S(1)}, f32[64,128]{1,0:T(8,128)S(1)}, s32[64,128]{1,0:T(8,128)S(1)}, f32[8,128]{1,0:T(8,128)S(1)}) custom-call(f32[1,2,64,128]{3,2,1,0:T(8,128)} %forcing_hbm.1, f32[1,2,64,128]{3,2,1,0:T(8,128)} %previous_hbm.1, f32[2,64,128]{2,1,0:T(8,128)} %initial_hbm.1, f32[2,8]{1,0:T(2,128)} %zones_hbm.1, ...), custom_call_target="tpu_custom_call" | custom-call | flops 4000 | bytes 500000 | tf_op jit(solution)/shard_map/stack_arrays/pallas_call | solution.py:318
  1.6 4.1 %collective-permute-start.1 = (f32[2,64,128]{2,1,0:T(8,128)S(1)}, f32[2,64,128]{2,1,0:T(8,128)S(1)}, u32[]{:S(2)}, u32[]{:S(2)}) collective-permute-start(f32[2,64,128]{2,1,0:T(8,128)S(1)} %get-tuple-element.14.refs_0_), channel_id=1, source_target_pairs={{0,16},{8,24},{16,0},{24,8},{1,17},{9,25},{17,1},{25,9},{2,18},{10... | collective-permute-start | bytes 196616 | tf_op jit(solution)/shard_map/ppermute | solution.py:298
  5.7 1.3 %collective-permute-start.2 = (f32[2,64,128]{2,1,0:T(8,128)S(1)}, f32[2,64,128]{2,1,0:T(8,128)S(1)}, u32[]{:S(2)}, u32[]{:S(2)}) collective-permute-start(f32[2,64,128]{2,1,0:T(8,128)S(1)} %get-tuple-element.15), channel_id=1, source_target_pairs={{0,24},{8,16},{16,8},{24,0},{1,25},{9,17},{17,9},{25,1},{2,26},{10... | collective-permute-start | bytes 196616 | tf_op jit(solution)/shard_map/ppermute | solution.py:298
  7.1 0.2 collective-permute-start
  7.3 0.4 %factor_lines.1 = (f32[4,6,64,128]{3,2,1,0:T(8,128)S(1)}, f32[4,3,64,128]{3,2,1,0:T(8,128)S(1)}) custom-call(f32[8,128]{1,0:T(8,128)S(1)} %get-tuple-element.17.rows_ref, s32[64,128]{1,0:T(8,128)S(1)} %get-tuple-element.18.faces_ref), custom_call_target="tpu_custom_call" | custom-call | flops 4000000 | bytes 3000000 | tf_op jit(solution)/shard_map/factor_lines/pallas_call | solution.py:352
  7.7 1.8 %collective-permute-done.1.refs_2_ = f32[2,64,128]{2,1,0:T(8,128)S(1)} collective-permute-done((f32[2,64,128]{2,1,0:T(8,128)S(1)}, f32[2,64,128]{2,1,0:T(8,128)S(1)}, u32[]{:S(2)}, u32[]{:S(2)}) %collective-permute-start.1) | collective-permute-done | bytes 65568 | tf_op jit(solution)/shard_map/ppermute | solution.py:298
  9.5 2.5 %collective-permute-done.2.refs_3_ = f32[2,64,128]{2,1,0:T(8,128)S(1)} collective-permute-done((f32[2,64,128]{2,1,0:T(8,128)S(1)}, f32[2,64,128]{2,1,0:T(8,128)S(1)}, u32[]{:S(2)}, u32[]{:S(2)}) %collective-permute-start.2) | collective-permute-done | bytes 65568 | tf_op jit(solution)/shard_map/ppermute | solution.py:298
  11.9 0.1 collective-permute-done.refs_1_
  12.0 0.3 %solve_lines.1 = (f32[64,128]{1,0:T(8,128)S(1)}, f32[64,128]{1,0:T(8,128)S(1)}, f32[16,1,128]{2,1,0:T(1,128)S(1)}) custom-call(f32[2,64,128]{2,1,0:T(8,128)S(1)} %get-tuple-element.14.refs_0_, f32[2,64,128]{2,1,0:T(8,128)S(1)} %collective-permute-done.refs_1_, f32[2,64,128]{2,1,0:T(8,128)S(1)} %collective-permute-done.1.refs_2_, ...), custom_call_target="tpu_custom_call" | custom-call | flops 4000000 | bytes 3000000 | tf_op jit(solution)/shard_map/solve_lines/pallas_call | solution.py:364
  12.3 0.8 %collective-permute-start.3 = (f32[64,128]{1,0:T(8,128)S(1)}, f32[64,128]{1,0:T(8,128)S(1)}, u32[]{:S(2)}, u32[]{:S(2)}) collective-permute-start(f32[64,128]{1,0:T(8,128)S(1)} %get-tuple-element.22), channel_id=1, source_target_pairs={{0,8},{8,0},{16,24},{24,16},{1,9},{9,1},{17,25},{25,17},{2,10},{10... | collective-permute-start | bytes 98312 | tf_op jit(solution)/shard_map/ppermute | solution.py:298
  13.1 9.8 %all_to_all.5.squares_ref = f32[16,1,128]{2,1,0:T(1,128)S(1)} all-to-all(f32[16,1,128]{2,1,0:T(1,128)S(1)} %get-tuple-element.23), channel_id=1, replica_groups={{0,1,2,3,4,5,6,7,8,9,10,11,12,13,14,15},{16,17,18,19,20,21,22,23,24,25,..., dimensions={0} | all-to-all | bytes 16384 | tf_op jit(solution)/shard_map/all_to_all | solution.py:382
  22.9 0.0 collective-permute-done.3.got_ref
  22.9 1.2 %join_species.1 = (f32[1,2,64,128]{3,2,1,0:T(8,128)}, f32[1,1]{1,0:T(1,128)}) custom-call(f32[64,128]{1,0:T(8,128)S(1)} %get-tuple-element.21.own_ref, f32[64,128]{1,0:T(8,128)S(1)} %collective-permute-done.3.got_ref, f32[16,1,128]{2,1,0:T(1,128)S(1)} %all_to_all.5.squares_ref), custom_call_target="tpu_custom_call" | custom-call | flops 4000 | bytes 100000 | tf_op jit(solution)/shard_map/join_species/pallas_call | solution.py:386
Async XLA Ops:
  1.6 7.9 %collective-permute-start.1 = (f32[2,64,128]{2,1,0:T(8,128)S(1)}, f32[2,64,128]{2,1,0:T(8,128)S(1)}, u32[]{:S(2)}, u32[]{:S(2)}) collective-permute-start(f32[2,64,128]{2,1,0:T(8,128)S(1)} %get-tuple-element.14.refs_0_), channel_id=1, source_target_pairs={{0,16},{8,24},{16,0},{24,8},{1,17},{9,25},{17,1},{25,9},{2,18},{10... | collective-permute-start | bytes 196616 | tf_op jit(solution)/shard_map/ppermute | solution.py:298
  5.7 6.2 %collective-permute-start.2 = (f32[2,64,128]{2,1,0:T(8,128)S(1)}, f32[2,64,128]{2,1,0:T(8,128)S(1)}, u32[]{:S(2)}, u32[]{:S(2)}) collective-permute-start(f32[2,64,128]{2,1,0:T(8,128)S(1)} %get-tuple-element.15), channel_id=1, source_target_pairs={{0,24},{8,16},{16,8},{24,0},{1,25},{9,17},{17,9},{25,1},{2,26},{10... | collective-permute-start | bytes 196616 | tf_op jit(solution)/shard_map/ppermute | solution.py:298
  7.1 5.0 %collective-permute-start = (f32[2,64,128]{2,1,0:T(8,128)S(1)}, f32[2,64,128]{2,1,0:T(8,128)S(1)}, u32[]{:S(2)}, u32[]{:S(2)}) collective-permute-start(f32[2,64,128]{2,1,0:T(8,128)S(1)} %get-tuple-element.15), channel_id=1, source_target_pairs={{0,8},{8,0},{16,24},{24,16},{1,9},{9,1},{17,25},{25,17},{2,10},{10... | collective-permute-start | bytes 196616 | tf_op jit(solution)/shard_map/ppermute | solution.py:298
  12.3 10.6 %collective-permute-start.3 = (f32[64,128]{1,0:T(8,128)S(1)}, f32[64,128]{1,0:T(8,128)S(1)}, u32[]{:S(2)}, u32[]{:S(2)}) collective-permute-start(f32[64,128]{1,0:T(8,128)S(1)} %get-tuple-element.22), channel_id=1, source_target_pairs={{0,8},{8,0},{16,24},{24,16},{1,9},{9,1},{17,25},{25,17},{2,10},{10... | collective-permute-start | bytes 98312 | tf_op jit(solution)/shard_map/ppermute | solution.py:298

commit v8 on v7

--- a/solution.py
+++ b/solution.py
@@ -280,15 +280,19 @@
     sum_ref[...] = jnp.broadcast_to(jnp.sum(total, axis=0, keepdims=True), sum_ref.shape)
 
 
-def join_kernel(entry_count, own_ref, got_ref, squares_ref, new_hbm, norm_ref, sems):
+def join_kernel(
+    entry_count, own_ref, got_ref, squares_ref, new_hbm, norm_hbm, norm_ref, sems
+):
     species = lax.axis_index("tm") % 2
     copies = (
         pltpu.make_async_copy(own_ref, new_hbm.at[0, species], sems.at[0]),
         pltpu.make_async_copy(got_ref, new_hbm.at[0, 1 - species], sems.at[1]),
-    )
-    for copy in copies:
-        copy.start()
+        pltpu.make_async_copy(norm_ref, norm_hbm, sems.at[2]),
+    )
+    copies[0].start()
+    copies[1].start()
     norm_ref[0, 0] = jnp.sqrt(jnp.sum(squares_ref[...]) / entry_count)
+    copies[2].start()
     for copy in copies:
         copy.wait()
 
@@ -376,7 +380,7 @@
     )(*stacks, initial, near, far)
     got = exchange(give, "tm", 1)
     groups = [
-        [(step + half) * space + index for half in range(2) for index in range(space)]
+        [step * space + index for index in reversed(range(2 * space))]
         for step in range(0, length, 2)
     ]
     squares = lax.all_to_all(
@@ -390,8 +394,8 @@
             jax.ShapeDtypeStruct((1, 1), jnp.float32),
         ),
         in_specs=[whole] * 3,
-        out_specs=(outside, pl.BlockSpec(memory_space=pltpu.SMEM)),
-        scratch_shapes=[pltpu.SemaphoreType.DMA((2,))],
+        out_specs=(outside, outside),
+        scratch_shapes=[pltpu.SMEM((1, 1), jnp.float32), pltpu.SemaphoreType.DMA((3,))],
         compiler_params=params,
         cost_estimate=pl.CostEstimate(flops=4000, bytes_accessed=100000, transcendentals=0),
         name="join_species",

time: 24.3 us -> 21.4 us (0.88)
  blocking collectives: 9.81 us -> 7.29 us
  Pallas kernels: 2.83 us -> 2.37 us
    all_to_all x1, blocking collectives: 9.81 us -> 7.29 us  [shards(): lax.all_to_all(squares, ('tm', 'space'), 0, 0, axis_index_groups=groups,...]
    pallas_call x1, Pallas kernels: 1.18 us -> 0.72 us  [shards(): pl.pallas_call(functools.partial(join_kernel, entry_count), out_shape=(ja...]
where the time goes in v8:
time: 21.4 us; the launch traced here: 21.1 us
  blocking collectives  7.29 us (34%)
  starting transfers between devices  6.5 us (30%)
  waiting for transfers between devices  4.32 us (20%)
  Pallas kernels  2.37 us (11%)
  between operations  0.65 us (3%)
    all_to_all x1, blocking collectives, shards(): lax.all_to_all(squares, ('tm', 'space'), 0, 0, axis_index_groups=groups,...  7.29 us
    ppermute x4, starting transfers between devices, exchange(): return lax.ppermute(value, axis, pairs)  6.5 us
    ppermute x4, waiting for transfers between devices, exchange(): return lax.ppermute(value, axis, pairs)  4.32 us
    pallas_call x1, Pallas kernels, shards(): pl.pallas_call(stack_kernel, out_shape=(pltpu.VMEM((2, cells, lanes), jnp...  0.96 us
    pallas_call x1, Pallas kernels, shards(): pl.pallas_call(functools.partial(join_kernel, entry_count), out_shape=(ja...  0.72 us
  transfers between devices with their start and end apart: 4, of which 3 were waited for; matrix products, arithmetic and copies ran while one was open for 0% of the time, Pallas kernels for 2%

profile of v8, /device:TPU:0, one launch (start us, length us, event | category | flops | bytes accessed | tf_op | source)
XLA Modules:
  0.0 21.1 jit_solution(13342394469524336565)
XLA Ops:
  0.6 1.0 %stack_arrays.1 = (f32[2,64,128]{2,1,0:T(8,128)S(1)}, f32[2,64,128]{2,1,0:T(8,128)S(1)}, f32[64,128]{1,0:T(8,128)S(1)}, s32[64,128]{1,0:T(8,128)S(1)}, f32[8,128]{1,0:T(8,128)S(1)}) custom-call(f32[1,2,64,128]{3,2,1,0:T(8,128)} %forcing_hbm.1, f32[1,2,64,128]{3,2,1,0:T(8,128)} %previous_hbm.1, f32[2,64,128]{2,1,0:T(8,128)} %initial_hbm.1, f32[2,8]{1,0:T(2,128)} %zones_hbm.1, ...), custom_call_target="tpu_custom_call" | custom-call | flops 4000 | bytes 500000 | tf_op jit(solution)/shard_map/stack_arrays/pallas_call | solution.py:322
  1.6 4.1 %collective-permute-start.1 = (f32[2,64,128]{2,1,0:T(8,128)S(1)}, f32[2,64,128]{2,1,0:T(8,128)S(1)}, u32[]{:S(2)}, u32[]{:S(2)}) collective-permute-start(f32[2,64,128]{2,1,0:T(8,128)S(1)} %get-tuple-element.14.refs_0_), channel_id=1, source_target_pairs={{0,16},{8,24},{16,0},{24,8},{1,17},{9,25},{17,1},{25,9},{2,18},{10... | collective-permute-start | bytes 196616 | tf_op jit(solution)/shard_map/ppermute | solution.py:302
  5.7 1.3 %collective-permute-start.2 = (f32[2,64,128]{2,1,0:T(8,128)S(1)}, f32[2,64,128]{2,1,0:T(8,128)S(1)}, u32[]{:S(2)}, u32[]{:S(2)}) collective-permute-start(f32[2,64,128]{2,1,0:T(8,128)S(1)} %get-tuple-element.15), channel_id=1, source_target_pairs={{0,24},{8,16},{16,8},{24,0},{1,25},{9,17},{17,9},{25,1},{2,26},{10... | collective-permute-start | bytes 196616 | tf_op jit(solution)/shard_map/ppermute | solution.py:302
  7.1 0.2 %collective-permute-start = (f32[2,64,128]{2,1,0:T(8,128)S(1)}, f32[2,64,128]{2,1,0:T(8,128)S(1)}, u32[]{:S(2)}, u32[]{:S(2)}) collective-permute-start(f32[2,64,128]{2,1,0:T(8,128)S(1)} %get-tuple-element.15), channel_id=1, source_target_pairs={{0,8},{8,0},{16,24},{24,16},{1,9},{9,1},{17,25},{25,17},{2,10},{10... | collective-permute-start | bytes 196616 | tf_op jit(solution)/shard_map/ppermute | solution.py:302
  7.3 0.4 %factor_lines.1 = (f32[4,6,64,128]{3,2,1,0:T(8,128)S(1)}, f32[4,3,64,128]{3,2,1,0:T(8,128)S(1)}) custom-call(f32[8,128]{1,0:T(8,128)S(1)} %get-tuple-element.17.rows_ref, s32[64,128]{1,0:T(8,128)S(1)} %get-tuple-element.18.faces_ref), custom_call_target="tpu_custom_call" | custom-call | flops 4000000 | bytes 3000000 | tf_op jit(solution)/shard_map/factor_lines/pallas_call | solution.py:356
  7.7 1.8 %collective-permute-done.1.refs_2_ = f32[2,64,128]{2,1,0:T(8,128)S(1)} collective-permute-done((f32[2,64,128]{2,1,0:T(8,128)S(1)}, f32[2,64,128]{2,1,0:T(8,128)S(1)}, u32[]{:S(2)}, u32[]{:S(2)}) %collective-permute-start.1) | collective-permute-done | bytes 65568 | tf_op jit(solution)/shard_map/ppermute | solution.py:302
  9.5 2.5 %collective-permute-done.2.refs_3_ = f32[2,64,128]{2,1,0:T(8,128)S(1)} collective-permute-done((f32[2,64,128]{2,1,0:T(8,128)S(1)}, f32[2,64,128]{2,1,0:T(8,128)S(1)}, u32[]{:S(2)}, u32[]{:S(2)}) %collective-permute-start.2) | collective-permute-done | bytes 65568 | tf_op jit(solution)/shard_map/ppermute | solution.py:302
  11.9 0.1 collective-permute-done.refs_1_
  12.0 0.3 %solve_lines.1 = (f32[64,128]{1,0:T(8,128)S(1)}, f32[64,128]{1,0:T(8,128)S(1)}, f32[16,1,128]{2,1,0:T(1,128)S(1)}) custom-call(f32[2,64,128]{2,1,0:T(8,128)S(1)} %get-tuple-element.14.refs_0_, f32[2,64,128]{2,1,0:T(8,128)S(1)} %collective-permute-done.refs_1_, f32[2,64,128]{2,1,0:T(8,128)S(1)} %collective-permute-done.1.refs_2_, ...), custom_call_target="tpu_custom_call" | custom-call | flops 4000000 | bytes 3000000 | tf_op jit(solution)/shard_map/solve_lines/pallas_call | solution.py:368
  12.3 0.8 %collective-permute-start.3 = (f32[64,128]{1,0:T(8,128)S(1)}, f32[64,128]{1,0:T(8,128)S(1)}, u32[]{:S(2)}, u32[]{:S(2)}) collective-permute-start(f32[64,128]{1,0:T(8,128)S(1)} %get-tuple-element.22), channel_id=1, source_target_pairs={{0,8},{8,0},{16,24},{24,16},{1,9},{9,1},{17,25},{25,17},{2,10},{10... | collective-permute-start | bytes 98312 | tf_op jit(solution)/shard_map/ppermute | solution.py:302
  13.1 7.3 %all_to_all.5.squares_ref = f32[16,1,128]{2,1,0:T(1,128)S(1)} all-to-all(f32[16,1,128]{2,1,0:T(1,128)S(1)} %get-tuple-element.23), channel_id=1, replica_groups={{15,14,13,12,11,10,9,8,7,6,5,4,3,2,1,0},{31,30,29,28,27,26,25,24,23,22,..., dimensions={0} | all-to-all | bytes 16384 | tf_op jit(solution)/shard_map/all_to_all | solution.py:386
  20.4 0.0 collective-permute-done.3.got_ref
  20.4 0.7 %join_species.1 = (f32[1,2,64,128]{3,2,1,0:T(8,128)}, f32[1,1]{1,0:T(1,128)}) custom-call(f32[64,128]{1,0:T(8,128)S(1)} %get-tuple-element.21.own_ref, f32[64,128]{1,0:T(8,128)S(1)} %collective-permute-done.3.got_ref, f32[16,1,128]{2,1,0:T(1,128)S(1)} %all_to_all.5.squares_ref), custom_call_target="tpu_custom_call" | custom-call | flops 4000 | bytes 100000 | tf_op jit(solution)/shard_map/join_species/pallas_call | solution.py:390
Async XLA Ops:
  1.6 7.9 %collective-permute-start.1 = (f32[2,64,128]{2,1,0:T(8,128)S(1)}, f32[2,64,128]{2,1,0:T(8,128)S(1)}, u32[]{:S(2)}, u32[]{:S(2)}) collective-permute-start(f32[2,64,128]{2,1,0:T(8,128)S(1)} %get-tuple-element.14.refs_0_), channel_id=1, source_target_pairs={{0,16},{8,24},{16,0},{24,8},{1,17},{9,25},{17,1},{25,9},{2,18},{10... | collective-permute-start | bytes 196616 | tf_op jit(solution)/shard_map/ppermute | solution.py:302
  5.7 6.2 %collective-permute-start.2 = (f32[2,64,128]{2,1,0:T(8,128)S(1)}, f32[2,64,128]{2,1,0:T(8,128)S(1)}, u32[]{:S(2)}, u32[]{:S(2)}) collective-permute-start(f32[2,64,128]{2,1,0:T(8,128)S(1)} %get-tuple-element.15), channel_id=1, source_target_pairs={{0,24},{8,16},{16,8},{24,0},{1,25},{9,17},{17,9},{25,1},{2,26},{10... | collective-permute-start | bytes 196616 | tf_op jit(solution)/shard_map/ppermute | solution.py:302
  7.1 5.0 %collective-permute-start = (f32[2,64,128]{2,1,0:T(8,128)S(1)}, f32[2,64,128]{2,1,0:T(8,128)S(1)}, u32[]{:S(2)}, u32[]{:S(2)}) collective-permute-start(f32[2,64,128]{2,1,0:T(8,128)S(1)} %get-tuple-element.15), channel_id=1, source_target_pairs={{0,8},{8,0},{16,24},{24,16},{1,9},{9,1},{17,25},{25,17},{2,10},{10... | collective-permute-start | bytes 196616 | tf_op jit(solution)/shard_map/ppermute | solution.py:302
  12.3 8.1 %collective-permute-start.3 = (f32[64,128]{1,0:T(8,128)S(1)}, f32[64,128]{1,0:T(8,128)S(1)}, u32[]{:S(2)}, u32[]{:S(2)}) collective-permute-start(f32[64,128]{1,0:T(8,128)S(1)} %get-tuple-element.22), channel_id=1, source_target_pairs={{0,8},{8,0},{16,24},{24,16},{1,9},{9,1},{17,25},{25,17},{2,10},{10... | collective-permute-start | bytes 98312 | tf_op jit(solution)/shard_map/ppermute | solution.py:302

commit v9 on v8

--- a/solution.py
+++ b/solution.py
@@ -90,24 +90,44 @@
     return term if total is None else total + term
 
 
-def stack_kernel(
-    forcing_hbm,
-    previous_hbm,
+def start_all(pairs, sems):
+    copies = [
+        pltpu.make_async_copy(source, target, sems.at[index])
+        for index, (source, target) in enumerate(pairs)
+    ]
+    for copy in copies:
+        copy.start()
+    return copies
+
+
+def stack_kernel(forcing_hbm, previous_hbm, mine_ref, other_ref, sems):
+    species = lax.axis_index("tm") % 2
+    pairs = (
+        (forcing_hbm.at[0, species], mine_ref.at[0]),
+        (previous_hbm.at[0, species], mine_ref.at[1]),
+        (forcing_hbm.at[0, 1 - species], other_ref.at[0]),
+        (previous_hbm.at[0, 1 - species], other_ref.at[1]),
+    )
+    for copy in start_all(pairs, sems):
+        copy.wait()
+
+
+def factor_kernel(
+    length,
     initial_hbm,
     zones_hbm,
     drift_hbm,
     zone_hbm,
     flag_hbm,
     faces_hbm,
-    mine_ref,
-    other_ref,
+    near_ref,
+    far_ref,
     initial_ref,
-    faces_ref,
-    rows_ref,
     zones_ref,
     drift_ref,
     zone_ref,
     flag_ref,
+    faces_ref,
     sems,
 ):
     species = lax.axis_index("tm") % 2
@@ -116,41 +136,22 @@
         (drift_hbm, drift_ref),
         (zone_hbm, zone_ref),
         (flag_hbm, flag_ref),
-        (forcing_hbm.at[0, species], mine_ref.at[0]),
-        (previous_hbm.at[0, species], mine_ref.at[1]),
-        (forcing_hbm.at[0, 1 - species], other_ref.at[0]),
-        (previous_hbm.at[0, 1 - species], other_ref.at[1]),
         (faces_hbm, faces_ref),
         (initial_hbm.at[species], initial_ref),
     )
-    copies = [
-        pltpu.make_async_copy(source, target, sems.at[index])
-        for index, (source, target) in enumerate(pairs)
-    ]
-    for copy in copies:
-        copy.start()
-    for copy in copies[:4]:
+    for copy in start_all(pairs, sems):
         copy.wait()
     zone = zone_ref[...]
     diffusion = jnp.zeros(zone.shape, jnp.float32)
     for index in range(zones_ref.shape[1]):
         diffusion = jnp.where(zone == index, zones_ref[species, index], diffusion)
-    rows_ref[0:1] = diffusion
-    rows_ref[1:2] = jnp.full(zone.shape, drift_ref[species], jnp.float32)
-    rows_ref[2:3] = flag_ref[...].astype(jnp.float32)
-    for copy in copies[4:]:
-        copy.wait()
-
-
-def factor_kernel(length, rows_ref, faces_ref, near_ref, far_ref):
+    drift = drift_ref[species]
     cells, lanes = faces_ref.shape
     faces = faces_ref[...].astype(jnp.float32)
     row = lax.broadcasted_iota(jnp.int32, (cells, lanes), 0)
     link_above = jnp.where(row == cells - 1, 0.0, faces)
     link_below = jnp.where(row == 0, 0.0, roll_down(faces, 1))
-    ground = jnp.where(row == 0, rows_ref[2:3], 0.0)
-    diffusion = rows_ref[0:1]
-    drift = rows_ref[1:2]
+    ground = jnp.where(row == 0, flag_ref[...].astype(jnp.float32), 0.0)
     below = -(diffusion + drift) * link_below
     above = -diffusion * link_above
     centre = diffusion * (link_below + link_above) + drift + 2.0 * diffusion * ground
@@ -319,52 +320,44 @@
     outside = pl.BlockSpec(memory_space=pltpu.HBM)
     count = planes(length)
     params = pltpu.CompilerParams(vmem_limit_bytes=40 * 1024 * 1024)
-    mine, other, initial, faces, rows = pl.pallas_call(
+    alone = pltpu.CompilerParams(vmem_limit_bytes=56 * 1024 * 1024)
+    mine, other = pl.pallas_call(
         stack_kernel,
         out_shape=(
             pltpu.VMEM((2, cells, lanes), jnp.float32),
             pltpu.VMEM((2, cells, lanes), jnp.float32),
+        ),
+        in_specs=[outside] * 2,
+        out_specs=[whole] * 2,
+        scratch_shapes=[pltpu.SemaphoreType.DMA((4,))],
+        compiler_params=alone,
+        cost_estimate=pl.CostEstimate(flops=4000, bytes_accessed=500000, transcendentals=0),
+        name="stack_arrays",
+    )(forcing, previous)
+    stacks = [mine]
+    for bits in range(1, length):
+        stacks.append(exchange(other if bits % 2 else mine, "tm", bits))
+    near, far, initial = pl.pallas_call(
+        functools.partial(factor_kernel, length),
+        out_shape=(
+            pltpu.VMEM((count, 2 * near_steps, cells, lanes), jnp.float32),
+            pltpu.VMEM((count, 3, cells, lanes), jnp.float32),
             pltpu.VMEM((cells, lanes), jnp.float32),
-            pltpu.VMEM((cells, lanes), jnp.int32),
-            pltpu.VMEM((tile, lanes), jnp.float32),
         ),
-        in_specs=[outside] * 8,
-        out_specs=[whole] * 5,
+        in_specs=[outside] * 6,
+        out_specs=[whole] * 3,
         scratch_shapes=[
             pltpu.SMEM(zone_diffusion.shape, jnp.float32),
             pltpu.SMEM(drift_rate.shape, jnp.float32),
             pltpu.VMEM((1, lanes), jnp.int32),
             pltpu.VMEM((1, lanes), jnp.int32),
-            pltpu.SemaphoreType.DMA((10,)),
+            pltpu.VMEM((cells, lanes), jnp.int32),
+            pltpu.SemaphoreType.DMA((6,)),
         ],
-        compiler_params=pltpu.CompilerParams(vmem_limit_bytes=62 * 1024 * 1024),
-        cost_estimate=pl.CostEstimate(flops=4000, bytes_accessed=500000, transcendentals=0),
-        name="stack_arrays",
-    )(
-        forcing,
-        previous,
-        initial_state,
-        zone_diffusion,
-        drift_rate,
-        column_zone[None],
-        bottom_flag[None],
-        open_faces,
-    )
-    stacks = [mine]
-    for bits in range(1, length):
-        stacks.append(exchange(other if bits % 2 else mine, "tm", bits))
-    near, far = pl.pallas_call(
-        functools.partial(factor_kernel, length),
-        out_shape=(
-            jax.ShapeDtypeStruct((count, 2 * near_steps, cells, lanes), jnp.float32),
-            jax.ShapeDtypeStruct((count, 3, cells, lanes), jnp.float32),
-        ),
-        in_specs=[whole] * 2,
-        out_specs=[whole] * 2,
-        compiler_params=params,
+        compiler_params=alone,
         cost_estimate=pl.CostEstimate(flops=4000000, bytes_accessed=3000000, transcendentals=0),
         name="factor_lines",
-    )(rows, faces)
+    )(initial_state, zone_diffusion, drift_rate, column_zone[None], bottom_flag[None], open_faces)
     own, give, squares = pl.pallas_call(
         functools.partial(sweep_kernel, length),
         out_shape=(

time: 21.4 us -> 21.3 us (level)
  waiting for transfers between devices: 4.32 us -> 3.43 us
  Pallas kernels: 2.37 us -> 3.15 us
    pallas_call x1, Pallas kernels: 0.41 us -> 1.3 us  [shards(): pl.pallas_call(functools.partial(factor_kernel, length), out_shape=(pltpu...]
    ppermute x4, waiting for transfers between devices: 4.32 us -> 3.43 us  [exchange(): return lax.ppermute(value, axis, pairs)]
  transfers between devices with their start and end apart: 4 -> 4, of which waited for: 3 -> 3; matrix products, arithmetic and copies ran while one was open for 0% -> 0% of each run, Pallas kernels for 2% -> 6%
where the time goes in v9:
time: 21.3 us; the launch traced here: 21 us
  blocking collectives  7.29 us (34%)
  starting transfers between devices  6.5 us (31%)
  waiting for transfers between devices  3.43 us (16%)
  Pallas kernels  3.15 us (15%)
  between operations  0.65 us (3%)
    all_to_all x1, blocking collectives, shards(): lax.all_to_all(squares, ('tm', 'space'), 0, 0, axis_index_groups=groups,...  7.29 us
    ppermute x4, starting transfers between devices, exchange(): return lax.ppermute(value, axis, pairs)  6.5 us
    ppermute x4, waiting for transfers between devices, exchange(): return lax.ppermute(value, axis, pairs)  3.43 us
    pallas_call x1, Pallas kernels, shards(): pl.pallas_call(functools.partial(factor_kernel, length), out_shape=(pltpu...  1.3 us
    pallas_call x1, Pallas kernels, shards(): pl.pallas_call(stack_kernel, out_shape=(pltpu.VMEM((2, cells, lanes), jnp...  0.86 us
    pallas_call x1, Pallas kernels, shards(): pl.pallas_call(functools.partial(join_kernel, entry_count), out_shape=(ja...  0.72 us
  transfers between devices with their start and end apart: 4, of which 3 were waited for; matrix products, arithmetic and copies ran while one was open for 0% of the time, Pallas kernels for 6%

profile of v9, /device:TPU:0, one launch (start us, length us, event | category | flops | bytes accessed | tf_op | source)
XLA Modules:
  0.0 21.0 jit_solution(18425824481936388280)
XLA Ops:
  0.6 0.9 %stack_arrays.1 = (f32[2,64,128]{2,1,0:T(8,128)S(1)}, f32[2,64,128]{2,1,0:T(8,128)S(1)}) custom-call(f32[1,2,64,128]{3,2,1,0:T(8,128)} %forcing_hbm.1, f32[1,2,64,128]{3,2,1,0:T(8,128)} %previous_hbm.1), custom_call_target="tpu_custom_call" | custom-call | flops 4000 | bytes 500000 | tf_op jit(solution)/shard_map/stack_arrays/pallas_call | solution.py:324
  1.5 4.1 %collective-permute-start.1 = (f32[2,64,128]{2,1,0:T(8,128)S(1)}, f32[2,64,128]{2,1,0:T(8,128)S(1)}, u32[]{:S(2)}, u32[]{:S(2)}) collective-permute-start(f32[2,64,128]{2,1,0:T(8,128)S(1)} %get-tuple-element.12.refs_0_), channel_id=1, source_target_pairs={{0,16},{8,24},{16,0},{24,8},{1,17},{9,25},{17,1},{25,9},{2,18},{10... | collective-permute-start | bytes 196616 | tf_op jit(solution)/shard_map/ppermute | solution.py:303
  5.6 1.3 %collective-permute-start.2 = (f32[2,64,128]{2,1,0:T(8,128)S(1)}, f32[2,64,128]{2,1,0:T(8,128)S(1)}, u32[]{:S(2)}, u32[]{:S(2)}) collective-permute-start(f32[2,64,128]{2,1,0:T(8,128)S(1)} %get-tuple-element.13), channel_id=1, source_target_pairs={{0,24},{8,16},{16,8},{24,0},{1,25},{9,17},{17,9},{25,1},{2,26},{10... | collective-permute-start | bytes 196616 | tf_op jit(solution)/shard_map/ppermute | solution.py:303
  6.9 0.2 %collective-permute-start = (f32[2,64,128]{2,1,0:T(8,128)S(1)}, f32[2,64,128]{2,1,0:T(8,128)S(1)}, u32[]{:S(2)}, u32[]{:S(2)}) collective-permute-start(f32[2,64,128]{2,1,0:T(8,128)S(1)} %get-tuple-element.13), channel_id=1, source_target_pairs={{0,8},{8,0},{16,24},{24,16},{1,9},{9,1},{17,25},{25,17},{2,10},{10... | collective-permute-start | bytes 196616 | tf_op jit(solution)/shard_map/ppermute | solution.py:303
  7.2 1.3 %factor_lines.1 = (f32[4,6,64,128]{3,2,1,0:T(8,128)S(1)}, f32[4,3,64,128]{3,2,1,0:T(8,128)S(1)}, f32[64,128]{1,0:T(8,128)S(1)}) custom-call(f32[2,64,128]{2,1,0:T(8,128)} %initial_hbm.1, f32[2,8]{1,0:T(2,128)} %zones_hbm.1, f32[2]{0:T(128)} %drift_hbm.1, s32[1,128]{1,0:T(1,128)} %bitcast.3, s32[1,128]{1,0:T(1,128)} %bitcast.4, s32[64,128]{1,0:T(8,128)} %faces_hbm.1), custom_call_target="tpu_custom_call" | custom-call | flops 4000000 | bytes 3000000 | tf_op jit(solution)/shard_map/factor_lines/pallas_call | solution.py:340
  8.5 0.9 %collective-permute-done.1.refs_2_ = f32[2,64,128]{2,1,0:T(8,128)S(1)} collective-permute-done((f32[2,64,128]{2,1,0:T(8,128)S(1)}, f32[2,64,128]{2,1,0:T(8,128)S(1)}, u32[]{:S(2)}, u32[]{:S(2)}) %collective-permute-start.1) | collective-permute-done | bytes 65568 | tf_op jit(solution)/shard_map/ppermute | solution.py:303
  9.4 2.5 %collective-permute-done.2.refs_3_ = f32[2,64,128]{2,1,0:T(8,128)S(1)} collective-permute-done((f32[2,64,128]{2,1,0:T(8,128)S(1)}, f32[2,64,128]{2,1,0:T(8,128)S(1)}, u32[]{:S(2)}, u32[]{:S(2)}) %collective-permute-start.2) | collective-permute-done | bytes 65568 | tf_op jit(solution)/shard_map/ppermute | solution.py:303
  11.8 0.1 collective-permute-done.refs_1_
  11.9 0.3 %solve_lines.1 = (f32[64,128]{1,0:T(8,128)S(1)}, f32[64,128]{1,0:T(8,128)S(1)}, f32[16,1,128]{2,1,0:T(1,128)S(1)}) custom-call(f32[2,64,128]{2,1,0:T(8,128)S(1)} %get-tuple-element.12.refs_0_, f32[2,64,128]{2,1,0:T(8,128)S(1)} %collective-permute-done.refs_1_, f32[2,64,128]{2,1,0:T(8,128)S(1)} %collective-permute-done.1.refs_2_, ...), custom_call_target="tpu_custom_call" | custom-call | flops 4000000 | bytes 3000000 | tf_op jit(solution)/shard_map/solve_lines/pallas_call | solution.py:361
  12.2 0.8 %collective-permute-start.3 = (f32[64,128]{1,0:T(8,128)S(1)}, f32[64,128]{1,0:T(8,128)S(1)}, u32[]{:S(2)}, u32[]{:S(2)}) collective-permute-start(f32[64,128]{1,0:T(8,128)S(1)} %get-tuple-element.18), channel_id=1, source_target_pairs={{0,8},{8,0},{16,24},{24,16},{1,9},{9,1},{17,25},{25,17},{2,10},{10... | collective-permute-start | bytes 98312 | tf_op jit(solution)/shard_map/ppermute | solution.py:303
  13.0 7.3 %all_to_all.5.squares_ref = f32[16,1,128]{2,1,0:T(1,128)S(1)} all-to-all(f32[16,1,128]{2,1,0:T(1,128)S(1)} %get-tuple-element.19), channel_id=1, replica_groups={{15,14,13,12,11,10,9,8,7,6,5,4,3,2,1,0},{31,30,29,28,27,26,25,24,23,22,..., dimensions={0} | all-to-all | bytes 16384 | tf_op jit(solution)/shard_map/all_to_all | solution.py:379
  20.3 0.0 collective-permute-done.3.got_ref
  20.3 0.7 %join_species.1 = (f32[1,2,64,128]{3,2,1,0:T(8,128)}, f32[1,1]{1,0:T(1,128)}) custom-call(f32[64,128]{1,0:T(8,128)S(1)} %get-tuple-element.17.own_ref, f32[64,128]{1,0:T(8,128)S(1)} %collective-permute-done.3.got_ref, f32[16,1,128]{2,1,0:T(1,128)S(1)} %all_to_all.5.squares_ref), custom_call_target="tpu_custom_call" | custom-call | flops 4000 | bytes 100000 | tf_op jit(solution)/shard_map/join_species/pallas_call | solution.py:383
Async XLA Ops:
  1.5 7.9 %collective-permute-start.1 = (f32[2,64,128]{2,1,0:T(8,128)S(1)}, f32[2,64,128]{2,1,0:T(8,128)S(1)}, u32[]{:S(2)}, u32[]{:S(2)}) collective-permute-start(f32[2,64,128]{2,1,0:T(8,128)S(1)} %get-tuple-element.12.refs_0_), channel_id=1, source_target_pairs={{0,16},{8,24},{16,0},{24,8},{1,17},{9,25},{17,1},{25,9},{2,18},{10... | collective-permute-start | bytes 196616 | tf_op jit(solution)/shard_map/ppermute | solution.py:303
  5.6 6.2 %collective-permute-start.2 = (f32[2,64,128]{2,1,0:T(8,128)S(1)}, f32[2,64,128]{2,1,0:T(8,128)S(1)}, u32[]{:S(2)}, u32[]{:S(2)}) collective-permute-start(f32[2,64,128]{2,1,0:T(8,128)S(1)} %get-tuple-element.13), channel_id=1, source_target_pairs={{0,24},{8,16},{16,8},{24,0},{1,25},{9,17},{17,9},{25,1},{2,26},{10... | collective-permute-start | bytes 196616 | tf_op jit(solution)/shard_map/ppermute | solution.py:303
  6.9 5.0 %collective-permute-start = (f32[2,64,128]{2,1,0:T(8,128)S(1)}, f32[2,64,128]{2,1,0:T(8,128)S(1)}, u32[]{:S(2)}, u32[]{:S(2)}) collective-permute-start(f32[2,64,128]{2,1,0:T(8,128)S(1)} %get-tuple-element.13), channel_id=1, source_target_pairs={{0,8},{8,0},{16,24},{24,16},{1,9},{9,1},{17,25},{25,17},{2,10},{10... | collective-permute-start | bytes 196616 | tf_op jit(solution)/shard_map/ppermute | solution.py:303
  12.2 8.1 %collective-permute-start.3 = (f32[64,128]{1,0:T(8,128)S(1)}, f32[64,128]{1,0:T(8,128)S(1)}, u32[]{:S(2)}, u32[]{:S(2)}) collective-permute-start(f32[64,128]{1,0:T(8,128)S(1)} %get-tuple-element.18), channel_id=1, source_target_pairs={{0,8},{8,0},{16,24},{24,16},{1,9},{9,1},{17,25},{25,17},{2,10},{10... | collective-permute-start | bytes 98312 | tf_op jit(solution)/shard_map/ppermute | solution.py:303

commit v10 on v9

--- a/solution.py
+++ b/solution.py
@@ -372,10 +372,9 @@
         name="solve_lines",
     )(*stacks, initial, near, far)
     got = exchange(give, "tm", 1)
-    groups = [
-        [step * space + index for index in reversed(range(2 * space))]
-        for step in range(0, length, 2)
-    ]
+    last = 2 * space - 1
+    order = [last, *range(2, last, 2), *range(3, last, 2), 1, 0]
+    groups = [[step * space + index for index in order] for step in range(0, length, 2)]
     squares = lax.all_to_all(
         squares, ("tm", "space"), 0, 0, axis_index_groups=groups, tiled=True
     )

time: 21.3 us -> 21.3 us (level)
  no operation moved by 1% of the time
where the time goes in v10:
time: 21.3 us; the launch traced here: 21 us
  blocking collectives  7.27 us (34%)
  starting transfers between devices  6.5 us (31%)
  waiting for transfers between devices  3.43 us (16%)
  Pallas kernels  3.15 us (15%)
  between operations  0.65 us (3%)
    all_to_all x1, blocking collectives, shards(): lax.all_to_all(squares, ('tm', 'space'), 0, 0, axis_index_groups=groups,...  7.27 us
    ppermute x4, starting transfers between devices, exchange(): return lax.ppermute(value, axis, pairs)  6.5 us
    ppermute x4, waiting for transfers between devices, exchange(): return lax.ppermute(value, axis, pairs)  3.43 us
    pallas_call x1, Pallas kernels, shards(): pl.pallas_call(functools.partial(factor_kernel, length), out_shape=(pltpu...  1.3 us
    pallas_call x1, Pallas kernels, shards(): pl.pallas_call(stack_kernel, out_shape=(pltpu.VMEM((2, cells, lanes), jnp...  0.86 us
    pallas_call x1, Pallas kernels, shards(): pl.pallas_call(functools.partial(join_kernel, entry_count), out_shape=(ja...  0.72 us
  transfers between devices with their start and end apart: 4, of which 3 were waited for; matrix products, arithmetic and copies ran while one was open for 0% of the time, Pallas kernels for 6%

profile of v10, /device:TPU:0, one launch (start us, length us, event | category | flops | bytes accessed | tf_op | source)
XLA Modules:
  0.0 21.0 jit_solution(7203347970583995086)
XLA Ops:
  0.6 0.9 %stack_arrays.1 = (f32[2,64,128]{2,1,0:T(8,128)S(1)}, f32[2,64,128]{2,1,0:T(8,128)S(1)}) custom-call(f32[1,2,64,128]{3,2,1,0:T(8,128)} %forcing_hbm.1, f32[1,2,64,128]{3,2,1,0:T(8,128)} %previous_hbm.1), custom_call_target="tpu_custom_call" | custom-call | flops 4000 | bytes 500000 | tf_op jit(solution)/shard_map/stack_arrays/pallas_call | solution.py:324
  1.5 4.1 %collective-permute-start.1 = (f32[2,64,128]{2,1,0:T(8,128)S(1)}, f32[2,64,128]{2,1,0:T(8,128)S(1)}, u32[]{:S(2)}, u32[]{:S(2)}) collective-permute-start(f32[2,64,128]{2,1,0:T(8,128)S(1)} %get-tuple-element.12.refs_0_), channel_id=1, source_target_pairs={{0,16},{8,24},{16,0},{24,8},{1,17},{9,25},{17,1},{25,9},{2,18},{10... | collective-permute-start | bytes 196616 | tf_op jit(solution)/shard_map/ppermute | solution.py:303
  5.6 1.3 %collective-permute-start.2 = (f32[2,64,128]{2,1,0:T(8,128)S(1)}, f32[2,64,128]{2,1,0:T(8,128)S(1)}, u32[]{:S(2)}, u32[]{:S(2)}) collective-permute-start(f32[2,64,128]{2,1,0:T(8,128)S(1)} %get-tuple-element.13), channel_id=1, source_target_pairs={{0,24},{8,16},{16,8},{24,0},{1,25},{9,17},{17,9},{25,1},{2,26},{10... | collective-permute-start | bytes 196616 | tf_op jit(solution)/shard_map/ppermute | solution.py:303
  6.9 0.2 %collective-permute-start = (f32[2,64,128]{2,1,0:T(8,128)S(1)}, f32[2,64,128]{2,1,0:T(8,128)S(1)}, u32[]{:S(2)}, u32[]{:S(2)}) collective-permute-start(f32[2,64,128]{2,1,0:T(8,128)S(1)} %get-tuple-element.13), channel_id=1, source_target_pairs={{0,8},{8,0},{16,24},{24,16},{1,9},{9,1},{17,25},{25,17},{2,10},{10... | collective-permute-start | bytes 196616 | tf_op jit(solution)/shard_map/ppermute | solution.py:303
  7.2 1.3 %factor_lines.1 = (f32[4,6,64,128]{3,2,1,0:T(8,128)S(1)}, f32[4,3,64,128]{3,2,1,0:T(8,128)S(1)}, f32[64,128]{1,0:T(8,128)S(1)}) custom-call(f32[2,64,128]{2,1,0:T(8,128)} %initial_hbm.1, f32[2,8]{1,0:T(2,128)} %zones_hbm.1, f32[2]{0:T(128)} %drift_hbm.1, s32[1,128]{1,0:T(1,128)} %bitcast.3, s32[1,128]{1,0:T(1,128)} %bitcast.4, s32[64,128]{1,0:T(8,128)} %faces_hbm.1), custom_call_target="tpu_custom_call" | custom-call | flops 4000000 | bytes 3000000 | tf_op jit(solution)/shard_map/factor_lines/pallas_call | solution.py:340
  8.5 0.9 %collective-permute-done.1.refs_2_ = f32[2,64,128]{2,1,0:T(8,128)S(1)} collective-permute-done((f32[2,64,128]{2,1,0:T(8,128)S(1)}, f32[2,64,128]{2,1,0:T(8,128)S(1)}, u32[]{:S(2)}, u32[]{:S(2)}) %collective-permute-start.1) | collective-permute-done | bytes 65568 | tf_op jit(solution)/shard_map/ppermute | solution.py:303
  9.4 2.5 %collective-permute-done.2.refs_3_ = f32[2,64,128]{2,1,0:T(8,128)S(1)} collective-permute-done((f32[2,64,128]{2,1,0:T(8,128)S(1)}, f32[2,64,128]{2,1,0:T(8,128)S(1)}, u32[]{:S(2)}, u32[]{:S(2)}) %collective-permute-start.2) | collective-permute-done | bytes 65568 | tf_op jit(solution)/shard_map/ppermute | solution.py:303
  11.8 0.1 collective-permute-done.refs_1_
  11.9 0.3 %solve_lines.1 = (f32[64,128]{1,0:T(8,128)S(1)}, f32[64,128]{1,0:T(8,128)S(1)}, f32[16,1,128]{2,1,0:T(1,128)S(1)}) custom-call(f32[2,64,128]{2,1,0:T(8,128)S(1)} %get-tuple-element.12.refs_0_, f32[2,64,128]{2,1,0:T(8,128)S(1)} %collective-permute-done.refs_1_, f32[2,64,128]{2,1,0:T(8,128)S(1)} %collective-permute-done.1.refs_2_, ...), custom_call_target="tpu_custom_call" | custom-call | flops 4000000 | bytes 3000000 | tf_op jit(solution)/shard_map/solve_lines/pallas_call | solution.py:361
  12.2 0.8 %collective-permute-start.3 = (f32[64,128]{1,0:T(8,128)S(1)}, f32[64,128]{1,0:T(8,128)S(1)}, u32[]{:S(2)}, u32[]{:S(2)}) collective-permute-start(f32[64,128]{1,0:T(8,128)S(1)} %get-tuple-element.18), channel_id=1, source_target_pairs={{0,8},{8,0},{16,24},{24,16},{1,9},{9,1},{17,25},{25,17},{2,10},{10... | collective-permute-start | bytes 98312 | tf_op jit(solution)/shard_map/ppermute | solution.py:303
  13.0 7.3 %all_to_all.5.squares_ref = f32[16,1,128]{2,1,0:T(1,128)S(1)} all-to-all(f32[16,1,128]{2,1,0:T(1,128)S(1)} %get-tuple-element.19), channel_id=1, replica_groups={{15,2,4,6,8,10,12,14,3,5,7,9,11,13,1,0},{31,18,20,22,24,26,28,30,19,21,..., dimensions={0} | all-to-all | bytes 16384 | tf_op jit(solution)/shard_map/all_to_all | solution.py:378
  20.3 0.0 collective-permute-done.3.got_ref
  20.3 0.7 %join_species.1 = (f32[1,2,64,128]{3,2,1,0:T(8,128)}, f32[1,1]{1,0:T(1,128)}) custom-call(f32[64,128]{1,0:T(8,128)S(1)} %get-tuple-element.17.own_ref, f32[64,128]{1,0:T(8,128)S(1)} %collective-permute-done.3.got_ref, f32[16,1,128]{2,1,0:T(1,128)S(1)} %all_to_all.5.squares_ref), custom_call_target="tpu_custom_call" | custom-call | flops 4000 | bytes 100000 | tf_op jit(solution)/shard_map/join_species/pallas_call | solution.py:382
Async XLA Ops:
  1.5 7.9 %collective-permute-start.1 = (f32[2,64,128]{2,1,0:T(8,128)S(1)}, f32[2,64,128]{2,1,0:T(8,128)S(1)}, u32[]{:S(2)}, u32[]{:S(2)}) collective-permute-start(f32[2,64,128]{2,1,0:T(8,128)S(1)} %get-tuple-element.12.refs_0_), channel_id=1, source_target_pairs={{0,16},{8,24},{16,0},{24,8},{1,17},{9,25},{17,1},{25,9},{2,18},{10... | collective-permute-start | bytes 196616 | tf_op jit(solution)/shard_map/ppermute | solution.py:303
  5.6 6.2 %collective-permute-start.2 = (f32[2,64,128]{2,1,0:T(8,128)S(1)}, f32[2,64,128]{2,1,0:T(8,128)S(1)}, u32[]{:S(2)}, u32[]{:S(2)}) collective-permute-start(f32[2,64,128]{2,1,0:T(8,128)S(1)} %get-tuple-element.13), channel_id=1, source_target_pairs={{0,24},{8,16},{16,8},{24,0},{1,25},{9,17},{17,9},{25,1},{2,26},{10... | collective-permute-start | bytes 196616 | tf_op jit(solution)/shard_map/ppermute | solution.py:303
  6.9 5.0 %collective-permute-start = (f32[2,64,128]{2,1,0:T(8,128)S(1)}, f32[2,64,128]{2,1,0:T(8,128)S(1)}, u32[]{:S(2)}, u32[]{:S(2)}) collective-permute-start(f32[2,64,128]{2,1,0:T(8,128)S(1)} %get-tuple-element.13), channel_id=1, source_target_pairs={{0,8},{8,0},{16,24},{24,16},{1,9},{9,1},{17,25},{25,17},{2,10},{10... | collective-permute-start | bytes 196616 | tf_op jit(solution)/shard_map/ppermute | solution.py:303
  12.2 8.1 %collective-permute-start.3 = (f32[64,128]{1,0:T(8,128)S(1)}, f32[64,128]{1,0:T(8,128)S(1)}, u32[]{:S(2)}, u32[]{:S(2)}) collective-permute-start(f32[64,128]{1,0:T(8,128)S(1)} %get-tuple-element.18), channel_id=1, source_target_pairs={{0,8},{8,0},{16,24},{24,16},{1,9},{9,1},{17,25},{25,17},{2,10},{10... | collective-permute-start | bytes 98312 | tf_op jit(solution)/shard_map/ppermute | solution.py:303

commit v11 on v10

--- a/solution.py
+++ b/solution.py
@@ -373,7 +373,7 @@
     )(*stacks, initial, near, far)
     got = exchange(give, "tm", 1)
     last = 2 * space - 1
-    order = [last, *range(2, last, 2), *range(3, last, 2), 1, 0]
+    order = [last, *range(last)]
     groups = [[step * space + index for index in order] for step in range(0, length, 2)]
     squares = lax.all_to_all(
         squares, ("tm", "space"), 0, 0, axis_index_groups=groups, tiled=True

time: 21.3 us -> 21.4 us (level)
  no operation moved by 1% of the time
where the time goes in v11:
time: 21.4 us; the launch traced here: 21.1 us
  blocking collectives  7.36 us (34%)
  starting transfers between devices  6.5 us (30%)
  waiting for transfers between devices  3.43 us (16%)
  Pallas kernels  3.15 us (15%)
  between operations  0.65 us (3%)
    all_to_all x1, blocking collectives, shards(): lax.all_to_all(squares, ('tm', 'space'), 0, 0, axis_index_groups=groups,...  7.36 us
    ppermute x4, starting transfers between devices, exchange(): return lax.ppermute(value, axis, pairs)  6.5 us
    ppermute x4, waiting for transfers between devices, exchange(): return lax.ppermute(value, axis, pairs)  3.43 us
    pallas_call x1, Pallas kernels, shards(): pl.pallas_call(functools.partial(factor_kernel, length), out_shape=(pltpu...  1.3 us
    pallas_call x1, Pallas kernels, shards(): pl.pallas_call(stack_kernel, out_shape=(pltpu.VMEM((2, cells, lanes), jnp...  0.86 us
    pallas_call x1, Pallas kernels, shards(): pl.pallas_call(functools.partial(join_kernel, entry_count), out_shape=(ja...  0.72 us
  transfers between devices with their start and end apart: 4, of which 3 were waited for; matrix products, arithmetic and copies ran while one was open for 0% of the time, Pallas kernels for 6%

profile of v11, /device:TPU:0, one launch (start us, length us, event | category | flops | bytes accessed | tf_op | source)
XLA Modules:
  0.0 21.1 jit_solution(5466751167428270555)
XLA Ops:
  0.6 0.9 %stack_arrays.1 = (f32[2,64,128]{2,1,0:T(8,128)S(1)}, f32[2,64,128]{2,1,0:T(8,128)S(1)}) custom-call(f32[1,2,64,128]{3,2,1,0:T(8,128)} %forcing_hbm.1, f32[1,2,64,128]{3,2,1,0:T(8,128)} %previous_hbm.1), custom_call_target="tpu_custom_call" | custom-call | flops 4000 | bytes 500000 | tf_op jit(solution)/shard_map/stack_arrays/pallas_call | solution.py:324
  1.5 4.1 %collective-permute-start.1 = (f32[2,64,128]{2,1,0:T(8,128)S(1)}, f32[2,64,128]{2,1,0:T(8,128)S(1)}, u32[]{:S(2)}, u32[]{:S(2)}) collective-permute-start(f32[2,64,128]{2,1,0:T(8,128)S(1)} %get-tuple-element.12.refs_0_), channel_id=1, source_target_pairs={{0,16},{8,24},{16,0},{24,8},{1,17},{9,25},{17,1},{25,9},{2,18},{10... | collective-permute-start | bytes 196616 | tf_op jit(solution)/shard_map/ppermute | solution.py:303
  5.6 1.3 %collective-permute-start.2 = (f32[2,64,128]{2,1,0:T(8,128)S(1)}, f32[2,64,128]{2,1,0:T(8,128)S(1)}, u32[]{:S(2)}, u32[]{:S(2)}) collective-permute-start(f32[2,64,128]{2,1,0:T(8,128)S(1)} %get-tuple-element.13), channel_id=1, source_target_pairs={{0,24},{8,16},{16,8},{24,0},{1,25},{9,17},{17,9},{25,1},{2,26},{10... | collective-permute-start | bytes 196616 | tf_op jit(solution)/shard_map/ppermute | solution.py:303
  6.9 0.2 %collective-permute-start = (f32[2,64,128]{2,1,0:T(8,128)S(1)}, f32[2,64,128]{2,1,0:T(8,128)S(1)}, u32[]{:S(2)}, u32[]{:S(2)}) collective-permute-start(f32[2,64,128]{2,1,0:T(8,128)S(1)} %get-tuple-element.13), channel_id=1, source_target_pairs={{0,8},{8,0},{16,24},{24,16},{1,9},{9,1},{17,25},{25,17},{2,10},{10... | collective-permute-start | bytes 196616 | tf_op jit(solution)/shard_map/ppermute | solution.py:303
  7.2 1.3 %factor_lines.1 = (f32[4,6,64,128]{3,2,1,0:T(8,128)S(1)}, f32[4,3,64,128]{3,2,1,0:T(8,128)S(1)}, f32[64,128]{1,0:T(8,128)S(1)}) custom-call(f32[2,64,128]{2,1,0:T(8,128)} %initial_hbm.1, f32[2,8]{1,0:T(2,128)} %zones_hbm.1, f32[2]{0:T(128)} %drift_hbm.1, s32[1,128]{1,0:T(1,128)} %bitcast.3, s32[1,128]{1,0:T(1,128)} %bitcast.4, s32[64,128]{1,0:T(8,128)} %faces_hbm.1), custom_call_target="tpu_custom_call" | custom-call | flops 4000000 | bytes 3000000 | tf_op jit(solution)/shard_map/factor_lines/pallas_call | solution.py:340
  8.5 0.9 %collective-permute-done.1.refs_2_ = f32[2,64,128]{2,1,0:T(8,128)S(1)} collective-permute-done((f32[2,64,128]{2,1,0:T(8,128)S(1)}, f32[2,64,128]{2,1,0:T(8,128)S(1)}, u32[]{:S(2)}, u32[]{:S(2)}) %collective-permute-start.1) | collective-permute-done | bytes 65568 | tf_op jit(solution)/shard_map/ppermute | solution.py:303
  9.4 2.5 %collective-permute-done.2.refs_3_ = f32[2,64,128]{2,1,0:T(8,128)S(1)} collective-permute-done((f32[2,64,128]{2,1,0:T(8,128)S(1)}, f32[2,64,128]{2,1,0:T(8,128)S(1)}, u32[]{:S(2)}, u32[]{:S(2)}) %collective-permute-start.2) | collective-permute-done | bytes 65568 | tf_op jit(solution)/shard_map/ppermute | solution.py:303
  11.8 0.1 collective-permute-done.refs_1_
  11.9 0.3 %solve_lines.1 = (f32[64,128]{1,0:T(8,128)S(1)}, f32[64,128]{1,0:T(8,128)S(1)}, f32[16,1,128]{2,1,0:T(1,128)S(1)}) custom-call(f32[2,64,128]{2,1,0:T(8,128)S(1)} %get-tuple-element.12.refs_0_, f32[2,64,128]{2,1,0:T(8,128)S(1)} %collective-permute-done.refs_1_, f32[2,64,128]{2,1,0:T(8,128)S(1)} %collective-permute-done.1.refs_2_, ...), custom_call_target="tpu_custom_call" | custom-call | flops 4000000 | bytes 3000000 | tf_op jit(solution)/shard_map/solve_lines/pallas_call | solution.py:361
  12.2 0.8 %collective-permute-start.3 = (f32[64,128]{1,0:T(8,128)S(1)}, f32[64,128]{1,0:T(8,128)S(1)}, u32[]{:S(2)}, u32[]{:S(2)}) collective-permute-start(f32[64,128]{1,0:T(8,128)S(1)} %get-tuple-element.18), channel_id=1, source_target_pairs={{0,8},{8,0},{16,24},{24,16},{1,9},{9,1},{17,25},{25,17},{2,10},{10... | collective-permute-start | bytes 98312 | tf_op jit(solution)/shard_map/ppermute | solution.py:303
  13.0 7.4 %all_to_all.5.squares_ref = f32[16,1,128]{2,1,0:T(1,128)S(1)} all-to-all(f32[16,1,128]{2,1,0:T(1,128)S(1)} %get-tuple-element.19), channel_id=1, replica_groups={{15,0,1,2,3,4,5,6,7,8,9,10,11,12,13,14},{31,16,17,18,19,20,21,22,23,24,..., dimensions={0} | all-to-all | bytes 16384 | tf_op jit(solution)/shard_map/all_to_all | solution.py:378
  20.4 0.0 collective-permute-done.3.got_ref
  20.4 0.7 %join_species.1 = (f32[1,2,64,128]{3,2,1,0:T(8,128)}, f32[1,1]{1,0:T(1,128)}) custom-call(f32[64,128]{1,0:T(8,128)S(1)} %get-tuple-element.17.own_ref, f32[64,128]{1,0:T(8,128)S(1)} %collective-permute-done.3.got_ref, f32[16,1,128]{2,1,0:T(1,128)S(1)} %all_to_all.5.squares_ref), custom_call_target="tpu_custom_call" | custom-call | flops 4000 | bytes 100000 | tf_op jit(solution)/shard_map/join_species/pallas_call | solution.py:382
Async XLA Ops:
  1.5 7.9 %collective-permute-start.1 = (f32[2,64,128]{2,1,0:T(8,128)S(1)}, f32[2,64,128]{2,1,0:T(8,128)S(1)}, u32[]{:S(2)}, u32[]{:S(2)}) collective-permute-start(f32[2,64,128]{2,1,0:T(8,128)S(1)} %get-tuple-element.12.refs_0_), channel_id=1, source_target_pairs={{0,16},{8,24},{16,0},{24,8},{1,17},{9,25},{17,1},{25,9},{2,18},{10... | collective-permute-start | bytes 196616 | tf_op jit(solution)/shard_map/ppermute | solution.py:303
  5.6 6.2 %collective-permute-start.2 = (f32[2,64,128]{2,1,0:T(8,128)S(1)}, f32[2,64,128]{2,1,0:T(8,128)S(1)}, u32[]{:S(2)}, u32[]{:S(2)}) collective-permute-start(f32[2,64,128]{2,1,0:T(8,128)S(1)} %get-tuple-element.13), channel_id=1, source_target_pairs={{0,24},{8,16},{16,8},{24,0},{1,25},{9,17},{17,9},{25,1},{2,26},{10... | collective-permute-start | bytes 196616 | tf_op jit(solution)/shard_map/ppermute | solution.py:303
  6.9 5.0 %collective-permute-start = (f32[2,64,128]{2,1,0:T(8,128)S(1)}, f32[2,64,128]{2,1,0:T(8,128)S(1)}, u32[]{:S(2)}, u32[]{:S(2)}) collective-permute-start(f32[2,64,128]{2,1,0:T(8,128)S(1)} %get-tuple-element.13), channel_id=1, source_target_pairs={{0,8},{8,0},{16,24},{24,16},{1,9},{9,1},{17,25},{25,17},{2,10},{10... | collective-permute-start | bytes 196616 | tf_op jit(solution)/shard_map/ppermute | solution.py:303
  12.2 8.2 %collective-permute-start.3 = (f32[64,128]{1,0:T(8,128)S(1)}, f32[64,128]{1,0:T(8,128)S(1)}, u32[]{:S(2)}, u32[]{:S(2)}) collective-permute-start(f32[64,128]{1,0:T(8,128)S(1)} %get-tuple-element.18), channel_id=1, source_target_pairs={{0,8},{8,0},{16,24},{24,16},{1,9},{9,1},{17,25},{25,17},{2,10},{10... | collective-permute-start | bytes 98312 | tf_op jit(solution)/shard_map/ppermute | solution.py:303

commit v12 on v11

--- a/solution.py
+++ b/solution.py
@@ -372,8 +372,7 @@
         name="solve_lines",
     )(*stacks, initial, near, far)
     got = exchange(give, "tm", 1)
-    last = 2 * space - 1
-    order = [last, *range(last)]
+    order = [*reversed(range(space)), *reversed(range(space, 2 * space))]
     groups = [[step * space + index for index in order] for step in range(0, length, 2)]
     squares = lax.all_to_all(
         squares, ("tm", "space"), 0, 0, axis_index_groups=groups, tiled=True

time: 21.4 us -> 21.8 us (1.019)
  blocking collectives: 7.36 us -> 7.74 us
    all_to_all x1, blocking collectives: 7.36 us -> 7.74 us  [shards(): lax.all_to_all(squares, ('tm', 'space'), 0, 0, axis_index_groups=groups,...]
where the time goes in v12:
time: 21.8 us; the launch traced here: 21.5 us
  blocking collectives  7.74 us (36%)
  starting transfers between devices  6.5 us (30%)
  waiting for transfers between devices  3.43 us (16%)
  Pallas kernels  3.15 us (14%)
  between operations  0.65 us (3%)
    all_to_all x1, blocking collectives, shards(): lax.all_to_all(squares, ('tm', 'space'), 0, 0, axis_index_groups=groups,...  7.74 us
    ppermute x4, starting transfers between devices, exchange(): return lax.ppermute(value, axis, pairs)  6.5 us
    ppermute x4, waiting for transfers between devices, exchange(): return lax.ppermute(value, axis, pairs)  3.43 us
    pallas_call x1, Pallas kernels, shards(): pl.pallas_call(functools.partial(factor_kernel, length), out_shape=(pltpu...  1.3 us
    pallas_call x1, Pallas kernels, shards(): pl.pallas_call(stack_kernel, out_shape=(pltpu.VMEM((2, cells, lanes), jnp...  0.86 us
    pallas_call x1, Pallas kernels, shards(): pl.pallas_call(functools.partial(join_kernel, entry_count), out_shape=(ja...  0.72 us
  transfers between devices with their start and end apart: 4, of which 3 were waited for; matrix products, arithmetic and copies ran while one was open for 0% of the time, Pallas kernels for 6%

profile of v12, /device:TPU:0, one launch (start us, length us, event | category | flops | bytes accessed | tf_op | source)
XLA Modules:
  0.0 21.5 jit_solution(13642601904059720268)
XLA Ops:
  0.6 0.9 %stack_arrays.1 = (f32[2,64,128]{2,1,0:T(8,128)S(1)}, f32[2,64,128]{2,1,0:T(8,128)S(1)}) custom-call(f32[1,2,64,128]{3,2,1,0:T(8,128)} %forcing_hbm.1, f32[1,2,64,128]{3,2,1,0:T(8,128)} %previous_hbm.1), custom_call_target="tpu_custom_call" | custom-call | flops 4000 | bytes 500000 | tf_op jit(solution)/shard_map/stack_arrays/pallas_call | solution.py:324
  1.5 4.1 %collective-permute-start.1 = (f32[2,64,128]{2,1,0:T(8,128)S(1)}, f32[2,64,128]{2,1,0:T(8,128)S(1)}, u32[]{:S(2)}, u32[]{:S(2)}) collective-permute-start(f32[2,64,128]{2,1,0:T(8,128)S(1)} %get-tuple-element.12.refs_0_), channel_id=1, source_target_pairs={{0,16},{8,24},{16,0},{24,8},{1,17},{9,25},{17,1},{25,9},{2,18},{10... | collective-permute-start | bytes 196616 | tf_op jit(solution)/shard_map/ppermute | solution.py:303
  5.6 1.3 %collective-permute-start.2 = (f32[2,64,128]{2,1,0:T(8,128)S(1)}, f32[2,64,128]{2,1,0:T(8,128)S(1)}, u32[]{:S(2)}, u32[]{:S(2)}) collective-permute-start(f32[2,64,128]{2,1,0:T(8,128)S(1)} %get-tuple-element.13), channel_id=1, source_target_pairs={{0,24},{8,16},{16,8},{24,0},{1,25},{9,17},{17,9},{25,1},{2,26},{10... | collective-permute-start | bytes 196616 | tf_op jit(solution)/shard_map/ppermute | solution.py:303
  6.9 0.2 %collective-permute-start = (f32[2,64,128]{2,1,0:T(8,128)S(1)}, f32[2,64,128]{2,1,0:T(8,128)S(1)}, u32[]{:S(2)}, u32[]{:S(2)}) collective-permute-start(f32[2,64,128]{2,1,0:T(8,128)S(1)} %get-tuple-element.13), channel_id=1, source_target_pairs={{0,8},{8,0},{16,24},{24,16},{1,9},{9,1},{17,25},{25,17},{2,10},{10... | collective-permute-start | bytes 196616 | tf_op jit(solution)/shard_map/ppermute | solution.py:303
  7.2 1.3 %factor_lines.1 = (f32[4,6,64,128]{3,2,1,0:T(8,128)S(1)}, f32[4,3,64,128]{3,2,1,0:T(8,128)S(1)}, f32[64,128]{1,0:T(8,128)S(1)}) custom-call(f32[2,64,128]{2,1,0:T(8,128)} %initial_hbm.1, f32[2,8]{1,0:T(2,128)} %zones_hbm.1, f32[2]{0:T(128)} %drift_hbm.1, s32[1,128]{1,0:T(1,128)} %bitcast.3, s32[1,128]{1,0:T(1,128)} %bitcast.4, s32[64,128]{1,0:T(8,128)} %faces_hbm.1), custom_call_target="tpu_custom_call" | custom-call | flops 4000000 | bytes 3000000 | tf_op jit(solution)/shard_map/factor_lines/pallas_call | solution.py:340
  8.5 0.9 %collective-permute-done.1.refs_2_ = f32[2,64,128]{2,1,0:T(8,128)S(1)} collective-permute-done((f32[2,64,128]{2,1,0:T(8,128)S(1)}, f32[2,64,128]{2,1,0:T(8,128)S(1)}, u32[]{:S(2)}, u32[]{:S(2)}) %collective-permute-start.1) | collective-permute-done | bytes 65568 | tf_op jit(solution)/shard_map/ppermute | solution.py:303
  9.4 2.5 %collective-permute-done.2.refs_3_ = f32[2,64,128]{2,1,0:T(8,128)S(1)} collective-permute-done((f32[2,64,128]{2,1,0:T(8,128)S(1)}, f32[2,64,128]{2,1,0:T(8,128)S(1)}, u32[]{:S(2)}, u32[]{:S(2)}) %collective-permute-start.2) | collective-permute-done | bytes 65568 | tf_op jit(solution)/shard_map/ppermute | solution.py:303
  11.8 0.1 collective-permute-done.refs_1_
  11.9 0.3 %solve_lines.1 = (f32[64,128]{1,0:T(8,128)S(1)}, f32[64,128]{1,0:T(8,128)S(1)}, f32[16,1,128]{2,1,0:T(1,128)S(1)}) custom-call(f32[2,64,128]{2,1,0:T(8,128)S(1)} %get-tuple-element.12.refs_0_, f32[2,64,128]{2,1,0:T(8,128)S(1)} %collective-permute-done.refs_1_, f32[2,64,128]{2,1,0:T(8,128)S(1)} %collective-permute-done.1.refs_2_, ...), custom_call_target="tpu_custom_call" | custom-call | flops 4000000 | bytes 3000000 | tf_op jit(solution)/shard_map/solve_lines/pallas_call | solution.py:361
  12.2 0.8 %collective-permute-start.3 = (f32[64,128]{1,0:T(8,128)S(1)}, f32[64,128]{1,0:T(8,128)S(1)}, u32[]{:S(2)}, u32[]{:S(2)}) collective-permute-start(f32[64,128]{1,0:T(8,128)S(1)} %get-tuple-element.18), channel_id=1, source_target_pairs={{0,8},{8,0},{16,24},{24,16},{1,9},{9,1},{17,25},{25,17},{2,10},{10... | collective-permute-start | bytes 98312 | tf_op jit(solution)/shard_map/ppermute | solution.py:303
  13.0 7.7 %all_to_all.5.squares_ref = f32[16,1,128]{2,1,0:T(1,128)S(1)} all-to-all(f32[16,1,128]{2,1,0:T(1,128)S(1)} %get-tuple-element.19), channel_id=1, replica_groups={{7,6,5,4,3,2,1,0,15,14,13,12,11,10,9,8},{23,22,21,20,19,18,17,16,31,30,..., dimensions={0} | all-to-all | bytes 16384 | tf_op jit(solution)/shard_map/all_to_all | solution.py:377
  20.8 0.0 collective-permute-done.3.got_ref
  20.8 0.7 %join_species.1 = (f32[1,2,64,128]{3,2,1,0:T(8,128)}, f32[1,1]{1,0:T(1,128)}) custom-call(f32[64,128]{1,0:T(8,128)S(1)} %get-tuple-element.17.own_ref, f32[64,128]{1,0:T(8,128)S(1)} %collective-permute-done.3.got_ref, f32[16,1,128]{2,1,0:T(1,128)S(1)} %all_to_all.5.squares_ref), custom_call_target="tpu_custom_call" | custom-call | flops 4000 | bytes 100000 | tf_op jit(solution)/shard_map/join_species/pallas_call | solution.py:381
Async XLA Ops:
  1.5 7.9 %collective-permute-start.1 = (f32[2,64,128]{2,1,0:T(8,128)S(1)}, f32[2,64,128]{2,1,0:T(8,128)S(1)}, u32[]{:S(2)}, u32[]{:S(2)}) collective-permute-start(f32[2,64,128]{2,1,0:T(8,128)S(1)} %get-tuple-element.12.refs_0_), channel_id=1, source_target_pairs={{0,16},{8,24},{16,0},{24,8},{1,17},{9,25},{17,1},{25,9},{2,18},{10... | collective-permute-start | bytes 196616 | tf_op jit(solution)/shard_map/ppermute | solution.py:303
  5.6 6.2 %collective-permute-start.2 = (f32[2,64,128]{2,1,0:T(8,128)S(1)}, f32[2,64,128]{2,1,0:T(8,128)S(1)}, u32[]{:S(2)}, u32[]{:S(2)}) collective-permute-start(f32[2,64,128]{2,1,0:T(8,128)S(1)} %get-tuple-element.13), channel_id=1, source_target_pairs={{0,24},{8,16},{16,8},{24,0},{1,25},{9,17},{17,9},{25,1},{2,26},{10... | collective-permute-start | bytes 196616 | tf_op jit(solution)/shard_map/ppermute | solution.py:303
  6.9 5.0 %collective-permute-start = (f32[2,64,128]{2,1,0:T(8,128)S(1)}, f32[2,64,128]{2,1,0:T(8,128)S(1)}, u32[]{:S(2)}, u32[]{:S(2)}) collective-permute-start(f32[2,64,128]{2,1,0:T(8,128)S(1)} %get-tuple-element.13), channel_id=1, source_target_pairs={{0,8},{8,0},{16,24},{24,16},{1,9},{9,1},{17,25},{25,17},{2,10},{10... | collective-permute-start | bytes 196616 | tf_op jit(solution)/shard_map/ppermute | solution.py:303
  12.2 8.6 %collective-permute-start.3 = (f32[64,128]{1,0:T(8,128)S(1)}, f32[64,128]{1,0:T(8,128)S(1)}, u32[]{:S(2)}, u32[]{:S(2)}) collective-permute-start(f32[64,128]{1,0:T(8,128)S(1)} %get-tuple-element.18), channel_id=1, source_target_pairs={{0,8},{8,0},{16,24},{24,16},{1,9},{9,1},{17,25},{25,17},{2,10},{10... | collective-permute-start | bytes 98312 | tf_op jit(solution)/shard_map/ppermute | solution.py:303

commit v13 on v10

--- a/solution.py
+++ b/solution.py
@@ -363,7 +363,7 @@
         out_shape=(
             pltpu.VMEM((cells, lanes), jnp.float32),
             pltpu.VMEM((cells, lanes), jnp.float32),
-            pltpu.VMEM((2 * space, 1, lanes), jnp.float32),
+            pltpu.VMEM((1, lanes), jnp.float32),
         ),
         in_specs=[whole] * (length + 3),
         out_specs=[whole] * 3,
@@ -375,9 +375,7 @@
     last = 2 * space - 1
     order = [last, *range(2, last, 2), *range(3, last, 2), 1, 0]
     groups = [[step * space + index for index in order] for step in range(0, length, 2)]
-    squares = lax.all_to_all(
-        squares, ("tm", "space"), 0, 0, axis_index_groups=groups, tiled=True
-    )
+    squares = lax.all_gather(squares, ("tm", "space"), axis_index_groups=groups, tiled=True)
     entry_count = length * space * forcing.shape[1] * cells * lanes
     new_iterate, norm = pl.pallas_call(
         functools.partial(join_kernel, entry_count),

time: 21.3 us -> 43.1 us (2.02)
  the two profiles are of different devices: /device:TPU:0 before, /device:TPU:24 now
where the time goes in v13:
time: 43.1 us; the launch traced here: 42.8 us
  blocking collectives  30.8 us (71%)
  starting transfers between devices  4.76 us (11%)
  waiting for transfers between devices  3.5 us (8%)
  Pallas kernels  3.13 us (7%)
  between operations  0.65 us (2%)
    all_gather x1, blocking collectives, shards(): lax.all_gather(squares, ('tm', 'space'), axis_index_groups=groups, tiled=...  30.8 us
    ppermute x4, starting transfers between devices, exchange(): return lax.ppermute(value, axis, pairs)  4.76 us
    ppermute x4, waiting for transfers between devices, exchange(): return lax.ppermute(value, axis, pairs)  3.5 us
    pallas_call x1, Pallas kernels, shards(): pl.pallas_call(functools.partial(factor_kernel, length), out_shape=(pltpu...  1.3 us
  transfers between devices with their start and end apart: 4, of which 2 were waited for; matrix products, arithmetic and copies ran while one was open for 0% of the time, Pallas kernels for 3%

profile of v13, /device:TPU:24, one launch (start us, length us, event | category | flops | bytes accessed | tf_op | source)
XLA Modules:
  0.0 42.8 jit_solution(7415419052702094245)
XLA Ops:
  0.6 0.9 %stack_arrays.1 = (f32[2,64,128]{2,1,0:T(8,128)S(1)}, f32[2,64,128]{2,1,0:T(8,128)S(1)}) custom-call(f32[1,2,64,128]{3,2,1,0:T(8,128)} %forcing_hbm.1, f32[1,2,64,128]{3,2,1,0:T(8,128)} %previous_hbm.1), custom_call_target="tpu_custom_call" | custom-call | flops 4000 | bytes 500000 | tf_op jit(solution)/shard_map/stack_arrays/pallas_call | solution.py:324
  1.5 0.4 collective-permute-start.1
  1.9 2.5 %collective-permute-start.2 = (f32[2,64,128]{2,1,0:T(8,128)S(1)}, f32[2,64,128]{2,1,0:T(8,128)S(1)}, u32[]{:S(2)}, u32[]{:S(2)}) collective-permute-start(f32[2,64,128]{2,1,0:T(8,128)S(1)} %get-tuple-element.13), channel_id=1, source_target_pairs={{0,24},{8,16},{16,8},{24,0},{1,25},{9,17},{17,9},{25,1},{2,26},{10... | collective-permute-start | bytes 196616 | tf_op jit(solution)/shard_map/ppermute | solution.py:303
  4.4 0.7 %collective-permute-start = (f32[2,64,128]{2,1,0:T(8,128)S(1)}, f32[2,64,128]{2,1,0:T(8,128)S(1)}, u32[]{:S(2)}, u32[]{:S(2)}) collective-permute-start(f32[2,64,128]{2,1,0:T(8,128)S(1)} %get-tuple-element.13), channel_id=1, source_target_pairs={{0,8},{8,0},{16,24},{24,16},{1,9},{9,1},{17,25},{25,17},{2,10},{10... | collective-permute-start | bytes 196616 | tf_op jit(solution)/shard_map/ppermute | solution.py:303
  5.0 1.3 %factor_lines.1 = (f32[4,6,64,128]{3,2,1,0:T(8,128)S(1)}, f32[4,3,64,128]{3,2,1,0:T(8,128)S(1)}, f32[64,128]{1,0:T(8,128)S(1)}) custom-call(f32[2,64,128]{2,1,0:T(8,128)} %initial_hbm.1, f32[2,8]{1,0:T(2,128)} %zones_hbm.1, f32[2]{0:T(128)} %drift_hbm.1, s32[1,128]{1,0:T(1,128)} %bitcast.7, s32[1,128]{1,0:T(1,128)} %bitcast.8, s32[64,128]{1,0:T(8,128)} %faces_hbm.1), custom_call_target="tpu_custom_call" | custom-call | flops 4000000 | bytes 3000000 | tf_op jit(solution)/shard_map/factor_lines/pallas_call | solution.py:340
  6.4 3.1 %collective-permute-done.1.refs_2_ = f32[2,64,128]{2,1,0:T(8,128)S(1)} collective-permute-done((f32[2,64,128]{2,1,0:T(8,128)S(1)}, f32[2,64,128]{2,1,0:T(8,128)S(1)}, u32[]{:S(2)}, u32[]{:S(2)}) %collective-permute-start.1) | collective-permute-done | bytes 65568 | tf_op jit(solution)/shard_map/ppermute | solution.py:303
  9.4 0.0 collective-permute-done.2.refs_3_
  9.4 0.4 collective-permute-done.refs_1_
  9.9 0.3 solve_lines.1
  10.1 1.2 %collective-permute-start.3 = (f32[64,128]{1,0:T(8,128)S(1)}, f32[64,128]{1,0:T(8,128)S(1)}, u32[]{:S(2)}, u32[]{:S(2)}) collective-permute-start(f32[64,128]{1,0:T(8,128)S(1)} %get-tuple-element.18), channel_id=1, source_target_pairs={{0,8},{8,0},{16,24},{24,16},{1,9},{9,1},{17,25},{25,17},{2,10},{10... | collective-permute-start | bytes 98312 | tf_op jit(solution)/shard_map/ppermute | solution.py:303
  11.3 30.8 %all-gather = f32[16,1,128]{2,1,0:T(1,128)S(1)} all-gather(f32[1,1,128]{2,1,0:T(1,128)S(1)} %bitcast.6), channel_id=1, replica_groups={{15,2,4,6,8,10,12,14,3,5,7,9,11,13,1,0},{31,18,20,22,24,26,28,30,19,21,..., dimensions={0}, use_global_device_ids=true | all-gather | bytes 8704 | tf_op jit(solution)/shard_map/all_gather | solution.py:378
  42.1 0.0 collective-permute-done.3.got_ref
  42.1 0.7 %join_species.1 = (f32[1,2,64,128]{3,2,1,0:T(8,128)}, f32[1,1]{1,0:T(1,128)}) custom-call(f32[64,128]{1,0:T(8,128)S(1)} %get-tuple-element.17.own_ref, f32[64,128]{1,0:T(8,128)S(1)} %collective-permute-done.3.got_ref, f32[16,128]{1,0:T(8,128)S(1)} %bitcast.5), custom_call_target="tpu_custom_call" | custom-call | flops 4000 | bytes 100000 | tf_op jit(solution)/shard_map/join_species/pallas_call | solution.py:380
Async XLA Ops:
  1.5 7.9 %collective-permute-start.1 = (f32[2,64,128]{2,1,0:T(8,128)S(1)}, f32[2,64,128]{2,1,0:T(8,128)S(1)}, u32[]{:S(2)}, u32[]{:S(2)}) collective-permute-start(f32[2,64,128]{2,1,0:T(8,128)S(1)} %get-tuple-element.12.refs_0_), channel_id=1, source_target_pairs={{0,16},{8,24},{16,0},{24,8},{1,17},{9,25},{17,1},{25,9},{2,18},{10... | collective-permute-start | bytes 196616 | tf_op jit(solution)/shard_map/ppermute | solution.py:303
  1.9 7.5 %collective-permute-start.2 = (f32[2,64,128]{2,1,0:T(8,128)S(1)}, f32[2,64,128]{2,1,0:T(8,128)S(1)}, u32[]{:S(2)}, u32[]{:S(2)}) collective-permute-start(f32[2,64,128]{2,1,0:T(8,128)S(1)} %get-tuple-element.13), channel_id=1, source_target_pairs={{0,24},{8,16},{16,8},{24,0},{1,25},{9,17},{17,9},{25,1},{2,26},{10... | collective-permute-start | bytes 196616 | tf_op jit(solution)/shard_map/ppermute | solution.py:303
  4.4 5.5 %collective-permute-start = (f32[2,64,128]{2,1,0:T(8,128)S(1)}, f32[2,64,128]{2,1,0:T(8,128)S(1)}, u32[]{:S(2)}, u32[]{:S(2)}) collective-permute-start(f32[2,64,128]{2,1,0:T(8,128)S(1)} %get-tuple-element.13), channel_id=1, source_target_pairs={{0,8},{8,0},{16,24},{24,16},{1,9},{9,1},{17,25},{25,17},{2,10},{10... | collective-permute-start | bytes 196616 | tf_op jit(solution)/shard_map/ppermute | solution.py:303
  10.1 32.0 %collective-permute-start.3 = (f32[64,128]{1,0:T(8,128)S(1)}, f32[64,128]{1,0:T(8,128)S(1)}, u32[]{:S(2)}, u32[]{:S(2)}) collective-permute-start(f32[64,128]{1,0:T(8,128)S(1)} %get-tuple-element.18), channel_id=1, source_target_pairs={{0,8},{8,0},{16,24},{24,16},{1,9},{9,1},{17,25},{25,17},{2,10},{10... | collective-permute-start | bytes 98312 | tf_op jit(solution)/shard_map/ppermute | solution.py:303

commit v14 on v12

--- a/solution.py
+++ b/solution.py
@@ -100,21 +100,82 @@
     return copies
 
 
-def stack_kernel(forcing_hbm, previous_hbm, mine_ref, other_ref, sems):
-    species = lax.axis_index("tm") % 2
+def line_operator(cells, lanes, species, zones_ref, drift_ref, zone_ref, flag_ref, faces_ref):
+    zone = zone_ref[...]
+    diffusion = jnp.zeros(zone.shape, jnp.float32)
+    for index in range(zones_ref.shape[1]):
+        diffusion = jnp.where(zone == index, zones_ref[species, index], diffusion)
+    drift = drift_ref[species]
+    faces = faces_ref[...].astype(jnp.float32)
+    row = lax.broadcasted_iota(jnp.int32, (cells, lanes), 0)
+    link_above = jnp.where(row == cells - 1, 0.0, faces)
+    link_below = jnp.where(row == 0, 0.0, roll_down(faces, 1))
+    ground = jnp.where(row == 0, flag_ref[...].astype(jnp.float32), 0.0)
+    below = -(diffusion + drift) * link_below
+    above = -diffusion * link_above
+    centre = diffusion * (link_below + link_above) + drift + 2.0 * diffusion * ground
+    return (below, centre, above)
+
+
+def stack_kernel(
+    length,
+    forcing_hbm,
+    previous_hbm,
+    zones_hbm,
+    drift_hbm,
+    zone_hbm,
+    flag_hbm,
+    faces_hbm,
+    mine_ref,
+    mine_before_ref,
+    other_ref,
+    other_before_ref,
+    zones_ref,
+    drift_ref,
+    zone_ref,
+    flag_ref,
+    faces_ref,
+    sems,
+):
+    me = lax.axis_index("tm")
+    species = me % 2
     pairs = (
-        (forcing_hbm.at[0, species], mine_ref.at[0]),
-        (previous_hbm.at[0, species], mine_ref.at[1]),
-        (forcing_hbm.at[0, 1 - species], other_ref.at[0]),
-        (previous_hbm.at[0, 1 - species], other_ref.at[1]),
+        (forcing_hbm.at[0, species], mine_ref),
+        (previous_hbm.at[0, species], mine_before_ref),
+        (forcing_hbm.at[0, 1 - species], other_ref),
+        (previous_hbm.at[0, 1 - species], other_before_ref),
+        (zones_hbm, zones_ref),
+        (drift_hbm, drift_ref),
+        (zone_hbm, zone_ref),
+        (flag_hbm, flag_ref),
+        (faces_hbm, faces_ref),
     )
     for copy in start_all(pairs, sems):
         copy.wait()
+
+    @pl.when(me == length - 1)
+    def shift_load():
+        cells, lanes = faces_ref.shape
+        for part, before in ((species, mine_before_ref[...]), (1 - species, other_before_ref[...])):
+            below, centre, above = line_operator(
+                cells, lanes, part, zones_ref, drift_ref, zone_ref, flag_ref, faces_ref
+            )
+            applied = (
+                before
+                + centre * before
+                + below * roll_down(before, 1)
+                + above * roll_up(before, 1)
+            )
+            if part is species:
+                mine_ref[...] = mine_ref[...] - applied
+            else:
+                other_ref[...] = other_ref[...] - applied
 
 
 def factor_kernel(
     length,
     initial_hbm,
+    previous_hbm,
     zones_hbm,
     drift_hbm,
     zone_hbm,
@@ -123,6 +184,7 @@
     near_ref,
     far_ref,
     initial_ref,
+    other_before_ref,
     zones_ref,
     drift_ref,
     zone_ref,
@@ -138,23 +200,14 @@
         (flag_hbm, flag_ref),
         (faces_hbm, faces_ref),
         (initial_hbm.at[species], initial_ref),
+        (previous_hbm.at[0, 1 - species], other_before_ref),
     )
     for copy in start_all(pairs, sems):
         copy.wait()
-    zone = zone_ref[...]
-    diffusion = jnp.zeros(zone.shape, jnp.float32)
-    for index in range(zones_ref.shape[1]):
-        diffusion = jnp.where(zone == index, zones_ref[species, index], diffusion)
-    drift = drift_ref[species]
     cells, lanes = faces_ref.shape
-    faces = faces_ref[...].astype(jnp.float32)
-    row = lax.broadcasted_iota(jnp.int32, (cells, lanes), 0)
-    link_above = jnp.where(row == cells - 1, 0.0, faces)
-    link_below = jnp.where(row == 0, 0.0, roll_down(faces, 1))
-    ground = jnp.where(row == 0, flag_ref[...].astype(jnp.float32), 0.0)
-    below = -(diffusion + drift) * link_below
-    above = -diffusion * link_above
-    centre = diffusion * (link_below + link_above) + drift + 2.0 * diffusion * ground
+    below, centre, above = line_operator(
+        cells, lanes, species, zones_ref, drift_ref, zone_ref, flag_ref, faces_ref
+    )
     plane = 0
     for unused, shift in frequencies(length):
         parts = len(shift)
@@ -207,14 +260,12 @@
 
 
 def sweep_kernel(length, *refs):
-    stacks = refs[:length]
-    initial_ref, near_ref, far_ref, own_ref, give_ref, sum_ref = refs[length:]
+    initial_ref, near_ref, far_ref, own_ref, give_ref = refs[length:]
     cells, lanes = initial_ref.shape
     log_alpha = math.log(alpha_corner)
     me = lax.axis_index("tm")
-    loads = in_order(me, [ref[0] for ref in stacks])
-    befores = in_order(me, [ref[1] for ref in stacks])
-    loads[0] = loads[0] + (initial_ref[...] - alpha_corner * befores[length - 1])
+    loads = in_order(me, [ref[...] for ref in refs[:length]])
+    loads[0] = loads[0] + initial_ref[...]
     scaled = [math.exp(log_alpha * n / length) * load for n, load in enumerate(loads)]
     spectrum = []
     plane = 0
@@ -256,7 +307,6 @@
             carry = value
         spectrum.append((j, parts, solved))
         plane += parts
-    total = jnp.zeros((tile, lanes), jnp.float32)
     for block in range(cells // tile):
         rows = slice(block * tile, (block + 1) * tile)
         steps = []
@@ -269,8 +319,6 @@
                     fresh = weighted(fresh, -parts * weights[1], solved[block][1])
             fresh = fresh * (math.exp(-log_alpha * n / length) / length)
             steps.append(fresh)
-            change = fresh - befores[n][rows]
-            total = total + change * change
         own = steps[0]
         give = steps[1]
         for n in range(1, length):
@@ -278,18 +326,47 @@
             give = jnp.where(me == n, steps[n ^ 1], give)
         own_ref[rows] = own
         give_ref[rows] = give
+
+
+def change_kernel(length, own_ref, give_ref, mine_before_ref, beside_before_ref, sum_ref):
+    cells, lanes = own_ref.shape
+    me = lax.axis_index("tm")
+    total = jnp.zeros((tile, lanes), jnp.float32)
+    for block in range(cells // tile):
+        rows = slice(block * tile, (block + 1) * tile)
+        own_before = jnp.where(me == length - 1, 0.0, mine_before_ref[rows])
+        give_before = jnp.where(me == (length - 1) ^ 1, 0.0, beside_before_ref[rows])
+        own_change = own_ref[rows] - own_before
+        give_change = give_ref[rows] - give_before
+        total = total + own_change * own_change + give_change * give_change
     sum_ref[...] = jnp.broadcast_to(jnp.sum(total, axis=0, keepdims=True), sum_ref.shape)
 
 
 def join_kernel(
-    entry_count, own_ref, got_ref, squares_ref, new_hbm, norm_hbm, norm_ref, sems
+    length,
+    entry_count,
+    own_ref,
+    got_ref,
+    mine_before_ref,
+    other_before_ref,
+    squares_ref,
+    new_hbm,
+    norm_hbm,
+    mine_ref,
+    other_ref,
+    norm_ref,
+    sems,
 ):
-    species = lax.axis_index("tm") % 2
+    me = lax.axis_index("tm")
+    species = me % 2
     copies = (
-        pltpu.make_async_copy(own_ref, new_hbm.at[0, species], sems.at[0]),
-        pltpu.make_async_copy(got_ref, new_hbm.at[0, 1 - species], sems.at[1]),
+        pltpu.make_async_copy(mine_ref, new_hbm.at[0, species], sems.at[0]),
+        pltpu.make_async_copy(other_ref, new_hbm.at[0, 1 - species], sems.at[1]),
         pltpu.make_async_copy(norm_ref, norm_hbm, sems.at[2]),
     )
+    last = me == length - 1
+    mine_ref[...] = own_ref[...] + jnp.where(last, mine_before_ref[...], 0.0)
+    other_ref[...] = got_ref[...] + jnp.where(last, other_before_ref[...], 0.0)
     copies[0].start()
     copies[1].start()
     norm_ref[0, 0] = jnp.sqrt(jnp.sum(squares_ref[...]) / entry_count)
@@ -319,78 +396,118 @@
     whole = pl.BlockSpec(memory_space=pltpu.VMEM)
     outside = pl.BlockSpec(memory_space=pltpu.HBM)
     count = planes(length)
+    everyone = length * space
     params = pltpu.CompilerParams(vmem_limit_bytes=40 * 1024 * 1024)
     alone = pltpu.CompilerParams(vmem_limit_bytes=56 * 1024 * 1024)
-    mine, other = pl.pallas_call(
-        stack_kernel,
+    mine, mine_before, other = pl.pallas_call(
+        functools.partial(stack_kernel, length),
         out_shape=(
-            pltpu.VMEM((2, cells, lanes), jnp.float32),
-            pltpu.VMEM((2, cells, lanes), jnp.float32),
+            pltpu.VMEM((cells, lanes), jnp.float32),
+            pltpu.VMEM((cells, lanes), jnp.float32),
+            pltpu.VMEM((cells, lanes), jnp.float32),
         ),
-        in_specs=[outside] * 2,
-        out_specs=[whole] * 2,
-        scratch_shapes=[pltpu.SemaphoreType.DMA((4,))],
+        in_specs=[outside] * 7,
+        out_specs=[whole] * 3,
+        scratch_shapes=[
+            pltpu.VMEM((cells, lanes), jnp.float32),
+            pltpu.SMEM(zone_diffusion.shape, jnp.float32),
+            pltpu.SMEM(drift_rate.shape, jnp.float32),
+            pltpu.VMEM((1, lanes), jnp.int32),
+            pltpu.VMEM((1, lanes), jnp.int32),
+            pltpu.VMEM((cells, lanes), jnp.int32),
+            pltpu.SemaphoreType.DMA((9,)),
+        ],
         compiler_params=alone,
         cost_estimate=pl.CostEstimate(flops=4000, bytes_accessed=500000, transcendentals=0),
         name="stack_arrays",
-    )(forcing, previous)
-    stacks = [mine]
+    )(
+        forcing,
+        previous,
+        zone_diffusion,
+        drift_rate,
+        column_zone[None],
+        bottom_flag[None],
+        open_faces,
+    )
+    loads = [mine]
     for bits in range(1, length):
-        stacks.append(exchange(other if bits % 2 else mine, "tm", bits))
-    near, far, initial = pl.pallas_call(
+        loads.append(exchange(other if bits % 2 else mine, "tm", bits))
+    near, far, initial, other_before = pl.pallas_call(
         functools.partial(factor_kernel, length),
         out_shape=(
             pltpu.VMEM((count, 2 * near_steps, cells, lanes), jnp.float32),
             pltpu.VMEM((count, 3, cells, lanes), jnp.float32),
             pltpu.VMEM((cells, lanes), jnp.float32),
+            pltpu.VMEM((cells, lanes), jnp.float32),
         ),
-        in_specs=[outside] * 6,
-        out_specs=[whole] * 3,
+        in_specs=[outside] * 7,
+        out_specs=[whole] * 4,
         scratch_shapes=[
             pltpu.SMEM(zone_diffusion.shape, jnp.float32),
             pltpu.SMEM(drift_rate.shape, jnp.float32),
             pltpu.VMEM((1, lanes), jnp.int32),
             pltpu.VMEM((1, lanes), jnp.int32),
             pltpu.VMEM((cells, lanes), jnp.int32),
-            pltpu.SemaphoreType.DMA((6,)),
+            pltpu.SemaphoreType.DMA((7,)),
         ],
         compiler_params=alone,
         cost_estimate=pl.CostEstimate(flops=4000000, bytes_accessed=3000000, transcendentals=0),
         name="factor_lines",
-    )(initial_state, zone_diffusion, drift_rate, column_zone[None], bottom_flag[None], open_faces)
-    own, give, squares = pl.pallas_call(
+    )(
+        initial_state,
+        previous,
+        zone_diffusion,
+        drift_rate,
+        column_zone[None],
+        bottom_flag[None],
+        open_faces,
+    )
+    own, give = pl.pallas_call(
         functools.partial(sweep_kernel, length),
         out_shape=(
             pltpu.VMEM((cells, lanes), jnp.float32),
             pltpu.VMEM((cells, lanes), jnp.float32),
-            pltpu.VMEM((2 * space, 1, lanes), jnp.float32),
         ),
         in_specs=[whole] * (length + 3),
-        out_specs=[whole] * 3,
+        out_specs=[whole] * 2,
         compiler_params=params,
         cost_estimate=pl.CostEstimate(flops=4000000, bytes_accessed=3000000, transcendentals=0),
         name="solve_lines",
-    )(*stacks, initial, near, far)
+    )(*loads, initial, near, far)
     got = exchange(give, "tm", 1)
-    order = [*reversed(range(space)), *reversed(range(space, 2 * space))]
-    groups = [[step * space + index for index in order] for step in range(0, length, 2)]
+    squares = pl.pallas_call(
+        functools.partial(change_kernel, length),
+        out_shape=pltpu.VMEM((everyone, 1, lanes), jnp.float32),
+        in_specs=[whole] * 4,
+        out_specs=whole,
+        compiler_params=params,
+        cost_estimate=pl.CostEstimate(flops=40000, bytes_accessed=200000, transcendentals=0),
+        name="change_squares",
+    )(own, give, mine_before, exchange(other_before, "tm", 1))
+    first = length // 2 * space + space - 1
+    order = [first] + [index for index in reversed(range(everyone)) if index != first]
     squares = lax.all_to_all(
-        squares, ("tm", "space"), 0, 0, axis_index_groups=groups, tiled=True
-    )
-    entry_count = length * space * forcing.shape[1] * cells * lanes
+        squares, ("tm", "space"), 0, 0, axis_index_groups=[order], tiled=True
+    )
+    entry_count = everyone * forcing.shape[1] * cells * lanes
     new_iterate, norm = pl.pallas_call(
-        functools.partial(join_kernel, entry_count),
+        functools.partial(join_kernel, length, entry_count),
         out_shape=(
             jax.ShapeDtypeStruct(forcing.shape, jnp.float32),
             jax.ShapeDtypeStruct((1, 1), jnp.float32),
         ),
-        in_specs=[whole] * 3,
+        in_specs=[whole] * 5,
         out_specs=(outside, outside),
-        scratch_shapes=[pltpu.SMEM((1, 1), jnp.float32), pltpu.SemaphoreType.DMA((3,))],
+        scratch_shapes=[
+            pltpu.VMEM((cells, lanes), jnp.float32),
+            pltpu.VMEM((cells, lanes), jnp.float32),
+            pltpu.SMEM((1, 1), jnp.float32),
+            pltpu.SemaphoreType.DMA((3,)),
+        ],
         compiler_params=params,
         cost_estimate=pl.CostEstimate(flops=4000, bytes_accessed=100000, transcendentals=0),
         name="join_species",
-    )(own, got, squares)
+    )(own, got, mine_before, other_before, squares)
     return (new_iterate, norm[0, 0])
 
 

time: 21.8 us -> 26 us (1.19)
  blocking collectives: 7.74 us -> 12.3 us
  waiting for transfers between devices: 3.43 us -> 1.87 us
  starting transfers between devices: 6.5 us -> 7.61 us
    all_to_all x1, blocking collectives: 7.74 us -> 12.3 us  [shards(): lax.all_to_all(squares, ('tm', 'space'), 0, 0, axis_index_groups=[order],...]
    ppermute x4 -> x5, waiting for transfers between devices: 3.43 us -> 1.87 us  [exchange(): return lax.ppermute(value, axis, pairs)]
    ppermute x4 -> x5, starting transfers between devices: 6.5 us -> 7.61 us  [exchange(): return lax.ppermute(value, axis, pairs)]
    pallas_call x2 -> x3, Pallas kernels: 1.57 us -> 1.72 us  [the longest x1 0.95 us: shards(): pl.pallas_call(functools.partial(stack_kernel, length), out_shape=(pltpu....]
  transfers between devices with their start and end apart: 4 -> 5, of which waited for: 3 -> 3; matrix products, arithmetic and copies ran while one was open for 0% -> 0% of each run, Pallas kernels for 6% -> 6%
where the time goes in v14:
time: 26 us; the launch traced here: 25.8 us
  blocking collectives  12.3 us (47%)
  starting transfers between devices  7.61 us (29%)
  Pallas kernels  3.27 us (13%)
  waiting for transfers between devices  1.87 us (7%)
  between operations  0.66 us (3%)
    all_to_all x1, blocking collectives, shards(): lax.all_to_all(squares, ('tm', 'space'), 0, 0, axis_index_groups=[order],...  12.3 us
    ppermute x5, starting transfers between devices, exchange(): return lax.ppermute(value, axis, pairs)  7.61 us
    ppermute x5, waiting for transfers between devices, exchange(): return lax.ppermute(value, axis, pairs)  1.87 us
    pallas_call x1, Pallas kernels, shards(): pl.pallas_call(functools.partial(factor_kernel, length), out_shape=(pltpu...  1.33 us
    pallas_call x1, Pallas kernels, shards(): pl.pallas_call(functools.partial(stack_kernel, length), out_shape=(pltpu....  0.95 us
    pallas_call x1, Pallas kernels, shards(): pl.pallas_call(functools.partial(join_kernel, length, entry_count), out_s...  0.73 us
  transfers between devices with their start and end apart: 5, of which 3 were waited for; matrix products, arithmetic and copies ran while one was open for 0% of the time, Pallas kernels for 6%

profile of v14, /device:TPU:0, one launch (start us, length us, event | category | flops | bytes accessed | tf_op | source)
XLA Modules:
  0.0 25.8 jit_solution(17363767857770421943)
XLA Ops:
  0.6 1.0 %stack_arrays.1 = (f32[64,128]{1,0:T(8,128)S(1)}, f32[64,128]{1,0:T(8,128)S(1)}, f32[64,128]{1,0:T(8,128)S(1)}) custom-call(f32[1,2,64,128]{3,2,1,0:T(8,128)} %forcing_hbm.1, f32[1,2,64,128]{3,2,1,0:T(8,128)} %previous_hbm.3, f32[2,8]{1,0:T(2,128)} %zones_hbm.3, f32[2]{0:T(128)} %drift_hbm.3, s32[1,128]{1,0:T(1,128)} %bitcast.3, s32[1,128]{1,0:T(1,128)} %bitcast.5, ...), custom_call_target="tpu_custom_call" | custom-call | flops 4000 | bytes 500000 | tf_op jit(solution)/shard_map/stack_arrays/pallas_call | solution.py:402
  1.6 4.1 %collective-permute-start.1 = (f32[64,128]{1,0:T(8,128)S(1)}, f32[64,128]{1,0:T(8,128)S(1)}, u32[]{:S(2)}, u32[]{:S(2)}) collective-permute-start(f32[64,128]{1,0:T(8,128)S(1)} %get-tuple-element.13.refs_0_), channel_id=1, source_target_pairs={{0,16},{8,24},{16,0},{24,8},{1,17},{9,25},{17,1},{25,9},{2,18},{10... | collective-permute-start | bytes 98312 | tf_op jit(solution)/shard_map/ppermute | solution.py:380
  5.7 1.3 %collective-permute-start.2 = (f32[64,128]{1,0:T(8,128)S(1)}, f32[64,128]{1,0:T(8,128)S(1)}, u32[]{:S(2)}, u32[]{:S(2)}) collective-permute-start(f32[64,128]{1,0:T(8,128)S(1)} %get-tuple-element.14), channel_id=1, source_target_pairs={{0,24},{8,16},{16,8},{24,0},{1,25},{9,17},{17,9},{25,1},{2,26},{10... | collective-permute-start | bytes 98312 | tf_op jit(solution)/shard_map/ppermute | solution.py:380
  7.0 0.3 %collective-permute-start = (f32[64,128]{1,0:T(8,128)S(1)}, f32[64,128]{1,0:T(8,128)S(1)}, u32[]{:S(2)}, u32[]{:S(2)}) collective-permute-start(f32[64,128]{1,0:T(8,128)S(1)} %get-tuple-element.14), channel_id=1, source_target_pairs={{0,8},{8,0},{16,24},{24,16},{1,9},{9,1},{17,25},{25,17},{2,10},{10... | collective-permute-start | bytes 98312 | tf_op jit(solution)/shard_map/ppermute | solution.py:380
  7.3 1.3 %factor_lines.1 = (f32[4,6,64,128]{3,2,1,0:T(8,128)S(1)}, f32[4,3,64,128]{3,2,1,0:T(8,128)S(1)}, f32[64,128]{1,0:T(8,128)S(1)}, f32[64,128]{1,0:T(8,128)S(1)}) custom-call(f32[2,64,128]{2,1,0:T(8,128)} %initial_hbm.1, f32[1,2,64,128]{3,2,1,0:T(8,128)} %previous_hbm.3, f32[2,8]{1,0:T(2,128)} %zones_hbm.3, f32[2]{0:T(128)} %drift_hbm.3, s32[1,128]{1,0:T(1,128)} %bitcast.4, ...), custom_call_target="tpu_custom_call" | custom-call | flops 4000000 | bytes 3000000 | tf_op jit(solution)/shard_map/factor_lines/pallas_call | solution.py:435
  8.7 1.8 %collective-permute-start.4 = (f32[64,128]{1,0:T(8,128)S(1)}, f32[64,128]{1,0:T(8,128)S(1)}, u32[]{:S(2)}, u32[]{:S(2)}) collective-permute-start(f32[64,128]{1,0:T(8,128)S(1)} %get-tuple-element.21.other_before_ref), channel_id=1, source_target_pairs={{0,8},{8,0},{16,24},{24,16},{1,9},{9,1},{17,25},{25,17},{2,10},{10... | collective-permute-start | bytes 98312 | tf_op jit(solution)/shard_map/ppermute | solution.py:380
  10.5 0.0 collective-permute-done.1.refs_2_
  10.5 1.0 %collective-permute-done.2.refs_3_ = f32[64,128]{1,0:T(8,128)S(1)} collective-permute-done((f32[64,128]{1,0:T(8,128)S(1)}, f32[64,128]{1,0:T(8,128)S(1)}, u32[]{:S(2)}, u32[]{:S(2)}) %collective-permute-start.2) | collective-permute-done | bytes 32800 | tf_op jit(solution)/shard_map/ppermute | solution.py:380
  11.5 0.1 collective-permute-done.refs_1_
  11.6 0.2 solve_lines.1
  11.9 0.1 collective-permute-start.3
  12.0 0.7 %collective-permute-done.4.beside_before_ref = f32[64,128]{1,0:T(8,128)S(1)} collective-permute-done((f32[64,128]{1,0:T(8,128)S(1)}, f32[64,128]{1,0:T(8,128)S(1)}, u32[]{:S(2)}, u32[]{:S(2)}) %collective-permute-start.4) | collective-permute-done | bytes 32800 | tf_op jit(solution)/shard_map/ppermute | solution.py:380
  12.7 12.3 %all_to_all.5.squares_ref = f32[32,1,128]{2,1,0:T(1,128)S(1)} all-to-all(f32[32,1,128]{2,1,0:T(1,128)S(1)} %change_squares.1), channel_id=1, replica_groups={{23,31,30,29,28,27,26,25,24,22,21,20,19,18,17,16,15,14,13,12,11,10,9,8,..., dimensions={0} | all-to-all | bytes 32768 | tf_op jit(solution)/shard_map/all_to_all | solution.py:489
  25.0 0.0 collective-permute-done.3.got_ref
  25.0 0.7 %join_species.1 = (f32[1,2,64,128]{3,2,1,0:T(8,128)}, f32[1,1]{1,0:T(1,128)}) custom-call(f32[64,128]{1,0:T(8,128)S(1)} %get-tuple-element.18.own_ref, f32[64,128]{1,0:T(8,128)S(1)} %collective-permute-done.3.got_ref, f32[64,128]{1,0:T(8,128)S(1)} %get-tuple-element.20.mine_before_ref, f32[64,128]{1,0:T(8,128)S(1)} %get-tuple-element.21.other_before_ref, ...), custom_call_target="tpu_custom_call" | custom-call | flops 4000 | bytes 100000 | tf_op jit(solution)/shard_map/join_species/pallas_call | solution.py:493
  (1 shorter events, 0.0 us)
Async XLA Ops:
  1.6 8.9 %collective-permute-start.1 = (f32[64,128]{1,0:T(8,128)S(1)}, f32[64,128]{1,0:T(8,128)S(1)}, u32[]{:S(2)}, u32[]{:S(2)}) collective-permute-start(f32[64,128]{1,0:T(8,128)S(1)} %get-tuple-element.13.refs_0_), channel_id=1, source_target_pairs={{0,16},{8,24},{16,0},{24,8},{1,17},{9,25},{17,1},{25,9},{2,18},{10... | collective-permute-start | bytes 98312 | tf_op jit(solution)/shard_map/ppermute | solution.py:380
  5.7 5.8 %collective-permute-start.2 = (f32[64,128]{1,0:T(8,128)S(1)}, f32[64,128]{1,0:T(8,128)S(1)}, u32[]{:S(2)}, u32[]{:S(2)}) collective-permute-start(f32[64,128]{1,0:T(8,128)S(1)} %get-tuple-element.14), channel_id=1, source_target_pairs={{0,24},{8,16},{16,8},{24,0},{1,25},{9,17},{17,9},{25,1},{2,26},{10... | collective-permute-start | bytes 98312 | tf_op jit(solution)/shard_map/ppermute | solution.py:380
  7.0 4.6 %collective-permute-start = (f32[64,128]{1,0:T(8,128)S(1)}, f32[64,128]{1,0:T(8,128)S(1)}, u32[]{:S(2)}, u32[]{:S(2)}) collective-permute-start(f32[64,128]{1,0:T(8,128)S(1)} %get-tuple-element.14), channel_id=1, source_target_pairs={{0,8},{8,0},{16,24},{24,16},{1,9},{9,1},{17,25},{25,17},{2,10},{10... | collective-permute-start | bytes 98312 | tf_op jit(solution)/shard_map/ppermute | solution.py:380
  8.7 4.0 %collective-permute-start.4 = (f32[64,128]{1,0:T(8,128)S(1)}, f32[64,128]{1,0:T(8,128)S(1)}, u32[]{:S(2)}, u32[]{:S(2)}) collective-permute-start(f32[64,128]{1,0:T(8,128)S(1)} %get-tuple-element.21.other_before_ref), channel_id=1, source_target_pairs={{0,8},{8,0},{16,24},{24,16},{1,9},{9,1},{17,25},{25,17},{2,10},{10... | collective-permute-start | bytes 98312 | tf_op jit(solution)/shard_map/ppermute | solution.py:380
  11.9 13.2 %collective-permute-start.3 = (f32[64,128]{1,0:T(8,128)S(1)}, f32[64,128]{1,0:T(8,128)S(1)}, u32[]{:S(2)}, u32[]{:S(2)}) collective-permute-start(f32[64,128]{1,0:T(8,128)S(1)} %get-tuple-element.19.give_ref), channel_id=1, source_target_pairs={{0,8},{8,0},{16,24},{24,16},{1,9},{9,1},{17,25},{25,17},{2,10},{10... | collective-permute-start | bytes 98312 | tf_op jit(solution)/shard_map/ppermute | solution.py:380

commit v15 on v9

--- a/solution.py
+++ b/solution.py
@@ -363,7 +363,7 @@
         out_shape=(
             pltpu.VMEM((cells, lanes), jnp.float32),
             pltpu.VMEM((cells, lanes), jnp.float32),
-            pltpu.VMEM((2 * space, 1, lanes), jnp.float32),
+            pltpu.VMEM((1, lanes), jnp.float32),
         ),
         in_specs=[whole] * (length + 3),
         out_specs=[whole] * 3,
@@ -371,13 +371,21 @@
         cost_estimate=pl.CostEstimate(flops=4000000, bytes_accessed=3000000, transcendentals=0),
         name="solve_lines",
     )(*stacks, initial, near, far)
+    last = 2 * space - 1
+    squares = squares + exchange(squares, "space", 1)
     got = exchange(give, "tm", 1)
     groups = [
-        [step * space + index for index in reversed(range(2 * space))]
+        [step * space + index for index in reversed(range(core, 2 * space, 2))]
         for step in range(0, length, 2)
+        for core in range(2)
     ]
     squares = lax.all_to_all(
-        squares, ("tm", "space"), 0, 0, axis_index_groups=groups, tiled=True
+        jnp.broadcast_to(squares[None], (space,) + squares.shape),
+        ("tm", "space"),
+        0,
+        0,
+        axis_index_groups=groups,
+        tiled=True,
     )
     entry_count = length * space * forcing.shape[1] * cells * lanes
     new_iterate, norm = pl.pallas_call(

time: 21.3 us -> 21.9 us (1.028)
  waiting for transfers between devices: 3.43 us -> 3.71 us
  blocking collectives: 7.29 us -> 7.52 us
    ppermute x4 -> x5, waiting for transfers between devices: 3.43 us -> 3.71 us  [exchange(): return lax.ppermute(value, axis, pairs)]
    all_to_all x1, blocking collectives: 7.29 us -> 7.52 us  [shards(): lax.all_to_all(jnp.broadcast_to(squares[None], (space,) + squares.shape),...]
    ppermute x4 -> x5, starting transfers between devices: 6.5 us -> 6.57 us  [exchange(): return lax.ppermute(value, axis, pairs)]
  transfers between devices with their start and end apart: 4 -> 5, of which waited for: 3 -> 4; matrix products, arithmetic and copies ran while one was open for 0% -> 0% of each run, Pallas kernels for 6% -> 6%
where the time goes in v15:
time: 21.9 us; the launch traced here: 21.6 us
  blocking collectives  7.52 us (34%)
  starting transfers between devices  6.57 us (30%)
  waiting for transfers between devices  3.71 us (17%)
  Pallas kernels  3.14 us (14%)
  between operations  0.66 us (3%)
    all_to_all x1, blocking collectives, shards(): lax.all_to_all(jnp.broadcast_to(squares[None], (space,) + squares.shape),...  7.52 us
    ppermute x5, starting transfers between devices, exchange(): return lax.ppermute(value, axis, pairs)  6.57 us
    ppermute x5, waiting for transfers between devices, exchange(): return lax.ppermute(value, axis, pairs)  3.71 us
    pallas_call x1, Pallas kernels, shards(): pl.pallas_call(functools.partial(factor_kernel, length), out_shape=(pltpu...  1.3 us
    pallas_call x1, Pallas kernels, shards(): pl.pallas_call(stack_kernel, out_shape=(pltpu.VMEM((2, cells, lanes), jnp...  0.86 us
    pallas_call x1, Pallas kernels, shards(): pl.pallas_call(functools.partial(join_kernel, entry_count), out_shape=(ja...  0.71 us
  transfers between devices with their start and end apart: 5, of which 4 were waited for; matrix products, arithmetic and copies ran while one was open for 0% of the time, Pallas kernels for 6%

profile of v15, /device:TPU:0, one launch (start us, length us, event | category | flops | bytes accessed | tf_op | source)
XLA Modules:
  0.0 21.6 jit_solution(1308968166591803384)
XLA Ops:
  0.6 0.9 %stack_arrays.1 = (f32[2,64,128]{2,1,0:T(8,128)S(1)}, f32[2,64,128]{2,1,0:T(8,128)S(1)}) custom-call(f32[1,2,64,128]{3,2,1,0:T(8,128)} %forcing_hbm.1, f32[1,2,64,128]{3,2,1,0:T(8,128)} %previous_hbm.1), custom_call_target="tpu_custom_call" | custom-call | flops 4000 | bytes 500000 | tf_op jit(solution)/shard_map/stack_arrays/pallas_call | solution.py:324
  1.5 4.1 %collective-permute-start.1 = (f32[2,64,128]{2,1,0:T(8,128)S(1)}, f32[2,64,128]{2,1,0:T(8,128)S(1)}, u32[]{:S(2)}, u32[]{:S(2)}) collective-permute-start(f32[2,64,128]{2,1,0:T(8,128)S(1)} %get-tuple-element.12.refs_0_), channel_id=1, source_target_pairs={{0,16},{8,24},{16,0},{24,8},{1,17},{9,25},{17,1},{25,9},{2,18},{10... | collective-permute-start | bytes 196616 | tf_op jit(solution)/shard_map/ppermute | solution.py:303
  5.6 1.3 %collective-permute-start.2 = (f32[2,64,128]{2,1,0:T(8,128)S(1)}, f32[2,64,128]{2,1,0:T(8,128)S(1)}, u32[]{:S(2)}, u32[]{:S(2)}) collective-permute-start(f32[2,64,128]{2,1,0:T(8,128)S(1)} %get-tuple-element.13), channel_id=1, source_target_pairs={{0,24},{8,16},{16,8},{24,0},{1,25},{9,17},{17,9},{25,1},{2,26},{10... | collective-permute-start | bytes 196616 | tf_op jit(solution)/shard_map/ppermute | solution.py:303
  6.9 0.2 %collective-permute-start = (f32[2,64,128]{2,1,0:T(8,128)S(1)}, f32[2,64,128]{2,1,0:T(8,128)S(1)}, u32[]{:S(2)}, u32[]{:S(2)}) collective-permute-start(f32[2,64,128]{2,1,0:T(8,128)S(1)} %get-tuple-element.13), channel_id=1, source_target_pairs={{0,8},{8,0},{16,24},{24,16},{1,9},{9,1},{17,25},{25,17},{2,10},{10... | collective-permute-start | bytes 196616 | tf_op jit(solution)/shard_map/ppermute | solution.py:303
  7.2 1.3 %factor_lines.1 = (f32[4,6,64,128]{3,2,1,0:T(8,128)S(1)}, f32[4,3,64,128]{3,2,1,0:T(8,128)S(1)}, f32[64,128]{1,0:T(8,128)S(1)}) custom-call(f32[2,64,128]{2,1,0:T(8,128)} %initial_hbm.1, f32[2,8]{1,0:T(2,128)} %zones_hbm.1, f32[2]{0:T(128)} %drift_hbm.1, s32[1,128]{1,0:T(1,128)} %bitcast.5, s32[1,128]{1,0:T(1,128)} %bitcast.6, s32[64,128]{1,0:T(8,128)} %faces_hbm.1), custom_call_target="tpu_custom_call" | custom-call | flops 4000000 | bytes 3000000 | tf_op jit(solution)/shard_map/factor_lines/pallas_call | solution.py:340
  8.5 0.9 %collective-permute-done.1.refs_2_ = f32[2,64,128]{2,1,0:T(8,128)S(1)} collective-permute-done((f32[2,64,128]{2,1,0:T(8,128)S(1)}, f32[2,64,128]{2,1,0:T(8,128)S(1)}, u32[]{:S(2)}, u32[]{:S(2)}) %collective-permute-start.1) | collective-permute-done | bytes 65568 | tf_op jit(solution)/shard_map/ppermute | solution.py:303
  9.4 2.5 %collective-permute-done.2.refs_3_ = f32[2,64,128]{2,1,0:T(8,128)S(1)} collective-permute-done((f32[2,64,128]{2,1,0:T(8,128)S(1)}, f32[2,64,128]{2,1,0:T(8,128)S(1)}, u32[]{:S(2)}, u32[]{:S(2)}) %collective-permute-start.2) | collective-permute-done | bytes 65568 | tf_op jit(solution)/shard_map/ppermute | solution.py:303
  11.8 0.1 collective-permute-done.refs_1_
  11.9 0.3 %solve_lines.1 = (f32[64,128]{1,0:T(8,128)S(1)}, f32[64,128]{1,0:T(8,128)S(1)}, f32[1,128]{1,0:T(1,128)S(1)}) custom-call(f32[2,64,128]{2,1,0:T(8,128)S(1)} %get-tuple-element.12.refs_0_, f32[2,64,128]{2,1,0:T(8,128)S(1)} %collective-permute-done.refs_1_, f32[2,64,128]{2,1,0:T(8,128)S(1)} %collective-permute-done.1.refs_2_, ...), custom_call_target="tpu_custom_call" | custom-call | flops 4000000 | bytes 3000000 | tf_op jit(solution)/shard_map/solve_lines/pallas_call | solution.py:361
  12.2 0.1 collective-permute-start.4
  12.3 0.8 %collective-permute-start.3 = (f32[64,128]{1,0:T(8,128)S(1)}, f32[64,128]{1,0:T(8,128)S(1)}, u32[]{:S(2)}, u32[]{:S(2)}) collective-permute-start(f32[64,128]{1,0:T(8,128)S(1)} %get-tuple-element.18), channel_id=1, source_target_pairs={{0,8},{8,0},{16,24},{24,16},{1,9},{9,1},{17,25},{25,17},{2,10},{10... | collective-permute-start | bytes 98312 | tf_op jit(solution)/shard_map/ppermute | solution.py:303
  13.1 0.3 %collective-permute-done.4 = f32[1,128]{1,0:T(1,128)S(1)} collective-permute-done((f32[1,128]{1,0:T(1,128)S(1)}, f32[1,128]{1,0:T(1,128)S(1)}, u32[]{:S(2)}, u32[]{:S(2)}) %collective-permute-start.4) | collective-permute-done | bytes 544 | tf_op jit(solution)/shard_map/ppermute | solution.py:303
  13.4 7.5 %all_to_all.5.squares_ref = f32[8,1,128]{2,1,0:T(1,128)S(1)} all-to-all(f32[8,1,128]{2,1,0:T(1,128)S(1)} %broadcast_in_dim.17), channel_id=1, replica_groups={{14,12,10,8,6,4,2,0},{15,13,11,9,7,5,3,1},{30,28,26,24,22,20,18,16},{31..., dimensions={0} | all-to-all | bytes 8192 | tf_op jit(solution)/shard_map/all_to_all | solution.py:382
  20.9 0.0 collective-permute-done.3.got_ref
  20.9 0.7 %join_species.1 = (f32[1,2,64,128]{3,2,1,0:T(8,128)}, f32[1,1]{1,0:T(1,128)}) custom-call(f32[64,128]{1,0:T(8,128)S(1)} %get-tuple-element.17.own_ref, f32[64,128]{1,0:T(8,128)S(1)} %collective-permute-done.3.got_ref, f32[8,1,128]{2,1,0:T(1,128)S(1)} %all_to_all.5.squares_ref), custom_call_target="tpu_custom_call" | custom-call | flops 4000 | bytes 100000 | tf_op jit(solution)/shard_map/join_species/pallas_call | solution.py:391
  (2 shorter events, 0.0 us)
Async XLA Ops:
  1.5 7.9 %collective-permute-start.1 = (f32[2,64,128]{2,1,0:T(8,128)S(1)}, f32[2,64,128]{2,1,0:T(8,128)S(1)}, u32[]{:S(2)}, u32[]{:S(2)}) collective-permute-start(f32[2,64,128]{2,1,0:T(8,128)S(1)} %get-tuple-element.12.refs_0_), channel_id=1, source_target_pairs={{0,16},{8,24},{16,0},{24,8},{1,17},{9,25},{17,1},{25,9},{2,18},{10... | collective-permute-start | bytes 196616 | tf_op jit(solution)/shard_map/ppermute | solution.py:303
  5.6 6.2 %collective-permute-start.2 = (f32[2,64,128]{2,1,0:T(8,128)S(1)}, f32[2,64,128]{2,1,0:T(8,128)S(1)}, u32[]{:S(2)}, u32[]{:S(2)}) collective-permute-start(f32[2,64,128]{2,1,0:T(8,128)S(1)} %get-tuple-element.13), channel_id=1, source_target_pairs={{0,24},{8,16},{16,8},{24,0},{1,25},{9,17},{17,9},{25,1},{2,26},{10... | collective-permute-start | bytes 196616 | tf_op jit(solution)/shard_map/ppermute | solution.py:303
  6.9 5.0 %collective-permute-start = (f32[2,64,128]{2,1,0:T(8,128)S(1)}, f32[2,64,128]{2,1,0:T(8,128)S(1)}, u32[]{:S(2)}, u32[]{:S(2)}) collective-permute-start(f32[2,64,128]{2,1,0:T(8,128)S(1)} %get-tuple-element.13), channel_id=1, source_target_pairs={{0,8},{8,0},{16,24},{24,16},{1,9},{9,1},{17,25},{25,17},{2,10},{10... | collective-permute-start | bytes 196616 | tf_op jit(solution)/shard_map/ppermute | solution.py:303
  12.2 1.2 %collective-permute-start.4 = (f32[1,128]{1,0:T(1,128)S(1)}, f32[1,128]{1,0:T(1,128)S(1)}, u32[]{:S(2)}, u32[]{:S(2)}) collective-permute-start(f32[1,128]{1,0:T(1,128)S(1)} %get-tuple-element.19), channel_id=1, source_target_pairs={{0,1},{1,0},{2,3},{3,2},{4,5},{5,4},{6,7},{7,6},{8,9},{9,8},{10,11... | collective-permute-start | bytes 1544 | tf_op jit(solution)/shard_map/ppermute | solution.py:303
  12.3 8.6 %collective-permute-start.3 = (f32[64,128]{1,0:T(8,128)S(1)}, f32[64,128]{1,0:T(8,128)S(1)}, u32[]{:S(2)}, u32[]{:S(2)}) collective-permute-start(f32[64,128]{1,0:T(8,128)S(1)} %get-tuple-element.18), channel_id=1, source_target_pairs={{0,8},{8,0},{16,24},{24,16},{1,9},{9,1},{17,25},{25,17},{2,10},{10... | collective-permute-start | bytes 98312 | tf_op jit(solution)/shard_map/ppermute | solution.py:303

commit v16 on v15

--- a/solution.py
+++ b/solution.py
@@ -375,7 +375,7 @@
     squares = squares + exchange(squares, "space", 1)
     got = exchange(give, "tm", 1)
     groups = [
-        [step * space + index for index in reversed(range(core, 2 * space, 2))]
+        [step * space + index for index in (*reversed(range(3 - core, 2 * space, 2)), core)]
         for step in range(0, length, 2)
         for core in range(2)
     ]

time: 21.9 us -> 21.3 us (0.973)
  the two profiles are of different devices: /device:TPU:0 before, /device:TPU:1 now
where the time goes in v16:
time: 21.3 us; the launch traced here: 21 us
  starting transfers between devices  7.35 us (35%)
  blocking collectives  7.14 us (34%)
  Pallas kernels  3.14 us (15%)
  waiting for transfers between devices  2.69 us (13%)
  between operations  0.66 us (3%)
    ppermute x5, starting transfers between devices, exchange(): return lax.ppermute(value, axis, pairs)  7.35 us
    all_to_all x1, blocking collectives, shards(): lax.all_to_all(jnp.broadcast_to(squares[None], (space,) + squares.shape),...  7.14 us
    ppermute x5, waiting for transfers between devices, exchange(): return lax.ppermute(value, axis, pairs)  2.69 us
    pallas_call x1, Pallas kernels, shards(): pl.pallas_call(functools.partial(factor_kernel, length), out_shape=(pltpu...  1.3 us
    pallas_call x1, Pallas kernels, shards(): pl.pallas_call(stack_kernel, out_shape=(pltpu.VMEM((2, cells, lanes), jnp...  0.86 us
    pallas_call x1, Pallas kernels, shards(): pl.pallas_call(functools.partial(join_kernel, entry_count), out_shape=(ja...  0.71 us
  transfers between devices with their start and end apart: 5, of which 2 were waited for; matrix products, arithmetic and copies ran while one was open for 0% of the time, Pallas kernels for 6%

profile of v16, /device:TPU:1, one launch (start us, length us, event | category | flops | bytes accessed | tf_op | source)
XLA Modules:
  0.0 21.0 jit_solution(17481630855481870971)
XLA Ops:
  0.6 0.9 %stack_arrays.1 = (f32[2,64,128]{2,1,0:T(8,128)S(1)}, f32[2,64,128]{2,1,0:T(8,128)S(1)}) custom-call(f32[1,2,64,128]{3,2,1,0:T(8,128)} %forcing_hbm.1, f32[1,2,64,128]{3,2,1,0:T(8,128)} %previous_hbm.1), custom_call_target="tpu_custom_call" | custom-call | flops 4000 | bytes 500000 | tf_op jit(solution)/shard_map/stack_arrays/pallas_call | solution.py:324
  1.5 3.2 %collective-permute-start.1 = (f32[2,64,128]{2,1,0:T(8,128)S(1)}, f32[2,64,128]{2,1,0:T(8,128)S(1)}, u32[]{:S(2)}, u32[]{:S(2)}) collective-permute-start(f32[2,64,128]{2,1,0:T(8,128)S(1)} %get-tuple-element.12.refs_0_), channel_id=1, source_target_pairs={{0,16},{8,24},{16,0},{24,8},{1,17},{9,25},{17,1},{25,9},{2,18},{10... | collective-permute-start | bytes 196616 | tf_op jit(solution)/shard_map/ppermute | solution.py:303
  4.7 1.1 %collective-permute-start.2 = (f32[2,64,128]{2,1,0:T(8,128)S(1)}, f32[2,64,128]{2,1,0:T(8,128)S(1)}, u32[]{:S(2)}, u32[]{:S(2)}) collective-permute-start(f32[2,64,128]{2,1,0:T(8,128)S(1)} %get-tuple-element.13), channel_id=1, source_target_pairs={{0,24},{8,16},{16,8},{24,0},{1,25},{9,17},{17,9},{25,1},{2,26},{10... | collective-permute-start | bytes 196616 | tf_op jit(solution)/shard_map/ppermute | solution.py:303
  5.8 0.2 collective-permute-start
  6.0 1.3 %factor_lines.1 = (f32[4,6,64,128]{3,2,1,0:T(8,128)S(1)}, f32[4,3,64,128]{3,2,1,0:T(8,128)S(1)}, f32[64,128]{1,0:T(8,128)S(1)}) custom-call(f32[2,64,128]{2,1,0:T(8,128)} %initial_hbm.1, f32[2,8]{1,0:T(2,128)} %zones_hbm.1, f32[2]{0:T(128)} %drift_hbm.1, s32[1,128]{1,0:T(1,128)} %bitcast.5, s32[1,128]{1,0:T(1,128)} %bitcast.6, s32[64,128]{1,0:T(8,128)} %faces_hbm.1), custom_call_target="tpu_custom_call" | custom-call | flops 4000000 | bytes 3000000 | tf_op jit(solution)/shard_map/factor_lines/pallas_call | solution.py:340
  7.3 0.0 collective-permute-done.1.refs_2_
  7.3 2.4 %collective-permute-done.2.refs_3_ = f32[2,64,128]{2,1,0:T(8,128)S(1)} collective-permute-done((f32[2,64,128]{2,1,0:T(8,128)S(1)}, f32[2,64,128]{2,1,0:T(8,128)S(1)}, u32[]{:S(2)}, u32[]{:S(2)}) %collective-permute-start.2) | collective-permute-done | bytes 65568 | tf_op jit(solution)/shard_map/ppermute | solution.py:303
  9.7 0.0 collective-permute-done.refs_1_
  9.7 0.3 %solve_lines.1 = (f32[64,128]{1,0:T(8,128)S(1)}, f32[64,128]{1,0:T(8,128)S(1)}, f32[1,128]{1,0:T(1,128)S(1)}) custom-call(f32[2,64,128]{2,1,0:T(8,128)S(1)} %get-tuple-element.12.refs_0_, f32[2,64,128]{2,1,0:T(8,128)S(1)} %collective-permute-done.refs_1_, f32[2,64,128]{2,1,0:T(8,128)S(1)} %collective-permute-done.1.refs_2_, ...), custom_call_target="tpu_custom_call" | custom-call | flops 4000000 | bytes 3000000 | tf_op jit(solution)/shard_map/solve_lines/pallas_call | solution.py:361
  9.9 2.4 %collective-permute-start.4 = (f32[1,128]{1,0:T(1,128)S(1)}, f32[1,128]{1,0:T(1,128)S(1)}, u32[]{:S(2)}, u32[]{:S(2)}) collective-permute-start(f32[1,128]{1,0:T(1,128)S(1)} %get-tuple-element.19), channel_id=1, source_target_pairs={{0,1},{1,0},{2,3},{3,2},{4,5},{5,4},{6,7},{7,6},{8,9},{9,8},{10,11... | collective-permute-start | bytes 1544 | tf_op jit(solution)/shard_map/ppermute | solution.py:303
  12.3 0.5 %collective-permute-start.3 = (f32[64,128]{1,0:T(8,128)S(1)}, f32[64,128]{1,0:T(8,128)S(1)}, u32[]{:S(2)}, u32[]{:S(2)}) collective-permute-start(f32[64,128]{1,0:T(8,128)S(1)} %get-tuple-element.18), channel_id=1, source_target_pairs={{0,8},{8,0},{16,24},{24,16},{1,9},{9,1},{17,25},{25,17},{2,10},{10... | collective-permute-start | bytes 98312 | tf_op jit(solution)/shard_map/ppermute | solution.py:303
  12.8 0.3 %collective-permute-done.4 = f32[1,128]{1,0:T(1,128)S(1)} collective-permute-done((f32[1,128]{1,0:T(1,128)S(1)}, f32[1,128]{1,0:T(1,128)S(1)}, u32[]{:S(2)}, u32[]{:S(2)}) %collective-permute-start.4) | collective-permute-done | bytes 544 | tf_op jit(solution)/shard_map/ppermute | solution.py:303
  13.1 7.1 %all_to_all.5.squares_ref = f32[8,1,128]{2,1,0:T(1,128)S(1)} all-to-all(f32[8,1,128]{2,1,0:T(1,128)S(1)} %broadcast_in_dim.17), channel_id=1, replica_groups={{15,13,11,9,7,5,3,0},{14,12,10,8,6,4,2,1},{31,29,27,25,23,21,19,16},{30..., dimensions={0} | all-to-all | bytes 8192 | tf_op jit(solution)/shard_map/all_to_all | solution.py:382
  20.3 0.0 collective-permute-done.3.got_ref
  20.3 0.7 %join_species.1 = (f32[1,2,64,128]{3,2,1,0:T(8,128)}, f32[1,1]{1,0:T(1,128)}) custom-call(f32[64,128]{1,0:T(8,128)S(1)} %get-tuple-element.17.own_ref, f32[64,128]{1,0:T(8,128)S(1)} %collective-permute-done.3.got_ref, f32[8,1,128]{2,1,0:T(1,128)S(1)} %all_to_all.5.squares_ref), custom_call_target="tpu_custom_call" | custom-call | flops 4000 | bytes 100000 | tf_op jit(solution)/shard_map/join_species/pallas_call | solution.py:391
  (2 shorter events, 0.0 us)
Async XLA Ops:
  1.5 5.8 %collective-permute-start.1 = (f32[2,64,128]{2,1,0:T(8,128)S(1)}, f32[2,64,128]{2,1,0:T(8,128)S(1)}, u32[]{:S(2)}, u32[]{:S(2)}) collective-permute-start(f32[2,64,128]{2,1,0:T(8,128)S(1)} %get-tuple-element.12.refs_0_), channel_id=1, source_target_pairs={{0,16},{8,24},{16,0},{24,8},{1,17},{9,25},{17,1},{25,9},{2,18},{10... | collective-permute-start | bytes 196616 | tf_op jit(solution)/shard_map/ppermute | solution.py:303
  4.7 5.0 %collective-permute-start.2 = (f32[2,64,128]{2,1,0:T(8,128)S(1)}, f32[2,64,128]{2,1,0:T(8,128)S(1)}, u32[]{:S(2)}, u32[]{:S(2)}) collective-permute-start(f32[2,64,128]{2,1,0:T(8,128)S(1)} %get-tuple-element.13), channel_id=1, source_target_pairs={{0,24},{8,16},{16,8},{24,0},{1,25},{9,17},{17,9},{25,1},{2,26},{10... | collective-permute-start | bytes 196616 | tf_op jit(solution)/shard_map/ppermute | solution.py:303
  5.8 3.9 %collective-permute-start = (f32[2,64,128]{2,1,0:T(8,128)S(1)}, f32[2,64,128]{2,1,0:T(8,128)S(1)}, u32[]{:S(2)}, u32[]{:S(2)}) collective-permute-start(f32[2,64,128]{2,1,0:T(8,128)S(1)} %get-tuple-element.13), channel_id=1, source_target_pairs={{0,8},{8,0},{16,24},{24,16},{1,9},{9,1},{17,25},{25,17},{2,10},{10... | collective-permute-start | bytes 196616 | tf_op jit(solution)/shard_map/ppermute | solution.py:303
  9.9 3.2 %collective-permute-start.4 = (f32[1,128]{1,0:T(1,128)S(1)}, f32[1,128]{1,0:T(1,128)S(1)}, u32[]{:S(2)}, u32[]{:S(2)}) collective-permute-start(f32[1,128]{1,0:T(1,128)S(1)} %get-tuple-element.19), channel_id=1, source_target_pairs={{0,1},{1,0},{2,3},{3,2},{4,5},{5,4},{6,7},{7,6},{8,9},{9,8},{10,11... | collective-permute-start | bytes 1544 | tf_op jit(solution)/shard_map/ppermute | solution.py:303
  12.3 8.0 %collective-permute-start.3 = (f32[64,128]{1,0:T(8,128)S(1)}, f32[64,128]{1,0:T(8,128)S(1)}, u32[]{:S(2)}, u32[]{:S(2)}) collective-permute-start(f32[64,128]{1,0:T(8,128)S(1)} %get-tuple-element.18), channel_id=1, source_target_pairs={{0,8},{8,0},{16,24},{24,16},{1,9},{9,1},{17,25},{25,17},{2,10},{10... | collective-permute-start | bytes 98312 | tf_op jit(solution)/shard_map/ppermute | solution.py:303

commit v17 on v10

--- a/solution.py
+++ b/solution.py
@@ -100,29 +100,19 @@
     return copies
 
 
-def stack_kernel(forcing_hbm, previous_hbm, mine_ref, other_ref, sems):
-    species = lax.axis_index("tm") % 2
-    pairs = (
-        (forcing_hbm.at[0, species], mine_ref.at[0]),
-        (previous_hbm.at[0, species], mine_ref.at[1]),
-        (forcing_hbm.at[0, 1 - species], other_ref.at[0]),
-        (previous_hbm.at[0, 1 - species], other_ref.at[1]),
-    )
-    for copy in start_all(pairs, sems):
-        copy.wait()
-
-
-def factor_kernel(
+def stack_kernel(
     length,
-    initial_hbm,
+    forcing_hbm,
+    previous_hbm,
     zones_hbm,
     drift_hbm,
     zone_hbm,
     flag_hbm,
     faces_hbm,
+    mine_ref,
+    other_ref,
     near_ref,
     far_ref,
-    initial_ref,
     zones_ref,
     drift_ref,
     zone_ref,
@@ -132,15 +122,30 @@
 ):
     species = lax.axis_index("tm") % 2
     pairs = (
+        (forcing_hbm.at[0, species], mine_ref.at[0]),
+        (previous_hbm.at[0, species], mine_ref.at[1]),
+        (forcing_hbm.at[0, 1 - species], other_ref.at[0]),
+        (previous_hbm.at[0, 1 - species], other_ref.at[1]),
         (zones_hbm, zones_ref),
         (drift_hbm, drift_ref),
         (zone_hbm, zone_ref),
         (flag_hbm, flag_ref),
         (faces_hbm, faces_ref),
-        (initial_hbm.at[species], initial_ref),
     )
     for copy in start_all(pairs, sems):
         copy.wait()
+
+    @pl.when(lax.axis_index("space") % 2 == 1)
+    def factor():
+        factor_lines(
+            length, zones_ref, drift_ref, zone_ref, flag_ref, faces_ref, near_ref, far_ref
+        )
+
+
+def factor_lines(
+    length, zones_ref, drift_ref, zone_ref, flag_ref, faces_ref, near_ref, far_ref
+):
+    species = lax.axis_index("tm") % 2
     zone = zone_ref[...]
     diffusion = jnp.zeros(zone.shape, jnp.float32)
     for index in range(zones_ref.shape[1]):
@@ -195,6 +200,42 @@
         plane += parts
 
 
+def factor_kernel(
+    length,
+    initial_hbm,
+    zones_hbm,
+    drift_hbm,
+    zone_hbm,
+    flag_hbm,
+    faces_hbm,
+    near_ref,
+    far_ref,
+    initial_ref,
+    zones_ref,
+    drift_ref,
+    zone_ref,
+    flag_ref,
+    faces_ref,
+    sems,
+):
+    pairs = (
+        (zones_hbm, zones_ref),
+        (drift_hbm, drift_ref),
+        (zone_hbm, zone_ref),
+        (flag_hbm, flag_ref),
+        (faces_hbm, faces_ref),
+        (initial_hbm.at[lax.axis_index("tm") % 2], initial_ref),
+    )
+    for copy in start_all(pairs, sems):
+        copy.wait()
+
+    @pl.when(lax.axis_index("space") % 2 == 0)
+    def factor():
+        factor_lines(
+            length, zones_ref, drift_ref, zone_ref, flag_ref, faces_ref, near_ref, far_ref
+        )
+
+
 def in_order(me, held):
     bit = 1
     while bit < len(held):
@@ -207,6 +248,19 @@
 
 
 def sweep_kernel(length, *refs):
+    *shared, near_even, far_even, near_odd, far_odd, own_ref, give_ref, sum_ref = refs
+    odd = lax.axis_index("space") % 2 == 1
+
+    @pl.when(odd)
+    def solve_odd():
+        sweep_lines(length, *shared, near_odd, far_odd, own_ref, give_ref, sum_ref)
+
+    @pl.when(jnp.logical_not(odd))
+    def solve_even():
+        sweep_lines(length, *shared, near_even, far_even, own_ref, give_ref, sum_ref)
+
+
+def sweep_lines(length, *refs):
     stacks = refs[:length]
     initial_ref, near_ref, far_ref, own_ref, give_ref, sum_ref = refs[length:]
     cells, lanes = initial_ref.shape
@@ -321,19 +375,31 @@
     count = planes(length)
     params = pltpu.CompilerParams(vmem_limit_bytes=40 * 1024 * 1024)
     alone = pltpu.CompilerParams(vmem_limit_bytes=56 * 1024 * 1024)
-    mine, other = pl.pallas_call(
-        stack_kernel,
+    near_shape = (count, 2 * near_steps, cells, lanes)
+    far_shape = (count, 3, cells, lanes)
+    operator_scratch = [
+        pltpu.SMEM(zone_diffusion.shape, jnp.float32),
+        pltpu.SMEM(drift_rate.shape, jnp.float32),
+        pltpu.VMEM((1, lanes), jnp.int32),
+        pltpu.VMEM((1, lanes), jnp.int32),
+        pltpu.VMEM((cells, lanes), jnp.int32),
+    ]
+    operator = (zone_diffusion, drift_rate, column_zone[None], bottom_flag[None], open_faces)
+    mine, other, near_odd, far_odd = pl.pallas_call(
+        functools.partial(stack_kernel, length),
         out_shape=(
             pltpu.VMEM((2, cells, lanes), jnp.float32),
             pltpu.VMEM((2, cells, lanes), jnp.float32),
+            pltpu.VMEM(near_shape, jnp.float32),
+            pltpu.VMEM(far_shape, jnp.float32),
         ),
-        in_specs=[outside] * 2,
-        out_specs=[whole] * 2,
-        scratch_shapes=[pltpu.SemaphoreType.DMA((4,))],
+        in_specs=[outside] * 7,
+        out_specs=[whole] * 4,
+        scratch_shapes=[*operator_scratch, pltpu.SemaphoreType.DMA((9,))],
         compiler_params=alone,
         cost_estimate=pl.CostEstimate(flops=4000, bytes_accessed=500000, transcendentals=0),
         name="stack_arrays",
-    )(forcing, previous)
+    )(forcing, previous, *operator)
     stacks = [mine]
     for bits in range(1, length):
         stacks.append(exchange(other if bits % 2 else mine, "tm", bits))
@@ -346,18 +412,11 @@
         ),
         in_specs=[outside] * 6,
         out_specs=[whole] * 3,
-        scratch_shapes=[
-            pltpu.SMEM(zone_diffusion.shape, jnp.float32),
-            pltpu.SMEM(drift_rate.shape, jnp.float32),
-            pltpu.VMEM((1, lanes), jnp.int32),
-            pltpu.VMEM((1, lanes), jnp.int32),
-            pltpu.VMEM((cells, lanes), jnp.int32),
-            pltpu.SemaphoreType.DMA((6,)),
-        ],
+        scratch_shapes=[*operator_scratch, pltpu.SemaphoreType.DMA((6,))],
         compiler_params=alone,
         cost_estimate=pl.CostEstimate(flops=4000000, bytes_accessed=3000000, transcendentals=0),
         name="factor_lines",
-    )(initial_state, zone_diffusion, drift_rate, column_zone[None], bottom_flag[None], open_faces)
+    )(initial_state, *operator)
     own, give, squares = pl.pallas_call(
         functools.partial(sweep_kernel, length),
         out_shape=(
@@ -365,12 +424,12 @@
             pltpu.VMEM((cells, lanes), jnp.float32),
             pltpu.VMEM((2 * space, 1, lanes), jnp.float32),
         ),
-        in_specs=[whole] * (length + 3),
+        in_specs=[whole] * (length + 5),
         out_specs=[whole] * 3,
         compiler_params=params,
         cost_estimate=pl.CostEstimate(flops=4000000, bytes_accessed=3000000, transcendentals=0),
         name="solve_lines",
-    )(*stacks, initial, near, far)
+    )(*stacks, initial, near, far, near_odd, far_odd)
     got = exchange(give, "tm", 1)
     last = 2 * space - 1
     order = [last, *range(2, last, 2), *range(3, last, 2), 1, 0]

time: 21.3 us -> 21.9 us (1.028)
  waiting for transfers between devices: 3.43 us -> 3.85 us
    ppermute x4, waiting for transfers between devices: 3.43 us -> 3.85 us  [exchange(): return lax.ppermute(value, axis, pairs)]
where the time goes in v17:
time: 21.9 us; the launch traced here: 21.6 us
  blocking collectives  7.28 us (33%)
  starting transfers between devices  6.54 us (30%)
  waiting for transfers between devices  3.85 us (18%)
  Pallas kernels  3.24 us (15%)
  between operations  0.65 us (3%)
    all_to_all x1, blocking collectives, shards(): lax.all_to_all(squares, ('tm', 'space'), 0, 0, axis_index_groups=groups,...  7.28 us
    ppermute x4, starting transfers between devices, exchange(): return lax.ppermute(value, axis, pairs)  6.54 us
    ppermute x4, waiting for transfers between devices, exchange(): return lax.ppermute(value, axis, pairs)  3.85 us
    pallas_call x1, Pallas kernels, shards(): pl.pallas_call(functools.partial(factor_kernel, length), out_shape=(pltpu...  1.3 us
    pallas_call x1, Pallas kernels, shards(): pl.pallas_call(functools.partial(stack_kernel, length), out_shape=(pltpu....  0.95 us
    pallas_call x1, Pallas kernels, shards(): pl.pallas_call(functools.partial(join_kernel, entry_count), out_shape=(ja...  0.72 us
  transfers between devices with their start and end apart: 4, of which 3 were waited for; matrix products, arithmetic and copies ran while one was open for 0% of the time, Pallas kernels for 6%

profile of v17, /device:TPU:0, one launch (start us, length us, event | category | flops | bytes accessed | tf_op | source)
XLA Modules:
  0.0 21.6 jit_solution(5786591688107571746)
XLA Ops:
  0.6 1.0 %stack_arrays.1 = (f32[2,64,128]{2,1,0:T(8,128)S(1)}, f32[2,64,128]{2,1,0:T(8,128)S(1)}, f32[4,6,64,128]{3,2,1,0:T(8,128)S(1)}, f32[4,3,64,128]{3,2,1,0:T(8,128)S(1)}) custom-call(f32[1,2,64,128]{3,2,1,0:T(8,128)} %forcing_hbm.1, f32[1,2,64,128]{3,2,1,0:T(8,128)} %previous_hbm.1, f32[2,8]{1,0:T(2,128)} %zones_hbm.3, f32[2]{0:T(128)} %drift_hbm.3, ...), custom_call_target="tpu_custom_call" | custom-call | flops 4000 | bytes 500000 | tf_op jit(solution)/shard_map/stack_arrays/pallas_call | solution.py:388
  1.6 4.1 %collective-permute-start.1 = (f32[2,64,128]{2,1,0:T(8,128)S(1)}, f32[2,64,128]{2,1,0:T(8,128)S(1)}, u32[]{:S(2)}, u32[]{:S(2)}) collective-permute-start(f32[2,64,128]{2,1,0:T(8,128)S(1)} %get-tuple-element.14.refs_0_), channel_id=1, source_target_pairs={{0,16},{8,24},{16,0},{24,8},{1,17},{9,25},{17,1},{25,9},{2,18},{10... | collective-permute-start | bytes 196616 | tf_op jit(solution)/shard_map/ppermute | solution.py:357
  5.7 1.3 %collective-permute-start.2 = (f32[2,64,128]{2,1,0:T(8,128)S(1)}, f32[2,64,128]{2,1,0:T(8,128)S(1)}, u32[]{:S(2)}, u32[]{:S(2)}) collective-permute-start(f32[2,64,128]{2,1,0:T(8,128)S(1)} %get-tuple-element.15), channel_id=1, source_target_pairs={{0,24},{8,16},{16,8},{24,0},{1,25},{9,17},{17,9},{25,1},{2,26},{10... | collective-permute-start | bytes 196616 | tf_op jit(solution)/shard_map/ppermute | solution.py:357
  7.0 0.2 %collective-permute-start = (f32[2,64,128]{2,1,0:T(8,128)S(1)}, f32[2,64,128]{2,1,0:T(8,128)S(1)}, u32[]{:S(2)}, u32[]{:S(2)}) collective-permute-start(f32[2,64,128]{2,1,0:T(8,128)S(1)} %get-tuple-element.15), channel_id=1, source_target_pairs={{0,8},{8,0},{16,24},{24,16},{1,9},{9,1},{17,25},{25,17},{2,10},{10... | collective-permute-start | bytes 196616 | tf_op jit(solution)/shard_map/ppermute | solution.py:357
  7.3 1.3 %factor_lines.1 = (f32[4,6,64,128]{3,2,1,0:T(8,128)S(1)}, f32[4,3,64,128]{3,2,1,0:T(8,128)S(1)}, f32[64,128]{1,0:T(8,128)S(1)}) custom-call(f32[2,64,128]{2,1,0:T(8,128)} %initial_hbm.1, f32[2,8]{1,0:T(2,128)} %zones_hbm.3, f32[2]{0:T(128)} %drift_hbm.3, s32[1,128]{1,0:T(1,128)} %bitcast.4, s32[1,128]{1,0:T(1,128)} %bitcast.6, s32[64,128]{1,0:T(8,128)} %faces_hbm.3), custom_call_target="tpu_custom_call" | custom-call | flops 4000000 | bytes 3000000 | tf_op jit(solution)/shard_map/factor_lines/pallas_call | solution.py:406
  8.6 1.2 %collective-permute-done.1.refs_2_ = f32[2,64,128]{2,1,0:T(8,128)S(1)} collective-permute-done((f32[2,64,128]{2,1,0:T(8,128)S(1)}, f32[2,64,128]{2,1,0:T(8,128)S(1)}, u32[]{:S(2)}, u32[]{:S(2)}) %collective-permute-start.1) | collective-permute-done | bytes 65568 | tf_op jit(solution)/shard_map/ppermute | solution.py:357
  9.8 2.4 %collective-permute-done.2.refs_3_ = f32[2,64,128]{2,1,0:T(8,128)S(1)} collective-permute-done((f32[2,64,128]{2,1,0:T(8,128)S(1)}, f32[2,64,128]{2,1,0:T(8,128)S(1)}, u32[]{:S(2)}, u32[]{:S(2)}) %collective-permute-start.2) | collective-permute-done | bytes 65568 | tf_op jit(solution)/shard_map/ppermute | solution.py:357
  12.2 0.2 collective-permute-done.refs_1_
  12.4 0.3 %solve_lines.1 = (f32[64,128]{1,0:T(8,128)S(1)}, f32[64,128]{1,0:T(8,128)S(1)}, f32[16,1,128]{2,1,0:T(1,128)S(1)}) custom-call(f32[2,64,128]{2,1,0:T(8,128)S(1)} %get-tuple-element.14.refs_0_, f32[2,64,128]{2,1,0:T(8,128)S(1)} %collective-permute-done.refs_1_, f32[2,64,128]{2,1,0:T(8,128)S(1)} %collective-permute-done.1.refs_2_, ...), custom_call_target="tpu_custom_call" | custom-call | flops 4000000 | bytes 3000000 | tf_op jit(solution)/shard_map/solve_lines/pallas_call | solution.py:420
  12.7 0.9 %collective-permute-start.3 = (f32[64,128]{1,0:T(8,128)S(1)}, f32[64,128]{1,0:T(8,128)S(1)}, u32[]{:S(2)}, u32[]{:S(2)}) collective-permute-start(f32[64,128]{1,0:T(8,128)S(1)} %get-tuple-element.22), channel_id=1, source_target_pairs={{0,8},{8,0},{16,24},{24,16},{1,9},{9,1},{17,25},{25,17},{2,10},{10... | collective-permute-start | bytes 98312 | tf_op jit(solution)/shard_map/ppermute | solution.py:357
  13.6 7.3 %all_to_all.5.squares_ref = f32[16,1,128]{2,1,0:T(1,128)S(1)} all-to-all(f32[16,1,128]{2,1,0:T(1,128)S(1)} %get-tuple-element.23), channel_id=1, replica_groups={{15,2,4,6,8,10,12,14,3,5,7,9,11,13,1,0},{31,18,20,22,24,26,28,30,19,21,..., dimensions={0} | all-to-all | bytes 16384 | tf_op jit(solution)/shard_map/all_to_all | solution.py:437
  20.8 0.0 collective-permute-done.3.got_ref
  20.8 0.7 %join_species.1 = (f32[1,2,64,128]{3,2,1,0:T(8,128)}, f32[1,1]{1,0:T(1,128)}) custom-call(f32[64,128]{1,0:T(8,128)S(1)} %get-tuple-element.21.own_ref, f32[64,128]{1,0:T(8,128)S(1)} %collective-permute-done.3.got_ref, f32[16,1,128]{2,1,0:T(1,128)S(1)} %all_to_all.5.squares_ref), custom_call_target="tpu_custom_call" | custom-call | flops 4000 | bytes 100000 | tf_op jit(solution)/shard_map/join_species/pallas_call | solution.py:441
Async XLA Ops:
  1.6 8.2 %collective-permute-start.1 = (f32[2,64,128]{2,1,0:T(8,128)S(1)}, f32[2,64,128]{2,1,0:T(8,128)S(1)}, u32[]{:S(2)}, u32[]{:S(2)}) collective-permute-start(f32[2,64,128]{2,1,0:T(8,128)S(1)} %get-tuple-element.14.refs_0_), channel_id=1, source_target_pairs={{0,16},{8,24},{16,0},{24,8},{1,17},{9,25},{17,1},{25,9},{2,18},{10... | collective-permute-start | bytes 196616 | tf_op jit(solution)/shard_map/ppermute | solution.py:357
  5.7 6.5 %collective-permute-start.2 = (f32[2,64,128]{2,1,0:T(8,128)S(1)}, f32[2,64,128]{2,1,0:T(8,128)S(1)}, u32[]{:S(2)}, u32[]{:S(2)}) collective-permute-start(f32[2,64,128]{2,1,0:T(8,128)S(1)} %get-tuple-element.15), channel_id=1, source_target_pairs={{0,24},{8,16},{16,8},{24,0},{1,25},{9,17},{17,9},{25,1},{2,26},{10... | collective-permute-start | bytes 196616 | tf_op jit(solution)/shard_map/ppermute | solution.py:357
  7.0 5.4 %collective-permute-start = (f32[2,64,128]{2,1,0:T(8,128)S(1)}, f32[2,64,128]{2,1,0:T(8,128)S(1)}, u32[]{:S(2)}, u32[]{:S(2)}) collective-permute-start(f32[2,64,128]{2,1,0:T(8,128)S(1)} %get-tuple-element.15), channel_id=1, source_target_pairs={{0,8},{8,0},{16,24},{24,16},{1,9},{9,1},{17,25},{25,17},{2,10},{10... | collective-permute-start | bytes 196616 | tf_op jit(solution)/shard_map/ppermute | solution.py:357
  12.7 8.1 %collective-permute-start.3 = (f32[64,128]{1,0:T(8,128)S(1)}, f32[64,128]{1,0:T(8,128)S(1)}, u32[]{:S(2)}, u32[]{:S(2)}) collective-permute-start(f32[64,128]{1,0:T(8,128)S(1)} %get-tuple-element.22), channel_id=1, source_target_pairs={{0,8},{8,0},{16,24},{24,16},{1,9},{9,1},{17,25},{25,17},{2,10},{10... | collective-permute-start | bytes 98312 | tf_op jit(solution)/shard_map/ppermute | solution.py:357

commit v18 on v10

--- a/solution.py
+++ b/solution.py
@@ -102,12 +102,13 @@
 
 def stack_kernel(forcing_hbm, previous_hbm, mine_ref, other_ref, sems):
     species = lax.axis_index("tm") % 2
-    pairs = (
-        (forcing_hbm.at[0, species], mine_ref.at[0]),
-        (previous_hbm.at[0, species], mine_ref.at[1]),
-        (forcing_hbm.at[0, 1 - species], other_ref.at[0]),
-        (previous_hbm.at[0, 1 - species], other_ref.at[1]),
-    )
+    half = mine_ref.shape[1] // 2
+    pairs = [
+        (source.at[0, part, rows], target.at[slot, rows])
+        for target, part in ((mine_ref, species), (other_ref, 1 - species))
+        for slot, source in enumerate((forcing_hbm, previous_hbm))
+        for rows in (pl.ds(0, half), pl.ds(half, half))
+    ]
     for copy in start_all(pairs, sems):
         copy.wait()
 
@@ -278,7 +279,7 @@
             give = jnp.where(me == n, steps[n ^ 1], give)
         own_ref[rows] = own
         give_ref[rows] = give
-    sum_ref[...] = jnp.broadcast_to(jnp.sum(total, axis=0, keepdims=True), sum_ref.shape)
+    sum_ref[...] = jnp.full(sum_ref.shape, jnp.sum(total), jnp.float32)
 
 
 def join_kernel(
@@ -292,7 +293,7 @@
     )
     copies[0].start()
     copies[1].start()
-    norm_ref[0, 0] = jnp.sqrt(jnp.sum(squares_ref[...]) / entry_count)
+    norm_ref[0, 0] = jnp.sqrt(jnp.sum(squares_ref[...], axis=0)[0, 0] / entry_count)
     copies[2].start()
     for copy in copies:
         copy.wait()
@@ -329,7 +330,7 @@
         ),
         in_specs=[outside] * 2,
         out_specs=[whole] * 2,
-        scratch_shapes=[pltpu.SemaphoreType.DMA((4,))],
+        scratch_shapes=[pltpu.SemaphoreType.DMA((8,))],
         compiler_params=alone,
         cost_estimate=pl.CostEstimate(flops=4000, bytes_accessed=500000, transcendentals=0),
         name="stack_arrays",

time: 21.3 us -> 21.5 us (level)
  no operation moved by 1% of the time
where the time goes in v18:
time: 21.5 us; the launch traced here: 21.1 us
  blocking collectives  7.27 us (34%)
  starting transfers between devices  6.5 us (30%)
  waiting for transfers between devices  3.43 us (16%)
  Pallas kernels  3.29 us (15%)
  between operations  0.66 us (3%)
    all_to_all x1, blocking collectives, shards(): lax.all_to_all(squares, ('tm', 'space'), 0, 0, axis_index_groups=groups,...  7.27 us
    ppermute x4, starting transfers between devices, exchange(): return lax.ppermute(value, axis, pairs)  6.5 us
    ppermute x4, waiting for transfers between devices, exchange(): return lax.ppermute(value, axis, pairs)  3.43 us
    pallas_call x1, Pallas kernels, shards(): pl.pallas_call(functools.partial(factor_kernel, length), out_shape=(pltpu...  1.3 us
    pallas_call x1, Pallas kernels, shards(): pl.pallas_call(stack_kernel, out_shape=(pltpu.VMEM((2, cells, lanes), jnp...  0.92 us
    pallas_call x1, Pallas kernels, shards(): pl.pallas_call(functools.partial(join_kernel, entry_count), out_shape=(ja...  0.67 us
  transfers between devices with their start and end apart: 4, of which 3 were waited for; matrix products, arithmetic and copies ran while one was open for 0% of the time, Pallas kernels for 6%

profile of v18, /device:TPU:0, one launch (start us, length us, event | category | flops | bytes accessed | tf_op | source)
XLA Modules:
  0.0 21.1 jit_solution(10364342507848418739)
XLA Ops:
  0.6 0.9 %stack_arrays.1 = (f32[2,64,128]{2,1,0:T(8,128)S(1)}, f32[2,64,128]{2,1,0:T(8,128)S(1)}) custom-call(f32[1,2,64,128]{3,2,1,0:T(8,128)} %forcing_hbm.1, f32[1,2,64,128]{3,2,1,0:T(8,128)} %previous_hbm.1), custom_call_target="tpu_custom_call" | custom-call | flops 4000 | bytes 500000 | tf_op jit(solution)/shard_map/stack_arrays/pallas_call | solution.py:325
  1.6 4.1 %collective-permute-start.1 = (f32[2,64,128]{2,1,0:T(8,128)S(1)}, f32[2,64,128]{2,1,0:T(8,128)S(1)}, u32[]{:S(2)}, u32[]{:S(2)}) collective-permute-start(f32[2,64,128]{2,1,0:T(8,128)S(1)} %get-tuple-element.12.refs_0_), channel_id=1, source_target_pairs={{0,16},{8,24},{16,0},{24,8},{1,17},{9,25},{17,1},{25,9},{2,18},{10... | collective-permute-start | bytes 196616 | tf_op jit(solution)/shard_map/ppermute | solution.py:304
  5.7 1.3 %collective-permute-start.2 = (f32[2,64,128]{2,1,0:T(8,128)S(1)}, f32[2,64,128]{2,1,0:T(8,128)S(1)}, u32[]{:S(2)}, u32[]{:S(2)}) collective-permute-start(f32[2,64,128]{2,1,0:T(8,128)S(1)} %get-tuple-element.13), channel_id=1, source_target_pairs={{0,24},{8,16},{16,8},{24,0},{1,25},{9,17},{17,9},{25,1},{2,26},{10... | collective-permute-start | bytes 196616 | tf_op jit(solution)/shard_map/ppermute | solution.py:304
  7.0 0.2 %collective-permute-start = (f32[2,64,128]{2,1,0:T(8,128)S(1)}, f32[2,64,128]{2,1,0:T(8,128)S(1)}, u32[]{:S(2)}, u32[]{:S(2)}) collective-permute-start(f32[2,64,128]{2,1,0:T(8,128)S(1)} %get-tuple-element.13), channel_id=1, source_target_pairs={{0,8},{8,0},{16,24},{24,16},{1,9},{9,1},{17,25},{25,17},{2,10},{10... | collective-permute-start | bytes 196616 | tf_op jit(solution)/shard_map/ppermute | solution.py:304
  7.2 1.3 %factor_lines.1 = (f32[4,6,64,128]{3,2,1,0:T(8,128)S(1)}, f32[4,3,64,128]{3,2,1,0:T(8,128)S(1)}, f32[64,128]{1,0:T(8,128)S(1)}) custom-call(f32[2,64,128]{2,1,0:T(8,128)} %initial_hbm.1, f32[2,8]{1,0:T(2,128)} %zones_hbm.1, f32[2]{0:T(128)} %drift_hbm.1, s32[1,128]{1,0:T(1,128)} %bitcast.3, s32[1,128]{1,0:T(1,128)} %bitcast.4, s32[64,128]{1,0:T(8,128)} %faces_hbm.1), custom_call_target="tpu_custom_call" | custom-call | flops 4000000 | bytes 3000000 | tf_op jit(solution)/shard_map/factor_lines/pallas_call | solution.py:341
  8.5 0.9 %collective-permute-done.1.refs_2_ = f32[2,64,128]{2,1,0:T(8,128)S(1)} collective-permute-done((f32[2,64,128]{2,1,0:T(8,128)S(1)}, f32[2,64,128]{2,1,0:T(8,128)S(1)}, u32[]{:S(2)}, u32[]{:S(2)}) %collective-permute-start.1) | collective-permute-done | bytes 65568 | tf_op jit(solution)/shard_map/ppermute | solution.py:304
  9.4 2.5 %collective-permute-done.2.refs_3_ = f32[2,64,128]{2,1,0:T(8,128)S(1)} collective-permute-done((f32[2,64,128]{2,1,0:T(8,128)S(1)}, f32[2,64,128]{2,1,0:T(8,128)S(1)}, u32[]{:S(2)}, u32[]{:S(2)}) %collective-permute-start.2) | collective-permute-done | bytes 65568 | tf_op jit(solution)/shard_map/ppermute | solution.py:304
  11.9 0.1 collective-permute-done.refs_1_
  12.0 0.4 %solve_lines.1 = (f32[64,128]{1,0:T(8,128)S(1)}, f32[64,128]{1,0:T(8,128)S(1)}, f32[16,1,128]{2,1,0:T(1,128)S(1)}) custom-call(f32[2,64,128]{2,1,0:T(8,128)S(1)} %get-tuple-element.12.refs_0_, f32[2,64,128]{2,1,0:T(8,128)S(1)} %collective-permute-done.refs_1_, f32[2,64,128]{2,1,0:T(8,128)S(1)} %collective-permute-done.1.refs_2_, ...), custom_call_target="tpu_custom_call" | custom-call | flops 4000000 | bytes 3000000 | tf_op jit(solution)/shard_map/solve_lines/pallas_call | solution.py:362
  12.4 0.8 %collective-permute-start.3 = (f32[64,128]{1,0:T(8,128)S(1)}, f32[64,128]{1,0:T(8,128)S(1)}, u32[]{:S(2)}, u32[]{:S(2)}) collective-permute-start(f32[64,128]{1,0:T(8,128)S(1)} %get-tuple-element.18), channel_id=1, source_target_pairs={{0,8},{8,0},{16,24},{24,16},{1,9},{9,1},{17,25},{25,17},{2,10},{10... | collective-permute-start | bytes 98312 | tf_op jit(solution)/shard_map/ppermute | solution.py:304
  13.2 7.3 %all_to_all.5.squares_ref = f32[16,1,128]{2,1,0:T(1,128)S(1)} all-to-all(f32[16,1,128]{2,1,0:T(1,128)S(1)} %get-tuple-element.19), channel_id=1, replica_groups={{15,2,4,6,8,10,12,14,3,5,7,9,11,13,1,0},{31,18,20,22,24,26,28,30,19,21,..., dimensions={0} | all-to-all | bytes 16384 | tf_op jit(solution)/shard_map/all_to_all | solution.py:379
  20.5 0.0 collective-permute-done.3.got_ref
  20.5 0.7 %join_species.1 = (f32[1,2,64,128]{3,2,1,0:T(8,128)}, f32[1,1]{1,0:T(1,128)}) custom-call(f32[64,128]{1,0:T(8,128)S(1)} %get-tuple-element.17.own_ref, f32[64,128]{1,0:T(8,128)S(1)} %collective-permute-done.3.got_ref, f32[16,1,128]{2,1,0:T(1,128)S(1)} %all_to_all.5.squares_ref), custom_call_target="tpu_custom_call" | custom-call | flops 4000 | bytes 100000 | tf_op jit(solution)/shard_map/join_species/pallas_call | solution.py:383
Async XLA Ops:
  1.6 7.9 %collective-permute-start.1 = (f32[2,64,128]{2,1,0:T(8,128)S(1)}, f32[2,64,128]{2,1,0:T(8,128)S(1)}, u32[]{:S(2)}, u32[]{:S(2)}) collective-permute-start(f32[2,64,128]{2,1,0:T(8,128)S(1)} %get-tuple-element.12.refs_0_), channel_id=1, source_target_pairs={{0,16},{8,24},{16,0},{24,8},{1,17},{9,25},{17,1},{25,9},{2,18},{10... | collective-permute-start | bytes 196616 | tf_op jit(solution)/shard_map/ppermute | solution.py:304
  5.7 6.2 %collective-permute-start.2 = (f32[2,64,128]{2,1,0:T(8,128)S(1)}, f32[2,64,128]{2,1,0:T(8,128)S(1)}, u32[]{:S(2)}, u32[]{:S(2)}) collective-permute-start(f32[2,64,128]{2,1,0:T(8,128)S(1)} %get-tuple-element.13), channel_id=1, source_target_pairs={{0,24},{8,16},{16,8},{24,0},{1,25},{9,17},{17,9},{25,1},{2,26},{10... | collective-permute-start | bytes 196616 | tf_op jit(solution)/shard_map/ppermute | solution.py:304
  7.0 5.0 %collective-permute-start = (f32[2,64,128]{2,1,0:T(8,128)S(1)}, f32[2,64,128]{2,1,0:T(8,128)S(1)}, u32[]{:S(2)}, u32[]{:S(2)}) collective-permute-start(f32[2,64,128]{2,1,0:T(8,128)S(1)} %get-tuple-element.13), channel_id=1, source_target_pairs={{0,8},{8,0},{16,24},{24,16},{1,9},{9,1},{17,25},{25,17},{2,10},{10... | collective-permute-start | bytes 196616 | tf_op jit(solution)/shard_map/ppermute | solution.py:304
  12.4 8.1 %collective-permute-start.3 = (f32[64,128]{1,0:T(8,128)S(1)}, f32[64,128]{1,0:T(8,128)S(1)}, u32[]{:S(2)}, u32[]{:S(2)}) collective-permute-start(f32[64,128]{1,0:T(8,128)S(1)} %get-tuple-element.18), channel_id=1, source_target_pairs={{0,8},{8,0},{16,24},{24,16},{1,9},{9,1},{17,25},{25,17},{2,10},{10... | collective-permute-start | bytes 98312 | tf_op jit(solution)/shard_map/ppermute | solution.py:304

commit v19 on v10

--- a/solution.py
+++ b/solution.py
@@ -90,6 +90,10 @@
     return term if total is None else total + term
 
 
+def species_of(step):
+    return (step ^ (step >> 1)) & 1
+
+
 def start_all(pairs, sems):
     copies = [
         pltpu.make_async_copy(source, target, sems.at[index])
@@ -101,7 +105,7 @@
 
 
 def stack_kernel(forcing_hbm, previous_hbm, mine_ref, other_ref, sems):
-    species = lax.axis_index("tm") % 2
+    species = species_of(lax.axis_index("tm"))
     pairs = (
         (forcing_hbm.at[0, species], mine_ref.at[0]),
         (previous_hbm.at[0, species], mine_ref.at[1]),
@@ -130,7 +134,7 @@
     faces_ref,
     sems,
 ):
-    species = lax.axis_index("tm") % 2
+    species = species_of(lax.axis_index("tm"))
     pairs = (
         (zones_hbm, zones_ref),
         (drift_hbm, drift_ref),
@@ -284,7 +288,7 @@
 def join_kernel(
     entry_count, own_ref, got_ref, squares_ref, new_hbm, norm_hbm, norm_ref, sems
 ):
-    species = lax.axis_index("tm") % 2
+    species = species_of(lax.axis_index("tm"))
     copies = (
         pltpu.make_async_copy(own_ref, new_hbm.at[0, species], sems.at[0]),
         pltpu.make_async_copy(got_ref, new_hbm.at[0, 1 - species], sems.at[1]),
@@ -336,7 +340,7 @@
     )(forcing, previous)
     stacks = [mine]
     for bits in range(1, length):
-        stacks.append(exchange(other if bits % 2 else mine, "tm", bits))
+        stacks.append(exchange(other if species_of(bits) else mine, "tm", bits))
     near, far, initial = pl.pallas_call(
         functools.partial(factor_kernel, length),
         out_shape=(

time: 21.3 us -> 21.7 us (1.019)
  starting transfers between devices: 6.5 us -> 6.9 us
  blocking collectives: 7.27 us -> 7.01 us
  waiting for transfers between devices: 3.43 us -> 3.66 us
    ppermute x4, starting transfers between devices: 6.5 us -> 6.9 us  [exchange(): return lax.ppermute(value, axis, pairs)]
    all_to_all x1, blocking collectives: 7.27 us -> 7.01 us  [shards(): lax.all_to_all(squares, ('tm', 'space'), 0, 0, axis_index_groups=groups,...]
    ppermute x4, waiting for transfers between devices: 3.43 us -> 3.66 us  [exchange(): return lax.ppermute(value, axis, pairs)]
  transfers between devices with their start and end apart: 4 -> 4, of which waited for: 3 -> 2; matrix products, arithmetic and copies ran while one was open for 0% -> 0% of each run, Pallas kernels for 6% -> 6%
where the time goes in v19:
time: 21.7 us; the launch traced here: 21.4 us
  blocking collectives  7.01 us (32%)
  starting transfers between devices  6.9 us (32%)
  waiting for transfers between devices  3.66 us (17%)
  Pallas kernels  3.15 us (15%)
  between operations  0.65 us (3%)
    all_to_all x1, blocking collectives, shards(): lax.all_to_all(squares, ('tm', 'space'), 0, 0, axis_index_groups=groups,...  7.01 us
    ppermute x4, starting transfers between devices, exchange(): return lax.ppermute(value, axis, pairs)  6.9 us
    ppermute x4, waiting for transfers between devices, exchange(): return lax.ppermute(value, axis, pairs)  3.66 us
    pallas_call x1, Pallas kernels, shards(): pl.pallas_call(functools.partial(factor_kernel, length), out_shape=(pltpu...  1.3 us
    pallas_call x1, Pallas kernels, shards(): pl.pallas_call(stack_kernel, out_shape=(pltpu.VMEM((2, cells, lanes), jnp...  0.85 us
    pallas_call x1, Pallas kernels, shards(): pl.pallas_call(functools.partial(join_kernel, entry_count), out_shape=(ja...  0.72 us
  transfers between devices with their start and end apart: 4, of which 2 were waited for; matrix products, arithmetic and copies ran while one was open for 0% of the time, Pallas kernels for 6%

profile of v19, /device:TPU:0, one launch (start us, length us, event | category | flops | bytes accessed | tf_op | source)
XLA Modules:
  0.0 21.4 jit_solution(1077989369737735829)
XLA Ops:
  0.6 0.9 %stack_arrays.1 = (f32[2,64,128]{2,1,0:T(8,128)S(1)}, f32[2,64,128]{2,1,0:T(8,128)S(1)}) custom-call(f32[1,2,64,128]{3,2,1,0:T(8,128)} %forcing_hbm.1, f32[1,2,64,128]{3,2,1,0:T(8,128)} %previous_hbm.1), custom_call_target="tpu_custom_call" | custom-call | flops 4000 | bytes 500000 | tf_op jit(solution)/shard_map/stack_arrays/pallas_call | solution.py:328
  1.5 5.1 %collective-permute-start.2 = (f32[2,64,128]{2,1,0:T(8,128)S(1)}, f32[2,64,128]{2,1,0:T(8,128)S(1)}, u32[]{:S(2)}, u32[]{:S(2)}) collective-permute-start(f32[2,64,128]{2,1,0:T(8,128)S(1)} %get-tuple-element.12.refs_0_), channel_id=1, source_target_pairs={{0,24},{8,16},{16,8},{24,0},{1,25},{9,17},{17,9},{25,1},{2,26},{10... | collective-permute-start | bytes 196616 | tf_op jit(solution)/shard_map/ppermute | solution.py:307
  6.6 0.0 collective-permute-start.1
  6.6 0.6 %collective-permute-start = (f32[2,64,128]{2,1,0:T(8,128)S(1)}, f32[2,64,128]{2,1,0:T(8,128)S(1)}, u32[]{:S(2)}, u32[]{:S(2)}) collective-permute-start(f32[2,64,128]{2,1,0:T(8,128)S(1)} %get-tuple-element.13), channel_id=1, source_target_pairs={{0,8},{8,0},{16,24},{24,16},{1,9},{9,1},{17,25},{25,17},{2,10},{10... | collective-permute-start | bytes 196616 | tf_op jit(solution)/shard_map/ppermute | solution.py:307
  7.2 1.3 %factor_lines.1 = (f32[4,6,64,128]{3,2,1,0:T(8,128)S(1)}, f32[4,3,64,128]{3,2,1,0:T(8,128)S(1)}, f32[64,128]{1,0:T(8,128)S(1)}) custom-call(f32[2,64,128]{2,1,0:T(8,128)} %initial_hbm.1, f32[2,8]{1,0:T(2,128)} %zones_hbm.1, f32[2]{0:T(128)} %drift_hbm.1, s32[1,128]{1,0:T(1,128)} %bitcast.3, s32[1,128]{1,0:T(1,128)} %bitcast.4, s32[64,128]{1,0:T(8,128)} %faces_hbm.1), custom_call_target="tpu_custom_call" | custom-call | flops 4000000 | bytes 3000000 | tf_op jit(solution)/shard_map/factor_lines/pallas_call | solution.py:344
  8.6 0.6 %collective-permute-done.2.refs_3_ = f32[2,64,128]{2,1,0:T(8,128)S(1)} collective-permute-done((f32[2,64,128]{2,1,0:T(8,128)S(1)}, f32[2,64,128]{2,1,0:T(8,128)S(1)}, u32[]{:S(2)}, u32[]{:S(2)}) %collective-permute-start.2) | collective-permute-done | bytes 65568 | tf_op jit(solution)/shard_map/ppermute | solution.py:307
  9.2 3.0 %collective-permute-done.1.refs_2_ = f32[2,64,128]{2,1,0:T(8,128)S(1)} collective-permute-done((f32[2,64,128]{2,1,0:T(8,128)S(1)}, f32[2,64,128]{2,1,0:T(8,128)S(1)}, u32[]{:S(2)}, u32[]{:S(2)}) %collective-permute-start.1) | collective-permute-done | bytes 65568 | tf_op jit(solution)/shard_map/ppermute | solution.py:307
  12.2 0.0 collective-permute-done.refs_1_
  12.2 0.3 %solve_lines.1 = (f32[64,128]{1,0:T(8,128)S(1)}, f32[64,128]{1,0:T(8,128)S(1)}, f32[16,1,128]{2,1,0:T(1,128)S(1)}) custom-call(f32[2,64,128]{2,1,0:T(8,128)S(1)} %get-tuple-element.12.refs_0_, f32[2,64,128]{2,1,0:T(8,128)S(1)} %collective-permute-done.refs_1_, f32[2,64,128]{2,1,0:T(8,128)S(1)} %collective-permute-done.1.refs_2_, ...), custom_call_target="tpu_custom_call" | custom-call | flops 4000000 | bytes 3000000 | tf_op jit(solution)/shard_map/solve_lines/pallas_call | solution.py:365
  12.5 1.1 %collective-permute-start.3 = (f32[64,128]{1,0:T(8,128)S(1)}, f32[64,128]{1,0:T(8,128)S(1)}, u32[]{:S(2)}, u32[]{:S(2)}) collective-permute-start(f32[64,128]{1,0:T(8,128)S(1)} %get-tuple-element.18), channel_id=1, source_target_pairs={{0,8},{8,0},{16,24},{24,16},{1,9},{9,1},{17,25},{25,17},{2,10},{10... | collective-permute-start | bytes 98312 | tf_op jit(solution)/shard_map/ppermute | solution.py:307
  13.6 7.0 %all_to_all.5.squares_ref = f32[16,1,128]{2,1,0:T(1,128)S(1)} all-to-all(f32[16,1,128]{2,1,0:T(1,128)S(1)} %get-tuple-element.19), channel_id=1, replica_groups={{15,2,4,6,8,10,12,14,3,5,7,9,11,13,1,0},{31,18,20,22,24,26,28,30,19,21,..., dimensions={0} | all-to-all | bytes 16384 | tf_op jit(solution)/shard_map/all_to_all | solution.py:382
  20.6 0.0 collective-permute-done.3.got_ref
  20.7 0.7 %join_species.1 = (f32[1,2,64,128]{3,2,1,0:T(8,128)}, f32[1,1]{1,0:T(1,128)}) custom-call(f32[64,128]{1,0:T(8,128)S(1)} %get-tuple-element.17.own_ref, f32[64,128]{1,0:T(8,128)S(1)} %collective-permute-done.3.got_ref, f32[16,1,128]{2,1,0:T(1,128)S(1)} %all_to_all.5.squares_ref), custom_call_target="tpu_custom_call" | custom-call | flops 4000 | bytes 100000 | tf_op jit(solution)/shard_map/join_species/pallas_call | solution.py:386
Async XLA Ops:
  1.5 7.7 %collective-permute-start.2 = (f32[2,64,128]{2,1,0:T(8,128)S(1)}, f32[2,64,128]{2,1,0:T(8,128)S(1)}, u32[]{:S(2)}, u32[]{:S(2)}) collective-permute-start(f32[2,64,128]{2,1,0:T(8,128)S(1)} %get-tuple-element.12.refs_0_), channel_id=1, source_target_pairs={{0,24},{8,16},{16,8},{24,0},{1,25},{9,17},{17,9},{25,1},{2,26},{10... | collective-permute-start | bytes 196616 | tf_op jit(solution)/shard_map/ppermute | solution.py:307
  6.6 5.6 %collective-permute-start.1 = (f32[2,64,128]{2,1,0:T(8,128)S(1)}, f32[2,64,128]{2,1,0:T(8,128)S(1)}, u32[]{:S(2)}, u32[]{:S(2)}) collective-permute-start(f32[2,64,128]{2,1,0:T(8,128)S(1)} %get-tuple-element.13), channel_id=1, source_target_pairs={{0,16},{8,24},{16,0},{24,8},{1,17},{9,25},{17,1},{25,9},{2,18},{10... | collective-permute-start | bytes 196616 | tf_op jit(solution)/shard_map/ppermute | solution.py:307
  6.6 5.6 %collective-permute-start = (f32[2,64,128]{2,1,0:T(8,128)S(1)}, f32[2,64,128]{2,1,0:T(8,128)S(1)}, u32[]{:S(2)}, u32[]{:S(2)}) collective-permute-start(f32[2,64,128]{2,1,0:T(8,128)S(1)} %get-tuple-element.13), channel_id=1, source_target_pairs={{0,8},{8,0},{16,24},{24,16},{1,9},{9,1},{17,25},{25,17},{2,10},{10... | collective-permute-start | bytes 196616 | tf_op jit(solution)/shard_map/ppermute | solution.py:307
  12.5 8.2 %collective-permute-start.3 = (f32[64,128]{1,0:T(8,128)S(1)}, f32[64,128]{1,0:T(8,128)S(1)}, u32[]{:S(2)}, u32[]{:S(2)}) collective-permute-start(f32[64,128]{1,0:T(8,128)S(1)} %get-tuple-element.18), channel_id=1, source_target_pairs={{0,8},{8,0},{16,24},{24,16},{1,9},{9,1},{17,25},{25,17},{2,10},{10... | collective-permute-start | bytes 98312 | tf_op jit(solution)/shard_map/ppermute | solution.py:307

commit v20 on v10

--- a/solution.py
+++ b/solution.py
@@ -207,7 +207,7 @@
 
 
 def sweep_kernel(length, *refs):
-    stacks = refs[:length]
+    stacks = [refs[0], refs[length - 1], *refs[1 : length - 1]]
     initial_ref, near_ref, far_ref, own_ref, give_ref, sum_ref = refs[length:]
     cells, lanes = initial_ref.shape
     log_alpha = math.log(alpha_corner)
@@ -370,7 +370,7 @@
         compiler_params=params,
         cost_estimate=pl.CostEstimate(flops=4000000, bytes_accessed=3000000, transcendentals=0),
         name="solve_lines",
-    )(*stacks, initial, near, far)
+    )(stacks[0], *stacks[2:], stacks[1], initial, near, far)
     got = exchange(give, "tm", 1)
     last = 2 * space - 1
     order = [last, *range(2, last, 2), *range(3, last, 2), 1, 0]

time: 21.3 us -> 22.6 us (1.061)
  waiting for transfers between devices: 3.43 us -> 4.75 us
  starting transfers between devices: 6.5 us -> 5.75 us
  blocking collectives: 7.27 us -> 8.01 us
    ppermute x4, waiting for transfers between devices: 3.43 us -> 4.75 us  [exchange(): return lax.ppermute(value, axis, pairs)]
    ppermute x4, starting transfers between devices: 6.5 us -> 5.75 us  [exchange(): return lax.ppermute(value, axis, pairs)]
    all_to_all x1, blocking collectives: 7.27 us -> 8.01 us  [shards(): lax.all_to_all(squares, ('tm', 'space'), 0, 0, axis_index_groups=groups,...]
where the time goes in v20:
time: 22.6 us; the launch traced here: 22.3 us
  blocking collectives  8.01 us (35%)
  starting transfers between devices  5.75 us (25%)
  waiting for transfers between devices  4.75 us (21%)
  Pallas kernels  3.15 us (14%)
  between operations  0.66 us (3%)
    all_to_all x1, blocking collectives, shards(): lax.all_to_all(squares, ('tm', 'space'), 0, 0, axis_index_groups=groups,...  8.01 us
    ppermute x4, starting transfers between devices, exchange(): return lax.ppermute(value, axis, pairs)  5.75 us
    ppermute x4, waiting for transfers between devices, exchange(): return lax.ppermute(value, axis, pairs)  4.75 us
    pallas_call x1, Pallas kernels, shards(): pl.pallas_call(functools.partial(factor_kernel, length), out_shape=(pltpu...  1.3 us
    pallas_call x1, Pallas kernels, shards(): pl.pallas_call(stack_kernel, out_shape=(pltpu.VMEM((2, cells, lanes), jnp...  0.86 us
    pallas_call x1, Pallas kernels, shards(): pl.pallas_call(functools.partial(join_kernel, entry_count), out_shape=(ja...  0.72 us
  transfers between devices with their start and end apart: 4, of which 3 were waited for; matrix products, arithmetic and copies ran while one was open for 0% of the time, Pallas kernels for 6%

profile of v20, /device:TPU:0, one launch (start us, length us, event | category | flops | bytes accessed | tf_op | source)
XLA Modules:
  0.0 22.3 jit_solution(14433755997482007349)
XLA Ops:
  0.6 0.9 %stack_arrays.1 = (f32[2,64,128]{2,1,0:T(8,128)S(1)}, f32[2,64,128]{2,1,0:T(8,128)S(1)}) custom-call(f32[1,2,64,128]{3,2,1,0:T(8,128)} %forcing_hbm.1, f32[1,2,64,128]{3,2,1,0:T(8,128)} %previous_hbm.1), custom_call_target="tpu_custom_call" | custom-call | flops 4000 | bytes 500000 | tf_op jit(solution)/shard_map/stack_arrays/pallas_call | solution.py:324
  1.5 4.1 %collective-permute-start = (f32[2,64,128]{2,1,0:T(8,128)S(1)}, f32[2,64,128]{2,1,0:T(8,128)S(1)}, u32[]{:S(2)}, u32[]{:S(2)}) collective-permute-start(f32[2,64,128]{2,1,0:T(8,128)S(1)} %get-tuple-element.12.refs_0_), channel_id=1, source_target_pairs={{0,16},{8,24},{16,0},{24,8},{1,17},{9,25},{17,1},{25,9},{2,18},{10... | collective-permute-start | bytes 196616 | tf_op jit(solution)/shard_map/ppermute | solution.py:303
  5.6 1.6 %collective-permute-start.2 = (f32[2,64,128]{2,1,0:T(8,128)S(1)}, f32[2,64,128]{2,1,0:T(8,128)S(1)}, u32[]{:S(2)}, u32[]{:S(2)}) collective-permute-start(f32[2,64,128]{2,1,0:T(8,128)S(1)} %get-tuple-element.13), channel_id=1, source_target_pairs={{0,8},{8,0},{16,24},{24,16},{1,9},{9,1},{17,25},{25,17},{2,10},{10... | collective-permute-start | bytes 196616 | tf_op jit(solution)/shard_map/ppermute | solution.py:303
  7.2 0.0 collective-permute-start.1
  7.2 1.3 %factor_lines.1 = (f32[4,6,64,128]{3,2,1,0:T(8,128)S(1)}, f32[4,3,64,128]{3,2,1,0:T(8,128)S(1)}, f32[64,128]{1,0:T(8,128)S(1)}) custom-call(f32[2,64,128]{2,1,0:T(8,128)} %initial_hbm.1, f32[2,8]{1,0:T(2,128)} %zones_hbm.1, f32[2]{0:T(128)} %drift_hbm.1, s32[1,128]{1,0:T(1,128)} %bitcast.3, s32[1,128]{1,0:T(1,128)} %bitcast.4, s32[64,128]{1,0:T(8,128)} %faces_hbm.1), custom_call_target="tpu_custom_call" | custom-call | flops 4000000 | bytes 3000000 | tf_op jit(solution)/shard_map/factor_lines/pallas_call | solution.py:340
  8.5 0.2 collective-permute-done.refs_1_
  8.6 1.2 %collective-permute-done.2.refs_3_ = f32[2,64,128]{2,1,0:T(8,128)S(1)} collective-permute-done((f32[2,64,128]{2,1,0:T(8,128)S(1)}, f32[2,64,128]{2,1,0:T(8,128)S(1)}, u32[]{:S(2)}, u32[]{:S(2)}) %collective-permute-start.2) | collective-permute-done | bytes 65568 | tf_op jit(solution)/shard_map/ppermute | solution.py:303
  9.9 3.4 %collective-permute-done.1.refs_2_ = f32[2,64,128]{2,1,0:T(8,128)S(1)} collective-permute-done((f32[2,64,128]{2,1,0:T(8,128)S(1)}, f32[2,64,128]{2,1,0:T(8,128)S(1)}, u32[]{:S(2)}, u32[]{:S(2)}) %collective-permute-start.1) | collective-permute-done | bytes 65568 | tf_op jit(solution)/shard_map/ppermute | solution.py:303
  13.2 0.3 %solve_lines.1 = (f32[64,128]{1,0:T(8,128)S(1)}, f32[64,128]{1,0:T(8,128)S(1)}, f32[16,1,128]{2,1,0:T(1,128)S(1)}) custom-call(f32[2,64,128]{2,1,0:T(8,128)S(1)} %get-tuple-element.12.refs_0_, f32[2,64,128]{2,1,0:T(8,128)S(1)} %collective-permute-done.refs_1_, f32[2,64,128]{2,1,0:T(8,128)S(1)} %collective-permute-done.1.refs_2_, ...), custom_call_target="tpu_custom_call" | custom-call | flops 4000000 | bytes 3000000 | tf_op jit(solution)/shard_map/solve_lines/pallas_call | solution.py:361
  13.5 0.1 collective-permute-start.3
  13.6 8.0 %all_to_all.5.squares_ref = f32[16,1,128]{2,1,0:T(1,128)S(1)} all-to-all(f32[16,1,128]{2,1,0:T(1,128)S(1)} %get-tuple-element.19), channel_id=1, replica_groups={{15,2,4,6,8,10,12,14,3,5,7,9,11,13,1,0},{31,18,20,22,24,26,28,30,19,21,..., dimensions={0} | all-to-all | bytes 16384 | tf_op jit(solution)/shard_map/all_to_all | solution.py:378
  21.6 0.0 collective-permute-done.3.got_ref
  21.6 0.7 %join_species.1 = (f32[1,2,64,128]{3,2,1,0:T(8,128)}, f32[1,1]{1,0:T(1,128)}) custom-call(f32[64,128]{1,0:T(8,128)S(1)} %get-tuple-element.17.own_ref, f32[64,128]{1,0:T(8,128)S(1)} %collective-permute-done.3.got_ref, f32[16,1,128]{2,1,0:T(1,128)S(1)} %all_to_all.5.squares_ref), custom_call_target="tpu_custom_call" | custom-call | flops 4000 | bytes 100000 | tf_op jit(solution)/shard_map/join_species/pallas_call | solution.py:382
Async XLA Ops:
  1.5 7.2 %collective-permute-start = (f32[2,64,128]{2,1,0:T(8,128)S(1)}, f32[2,64,128]{2,1,0:T(8,128)S(1)}, u32[]{:S(2)}, u32[]{:S(2)}) collective-permute-start(f32[2,64,128]{2,1,0:T(8,128)S(1)} %get-tuple-element.12.refs_0_), channel_id=1, source_target_pairs={{0,16},{8,24},{16,0},{24,8},{1,17},{9,25},{17,1},{25,9},{2,18},{10... | collective-permute-start | bytes 196616 | tf_op jit(solution)/shard_map/ppermute | solution.py:303
  5.6 4.3 %collective-permute-start.2 = (f32[2,64,128]{2,1,0:T(8,128)S(1)}, f32[2,64,128]{2,1,0:T(8,128)S(1)}, u32[]{:S(2)}, u32[]{:S(2)}) collective-permute-start(f32[2,64,128]{2,1,0:T(8,128)S(1)} %get-tuple-element.13), channel_id=1, source_target_pairs={{0,8},{8,0},{16,24},{24,16},{1,9},{9,1},{17,25},{25,17},{2,10},{10... | collective-permute-start | bytes 196616 | tf_op jit(solution)/shard_map/ppermute | solution.py:303
  7.2 6.1 %collective-permute-start.1 = (f32[2,64,128]{2,1,0:T(8,128)S(1)}, f32[2,64,128]{2,1,0:T(8,128)S(1)}, u32[]{:S(2)}, u32[]{:S(2)}) collective-permute-start(f32[2,64,128]{2,1,0:T(8,128)S(1)} %get-tuple-element.13), channel_id=1, source_target_pairs={{0,24},{8,16},{16,8},{24,0},{1,25},{9,17},{17,9},{25,1},{2,26},{10... | collective-permute-start | bytes 196616 | tf_op jit(solution)/shard_map/ppermute | solution.py:303
  13.5 8.1 %collective-permute-start.3 = (f32[64,128]{1,0:T(8,128)S(1)}, f32[64,128]{1,0:T(8,128)S(1)}, u32[]{:S(2)}, u32[]{:S(2)}) collective-permute-start(f32[64,128]{1,0:T(8,128)S(1)} %get-tuple-element.18), channel_id=1, source_target_pairs={{0,8},{8,0},{16,24},{24,16},{1,9},{9,1},{17,25},{25,17},{2,10},{10... | collective-permute-start | bytes 98312 | tf_op jit(solution)/shard_map/ppermute | solution.py:303

commit v21 on v16

--- a/solution.py
+++ b/solution.py
@@ -374,10 +374,13 @@
     last = 2 * space - 1
     squares = squares + exchange(squares, "space", 1)
     got = exchange(give, "tm", 1)
+    first = [space * 2 - 1 - 2 * chip for chip in range(space - 1)] + [0]
+    first[space // 2] = space - 2
+    second = [space - 1] + [index ^ 1 for index in first if index != space - 2]
     groups = [
-        [step * space + index for index in (*reversed(range(3 - core, 2 * space, 2)), core)]
+        [step * space + index for index in order]
         for step in range(0, length, 2)
-        for core in range(2)
+        for order in (first, second)
     ]
     squares = lax.all_to_all(
         jnp.broadcast_to(squares[None], (space,) + squares.shape),

time: 21.3 us -> 21.7 us (1.019)
  the two profiles are of different devices: /device:TPU:1 before, /device:TPU:0 now
where the time goes in v21:
time: 21.7 us; the launch traced here: 21.4 us
  blocking collectives  7.28 us (34%)
  starting transfers between devices  6.57 us (30%)
  waiting for transfers between devices  3.71 us (17%)
  Pallas kernels  3.14 us (14%)
  between operations  0.66 us (3%)
    all_to_all x1, blocking collectives, shards(): lax.all_to_all(jnp.broadcast_to(squares[None], (space,) + squares.shape),...  7.28 us
    ppermute x5, starting transfers between devices, exchange(): return lax.ppermute(value, axis, pairs)  6.57 us
    ppermute x5, waiting for transfers between devices, exchange(): return lax.ppermute(value, axis, pairs)  3.71 us
    pallas_call x1, Pallas kernels, shards(): pl.pallas_call(functools.partial(factor_kernel, length), out_shape=(pltpu...  1.3 us
    pallas_call x1, Pallas kernels, shards(): pl.pallas_call(stack_kernel, out_shape=(pltpu.VMEM((2, cells, lanes), jnp...  0.86 us
    pallas_call x1, Pallas kernels, shards(): pl.pallas_call(functools.partial(join_kernel, entry_count), out_shape=(ja...  0.71 us
  transfers between devices with their start and end apart: 5, of which 4 were waited for; matrix products, arithmetic and copies ran while one was open for 0% of the time, Pallas kernels for 6%

profile of v21, /device:TPU:0, one launch (start us, length us, event | category | flops | bytes accessed | tf_op | source)
XLA Modules:
  0.0 21.4 jit_solution(8767173011534249285)
XLA Ops:
  0.6 0.9 %stack_arrays.1 = (f32[2,64,128]{2,1,0:T(8,128)S(1)}, f32[2,64,128]{2,1,0:T(8,128)S(1)}) custom-call(f32[1,2,64,128]{3,2,1,0:T(8,128)} %forcing_hbm.1, f32[1,2,64,128]{3,2,1,0:T(8,128)} %previous_hbm.1), custom_call_target="tpu_custom_call" | custom-call | flops 4000 | bytes 500000 | tf_op jit(solution)/shard_map/stack_arrays/pallas_call | solution.py:324
  1.5 4.1 %collective-permute-start.1 = (f32[2,64,128]{2,1,0:T(8,128)S(1)}, f32[2,64,128]{2,1,0:T(8,128)S(1)}, u32[]{:S(2)}, u32[]{:S(2)}) collective-permute-start(f32[2,64,128]{2,1,0:T(8,128)S(1)} %get-tuple-element.12.refs_0_), channel_id=1, source_target_pairs={{0,16},{8,24},{16,0},{24,8},{1,17},{9,25},{17,1},{25,9},{2,18},{10... | collective-permute-start | bytes 196616 | tf_op jit(solution)/shard_map/ppermute | solution.py:303
  5.6 1.3 %collective-permute-start.2 = (f32[2,64,128]{2,1,0:T(8,128)S(1)}, f32[2,64,128]{2,1,0:T(8,128)S(1)}, u32[]{:S(2)}, u32[]{:S(2)}) collective-permute-start(f32[2,64,128]{2,1,0:T(8,128)S(1)} %get-tuple-element.13), channel_id=1, source_target_pairs={{0,24},{8,16},{16,8},{24,0},{1,25},{9,17},{17,9},{25,1},{2,26},{10... | collective-permute-start | bytes 196616 | tf_op jit(solution)/shard_map/ppermute | solution.py:303
  6.9 0.2 %collective-permute-start = (f32[2,64,128]{2,1,0:T(8,128)S(1)}, f32[2,64,128]{2,1,0:T(8,128)S(1)}, u32[]{:S(2)}, u32[]{:S(2)}) collective-permute-start(f32[2,64,128]{2,1,0:T(8,128)S(1)} %get-tuple-element.13), channel_id=1, source_target_pairs={{0,8},{8,0},{16,24},{24,16},{1,9},{9,1},{17,25},{25,17},{2,10},{10... | collective-permute-start | bytes 196616 | tf_op jit(solution)/shard_map/ppermute | solution.py:303
  7.2 1.3 %factor_lines.1 = (f32[4,6,64,128]{3,2,1,0:T(8,128)S(1)}, f32[4,3,64,128]{3,2,1,0:T(8,128)S(1)}, f32[64,128]{1,0:T(8,128)S(1)}) custom-call(f32[2,64,128]{2,1,0:T(8,128)} %initial_hbm.1, f32[2,8]{1,0:T(2,128)} %zones_hbm.1, f32[2]{0:T(128)} %drift_hbm.1, s32[1,128]{1,0:T(1,128)} %bitcast.5, s32[1,128]{1,0:T(1,128)} %bitcast.6, s32[64,128]{1,0:T(8,128)} %faces_hbm.1), custom_call_target="tpu_custom_call" | custom-call | flops 4000000 | bytes 3000000 | tf_op jit(solution)/shard_map/factor_lines/pallas_call | solution.py:340
  8.5 0.9 %collective-permute-done.1.refs_2_ = f32[2,64,128]{2,1,0:T(8,128)S(1)} collective-permute-done((f32[2,64,128]{2,1,0:T(8,128)S(1)}, f32[2,64,128]{2,1,0:T(8,128)S(1)}, u32[]{:S(2)}, u32[]{:S(2)}) %collective-permute-start.1) | collective-permute-done | bytes 65568 | tf_op jit(solution)/shard_map/ppermute | solution.py:303
  9.4 2.5 %collective-permute-done.2.refs_3_ = f32[2,64,128]{2,1,0:T(8,128)S(1)} collective-permute-done((f32[2,64,128]{2,1,0:T(8,128)S(1)}, f32[2,64,128]{2,1,0:T(8,128)S(1)}, u32[]{:S(2)}, u32[]{:S(2)}) %collective-permute-start.2) | collective-permute-done | bytes 65568 | tf_op jit(solution)/shard_map/ppermute | solution.py:303
  11.8 0.1 collective-permute-done.refs_1_
  11.9 0.3 %solve_lines.1 = (f32[64,128]{1,0:T(8,128)S(1)}, f32[64,128]{1,0:T(8,128)S(1)}, f32[1,128]{1,0:T(1,128)S(1)}) custom-call(f32[2,64,128]{2,1,0:T(8,128)S(1)} %get-tuple-element.12.refs_0_, f32[2,64,128]{2,1,0:T(8,128)S(1)} %collective-permute-done.refs_1_, f32[2,64,128]{2,1,0:T(8,128)S(1)} %collective-permute-done.1.refs_2_, ...), custom_call_target="tpu_custom_call" | custom-call | flops 4000000 | bytes 3000000 | tf_op jit(solution)/shard_map/solve_lines/pallas_call | solution.py:361
  12.2 0.1 collective-permute-start.4
  12.3 0.8 %collective-permute-start.3 = (f32[64,128]{1,0:T(8,128)S(1)}, f32[64,128]{1,0:T(8,128)S(1)}, u32[]{:S(2)}, u32[]{:S(2)}) collective-permute-start(f32[64,128]{1,0:T(8,128)S(1)} %get-tuple-element.18), channel_id=1, source_target_pairs={{0,8},{8,0},{16,24},{24,16},{1,9},{9,1},{17,25},{25,17},{2,10},{10... | collective-permute-start | bytes 98312 | tf_op jit(solution)/shard_map/ppermute | solution.py:303
  13.1 0.3 %collective-permute-done.4 = f32[1,128]{1,0:T(1,128)S(1)} collective-permute-done((f32[1,128]{1,0:T(1,128)S(1)}, f32[1,128]{1,0:T(1,128)S(1)}, u32[]{:S(2)}, u32[]{:S(2)}) %collective-permute-start.4) | collective-permute-done | bytes 544 | tf_op jit(solution)/shard_map/ppermute | solution.py:303
  13.4 7.3 %all_to_all.5.squares_ref = f32[8,1,128]{2,1,0:T(1,128)S(1)} all-to-all(f32[8,1,128]{2,1,0:T(1,128)S(1)} %broadcast_in_dim.17), channel_id=1, replica_groups={{15,13,11,9,6,5,3,0},{7,14,12,10,8,4,2,1},{31,29,27,25,22,21,19,16},{23..., dimensions={0} | all-to-all | bytes 8192 | tf_op jit(solution)/shard_map/all_to_all | solution.py:385
  20.7 0.0 collective-permute-done.3.got_ref
  20.7 0.7 %join_species.1 = (f32[1,2,64,128]{3,2,1,0:T(8,128)}, f32[1,1]{1,0:T(1,128)}) custom-call(f32[64,128]{1,0:T(8,128)S(1)} %get-tuple-element.17.own_ref, f32[64,128]{1,0:T(8,128)S(1)} %collective-permute-done.3.got_ref, f32[8,1,128]{2,1,0:T(1,128)S(1)} %all_to_all.5.squares_ref), custom_call_target="tpu_custom_call" | custom-call | flops 4000 | bytes 100000 | tf_op jit(solution)/shard_map/join_species/pallas_call | solution.py:394
  (2 shorter events, 0.0 us)
Async XLA Ops:
  1.5 7.9 %collective-permute-start.1 = (f32[2,64,128]{2,1,0:T(8,128)S(1)}, f32[2,64,128]{2,1,0:T(8,128)S(1)}, u32[]{:S(2)}, u32[]{:S(2)}) collective-permute-start(f32[2,64,128]{2,1,0:T(8,128)S(1)} %get-tuple-element.12.refs_0_), channel_id=1, source_target_pairs={{0,16},{8,24},{16,0},{24,8},{1,17},{9,25},{17,1},{25,9},{2,18},{10... | collective-permute-start | bytes 196616 | tf_op jit(solution)/shard_map/ppermute | solution.py:303
  5.6 6.2 %collective-permute-start.2 = (f32[2,64,128]{2,1,0:T(8,128)S(1)}, f32[2,64,128]{2,1,0:T(8,128)S(1)}, u32[]{:S(2)}, u32[]{:S(2)}) collective-permute-start(f32[2,64,128]{2,1,0:T(8,128)S(1)} %get-tuple-element.13), channel_id=1, source_target_pairs={{0,24},{8,16},{16,8},{24,0},{1,25},{9,17},{17,9},{25,1},{2,26},{10... | collective-permute-start | bytes 196616 | tf_op jit(solution)/shard_map/ppermute | solution.py:303
  6.9 5.0 %collective-permute-start = (f32[2,64,128]{2,1,0:T(8,128)S(1)}, f32[2,64,128]{2,1,0:T(8,128)S(1)}, u32[]{:S(2)}, u32[]{:S(2)}) collective-permute-start(f32[2,64,128]{2,1,0:T(8,128)S(1)} %get-tuple-element.13), channel_id=1, source_target_pairs={{0,8},{8,0},{16,24},{24,16},{1,9},{9,1},{17,25},{25,17},{2,10},{10... | collective-permute-start | bytes 196616 | tf_op jit(solution)/shard_map/ppermute | solution.py:303
  12.2 1.2 %collective-permute-start.4 = (f32[1,128]{1,0:T(1,128)S(1)}, f32[1,128]{1,0:T(1,128)S(1)}, u32[]{:S(2)}, u32[]{:S(2)}) collective-permute-start(f32[1,128]{1,0:T(1,128)S(1)} %get-tuple-element.19), channel_id=1, source_target_pairs={{0,1},{1,0},{2,3},{3,2},{4,5},{5,4},{6,7},{7,6},{8,9},{9,8},{10,11... | collective-permute-start | bytes 1544 | tf_op jit(solution)/shard_map/ppermute | solution.py:303
  12.3 8.4 %collective-permute-start.3 = (f32[64,128]{1,0:T(8,128)S(1)}, f32[64,128]{1,0:T(8,128)S(1)}, u32[]{:S(2)}, u32[]{:S(2)}) collective-permute-start(f32[64,128]{1,0:T(8,128)S(1)} %get-tuple-element.18), channel_id=1, source_target_pairs={{0,8},{8,0},{16,24},{24,16},{1,9},{9,1},{17,25},{25,17},{2,10},{10... | collective-permute-start | bytes 98312 | tf_op jit(solution)/shard_map/ppermute | solution.py:303

commit v22 on v10

--- a/solution.py
+++ b/solution.py
@@ -278,7 +278,7 @@
             give = jnp.where(me == n, steps[n ^ 1], give)
         own_ref[rows] = own
         give_ref[rows] = give
-    sum_ref[...] = jnp.broadcast_to(jnp.sum(total, axis=0, keepdims=True), sum_ref.shape)
+    sum_ref[...] = jnp.broadcast_to(total[None], sum_ref.shape)
 
 
 def join_kernel(
@@ -292,7 +292,7 @@
     )
     copies[0].start()
     copies[1].start()
-    norm_ref[0, 0] = jnp.sqrt(jnp.sum(squares_ref[...]) / entry_count)
+    norm_ref[0, 0] = jnp.sqrt(jnp.sum(jnp.sum(squares_ref[...], axis=0)) / entry_count)
     copies[2].start()
     for copy in copies:
         copy.wait()
@@ -363,7 +363,7 @@
         out_shape=(
             pltpu.VMEM((cells, lanes), jnp.float32),
             pltpu.VMEM((cells, lanes), jnp.float32),
-            pltpu.VMEM((2 * space, 1, lanes), jnp.float32),
+            pltpu.VMEM((2 * space, tile, lanes), jnp.float32),
         ),
         in_specs=[whole] * (length + 3),
         out_specs=[whole] * 3,

time: 21.3 us -> 23.5 us (1.10)
  blocking collectives: 7.27 us -> 0 us
  starting transfers between devices: 6.5 us -> 11.8 us
  waiting for transfers between devices: 3.43 us -> 6.88 us
  Pallas kernels: 3.15 us -> 3.78 us
    all_to_all x1 -> x0, blocking collectives: 7.27 us -> none  [shards(): lax.all_to_all(squares, ('tm', 'space'), 0, 0, axis_index_groups=groups,...]
    all_to_all x0 -> x1, starting transfers between devices: none -> 5.7 us  [shards(): lax.all_to_all(squares, ('tm', 'space'), 0, 0, axis_index_groups=groups,...]
    ppermute x4, waiting for transfers between devices: 3.43 us -> 6.88 us  [exchange(): return lax.ppermute(value, axis, pairs)]
    pallas_call x1, Pallas kernels: 0.28 us -> 0.9 us  [shards(): pl.pallas_call(functools.partial(sweep_kernel, length), out_shape=(pltpu....]
    ppermute x4, starting transfers between devices: 6.5 us -> 6.14 us  [exchange(): return lax.ppermute(value, axis, pairs)]
  transfers between devices with their start and end apart: 4 -> 5, of which waited for: 3 -> 4; matrix products, arithmetic and copies ran while one was open for 0% -> 0% of each run, Pallas kernels for 6% -> 6%
where the time goes in v22:
time: 23.5 us; the launch traced here: 23.2 us
  starting transfers between devices  11.8 us (50%)
  waiting for transfers between devices  6.88 us (29%)
  Pallas kernels  3.78 us (16%)
  between operations  0.65 us (3%)
    ppermute x4, waiting for transfers between devices, exchange(): return lax.ppermute(value, axis, pairs)  6.88 us
    ppermute x4, starting transfers between devices, exchange(): return lax.ppermute(value, axis, pairs)  6.14 us
    all_to_all x1, starting transfers between devices, shards(): lax.all_to_all(squares, ('tm', 'space'), 0, 0, axis_index_groups=groups,...  5.7 us
    pallas_call x1, Pallas kernels, shards(): pl.pallas_call(functools.partial(factor_kernel, length), out_shape=(pltpu...  1.3 us
    pallas_call x1, Pallas kernels, shards(): pl.pallas_call(functools.partial(sweep_kernel, length), out_shape=(pltpu....  0.9 us
    pallas_call x1, Pallas kernels, shards(): pl.pallas_call(stack_kernel, out_shape=(pltpu.VMEM((2, cells, lanes), jnp...  0.86 us
    pallas_call x1, Pallas kernels, shards(): pl.pallas_call(functools.partial(join_kernel, entry_count), out_shape=(ja...  0.72 us
  transfers between devices with their start and end apart: 5, of which 4 were waited for; matrix products, arithmetic and copies ran while one was open for 0% of the time, Pallas kernels for 6%

profile of v22, /device:TPU:0, one launch (start us, length us, event | category | flops | bytes accessed | tf_op | source)
XLA Modules:
  0.0 23.2 jit_solution(6013324708885971669)
XLA Ops:
  0.6 0.9 %stack_arrays.1 = (f32[2,64,128]{2,1,0:T(8,128)S(1)}, f32[2,64,128]{2,1,0:T(8,128)S(1)}) custom-call(f32[1,2,64,128]{3,2,1,0:T(8,128)} %forcing_hbm.1, f32[1,2,64,128]{3,2,1,0:T(8,128)} %previous_hbm.1), custom_call_target="tpu_custom_call" | custom-call | flops 4000 | bytes 500000 | tf_op jit(solution)/shard_map/stack_arrays/pallas_call | solution.py:324
  1.5 4.1 %collective-permute-start.1 = (f32[2,64,128]{2,1,0:T(8,128)S(1)}, f32[2,64,128]{2,1,0:T(8,128)S(1)}, u32[]{:S(2)}, u32[]{:S(2)}) collective-permute-start(f32[2,64,128]{2,1,0:T(8,128)S(1)} %get-tuple-element.12.refs_0_), channel_id=1, source_target_pairs={{0,16},{8,24},{16,0},{24,8},{1,17},{9,25},{17,1},{25,9},{2,18},{10... | collective-permute-start | bytes 196616 | tf_op jit(solution)/shard_map/ppermute | solution.py:303
  5.6 1.3 %collective-permute-start.2 = (f32[2,64,128]{2,1,0:T(8,128)S(1)}, f32[2,64,128]{2,1,0:T(8,128)S(1)}, u32[]{:S(2)}, u32[]{:S(2)}) collective-permute-start(f32[2,64,128]{2,1,0:T(8,128)S(1)} %get-tuple-element.13), channel_id=1, source_target_pairs={{0,24},{8,16},{16,8},{24,0},{1,25},{9,17},{17,9},{25,1},{2,26},{10... | collective-permute-start | bytes 196616 | tf_op jit(solution)/shard_map/ppermute | solution.py:303
  6.9 0.2 collective-permute-start
  7.2 1.3 %factor_lines.1 = (f32[4,6,64,128]{3,2,1,0:T(8,128)S(1)}, f32[4,3,64,128]{3,2,1,0:T(8,128)S(1)}, f32[64,128]{1,0:T(8,128)S(1)}) custom-call(f32[2,64,128]{2,1,0:T(8,128)} %initial_hbm.1, f32[2,8]{1,0:T(2,128)} %zones_hbm.1, f32[2]{0:T(128)} %drift_hbm.1, s32[1,128]{1,0:T(1,128)} %bitcast.3, s32[1,128]{1,0:T(1,128)} %bitcast.4, s32[64,128]{1,0:T(8,128)} %faces_hbm.1), custom_call_target="tpu_custom_call" | custom-call | flops 4000000 | bytes 3000000 | tf_op jit(solution)/shard_map/factor_lines/pallas_call | solution.py:340
  8.5 0.9 %collective-permute-done.1.refs_2_ = f32[2,64,128]{2,1,0:T(8,128)S(1)} collective-permute-done((f32[2,64,128]{2,1,0:T(8,128)S(1)}, f32[2,64,128]{2,1,0:T(8,128)S(1)}, u32[]{:S(2)}, u32[]{:S(2)}) %collective-permute-start.1) | collective-permute-done | bytes 65568 | tf_op jit(solution)/shard_map/ppermute | solution.py:303
  9.4 2.5 %collective-permute-done.2.refs_3_ = f32[2,64,128]{2,1,0:T(8,128)S(1)} collective-permute-done((f32[2,64,128]{2,1,0:T(8,128)S(1)}, f32[2,64,128]{2,1,0:T(8,128)S(1)}, u32[]{:S(2)}, u32[]{:S(2)}) %collective-permute-start.2) | collective-permute-done | bytes 65568 | tf_op jit(solution)/shard_map/ppermute | solution.py:303
  11.8 0.1 collective-permute-done.refs_1_
  11.9 0.9 %solve_lines.1 = (f32[64,128]{1,0:T(8,128)S(1)}, f32[64,128]{1,0:T(8,128)S(1)}, f32[16,8,128]{2,1,0:T(8,128)}) custom-call(f32[2,64,128]{2,1,0:T(8,128)S(1)} %get-tuple-element.12.refs_0_, f32[2,64,128]{2,1,0:T(8,128)S(1)} %collective-permute-done.refs_1_, f32[2,64,128]{2,1,0:T(8,128)S(1)} %collective-permute-done.1.refs_2_, ...), custom_call_target="tpu_custom_call" | custom-call | flops 4000000 | bytes 3000000 | tf_op jit(solution)/shard_map/solve_lines/pallas_call | solution.py:361
  12.8 5.7 %all-to-all-start = ((f32[16,8,128]{2,1,0:T(8,128)}), f32[16,8,128]{2,1,0:T(8,128)S(1)}, u32[]{:S(2)}, u32[]{:S(2)}) async-start(f32[16,8,128]{2,1,0:T(8,128)} %get-tuple-element.19), calls=%async_computation | async-start | bytes 131072 | tf_op jit(solution)/shard_map/all_to_all | solution.py:378
  18.5 0.5 %collective-permute-start.3 = (f32[64,128]{1,0:T(8,128)S(1)}, f32[64,128]{1,0:T(8,128)S(1)}, u32[]{:S(2)}, u32[]{:S(2)}) collective-permute-start(f32[64,128]{1,0:T(8,128)S(1)} %get-tuple-element.18), channel_id=1, source_target_pairs={{0,8},{8,0},{16,24},{24,16},{1,9},{9,1},{17,25},{25,17},{2,10},{10... | collective-permute-start | bytes 98312 | tf_op jit(solution)/shard_map/ppermute | solution.py:303
  19.0 3.5 %collective-permute-done.3.got_ref = f32[64,128]{1,0:T(8,128)S(1)} collective-permute-done((f32[64,128]{1,0:T(8,128)S(1)}, f32[64,128]{1,0:T(8,128)S(1)}, u32[]{:S(2)}, u32[]{:S(2)}) %collective-permute-start.3) | collective-permute-done | bytes 32800 | tf_op jit(solution)/shard_map/ppermute | solution.py:303
  22.4 0.0 all-to-all-done.squares_ref
  22.4 0.7 %join_species.1 = (f32[1,2,64,128]{3,2,1,0:T(8,128)}, f32[1,1]{1,0:T(1,128)}) custom-call(f32[64,128]{1,0:T(8,128)S(1)} %get-tuple-element.17.own_ref, f32[64,128]{1,0:T(8,128)S(1)} %collective-permute-done.3.got_ref, f32[16,8,128]{2,1,0:T(8,128)S(1)} %all-to-all-done.squares_ref), custom_call_target="tpu_custom_call" | custom-call | flops 4000 | bytes 100000 | tf_op jit(solution)/shard_map/join_species/pallas_call | solution.py:382
Async XLA Ops:
  1.5 7.9 %collective-permute-start.1 = (f32[2,64,128]{2,1,0:T(8,128)S(1)}, f32[2,64,128]{2,1,0:T(8,128)S(1)}, u32[]{:S(2)}, u32[]{:S(2)}) collective-permute-start(f32[2,64,128]{2,1,0:T(8,128)S(1)} %get-tuple-element.12.refs_0_), channel_id=1, source_target_pairs={{0,16},{8,24},{16,0},{24,8},{1,17},{9,25},{17,1},{25,9},{2,18},{10... | collective-permute-start | bytes 196616 | tf_op jit(solution)/shard_map/ppermute | solution.py:303
  5.6 6.2 %collective-permute-start.2 = (f32[2,64,128]{2,1,0:T(8,128)S(1)}, f32[2,64,128]{2,1,0:T(8,128)S(1)}, u32[]{:S(2)}, u32[]{:S(2)}) collective-permute-start(f32[2,64,128]{2,1,0:T(8,128)S(1)} %get-tuple-element.13), channel_id=1, source_target_pairs={{0,24},{8,16},{16,8},{24,0},{1,25},{9,17},{17,9},{25,1},{2,26},{10... | collective-permute-start | bytes 196616 | tf_op jit(solution)/shard_map/ppermute | solution.py:303
  6.9 5.0 %collective-permute-start = (f32[2,64,128]{2,1,0:T(8,128)S(1)}, f32[2,64,128]{2,1,0:T(8,128)S(1)}, u32[]{:S(2)}, u32[]{:S(2)}) collective-permute-start(f32[2,64,128]{2,1,0:T(8,128)S(1)} %get-tuple-element.13), channel_id=1, source_target_pairs={{0,8},{8,0},{16,24},{24,16},{1,9},{9,1},{17,25},{25,17},{2,10},{10... | collective-permute-start | bytes 196616 | tf_op jit(solution)/shard_map/ppermute | solution.py:303
  12.8 9.6 %all-to-all-start = ((f32[16,8,128]{2,1,0:T(8,128)}), f32[16,8,128]{2,1,0:T(8,128)S(1)}, u32[]{:S(2)}, u32[]{:S(2)}) async-start(f32[16,8,128]{2,1,0:T(8,128)} %get-tuple-element.19), calls=%async_computation | async-start | bytes 131072 | tf_op jit(solution)/shard_map/all_to_all | solution.py:378
  18.5 3.9 %collective-permute-start.3 = (f32[64,128]{1,0:T(8,128)S(1)}, f32[64,128]{1,0:T(8,128)S(1)}, u32[]{:S(2)}, u32[]{:S(2)}) collective-permute-start(f32[64,128]{1,0:T(8,128)S(1)} %get-tuple-element.18), channel_id=1, source_target_pairs={{0,8},{8,0},{16,24},{24,16},{1,9},{9,1},{17,25},{25,17},{2,10},{10... | collective-permute-start | bytes 98312 | tf_op jit(solution)/shard_map/ppermute | solution.py:303

commit v23 on v10

--- a/solution.py
+++ b/solution.py
@@ -278,7 +278,12 @@
             give = jnp.where(me == n, steps[n ^ 1], give)
         own_ref[rows] = own
         give_ref[rows] = give
-    sum_ref[...] = jnp.broadcast_to(jnp.sum(total, axis=0, keepdims=True), sum_ref.shape)
+    row = jnp.sum(total, axis=0, keepdims=True)
+    shift = lanes // 2
+    while shift >= tile:
+        row = row + pltpu.roll(row, shift, 1)
+        shift //= 2
+    sum_ref[...] = jnp.broadcast_to(row[:, :tile], sum_ref.shape)
 
 
 def join_kernel(
@@ -363,7 +368,7 @@
         out_shape=(
             pltpu.VMEM((cells, lanes), jnp.float32),
             pltpu.VMEM((cells, lanes), jnp.float32),
-            pltpu.VMEM((2 * space, 1, lanes), jnp.float32),
+            pltpu.VMEM((2 * space, 1, tile), jnp.float32),
         ),
         in_specs=[whole] * (length + 3),
         out_specs=[whole] * 3,

time: 21.3 us -> 21.5 us (level)
  Pallas kernels: 3.15 us -> 3.43 us
    pallas_call x1, Pallas kernels: 0.28 us -> 0.55 us  [shards(): pl.pallas_call(functools.partial(sweep_kernel, length), out_shape=(pltpu....]
where the time goes in v23:
time: 21.5 us; the launch traced here: 21.2 us
  blocking collectives  7.27 us (34%)
  starting transfers between devices  6.44 us (30%)
  Pallas kernels  3.43 us (16%)
  waiting for transfers between devices  3.43 us (16%)
  between operations  0.65 us (3%)
    all_to_all x1, blocking collectives, shards(): lax.all_to_all(squares, ('tm', 'space'), 0, 0, axis_index_groups=groups,...  7.27 us
    ppermute x4, starting transfers between devices, exchange(): return lax.ppermute(value, axis, pairs)  6.44 us
    ppermute x4, waiting for transfers between devices, exchange(): return lax.ppermute(value, axis, pairs)  3.43 us
    pallas_call x1, Pallas kernels, shards(): pl.pallas_call(functools.partial(factor_kernel, length), out_shape=(pltpu...  1.3 us
    pallas_call x1, Pallas kernels, shards(): pl.pallas_call(stack_kernel, out_shape=(pltpu.VMEM((2, cells, lanes), jnp...  0.86 us
    pallas_call x1, Pallas kernels, shards(): pl.pallas_call(functools.partial(join_kernel, entry_count), out_shape=(ja...  0.72 us
    pallas_call x1, Pallas kernels, shards(): pl.pallas_call(functools.partial(sweep_kernel, length), out_shape=(pltpu....  0.55 us
  transfers between devices with their start and end apart: 4, of which 3 were waited for; matrix products, arithmetic and copies ran while one was open for 0% of the time, Pallas kernels for 6%

profile of v23, /device:TPU:0, one launch (start us, length us, event | category | flops | bytes accessed | tf_op | source)
XLA Modules:
  0.0 21.2 jit_solution(4222610105145836848)
XLA Ops:
  0.6 0.9 %stack_arrays.1 = (f32[2,64,128]{2,1,0:T(8,128)S(1)}, f32[2,64,128]{2,1,0:T(8,128)S(1)}) custom-call(f32[1,2,64,128]{3,2,1,0:T(8,128)} %forcing_hbm.1, f32[1,2,64,128]{3,2,1,0:T(8,128)} %previous_hbm.1), custom_call_target="tpu_custom_call" | custom-call | flops 4000 | bytes 500000 | tf_op jit(solution)/shard_map/stack_arrays/pallas_call | solution.py:329
  1.5 4.1 %collective-permute-start.1 = (f32[2,64,128]{2,1,0:T(8,128)S(1)}, f32[2,64,128]{2,1,0:T(8,128)S(1)}, u32[]{:S(2)}, u32[]{:S(2)}) collective-permute-start(f32[2,64,128]{2,1,0:T(8,128)S(1)} %get-tuple-element.12.refs_0_), channel_id=1, source_target_pairs={{0,16},{8,24},{16,0},{24,8},{1,17},{9,25},{17,1},{25,9},{2,18},{10... | collective-permute-start | bytes 196616 | tf_op jit(solution)/shard_map/ppermute | solution.py:308
  5.6 1.3 %collective-permute-start.2 = (f32[2,64,128]{2,1,0:T(8,128)S(1)}, f32[2,64,128]{2,1,0:T(8,128)S(1)}, u32[]{:S(2)}, u32[]{:S(2)}) collective-permute-start(f32[2,64,128]{2,1,0:T(8,128)S(1)} %get-tuple-element.13), channel_id=1, source_target_pairs={{0,24},{8,16},{16,8},{24,0},{1,25},{9,17},{17,9},{25,1},{2,26},{10... | collective-permute-start | bytes 196616 | tf_op jit(solution)/shard_map/ppermute | solution.py:308
  6.9 0.2 %collective-permute-start = (f32[2,64,128]{2,1,0:T(8,128)S(1)}, f32[2,64,128]{2,1,0:T(8,128)S(1)}, u32[]{:S(2)}, u32[]{:S(2)}) collective-permute-start(f32[2,64,128]{2,1,0:T(8,128)S(1)} %get-tuple-element.13), channel_id=1, source_target_pairs={{0,8},{8,0},{16,24},{24,16},{1,9},{9,1},{17,25},{25,17},{2,10},{10... | collective-permute-start | bytes 196616 | tf_op jit(solution)/shard_map/ppermute | solution.py:308
  7.2 1.3 %factor_lines.1 = (f32[4,6,64,128]{3,2,1,0:T(8,128)S(1)}, f32[4,3,64,128]{3,2,1,0:T(8,128)S(1)}, f32[64,128]{1,0:T(8,128)S(1)}) custom-call(f32[2,64,128]{2,1,0:T(8,128)} %initial_hbm.1, f32[2,8]{1,0:T(2,128)} %zones_hbm.1, f32[2]{0:T(128)} %drift_hbm.1, s32[1,128]{1,0:T(1,128)} %bitcast.3, s32[1,128]{1,0:T(1,128)} %bitcast.4, s32[64,128]{1,0:T(8,128)} %faces_hbm.1), custom_call_target="tpu_custom_call" | custom-call | flops 4000000 | bytes 3000000 | tf_op jit(solution)/shard_map/factor_lines/pallas_call | solution.py:345
  8.5 0.9 %collective-permute-done.1.refs_2_ = f32[2,64,128]{2,1,0:T(8,128)S(1)} collective-permute-done((f32[2,64,128]{2,1,0:T(8,128)S(1)}, f32[2,64,128]{2,1,0:T(8,128)S(1)}, u32[]{:S(2)}, u32[]{:S(2)}) %collective-permute-start.1) | collective-permute-done | bytes 65568 | tf_op jit(solution)/shard_map/ppermute | solution.py:308
  9.4 2.5 %collective-permute-done.2.refs_3_ = f32[2,64,128]{2,1,0:T(8,128)S(1)} collective-permute-done((f32[2,64,128]{2,1,0:T(8,128)S(1)}, f32[2,64,128]{2,1,0:T(8,128)S(1)}, u32[]{:S(2)}, u32[]{:S(2)}) %collective-permute-start.2) | collective-permute-done | bytes 65568 | tf_op jit(solution)/shard_map/ppermute | solution.py:308
  11.8 0.1 collective-permute-done.refs_1_
  11.9 0.6 %solve_lines.1 = (f32[64,128]{1,0:T(8,128)S(1)}, f32[64,128]{1,0:T(8,128)S(1)}, f32[16,1,8]{2,1,0:T(1,128)S(1)}) custom-call(f32[2,64,128]{2,1,0:T(8,128)S(1)} %get-tuple-element.12.refs_0_, f32[2,64,128]{2,1,0:T(8,128)S(1)} %collective-permute-done.refs_1_, f32[2,64,128]{2,1,0:T(8,128)S(1)} %collective-permute-done.1.refs_2_, ...), custom_call_target="tpu_custom_call" | custom-call | flops 4000000 | bytes 3000000 | tf_op jit(solution)/shard_map/solve_lines/pallas_call | solution.py:366
  12.5 0.8 %collective-permute-start.3 = (f32[64,128]{1,0:T(8,128)S(1)}, f32[64,128]{1,0:T(8,128)S(1)}, u32[]{:S(2)}, u32[]{:S(2)}) collective-permute-start(f32[64,128]{1,0:T(8,128)S(1)} %get-tuple-element.18), channel_id=1, source_target_pairs={{0,8},{8,0},{16,24},{24,16},{1,9},{9,1},{17,25},{25,17},{2,10},{10... | collective-permute-start | bytes 98312 | tf_op jit(solution)/shard_map/ppermute | solution.py:308
  13.2 7.3 %all_to_all.5.squares_ref = f32[16,1,8]{2,1,0:T(1,128)S(1)} all-to-all(f32[16,1,8]{2,1,0:T(1,128)S(1)} %get-tuple-element.19), channel_id=1, replica_groups={{15,2,4,6,8,10,12,14,3,5,7,9,11,13,1,0},{31,18,20,22,24,26,28,30,19,21,..., dimensions={0} | all-to-all | bytes 1024 | tf_op jit(solution)/shard_map/all_to_all | solution.py:383
  20.5 0.0 collective-permute-done.3.got_ref
  20.5 0.7 %join_species.1 = (f32[1,2,64,128]{3,2,1,0:T(8,128)}, f32[1,1]{1,0:T(1,128)}) custom-call(f32[64,128]{1,0:T(8,128)S(1)} %get-tuple-element.17.own_ref, f32[64,128]{1,0:T(8,128)S(1)} %collective-permute-done.3.got_ref, f32[16,1,8]{2,1,0:T(1,128)S(1)} %all_to_all.5.squares_ref), custom_call_target="tpu_custom_call" | custom-call | flops 4000 | bytes 100000 | tf_op jit(solution)/shard_map/join_species/pallas_call | solution.py:387
Async XLA Ops:
  1.5 7.9 %collective-permute-start.1 = (f32[2,64,128]{2,1,0:T(8,128)S(1)}, f32[2,64,128]{2,1,0:T(8,128)S(1)}, u32[]{:S(2)}, u32[]{:S(2)}) collective-permute-start(f32[2,64,128]{2,1,0:T(8,128)S(1)} %get-tuple-element.12.refs_0_), channel_id=1, source_target_pairs={{0,16},{8,24},{16,0},{24,8},{1,17},{9,25},{17,1},{25,9},{2,18},{10... | collective-permute-start | bytes 196616 | tf_op jit(solution)/shard_map/ppermute | solution.py:308
  5.6 6.2 %collective-permute-start.2 = (f32[2,64,128]{2,1,0:T(8,128)S(1)}, f32[2,64,128]{2,1,0:T(8,128)S(1)}, u32[]{:S(2)}, u32[]{:S(2)}) collective-permute-start(f32[2,64,128]{2,1,0:T(8,128)S(1)} %get-tuple-element.13), channel_id=1, source_target_pairs={{0,24},{8,16},{16,8},{24,0},{1,25},{9,17},{17,9},{25,1},{2,26},{10... | collective-permute-start | bytes 196616 | tf_op jit(solution)/shard_map/ppermute | solution.py:308
  6.9 5.0 %collective-permute-start = (f32[2,64,128]{2,1,0:T(8,128)S(1)}, f32[2,64,128]{2,1,0:T(8,128)S(1)}, u32[]{:S(2)}, u32[]{:S(2)}) collective-permute-start(f32[2,64,128]{2,1,0:T(8,128)S(1)} %get-tuple-element.13), channel_id=1, source_target_pairs={{0,8},{8,0},{16,24},{24,16},{1,9},{9,1},{17,25},{25,17},{2,10},{10... | collective-permute-start | bytes 196616 | tf_op jit(solution)/shard_map/ppermute | solution.py:308
  12.5 8.0 %collective-permute-start.3 = (f32[64,128]{1,0:T(8,128)S(1)}, f32[64,128]{1,0:T(8,128)S(1)}, u32[]{:S(2)}, u32[]{:S(2)}) collective-permute-start(f32[64,128]{1,0:T(8,128)S(1)} %get-tuple-element.18), channel_id=1, source_target_pairs={{0,8},{8,0},{16,24},{24,16},{1,9},{9,1},{17,25},{25,17},{2,10},{10... | collective-permute-start | bytes 98312 | tf_op jit(solution)/shard_map/ppermute | solution.py:308

commit v24 on v10

--- a/solution.py
+++ b/solution.py
@@ -363,7 +363,7 @@
         out_shape=(
             pltpu.VMEM((cells, lanes), jnp.float32),
             pltpu.VMEM((cells, lanes), jnp.float32),
-            pltpu.VMEM((2 * space, 1, lanes), jnp.float32),
+            pltpu.VMEM((2 * space, lanes), jnp.float32),
         ),
         in_specs=[whole] * (length + 3),
         out_specs=[whole] * 3,

time: 21.3 us -> 21.3 us (level)
  no operation moved by 1% of the time
where the time goes in v24:
time: 21.3 us; the launch traced here: 21 us
  blocking collectives  7.27 us (34%)
  starting transfers between devices  6.5 us (31%)
  waiting for transfers between devices  3.43 us (16%)
  Pallas kernels  3.13 us (15%)
  between operations  0.65 us (3%)
    all_to_all x1, blocking collectives, shards(): lax.all_to_all(squares, ('tm', 'space'), 0, 0, axis_index_groups=groups,...  7.27 us
    ppermute x4, starting transfers between devices, exchange(): return lax.ppermute(value, axis, pairs)  6.5 us
    ppermute x4, waiting for transfers between devices, exchange(): return lax.ppermute(value, axis, pairs)  3.43 us
    pallas_call x1, Pallas kernels, shards(): pl.pallas_call(functools.partial(factor_kernel, length), out_shape=(pltpu...  1.3 us
    pallas_call x1, Pallas kernels, shards(): pl.pallas_call(stack_kernel, out_shape=(pltpu.VMEM((2, cells, lanes), jnp...  0.86 us
    pallas_call x1, Pallas kernels, shards(): pl.pallas_call(functools.partial(join_kernel, entry_count), out_shape=(ja...  0.7 us
  transfers between devices with their start and end apart: 4, of which 3 were waited for; matrix products, arithmetic and copies ran while one was open for 0% of the time, Pallas kernels for 6%

profile of v24, /device:TPU:0, one launch (start us, length us, event | category | flops | bytes accessed | tf_op | source)
XLA Modules:
  0.0 21.0 jit_solution(7553700279364962691)
XLA Ops:
  0.6 0.9 %stack_arrays.1 = (f32[2,64,128]{2,1,0:T(8,128)S(1)}, f32[2,64,128]{2,1,0:T(8,128)S(1)}) custom-call(f32[1,2,64,128]{3,2,1,0:T(8,128)} %forcing_hbm.1, f32[1,2,64,128]{3,2,1,0:T(8,128)} %previous_hbm.1), custom_call_target="tpu_custom_call" | custom-call | flops 4000 | bytes 500000 | tf_op jit(solution)/shard_map/stack_arrays/pallas_call | solution.py:324
  1.5 4.1 %collective-permute-start.1 = (f32[2,64,128]{2,1,0:T(8,128)S(1)}, f32[2,64,128]{2,1,0:T(8,128)S(1)}, u32[]{:S(2)}, u32[]{:S(2)}) collective-permute-start(f32[2,64,128]{2,1,0:T(8,128)S(1)} %get-tuple-element.12.refs_0_), channel_id=1, source_target_pairs={{0,16},{8,24},{16,0},{24,8},{1,17},{9,25},{17,1},{25,9},{2,18},{10... | collective-permute-start | bytes 196616 | tf_op jit(solution)/shard_map/ppermute | solution.py:303
  5.6 1.3 %collective-permute-start.2 = (f32[2,64,128]{2,1,0:T(8,128)S(1)}, f32[2,64,128]{2,1,0:T(8,128)S(1)}, u32[]{:S(2)}, u32[]{:S(2)}) collective-permute-start(f32[2,64,128]{2,1,0:T(8,128)S(1)} %get-tuple-element.13), channel_id=1, source_target_pairs={{0,24},{8,16},{16,8},{24,0},{1,25},{9,17},{17,9},{25,1},{2,26},{10... | collective-permute-start | bytes 196616 | tf_op jit(solution)/shard_map/ppermute | solution.py:303
  6.9 0.2 %collective-permute-start = (f32[2,64,128]{2,1,0:T(8,128)S(1)}, f32[2,64,128]{2,1,0:T(8,128)S(1)}, u32[]{:S(2)}, u32[]{:S(2)}) collective-permute-start(f32[2,64,128]{2,1,0:T(8,128)S(1)} %get-tuple-element.13), channel_id=1, source_target_pairs={{0,8},{8,0},{16,24},{24,16},{1,9},{9,1},{17,25},{25,17},{2,10},{10... | collective-permute-start | bytes 196616 | tf_op jit(solution)/shard_map/ppermute | solution.py:303
  7.2 1.3 %factor_lines.1 = (f32[4,6,64,128]{3,2,1,0:T(8,128)S(1)}, f32[4,3,64,128]{3,2,1,0:T(8,128)S(1)}, f32[64,128]{1,0:T(8,128)S(1)}) custom-call(f32[2,64,128]{2,1,0:T(8,128)} %initial_hbm.1, f32[2,8]{1,0:T(2,128)} %zones_hbm.1, f32[2]{0:T(128)} %drift_hbm.1, s32[1,128]{1,0:T(1,128)} %bitcast.9, s32[1,128]{1,0:T(1,128)} %bitcast.10, s32[64,128]{1,0:T(8,128)} %faces_hbm.1), custom_call_target="tpu_custom_call" | custom-call | flops 4000000 | bytes 3000000 | tf_op jit(solution)/shard_map/factor_lines/pallas_call | solution.py:340
  8.5 0.9 %collective-permute-done.1.refs_2_ = f32[2,64,128]{2,1,0:T(8,128)S(1)} collective-permute-done((f32[2,64,128]{2,1,0:T(8,128)S(1)}, f32[2,64,128]{2,1,0:T(8,128)S(1)}, u32[]{:S(2)}, u32[]{:S(2)}) %collective-permute-start.1) | collective-permute-done | bytes 65568 | tf_op jit(solution)/shard_map/ppermute | solution.py:303
  9.4 2.5 %collective-permute-done.2.refs_3_ = f32[2,64,128]{2,1,0:T(8,128)S(1)} collective-permute-done((f32[2,64,128]{2,1,0:T(8,128)S(1)}, f32[2,64,128]{2,1,0:T(8,128)S(1)}, u32[]{:S(2)}, u32[]{:S(2)}) %collective-permute-start.2) | collective-permute-done | bytes 65568 | tf_op jit(solution)/shard_map/ppermute | solution.py:303
  11.8 0.1 collective-permute-done.refs_1_
  11.9 0.3 %solve_lines.1 = (f32[64,128]{1,0:T(8,128)S(1)}, f32[64,128]{1,0:T(8,128)S(1)}, f32[16,128]{1,0:T(8,128)S(1)}) custom-call(f32[2,64,128]{2,1,0:T(8,128)S(1)} %get-tuple-element.12.refs_0_, f32[2,64,128]{2,1,0:T(8,128)S(1)} %collective-permute-done.refs_1_, f32[2,64,128]{2,1,0:T(8,128)S(1)} %collective-permute-done.1.refs_2_, ...), custom_call_target="tpu_custom_call" | custom-call | flops 4000000 | bytes 3000000 | tf_op jit(solution)/shard_map/solve_lines/pallas_call | solution.py:361
  12.2 0.8 %collective-permute-start.3 = (f32[64,128]{1,0:T(8,128)S(1)}, f32[64,128]{1,0:T(8,128)S(1)}, u32[]{:S(2)}, u32[]{:S(2)}) collective-permute-start(f32[64,128]{1,0:T(8,128)S(1)} %get-tuple-element.18), channel_id=1, source_target_pairs={{0,8},{8,0},{16,24},{24,16},{1,9},{9,1},{17,25},{25,17},{2,10},{10... | collective-permute-start | bytes 98312 | tf_op jit(solution)/shard_map/ppermute | solution.py:303
  13.0 7.3 %all_to_all.11 = f32[16,1,128]{2,1,0:T(1,128)S(1)} all-to-all(f32[16,1,128]{2,1,0:T(1,128)S(1)} %bitcast.8), channel_id=1, replica_groups={{15,2,4,6,8,10,12,14,3,5,7,9,11,13,1,0},{31,18,20,22,24,26,28,30,19,21,..., dimensions={0} | all-to-all | bytes 16384 | tf_op jit(solution)/shard_map/all_to_all | solution.py:378
  20.3 0.0 collective-permute-done.3.got_ref
  20.3 0.7 %join_species.1 = (f32[1,2,64,128]{3,2,1,0:T(8,128)}, f32[1,1]{1,0:T(1,128)}) custom-call(f32[64,128]{1,0:T(8,128)S(1)} %get-tuple-element.17.own_ref, f32[64,128]{1,0:T(8,128)S(1)} %collective-permute-done.3.got_ref, f32[16,128]{1,0:T(8,128)S(1)} %bitcast.7), custom_call_target="tpu_custom_call" | custom-call | flops 4000 | bytes 100000 | tf_op jit(solution)/shard_map/join_species/pallas_call | solution.py:382
Async XLA Ops:
  1.5 7.9 %collective-permute-start.1 = (f32[2,64,128]{2,1,0:T(8,128)S(1)}, f32[2,64,128]{2,1,0:T(8,128)S(1)}, u32[]{:S(2)}, u32[]{:S(2)}) collective-permute-start(f32[2,64,128]{2,1,0:T(8,128)S(1)} %get-tuple-element.12.refs_0_), channel_id=1, source_target_pairs={{0,16},{8,24},{16,0},{24,8},{1,17},{9,25},{17,1},{25,9},{2,18},{10... | collective-permute-start | bytes 196616 | tf_op jit(solution)/shard_map/ppermute | solution.py:303
  5.6 6.2 %collective-permute-start.2 = (f32[2,64,128]{2,1,0:T(8,128)S(1)}, f32[2,64,128]{2,1,0:T(8,128)S(1)}, u32[]{:S(2)}, u32[]{:S(2)}) collective-permute-start(f32[2,64,128]{2,1,0:T(8,128)S(1)} %get-tuple-element.13), channel_id=1, source_target_pairs={{0,24},{8,16},{16,8},{24,0},{1,25},{9,17},{17,9},{25,1},{2,26},{10... | collective-permute-start | bytes 196616 | tf_op jit(solution)/shard_map/ppermute | solution.py:303
  6.9 5.0 %collective-permute-start = (f32[2,64,128]{2,1,0:T(8,128)S(1)}, f32[2,64,128]{2,1,0:T(8,128)S(1)}, u32[]{:S(2)}, u32[]{:S(2)}) collective-permute-start(f32[2,64,128]{2,1,0:T(8,128)S(1)} %get-tuple-element.13), channel_id=1, source_target_pairs={{0,8},{8,0},{16,24},{24,16},{1,9},{9,1},{17,25},{25,17},{2,10},{10... | collective-permute-start | bytes 196616 | tf_op jit(solution)/shard_map/ppermute | solution.py:303
  12.2 8.1 %collective-permute-start.3 = (f32[64,128]{1,0:T(8,128)S(1)}, f32[64,128]{1,0:T(8,128)S(1)}, u32[]{:S(2)}, u32[]{:S(2)}) collective-permute-start(f32[64,128]{1,0:T(8,128)S(1)} %get-tuple-element.18), channel_id=1, source_target_pairs={{0,8},{8,0},{16,24},{24,16},{1,9},{9,1},{17,25},{25,17},{2,10},{10... | collective-permute-start | bytes 98312 | tf_op jit(solution)/shard_map/ppermute | solution.py:303

commit v25 on v10

--- a/solution.py
+++ b/solution.py
@@ -292,7 +292,7 @@
     )
     copies[0].start()
     copies[1].start()
-    norm_ref[0, 0] = jnp.sqrt(jnp.sum(squares_ref[...]) / entry_count)
+    norm_ref[0, 0] = jnp.sqrt(jnp.sum(squares_ref[...]) * (1.0 / entry_count))
     copies[2].start()
     for copy in copies:
         copy.wait()

time: 21.3 us -> 21.3 us (level)
  no operation moved by 1% of the time
where the time goes in v25:
time: 21.3 us; the launch traced here: 21 us
  blocking collectives  7.27 us (34%)
  starting transfers between devices  6.5 us (31%)
  waiting for transfers between devices  3.43 us (16%)
  Pallas kernels  3.15 us (15%)
  between operations  0.65 us (3%)
    all_to_all x1, blocking collectives, shards(): lax.all_to_all(squares, ('tm', 'space'), 0, 0, axis_index_groups=groups,...  7.27 us
    ppermute x4, starting transfers between devices, exchange(): return lax.ppermute(value, axis, pairs)  6.5 us
    ppermute x4, waiting for transfers between devices, exchange(): return lax.ppermute(value, axis, pairs)  3.43 us
    pallas_call x1, Pallas kernels, shards(): pl.pallas_call(functools.partial(factor_kernel, length), out_shape=(pltpu...  1.3 us
    pallas_call x1, Pallas kernels, shards(): pl.pallas_call(stack_kernel, out_shape=(pltpu.VMEM((2, cells, lanes), jnp...  0.86 us
    pallas_call x1, Pallas kernels, shards(): pl.pallas_call(functools.partial(join_kernel, entry_count), out_shape=(ja...  0.72 us
  transfers between devices with their start and end apart: 4, of which 3 were waited for; matrix products, arithmetic and copies ran while one was open for 0% of the time, Pallas kernels for 6%

profile of v25, /device:TPU:0, one launch (start us, length us, event | category | flops | bytes accessed | tf_op | source)
XLA Modules:
  0.0 21.0 jit_solution(7203347970583995086)
XLA Ops:
  0.6 0.9 %stack_arrays.1 = (f32[2,64,128]{2,1,0:T(8,128)S(1)}, f32[2,64,128]{2,1,0:T(8,128)S(1)}) custom-call(f32[1,2,64,128]{3,2,1,0:T(8,128)} %forcing_hbm.1, f32[1,2,64,128]{3,2,1,0:T(8,128)} %previous_hbm.1), custom_call_target="tpu_custom_call" | custom-call | flops 4000 | bytes 500000 | tf_op jit(solution)/shard_map/stack_arrays/pallas_call | solution.py:324
  1.5 4.1 %collective-permute-start.1 = (f32[2,64,128]{2,1,0:T(8,128)S(1)}, f32[2,64,128]{2,1,0:T(8,128)S(1)}, u32[]{:S(2)}, u32[]{:S(2)}) collective-permute-start(f32[2,64,128]{2,1,0:T(8,128)S(1)} %get-tuple-element.12.refs_0_), channel_id=1, source_target_pairs={{0,16},{8,24},{16,0},{24,8},{1,17},{9,25},{17,1},{25,9},{2,18},{10... | collective-permute-start | bytes 196616 | tf_op jit(solution)/shard_map/ppermute | solution.py:303
  5.6 1.3 %collective-permute-start.2 = (f32[2,64,128]{2,1,0:T(8,128)S(1)}, f32[2,64,128]{2,1,0:T(8,128)S(1)}, u32[]{:S(2)}, u32[]{:S(2)}) collective-permute-start(f32[2,64,128]{2,1,0:T(8,128)S(1)} %get-tuple-element.13), channel_id=1, source_target_pairs={{0,24},{8,16},{16,8},{24,0},{1,25},{9,17},{17,9},{25,1},{2,26},{10... | collective-permute-start | bytes 196616 | tf_op jit(solution)/shard_map/ppermute | solution.py:303
  6.9 0.2 %collective-permute-start = (f32[2,64,128]{2,1,0:T(8,128)S(1)}, f32[2,64,128]{2,1,0:T(8,128)S(1)}, u32[]{:S(2)}, u32[]{:S(2)}) collective-permute-start(f32[2,64,128]{2,1,0:T(8,128)S(1)} %get-tuple-element.13), channel_id=1, source_target_pairs={{0,8},{8,0},{16,24},{24,16},{1,9},{9,1},{17,25},{25,17},{2,10},{10... | collective-permute-start | bytes 196616 | tf_op jit(solution)/shard_map/ppermute | solution.py:303
  7.2 1.3 %factor_lines.1 = (f32[4,6,64,128]{3,2,1,0:T(8,128)S(1)}, f32[4,3,64,128]{3,2,1,0:T(8,128)S(1)}, f32[64,128]{1,0:T(8,128)S(1)}) custom-call(f32[2,64,128]{2,1,0:T(8,128)} %initial_hbm.1, f32[2,8]{1,0:T(2,128)} %zones_hbm.1, f32[2]{0:T(128)} %drift_hbm.1, s32[1,128]{1,0:T(1,128)} %bitcast.3, s32[1,128]{1,0:T(1,128)} %bitcast.4, s32[64,128]{1,0:T(8,128)} %faces_hbm.1), custom_call_target="tpu_custom_call" | custom-call | flops 4000000 | bytes 3000000 | tf_op jit(solution)/shard_map/factor_lines/pallas_call | solution.py:340
  8.5 0.9 %collective-permute-done.1.refs_2_ = f32[2,64,128]{2,1,0:T(8,128)S(1)} collective-permute-done((f32[2,64,128]{2,1,0:T(8,128)S(1)}, f32[2,64,128]{2,1,0:T(8,128)S(1)}, u32[]{:S(2)}, u32[]{:S(2)}) %collective-permute-start.1) | collective-permute-done | bytes 65568 | tf_op jit(solution)/shard_map/ppermute | solution.py:303
  9.4 2.5 %collective-permute-done.2.refs_3_ = f32[2,64,128]{2,1,0:T(8,128)S(1)} collective-permute-done((f32[2,64,128]{2,1,0:T(8,128)S(1)}, f32[2,64,128]{2,1,0:T(8,128)S(1)}, u32[]{:S(2)}, u32[]{:S(2)}) %collective-permute-start.2) | collective-permute-done | bytes 65568 | tf_op jit(solution)/shard_map/ppermute | solution.py:303
  11.8 0.1 collective-permute-done.refs_1_
  11.9 0.3 %solve_lines.1 = (f32[64,128]{1,0:T(8,128)S(1)}, f32[64,128]{1,0:T(8,128)S(1)}, f32[16,1,128]{2,1,0:T(1,128)S(1)}) custom-call(f32[2,64,128]{2,1,0:T(8,128)S(1)} %get-tuple-element.12.refs_0_, f32[2,64,128]{2,1,0:T(8,128)S(1)} %collective-permute-done.refs_1_, f32[2,64,128]{2,1,0:T(8,128)S(1)} %collective-permute-done.1.refs_2_, ...), custom_call_target="tpu_custom_call" | custom-call | flops 4000000 | bytes 3000000 | tf_op jit(solution)/shard_map/solve_lines/pallas_call | solution.py:361
  12.2 0.8 %collective-permute-start.3 = (f32[64,128]{1,0:T(8,128)S(1)}, f32[64,128]{1,0:T(8,128)S(1)}, u32[]{:S(2)}, u32[]{:S(2)}) collective-permute-start(f32[64,128]{1,0:T(8,128)S(1)} %get-tuple-element.18), channel_id=1, source_target_pairs={{0,8},{8,0},{16,24},{24,16},{1,9},{9,1},{17,25},{25,17},{2,10},{10... | collective-permute-start | bytes 98312 | tf_op jit(solution)/shard_map/ppermute | solution.py:303
  13.0 7.3 %all_to_all.5.squares_ref = f32[16,1,128]{2,1,0:T(1,128)S(1)} all-to-all(f32[16,1,128]{2,1,0:T(1,128)S(1)} %get-tuple-element.19), channel_id=1, replica_groups={{15,2,4,6,8,10,12,14,3,5,7,9,11,13,1,0},{31,18,20,22,24,26,28,30,19,21,..., dimensions={0} | all-to-all | bytes 16384 | tf_op jit(solution)/shard_map/all_to_all | solution.py:378
  20.3 0.0 collective-permute-done.3.got_ref
  20.3 0.7 %join_species.1 = (f32[1,2,64,128]{3,2,1,0:T(8,128)}, f32[1,1]{1,0:T(1,128)}) custom-call(f32[64,128]{1,0:T(8,128)S(1)} %get-tuple-element.17.own_ref, f32[64,128]{1,0:T(8,128)S(1)} %collective-permute-done.3.got_ref, f32[16,1,128]{2,1,0:T(1,128)S(1)} %all_to_all.5.squares_ref), custom_call_target="tpu_custom_call" | custom-call | flops 4000 | bytes 100000 | tf_op jit(solution)/shard_map/join_species/pallas_call | solution.py:382
Async XLA Ops:
  1.5 7.9 %collective-permute-start.1 = (f32[2,64,128]{2,1,0:T(8,128)S(1)}, f32[2,64,128]{2,1,0:T(8,128)S(1)}, u32[]{:S(2)}, u32[]{:S(2)}) collective-permute-start(f32[2,64,128]{2,1,0:T(8,128)S(1)} %get-tuple-element.12.refs_0_), channel_id=1, source_target_pairs={{0,16},{8,24},{16,0},{24,8},{1,17},{9,25},{17,1},{25,9},{2,18},{10... | collective-permute-start | bytes 196616 | tf_op jit(solution)/shard_map/ppermute | solution.py:303
  5.6 6.2 %collective-permute-start.2 = (f32[2,64,128]{2,1,0:T(8,128)S(1)}, f32[2,64,128]{2,1,0:T(8,128)S(1)}, u32[]{:S(2)}, u32[]{:S(2)}) collective-permute-start(f32[2,64,128]{2,1,0:T(8,128)S(1)} %get-tuple-element.13), channel_id=1, source_target_pairs={{0,24},{8,16},{16,8},{24,0},{1,25},{9,17},{17,9},{25,1},{2,26},{10... | collective-permute-start | bytes 196616 | tf_op jit(solution)/shard_map/ppermute | solution.py:303
  6.9 5.0 %collective-permute-start = (f32[2,64,128]{2,1,0:T(8,128)S(1)}, f32[2,64,128]{2,1,0:T(8,128)S(1)}, u32[]{:S(2)}, u32[]{:S(2)}) collective-permute-start(f32[2,64,128]{2,1,0:T(8,128)S(1)} %get-tuple-element.13), channel_id=1, source_target_pairs={{0,8},{8,0},{16,24},{24,16},{1,9},{9,1},{17,25},{25,17},{2,10},{10... | collective-permute-start | bytes 196616 | tf_op jit(solution)/shard_map/ppermute | solution.py:303
  12.2 8.1 %collective-permute-start.3 = (f32[64,128]{1,0:T(8,128)S(1)}, f32[64,128]{1,0:T(8,128)S(1)}, u32[]{:S(2)}, u32[]{:S(2)}) collective-permute-start(f32[64,128]{1,0:T(8,128)S(1)} %get-tuple-element.18), channel_id=1, source_target_pairs={{0,8},{8,0},{16,24},{24,16},{1,9},{9,1},{17,25},{25,17},{2,10},{10... | collective-permute-start | bytes 98312 | tf_op jit(solution)/shard_map/ppermute | solution.py:303
